TPU v7x, 32 devices: a whole 2x2x4 slice. The times are simulated.
32 devices in a mesh: groups: 2 (over x), row: 8 (over z, y), col: 2 (over core).
Axes of the slice: x: 2, y: 2, z: 4, core: 2. Of those that a mesh axis runs over, the one named last changes fastest.
Arguments:
- points_x: bfloat16 [32768, 96], P(('groups', 'row', 'col')), parts along dimension 0, may hold values from -24 to 24
- points_y: bfloat16 [2048, 96], P(('groups', 'col', 'row')), parts along dimension 0, may hold values from -6 to 6
- mass_x: bfloat16 [32768], P(('groups', 'row', 'col')), parts along dimension 0, may hold values from -1 to 1
- mass_y: bfloat16 [2048], P(('groups', 'col', 'row')), parts along dimension 0, may hold values from -1 to 1
Outputs:
- f_potential: float32 [32768], P(('groups', 'row', 'col')), parts along dimension 0
- g_potential: float32 [2048], P(('groups', 'col', 'row')), parts along dimension 0
- grad_x: float32 [32768, 96], P(('groups', 'row', 'col')), parts along dimension 0
- grad_y: float32 [2048, 96], P(('groups', 'col', 'row')), parts along dimension 0
There are 2 independent parts, one for each index of `groups`. A program takes and returns all parts, laid end to end along the dimension named above; each array names one. Nothing has to cross between parts.
All inputs are finite; a program needn't handle non-finite values.
Results may differ from a plain program's by a relative error of at most 0.003.
Values may be sent and summed in bfloat16 or wider, within the bound.
No kernel may reach another device: no remote copies, remote signals or barrier semaphores. Data moves between devices by JAX's collectives and lax.ppermute only.
A program may use at most 64 MiB of HBM per device.

v0:
```python
import math

import jax
import jax.numpy as jnp
from jax import lax
from jax.sharding import PartitionSpec as P

ITERS = 2


epsilon = 0.02


def cost_block(xb, yv):
    xf = xb.astype(jnp.float32)
    yf = yv.astype(jnp.float32)
    xn = jnp.sum(xf * xf, axis=1)
    yn = jnp.sum(yf * yf, axis=1)
    cross = jnp.dot(xb, yv.T, preferred_element_type=jnp.float32)
    return (xn[:, None] + yn[None, :] - 2.0 * cross) * (1.0 / xb.shape[1])


def row_pass(blocks, y_rows, log_b, g_pot):

    def row_fn(xb):
        scores = log_b[None, :] + (g_pot[None, :] - cost_block(xb, y_rows)) / epsilon
        peak = jnp.max(scores, axis=1)
        total = jnp.sum(jnp.exp(scores - peak[:, None]), axis=1)
        return (peak, total)

    peak, total = lax.map(row_fn, blocks)
    peak = peak.reshape(-1)
    total = total.reshape(-1)
    whole = lax.pmax(peak, "col")
    total = lax.psum(total * jnp.exp(peak - whole), "col")
    peak = whole
    return -epsilon * (peak + jnp.log(total))


def column_pass(blocks, log_blocks, f_blocks, y_rows):
    width = y_rows.shape[0]

    def col_fn(carry, item):
        peak, total = carry
        xb, lab, fb = item
        scores = lab[:, None] + (fb[:, None] - cost_block(xb, y_rows)) / epsilon
        newpk = jnp.maximum(peak, jnp.max(scores, axis=0))
        total = total * jnp.exp(peak - newpk) + jnp.sum(jnp.exp(scores - newpk[None, :]), axis=0)
        return ((newpk, total), None)

    init = (jnp.full((width,), -jnp.inf, jnp.float32), jnp.zeros((width,), jnp.float32))
    (peak, total), unused = lax.scan(col_fn, init, (blocks, log_blocks, f_blocks))
    whole = lax.pmax(peak, "row")
    total = lax.psum(total * jnp.exp(peak - whole), "row")
    return -epsilon * (whole + jnp.log(total))


def weight_tile(xb, mb, fb, y_part, my_part, g_part):
    cost = cost_block(xb, y_part)
    return jnp.exp(
        mb[:, None] + my_part[None, :] + (fb[:, None] + g_part[None, :] - cost) / epsilon
    )


def on_device(points_x, points_y, mass_x, mass_y):
    xdev, width_f = points_x.shape
    ydev = points_y.shape[0]
    nx_all = xdev * lax.axis_size("row") * lax.axis_size("col")
    ny_all = ydev * lax.axis_size("row") * lax.axis_size("col")
    x_rows, mx_rows = (
        lax.all_gather(points_x, "col", axis=0, tiled=True),
        lax.all_gather(mass_x, "col", axis=0, tiled=True),
    )
    y_rows, my_rows = (
        lax.all_gather(points_y, "row", axis=0, tiled=True),
        lax.all_gather(mass_y, "row", axis=0, tiled=True),
    )
    mx_float = mx_rows.astype(jnp.float32)
    my_float = my_rows.astype(jnp.float32)
    log_a = mx_float - math.log(nx_all)
    log_b = my_float - math.log(ny_all)
    rows_all = x_rows.shape[0]
    blk = min(512, rows_all)
    count = rows_all // blk
    blocks = x_rows.reshape(count, blk, width_f)
    log_blocks = log_a.reshape(count, blk)
    mass_blocks = mx_float.reshape(count, blk)
    g_pot = jnp.zeros((y_rows.shape[0],), jnp.float32)
    f_pot = jnp.zeros((rows_all,), jnp.float32)
    for step in range(ITERS):
        f_pot = row_pass(blocks, y_rows, log_b, g_pot)
        g_pot = column_pass(blocks, log_blocks, f_pot.reshape(count, blk), y_rows)
    yf = y_rows.astype(jnp.float32)
    f_blocks = f_pot.reshape(count, blk)

    def grad_fn(carry, item):
        xb, mb, fb = item
        weight = weight_tile(xb, mb, fb, y_rows, my_float, g_pot)
        wrows = jnp.sum(weight, axis=1)
        wcols = jnp.sum(weight, axis=0)
        wb = weight.astype(jnp.bfloat16)
        xf = xb.astype(jnp.float32)
        gx = xf * wrows[:, None] - jnp.dot(wb, y_rows, preferred_element_type=jnp.float32)
        back = lax.dot_general(wb, xb, (((0,), (0,)), ((), ())), preferred_element_type=jnp.float32)
        carry = carry + yf * wcols[:, None] - back
        return (carry, gx)

    gy_term, gx_term = lax.scan(
        grad_fn, jnp.zeros((y_rows.shape[0], width_f), jnp.float32), (blocks, mass_blocks, f_blocks)
    )
    grad_y = lax.psum_scatter(gy_term, "row", scatter_dimension=0, tiled=True) / nx_all
    grad_x = (
        lax.psum_scatter(gx_term.reshape(rows_all, width_f), "col", scatter_dimension=0, tiled=True)
        / ny_all
    )
    f_out = lax.dynamic_slice_in_dim(f_pot, lax.axis_index("col") * xdev, xdev)
    g_out = lax.dynamic_slice_in_dim(g_pot, lax.axis_index("row") * ydev, ydev)
    return (f_out, g_out, grad_x, grad_y)


def solution(mesh):
    in_specs = (
        P(("groups", "row", "col"), None),
        P(("groups", "col", "row"), None),
        P(("groups", "row", "col")),
        P(("groups", "col", "row")),
    )
    out_specs = (
        P(("groups", "row", "col")),
        P(("groups", "col", "row")),
        P(("groups", "row", "col"), None),
        P(("groups", "col", "row"), None),
    )
    return jax.shard_map(
        on_device, mesh=mesh, in_specs=in_specs, out_specs=out_specs, check_vma=False
    )
```

profile of v0, /device:TPU:0, one launch (start us, length us, event | category | flops | bytes accessed | tf_op | source)
XLA Modules:
  0.0 260.7 jit_solution(10680311961846017823)
XLA Ops:
  10.0 23.1 %all-reduce = bf16[512]{0:T(512)(128)(2,1)S(1)} all-reduce(bf16[512]{0:T(512)(128)(2,1)S(1)} %dynamic-update-slice), channel_id=1, replica_groups=mesh['groups'=2,'row'=8,'col'=2] {'row'}, use_global_device_ids=true, to_apply=%add | all-reduce | flops 512 | bytes 2048
  33.8 1.8 all_gather.13
  36.3 30.5 %all_gather.15 = bf16[512,96]{1,0:T(8,128)(2,1)S(1)} all-gather(bf16[64,96]{1,0:T(8,128)(2,1)S(1)} %copy-done.1), channel_id=1, replica_groups=mesh['groups'=2,'row'=8,'col'=2] {'row'}, dimensions={0}, use_global_device_ids=true | all-gather | bytes 110592 | tf_op jit(solution)/shard_map/all_gather | solution.py:75
  66.9 0.9 copy-done
  67.8 2.1 all_gather.14
  70.3 4.0 %while.63 = (s32[]{:T(128)}, f32[4,512]{1,0:T(4,128)S(1)}, f32[4,512]{1,0:T(4,128)S(1)}, f32[512]{0:T(512)S(1)}, bf16[4,512,96]{2,1,0:T(8,128)(2,1)S(1)}, /*index=5*/bf16[512,96]{1,0:T(8,128)(2,1)S(1)}, s32[]{:T(128)}, s32[]{:T(128)}) while((s32[]{:T(128)}, f32[4,512]{1,0:T(4,128)S(1)}, f32[4,512]{1,0:T(4,128)S(1)}, f32[512]{0:T(512)S(1)}, ...), condition=%wide.region_5.6_spmd, body=%wide.region_0.5_spmd.sunk | while | flops 53245952 | bytes 2580589 | solution.py:31
  74.3 2.5 pmax.28
  76.8 2.5 psum.28
  79.3 3.8 %while.65 = (s32[]{:T(128)}, f32[512]{0:T(512)S(1)}, f32[512]{0:T(512)S(1)}, f32[4,512]{1,0:T(4,128)S(1)}, f32[4,512]{1,0:T(4,128)S(1)}, /*index=5*/bf16[4,512,9...) while((s32[]{:T(128)}, f32[512]{0:T(512)S(1)}, f32[512]{0:T(512)S(1)}, ...), condition=%wide.region_13.14_spmd.clone, body=%wide.region_8.13_spmd.clone.sunk | while | flops 53249536 | bytes 2603132 | solution.py:52
  83.1 17.1 %pmax.29 = f32[512]{0:T(512)S(1)} all-reduce(f32[512]{0:T(512)S(1)} %get-tuple-element.206), channel_id=1, replica_groups=mesh['groups'=2,'row'=8,'col'=2] {'row'}, use_global_device_ids=true, to_apply=%region_14.15 | all-reduce | flops 512 | bytes 4096 | tf_op jit(solution)/shard_map/pmax | solution.py:53
  100.3 19.1 %psum.29 = f32[512]{0:T(512)S(1)} all-reduce(f32[512]{0:T(512)S(1)} %exponential_multiply_fusion.3), channel_id=1, replica_groups=mesh['groups'=2,'row'=8,'col'=2] {'row'}, use_global_device_ids=true, to_apply=%region_15.16 | all-reduce | flops 512 | bytes 4096 | tf_op jit(solution)/shard_map/psum | solution.py:54
  119.4 4.0 %while.64 = (s32[]{:T(128)}, f32[4,512]{1,0:T(4,128)S(1)}, f32[4,512]{1,0:T(4,128)S(1)}, f32[512]{0:T(512)S(1)}, f32[512]{0:T(512)S(1)}, /*index=5*/bf16[4,512,9...) while((s32[]{:T(128)}, f32[4,512]{1,0:T(4,128)S(1)}, f32[4,512]{1,0:T(4,128)S(1)}, ...), condition=%wide.region_21.22_spmd, body=%wide.region_16.21_spmd.sunk | while | flops 53245952 | bytes 2582645 | solution.py:31
  123.4 2.5 pmax.30
  126.0 2.5 psum.30
  128.5 3.8 %while.66 = (s32[]{:T(128)}, f32[512]{0:T(512)S(1)}, f32[512]{0:T(512)S(1)}, f32[4,512]{1,0:T(4,128)S(1)}, f32[4,512]{1,0:T(4,128)S(1)}, /*index=5*/bf16[4,512,9...) while((s32[]{:T(128)}, f32[512]{0:T(512)S(1)}, f32[512]{0:T(512)S(1)}, ...), condition=%wide.region_29.30_spmd.clone, body=%wide.region_24.29_spmd.clone.sunk | while | flops 53249536 | bytes 2603132 | solution.py:52
  132.3 17.1 %pmax.31 = f32[512]{0:T(512)S(1)} all-reduce(f32[512]{0:T(512)S(1)} %get-tuple-element.210), channel_id=1, replica_groups=mesh['groups'=2,'row'=8,'col'=2] {'row'}, use_global_device_ids=true, to_apply=%region_30.31 | all-reduce | flops 512 | bytes 4096 | tf_op jit(solution)/shard_map/pmax | solution.py:53
  149.5 19.1 %psum.31 = f32[512]{0:T(512)S(1)} all-reduce(f32[512]{0:T(512)S(1)} %exponential_multiply_fusion.2), channel_id=1, replica_groups=mesh['groups'=2,'row'=8,'col'=2] {'row'}, use_global_device_ids=true, to_apply=%region_31.32 | all-reduce | flops 512 | bytes 4096 | tf_op jit(solution)/shard_map/psum | solution.py:54
  168.6 14.5 %while.67 = (s32[]{:T(128)}, f32[512,96]{0,1:T(8,128)S(1)}, f32[4,512,96]{1,0,2:T(4,128)S(1)}, f32[4,512]{1,0:T(4,128)S(1)}, f32[512]{0:T(512)S(1)}, /*index=5*/...) while((s32[]{:T(128)}, f32[512,96]{0,1:T(8,128)S(1)}, ...), condition=%wide.region_37.38_spmd.clone, body=%wide.region_32.37_spmd.clone.sunk | while | flops 154777600 | bytes 3899551 | solution.py:108
  168.8 0.7 fusion.97
  170.3 1.9 dynamic_update_slice.27
  172.4 0.7 fusion.97
  173.9 1.9 dynamic_update_slice.27
  176.1 0.7 fusion.97
  177.6 1.9 dynamic_update_slice.27
  179.7 0.7 fusion.97
  181.2 1.9 dynamic_update_slice.27
  183.1 0.8 copy.30
  184.0 1.1 copy.38
  186.3 56.2 %reduce-scatter.5.cloned.1.call-done = f32[64,96]{1,0:T(8,128)} async-done(((f32[512,96]{1,0:T(8,128)}), f32[64,96]{1,0:T(8,128)}) %reduce-scatter.5.cloned.1.call-update) | async-done | bytes 24592 | tf_op jit(solution)/shard_map/reduce_scatter | solution.py:111
  242.5 1.4 broadcast_multiply_fusion.1
  243.9 8.2 %reduce-scatter.3.cloned.1.call-done = f32[1024,96]{0,1:T(8,128)} async-done(((f32[2048,96]{0,1:T(8,128)}), f32[1024,96]{0,1:T(8,128)}) %reduce-scatter.3.cloned.1.call-update) | async-done | bytes 393232 | tf_op jit(solution)/shard_map/reduce_scatter | solution.py:113
  252.1 1.8 broadcast_multiply_fusion
  (171 shorter events, 24.2 us)
Async XLA Ops:
  7.2 235.4 %reduce-scatter.5.cloned.1.call-start = ((), (), s32[]{:S(2)}) async-start(), calls=%async_computation.3 | async-start | bytes 294912 | tf_op jit(solution)/shard_map/reduce_scatter | solution.py:111
  7.2 0.7 copy-start.4
  9.1 0.7 copy-start.3
  33.1 0.7 copy-start.2
  35.6 0.7 copy-start.1
  66.9 0.9 copy-start
  183.9 68.2 %reduce-scatter.3.cloned.1.call-start = ((), (), s32[]{:S(2)}) async-start(), calls=%async_computation.2 | async-start | bytes 1179648 | tf_op jit(solution)/shard_map/reduce_scatter | solution.py:113
Sparse Core Ops, SparseCore 0:
  184.0 58.4 reduce-scatter.4
  244.8 7.2 reduce-scatter.2
where the time goes:
time: 261 us
  blocking collectives  140 us (54%)
  waiting for transfers between devices  64.4 us (25%)
  local copies, waits for them, and re-layouts  17.1 us (7%)
  between operations  14.9 us (6%)
  matrix products  12.6 us (5%)
  other arithmetic  10.9 us (4%)
    reduce_scatter x1, waiting for transfers between devices, on_device(): lax.psum_scatter(gy_term, 'row', scatter_dimension=0, tiled=True) / nx_all  56.2 us
    psum x2, blocking collectives, column_pass(): total = lax.psum(total * jnp.exp(peak - whole), 'row')  38.2 us
    pmax x2, blocking collectives, column_pass(): whole = lax.pmax(peak, 'row')  34.3 us
    all_gather x1, blocking collectives, on_device(): lax.all_gather(points_y, 'row', axis=0, tiled=True)  30.5 us
    unnamed x1, blocking collectives  23.1 us
    dot_general x20, matrix products, cost_block(): cross = jnp.dot(xb, yv.T, preferred_element_type=jnp.float32)  10.4 us
    dynamic_update_slice x8, local copies, waits for them, and re-layouts, on_device(): lax.scan(grad_fn, jnp.zeros((y_rows.shape[0], width_f), jnp.float32), (bl...  8.25 us
    reduce_scatter x1, waiting for transfers between devices, on_device(): lax.psum_scatter(gx_term.reshape(rows_all, width_f), 'col', scatter_dimen...  8.16 us
  transfers between devices with their start and end apart: 2, of which 2 were waited for; matrix products, arithmetic and copies ran while one was open for 1% of the time, Pallas kernels for 0%

commit v1 on v0

v1 whole, which is shorter than its diff:
```python
import functools
import math

import jax
import jax.numpy as jnp
from jax import lax
from jax.experimental import pallas as pl
from jax.experimental.pallas import tpu as pltpu
from jax.sharding import PartitionSpec as P

ITERS = 2
EPSILON = 0.02
LOG2E = math.log2(math.e)
AXES = ("row", "col")
TILE = 256
STEP = 32
EXT = 32
F32 = jnp.float32
BF16 = jnp.bfloat16


def kappa_of(width):
    return 2.0 / (width * EPSILON)


def pieces(value):
    high = value.astype(BF16).astype(F32)
    rest = value - high
    mid = rest.astype(BF16).astype(F32)
    return high, mid, rest - mid


def select(index, values):
    out = jnp.zeros(index.shape, F32)
    for k, value in values.items():
        out = jnp.where(index == k, value, out)
    return out


def extras_y(index, c_term, mass):
    high, mid, low = pieces(c_term)
    return select(index, {0: high, 1: mid, 2: low, 3: 1.0, 4: 1.0, 5: 1.0, 6: mass})


def extras_x(index, b_term):
    high, mid, low = pieces(b_term)
    return select(index, {0: 1.0, 1: 1.0, 2: 1.0, 3: high, 4: mid, 5: low})


def rows_index(columns):
    return lax.broadcasted_iota(jnp.int32, (EXT, columns), 0)


def to_column(row):
    size = row.shape[1]
    eye = lax.broadcasted_iota(jnp.int32, (size, size), 0) == lax.broadcasted_iota(jnp.int32, (size, size), 1)
    return jnp.sum(jnp.where(eye, row, 0.0), axis=1, keepdims=True)


def to_row(column):
    size = column.shape[0]
    eye = lax.broadcasted_iota(jnp.int32, (size, size), 0) == lax.broadcasted_iota(jnp.int32, (size, size), 1)
    return jnp.sum(jnp.where(eye, column, 0.0), axis=0, keepdims=True)


def for_tiles(total, body):
    count = total // TILE
    if count <= 4:
        for t in range(count):
            body(pl.ds(t * TILE, TILE))
    else:

        @pl.loop(0, count)
        def _(t):
            body(pl.ds(pl.multiple_of(t * TILE, TILE), TILE))


def max_down(z_ref, rows):
    peak = z_ref[0:STEP, :]
    for r in range(STEP, rows, STEP):
        peak = jnp.maximum(peak, z_ref[r : r + STEP, :])
    return jnp.max(peak, axis=0, keepdims=True)


def exp_down(z_ref, rows, scale, shift=None, keep=()):
    total = jnp.zeros((STEP, TILE), F32)
    for r in range(0, rows, STEP):
        z = z_ref[r : r + STEP, :]
        if shift is not None:
            z = z - shift
        value = jnp.exp2(z * scale)
        total = total + value
        if keep:
            high = value.astype(BF16)
            keep[0][r : r + STEP, :] = high
            if len(keep) > 1:
                keep[1][r : r + STEP, :] = (value - high.astype(F32)).astype(BF16)
    return jnp.sum(total, axis=0, keepdims=True)


def lse_down(z_ref, rows, scale):
    peak = max_down(z_ref, rows)
    total = exp_down(z_ref, rows, scale, peak)
    return scale * peak + jnp.log(total) * LOG2E


def prep_kernel(log_ny, y_ref, my_ref, out_ref):
    width = y_ref.shape[1]
    y = y_ref[...]
    yf = y.astype(F32)
    norm = jnp.sum(yf * yf, axis=1, keepdims=True)
    mass = to_column(my_ref[...].astype(F32))
    c_term = (mass - log_ny) / kappa_of(width) - 0.5 * norm
    index = lax.broadcasted_iota(jnp.int32, (y.shape[0], EXT), 1)
    out_ref[:, :width] = y
    out_ref[:, width:] = extras_y(index, c_term, mass).astype(BF16)


def first_kernel(nd, log_nx, *refs):
    xt_ref, mx_ref = refs[:2]
    y_refs = refs[2 : 2 + nd]
    ya_ref, b_ref, l_ref, xa_ref, z_ref, zc_ref = refs[2 + nd :]
    width, n = xt_ref.shape
    yd = y_refs[0].shape[0]
    ny = nd * yd
    scale = kappa_of(width) * LOG2E
    me = lax.axis_index("row") * lax.axis_size("col") + lax.axis_index("col")
    for k in range(nd):
        ya_ref[pl.ds(pl.multiple_of((me ^ k) * yd, yd), yd), :] = y_refs[k][...]
    la2 = (mx_ref[...].astype(F32) - log_nx) * LOG2E
    xa_ref[:width, :] = xt_ref[...]
    xa_ref[width:, :] = extras_x(rows_index(n), jnp.zeros((1, n), F32)).astype(BF16)

    def row_tile(t):
        z_ref[...] = jnp.dot(ya_ref[...], xa_ref[:, t], preferred_element_type=F32)
        b_ref[:, t] = -lse_down(z_ref, ny, scale)

    for_tiles(n, row_tile)
    b_term = (la2 + b_ref[...]) / scale
    b_ref[...] = b_term
    xa_ref[width:, :] = extras_x(rows_index(n), b_term).astype(BF16)
    x_rows = xa_ref[...].T

    def col_tile(t):
        zc_ref[...] = lax.dot_general(x_rows, ya_ref[t, :], (((1,), (1,)), ((), ())), preferred_element_type=F32)
        l_ref[:, :, t] = jnp.broadcast_to(lse_down(zc_ref, n, scale)[None], (nd, 1, TILE))

    for_tiles(ny, col_tile)


def update_y(log_ny, scale, width, yt_ref, ya_ref, lse2):
    ny = ya_ref.shape[0]
    old = yt_ref[width:, :].astype(F32)
    c_old = (old[0:1] + old[1:2]) + old[2:3]
    mass = old[6:7]
    lb2 = (mass - log_ny) * LOG2E
    c_term = c_old + (lb2 - lse2) / scale
    return c_term, mass


def second_kernel(
    nd, log_nx, log_ny, xt_ref, mx_ref, ya0_ref, b1_ref, l_ref,
    f_ref, s_ref, g_ref, xa_ref, ya_ref, yt_ref, z_ref, zc_ref, ph_ref, pw_ref, gt_ref,
):
    width, n = xt_ref.shape
    ny = ya0_ref.shape[0]
    yd = ny // nd
    kappa = kappa_of(width)
    scale = kappa * LOG2E
    l_all = l_ref[...]
    peak = jnp.max(l_all, axis=0)
    lse2 = peak + jnp.log(jnp.sum(jnp.exp2(l_all - peak[None]), axis=0)) * LOG2E
    yt_ref[...] = ya0_ref[...].T
    c_term, mass = update_y(log_ny, scale, width, yt_ref, ya0_ref, lse2)
    ext = extras_y(rows_index(ny), c_term, mass)
    yt_ref[width:, :] = ext.astype(BF16)
    ya_ref[:, :width] = ya0_ref[:, :width]
    ya_ref[:, width:] = ext.T.astype(BF16)
    xt = xt_ref[...]
    xa_ref[:width, :] = xt
    xa_ref[width:, :] = extras_x(rows_index(n), b1_ref[...]).astype(BF16)

    def row_tile(t):
        z_ref[...] = jnp.dot(ya_ref[...], xa_ref[:, t], preferred_element_type=F32)
        f_ref[:, t] = exp_down(z_ref, ny, scale)

    for_tiles(n, row_tile)
    log_a = mx_ref[...].astype(F32) - log_nx
    b_term = b1_ref[...] + (log_a - jnp.log(f_ref[...])) / kappa
    xf = xt.astype(F32)
    f_ref[...] = jnp.sum(xf * xf, axis=0, keepdims=True) / width - EPSILON * (log_a - kappa * b_term)
    xa_ref[width:, :] = extras_x(rows_index(n), b_term).astype(BF16)
    x_rows = xa_ref[...].T

    def col_tile(t):
        zc_ref[...] = jnp.dot(x_rows, yt_ref[:, t], preferred_element_type=F32)
        total = exp_down(zc_ref, n, scale, None, (ph_ref, pw_ref))
        s_ref[:, t] = total
        moment = jnp.dot(xt, ph_ref[...], preferred_element_type=F32) + jnp.dot(xt, pw_ref[...], preferred_element_type=F32)
        gt_ref[:width, t] = yt_ref[:width, t].astype(F32) * total - moment

    for_tiles(ny, col_tile)
    high, mid, low = pieces(s_ref[...])
    c_high, c_mid, c_low = pieces(c_term)
    gt_ref[width:, :] = select(rows_index(ny), {0: high, 1: mid, 2: low, 3: c_high, 4: c_mid, 5: c_low})
    g_ref[...] = gt_ref[...].T.astype(BF16).reshape(nd, yd, width + EXT)


def grad_x_kernel(nd, log_nx, log_ny, *refs):
    xa_ref, ya1_ref, yt1_ref = refs[:3]
    s_refs = refs[3 : 3 + nd]
    out_ref, ya_ref, z_ref, w_ref = refs[3 + nd :]
    width = out_ref.shape[0]
    ny = ya1_ref.shape[0]
    kappa = kappa_of(width)
    scale = kappa * LOG2E
    total = s_refs[0][...]
    for ref in s_refs[1:]:
        total = total + ref[...]
    c_term, mass = update_y(log_ny, scale, width, yt1_ref, ya1_ref, jnp.log(total) * LOG2E)
    ext = extras_y(rows_index(ny), c_term + (log_nx + log_ny) / kappa, mass)
    ya_ref[:, :width] = ya1_ref[:, :width]
    ya_ref[:, width:] = ext.T.astype(BF16)

    def row_tile(t):
        z_ref[...] = jnp.dot(ya_ref[...], xa_ref[:, t], preferred_element_type=F32)
        total = exp_down(z_ref, ny, scale, None, (w_ref,))
        moved = jnp.dot(yt1_ref[:width, :], w_ref[...], preferred_element_type=F32)
        out_ref[:, t] = (xa_ref[:width, t].astype(F32) * total - moved) * (1.0 / ny)

    for_tiles(out_ref.shape[1], row_tile)


def grad_y_kernel(nd, y_ref, my_ref, g_ref, out_ref, pot_ref):
    yd, width = y_ref.shape
    total = g_ref[0].astype(F32)
    for k in range(1, nd):
        total = total + g_ref[k].astype(F32)
    part = total[:, width:]
    colsum = (part[:, 0:1] + part[:, 1:2]) + part[:, 2:3]
    c_term = ((part[:, 3:4] + part[:, 4:5]) + part[:, 5:6]) * (1.0 / nd)
    mass = to_column(my_ref[...].astype(F32))
    out_ref[...] = total[:, :width] * (jnp.exp(mass) / colsum)
    yf = y_ref[...].astype(F32)
    norm = jnp.sum(yf * yf, axis=1, keepdims=True)
    pot = norm / width - EPSILON * (jnp.log(colsum) - kappa_of(width) * c_term)
    pot_ref[...] = to_row(pot)


def call(kernel, outs, scratch, *args):
    return pl.pallas_call(
        kernel,
        out_shape=outs,
        in_specs=[pl.BlockSpec(memory_space=pltpu.VMEM)] * len(args),
        out_specs=jax.tree.map(lambda _: pl.BlockSpec(memory_space=pltpu.VMEM), outs),
        scratch_shapes=scratch,
        compiler_params=pltpu.CompilerParams(vmem_limit_bytes=40 * 1024 * 1024),
    )(*args)


def shape(dims, dtype=F32):
    return jax.ShapeDtypeStruct(dims, dtype)


def everyone(value, nd):
    return [value] + [lax.ppermute(value, AXES, [(s, s ^ k) for s in range(nd)]) for k in range(1, nd)]


def on_device(points_x, points_y, mass_x, mass_y):
    n, width = points_x.shape
    yd = points_y.shape[0]
    nd = lax.axis_size("row") * lax.axis_size("col")
    ny = nd * yd
    log_nx, log_ny = math.log(n * nd), math.log(ny)
    depth = width + EXT
    xt = points_x.T
    mx = mass_x.reshape(1, n)
    my = mass_y.reshape(1, yd)
    y_own = call(functools.partial(prep_kernel, log_ny), shape((yd, depth), BF16), [], points_y, my)
    y_blocks = everyone(y_own, nd)
    ya, b1, lse = call(
        functools.partial(first_kernel, nd, log_nx),
        (shape((ny, depth), BF16), shape((1, n)), shape((nd, 1, ny))),
        [pltpu.VMEM((depth, n), BF16), pltpu.VMEM((ny, TILE), F32), pltpu.VMEM((n, TILE), F32)],
        xt, mx, *y_blocks,
    )
    lse = lax.all_to_all(lse, AXES, 0, 0, tiled=True)
    f_pot, sums, g_part, xa, ya, yt = call(
        functools.partial(second_kernel, nd, log_nx, log_ny),
        (
            shape((1, n)), shape((1, ny)), shape((nd, yd, depth), BF16),
            shape((depth, n), BF16), shape((ny, depth), BF16), shape((depth, ny), BF16),
        ),
        [
            pltpu.VMEM((ny, TILE), F32), pltpu.VMEM((n, TILE), F32),
            pltpu.VMEM((n, TILE), BF16), pltpu.VMEM((n, TILE), BF16), pltpu.VMEM((depth, ny), F32),
        ],
        xt, mx, ya, b1, lse,
    )
    all_sums = everyone(sums, nd)
    g_all = lax.all_to_all(g_part, AXES, 0, 0, tiled=True)
    grad_xt = call(
        functools.partial(grad_x_kernel, nd, log_nx, log_ny),
        shape((width, n)),
        [pltpu.VMEM((ny, depth), BF16), pltpu.VMEM((ny, TILE), F32), pltpu.VMEM((ny, TILE), BF16)],
        xa, ya, yt, *all_sums,
    )
    grad_y, g_pot = call(
        functools.partial(grad_y_kernel, nd), (shape((yd, width)), shape((1, yd))), [], points_y, my, g_all
    )
    return f_pot.reshape(n), g_pot.reshape(yd), grad_xt.T, grad_y


def solution(mesh):
    in_specs = (
        P(("groups", "row", "col"), None),
        P(("groups", "col", "row"), None),
        P(("groups", "row", "col")),
        P(("groups", "col", "row")),
    )
    out_specs = (
        P(("groups", "row", "col")),
        P(("groups", "col", "row")),
        P(("groups", "row", "col"), None),
        P(("groups", "col", "row"), None),
    )
    return jax.shard_map(
        on_device, mesh=mesh, in_specs=in_specs, out_specs=out_specs, check_vma=False
    )
```

time: 261 us -> 78.5 us (0.30)
  blocking collectives: 140 us -> 11.7 us
  waiting for transfers between devices: 64.4 us -> 7.51 us
  starting transfers between devices: 0.08 us -> 44.7 us
  local copies, waits for them, and re-layouts: 17.1 us -> 2.31 us
  between operations: 14.9 us -> 0.7 us
  matrix products: 12.6 us -> 0 us
  Pallas kernels: 0 us -> 11.2 us
  other arithmetic: 10.9 us -> 0 us
    reduce_scatter x2 -> x0, waiting for transfers between devices: 64.4 us -> none  [the longest x1 56.2 us: on_device(): lax.psum_scatter(gy_term, 'row', scatter_dimension=0, tiled=True) / nx_all]
    psum x4 -> x0, blocking collectives: 43.2 us -> none  [the longest x2 38.2 us: column_pass(): total = lax.psum(total * jnp.exp(peak - whole), 'row')]
    ppermute x0 -> x30, starting transfers between devices: none -> 41.1 us  [everyone(): lax.ppermute(value, AXES, [(s, s ^ k) for s in range(nd)])]
    pmax x4 -> x0, blocking collectives: 39.3 us -> none  [the longest x2 34.3 us: column_pass(): whole = lax.pmax(peak, 'row')]
    all_gather x3 -> x0, blocking collectives: 34.4 us -> none  [the longest x1 30.5 us: on_device(): lax.all_gather(points_y, 'row', axis=0, tiled=True)]
    unnamed x1 -> x0, blocking collectives: 23.1 us -> none
    dot_general x28 -> x0, matrix products: 12.6 us -> none  [the longest x20 10.4 us: cost_block(): cross = jnp.dot(xb, yv.T, preferred_element_type=jnp.float32)]
    all_to_all x0 -> x1, blocking collectives: none -> 11.7 us  [on_device(): lse = lax.all_to_all(lse, AXES, 0, 0, tiled=True)]
  transfers between devices with their start and end apart: 2 -> 31, of which waited for: 2 -> 7; matrix products, arithmetic and copies ran while one was open for 1% -> 0% of each run, Pallas kernels for 0% -> 4%
where the time goes in v1:
time: 78.5 us; the launch traced here: 78.1 us
  starting transfers between devices  44.7 us (57%)
  blocking collectives  11.7 us (15%)
  Pallas kernels  11.2 us (14%)
  waiting for transfers between devices  7.51 us (10%)
  local copies, waits for them, and re-layouts  2.31 us (3%)
    ppermute x30, starting transfers between devices, everyone(): lax.ppermute(value, AXES, [(s, s ^ k) for s in range(nd)])  41.1 us
    all_to_all x1, blocking collectives, on_device(): lse = lax.all_to_all(lse, AXES, 0, 0, tiled=True)  11.7 us
    pallas_call x5, Pallas kernels, call(): pl.pallas_call(kernel, out_shape=outs, in_specs=[pl.BlockSpec(memory_spac...  11.2 us
    ppermute x30, waiting for transfers between devices, everyone(): lax.ppermute(value, AXES, [(s, s ^ k) for s in range(nd)])  7.51 us
    all_to_all x1, starting transfers between devices, on_device(): g_all = lax.all_to_all(g_part, AXES, 0, 0, tiled=True)  3.53 us
    unnamed x12, local copies, waits for them, and re-layouts  2.3 us
  transfers between devices with their start and end apart: 31, of which 7 were waited for; matrix products, arithmetic and copies ran while one was open for 0% of the time, Pallas kernels for 4%

profile of v1, /device:TPU:0, one launch (start us, length us, event | category | flops | bytes accessed | tf_op | source)
XLA Modules:
  0.0 78.1 jit_solution(3486231359442107772)
XLA Ops:
  0.6 0.6 copy-done.4
  1.3 0.7 copy-done.2
  2.2 5.5 %collective-permute-start.14 = (bf16[64,128]{1,0:T(8,128)(2,1)S(1)}, bf16[64,128]{1,0:T(8,128)(2,1)S(1)}, u32[]{:S(2)}, u32[]{:S(2)}) collective-permute-start(bf16[64,128]{1,0:T(8,128)(2,1)S(1)} %shard_map.75.refs_2_), channel_id=1, source_target_pairs={{0,15},{1,14},{2,13},{3,12},{4,11},{5,10},{6,9},{7,8},{8,7},{9,6},... | collective-permute-start | bytes 49160 | tf_op jit(solution)/shard_map/ppermute | solution.py:266
  7.6 0.6 collective-permute-start.13
  8.3 3.2 %collective-permute-start.12 = (bf16[64,128]{1,0:T(8,128)(2,1)S(1)}, bf16[64,128]{1,0:T(8,128)(2,1)S(1)}, u32[]{:S(2)}, u32[]{:S(2)}) collective-permute-start(bf16[64,128]{1,0:T(8,128)(2,1)S(1)} %shard_map.75.refs_2_), channel_id=1, source_target_pairs={{0,13},{1,12},{2,15},{3,14},{4,9},{5,8},{6,11},{7,10},{8,5},{9,4},... | collective-permute-start | bytes 49160 | tf_op jit(solution)/shard_map/ppermute | solution.py:266
  11.8 3.6 %collective-permute-start.9 = (bf16[64,128]{1,0:T(8,128)(2,1)S(1)}, bf16[64,128]{1,0:T(8,128)(2,1)S(1)}, u32[]{:S(2)}, u32[]{:S(2)}) collective-permute-start(bf16[64,128]{1,0:T(8,128)(2,1)S(1)} %shard_map.75.refs_2_), channel_id=1, source_target_pairs={{0,10},{1,11},{2,8},{3,9},{4,14},{5,15},{6,12},{7,13},{8,2},{9,3},... | collective-permute-start | bytes 49160 | tf_op jit(solution)/shard_map/ppermute | solution.py:266
  15.4 2.6 %collective-permute-start.7 = (bf16[64,128]{1,0:T(8,128)(2,1)S(1)}, bf16[64,128]{1,0:T(8,128)(2,1)S(1)}, u32[]{:S(2)}, u32[]{:S(2)}) collective-permute-start(bf16[64,128]{1,0:T(8,128)(2,1)S(1)} %shard_map.75.refs_2_), channel_id=1, source_target_pairs={{0,8},{1,9},{2,10},{3,11},{4,12},{5,13},{6,14},{7,15},{8,0},{9,1},... | collective-permute-start | bytes 49160 | tf_op jit(solution)/shard_map/ppermute | solution.py:266
  18.0 1.9 %collective-permute-start.6 = (bf16[64,128]{1,0:T(8,128)(2,1)S(1)}, bf16[64,128]{1,0:T(8,128)(2,1)S(1)}, u32[]{:S(2)}, u32[]{:S(2)}) collective-permute-start(bf16[64,128]{1,0:T(8,128)(2,1)S(1)} %shard_map.75.refs_2_), channel_id=1, source_target_pairs={{0,7},{1,6},{2,5},{3,4},{4,3},{5,2},{6,1},{7,0},{8,15},{9,14},{10,... | collective-permute-start | bytes 49160 | tf_op jit(solution)/shard_map/ppermute | solution.py:266
  19.9 0.8 %collective-permute-start.5 = (bf16[64,128]{1,0:T(8,128)(2,1)S(1)}, bf16[64,128]{1,0:T(8,128)(2,1)S(1)}, u32[]{:S(2)}, u32[]{:S(2)}) collective-permute-start(bf16[64,128]{1,0:T(8,128)(2,1)S(1)} %shard_map.75.refs_2_), channel_id=1, source_target_pairs={{0,6},{1,7},{2,4},{3,5},{4,2},{5,3},{6,0},{7,1},{8,14},{9,15},{10,... | collective-permute-start | bytes 49160 | tf_op jit(solution)/shard_map/ppermute | solution.py:266
  20.7 1.2 %collective-permute-start.4 = (bf16[64,128]{1,0:T(8,128)(2,1)S(1)}, bf16[64,128]{1,0:T(8,128)(2,1)S(1)}, u32[]{:S(2)}, u32[]{:S(2)}) collective-permute-start(bf16[64,128]{1,0:T(8,128)(2,1)S(1)} %shard_map.75.refs_2_), channel_id=1, source_target_pairs={{0,5},{1,4},{2,7},{3,6},{4,1},{5,0},{6,3},{7,2},{8,13},{9,12},{10,... | collective-permute-start | bytes 49160 | tf_op jit(solution)/shard_map/ppermute | solution.py:266
  22.4 1.0 %collective-permute-start.2 = (bf16[64,128]{1,0:T(8,128)(2,1)S(1)}, bf16[64,128]{1,0:T(8,128)(2,1)S(1)}, u32[]{:S(2)}, u32[]{:S(2)}) collective-permute-start(bf16[64,128]{1,0:T(8,128)(2,1)S(1)} %shard_map.75.refs_2_), channel_id=1, source_target_pairs={{0,3},{1,2},{2,1},{3,0},{4,7},{5,6},{6,5},{7,4},{8,11},{9,10},{10,... | collective-permute-start | bytes 49160 | tf_op jit(solution)/shard_map/ppermute | solution.py:266
  23.3 0.8 %collective-permute-start.1 = (bf16[64,128]{1,0:T(8,128)(2,1)S(1)}, bf16[64,128]{1,0:T(8,128)(2,1)S(1)}, u32[]{:S(2)}, u32[]{:S(2)}) collective-permute-start(bf16[64,128]{1,0:T(8,128)(2,1)S(1)} %shard_map.75.refs_2_), channel_id=1, source_target_pairs={{0,2},{1,3},{2,0},{3,1},{4,6},{5,7},{6,4},{7,5},{8,10},{9,11},{10,... | collective-permute-start | bytes 49160 | tf_op jit(solution)/shard_map/ppermute | solution.py:266
  24.7 1.0 %collective-permute-done.3.refs_6_ = bf16[64,128]{1,0:T(8,128)(2,1)S(1)} collective-permute-done((bf16[64,128]{1,0:T(8,128)(2,1)S(1)}, bf16[64,128]{1,0:T(8,128)(2,1)S(1)}, u32[]{:S(2)}, u32[]{:S(2)}) %collective-permute-start.3) | collective-permute-done | bytes 16416 | tf_op jit(solution)/shard_map/ppermute | solution.py:266
  25.6 1.5 %collective-permute-done.1.refs_4_ = bf16[64,128]{1,0:T(8,128)(2,1)S(1)} collective-permute-done((bf16[64,128]{1,0:T(8,128)(2,1)S(1)}, bf16[64,128]{1,0:T(8,128)(2,1)S(1)}, u32[]{:S(2)}, u32[]{:S(2)}) %collective-permute-start.1) | collective-permute-done | bytes 16416 | tf_op jit(solution)/shard_map/ppermute | solution.py:266
  27.1 0.9 %copy-done = bf16[1024,96]{0,1:T(8,128)(2,1)S(1)} copy-done((bf16[1024,96]{0,1:T(8,128)(2,1)S(1)}, bf16[1024,96]{0,1:T(8,128)(2,1)}, u32[]{:S(2)}) %copy-start) | copy-done | bytes 196632
  28.0 2.6 %shard_map.76 = (bf16[1024,128]{1,0:T(8,128)(2,1)S(1)}, f32[1,1024]{1,0:T(1,128)S(1)}, f32[16,1,1024]{2,1,0:T(1,128)S(1)}) custom-call(bf16[96,1024]{1,0:T(8,128)(2,1)S(1)} %bitcast.5, bf16[1,1024]{1,0:T(2,128)(2,1)S(1)} %reshape.20.refs_1_.mx_ref, bf16[64,128]{1,0:T(8,128)(2,1)S(1)} %shard_map.75.refs_2_, bf16[64,128]{1,0:T(8,128)(2,1)S(1)} %collective-permute-done.refs_3_, ...), custom_call_target="tpu_custom_call" | custom-call | tf_op jit(solution)/shard_map/pallas_call | solution.py:251
  30.6 11.7 %all_to_all.10.l_ref = f32[16,1,1024]{2,1,0:T(1,128)S(1)} all-to-all(f32[16,1,1024]{2,1,0:T(1,128)S(1)} %get-tuple-element.17), channel_id=1, replica_groups=mesh['groups'=2,'row'=8,'col'=2] {'row','col'}, dimensions={0} | all-to-all | bytes 131072 | tf_op jit(solution)/shard_map/all_to_all | solution.py:287
  42.3 4.5 %shard_map.77 = (f32[1,1024]{1,0:T(1,128)}, f32[1,1024]{1,0:T(1,128)S(1)}, bf16[16,64,128]{2,1,0:T(8,128)(2,1)}, bf16[128,1024]{1,0:T(8,128)(2,1)S(1)}, bf16[102...) custom-call(bf16[96,1024]{1,0:T(8,128)(2,1)S(1)} %bitcast.6, bf16[1,1024]{1,0:T(2,128)(2,1)S(1)} %reshape.20.refs_1_.mx_ref, ...), custom_call_target="tpu_custom_call" | custom-call | tf_op jit(solution)/shard_map/pallas_call | solution.py:251
  46.7 3.5 %all-to-all-start.1 = ((bf16[16,64,128]{2,1,0:T(8,128)(2,1)}), bf16[16,64,128]{2,1,0:T(8,128)(2,1)S(1)}, u32[]{:S(2)}, u32[]{:S(2)}) async-start(bf16[16,64,128]{2,1,0:T(8,128)(2,1)} %get-tuple-element.19), calls=%async_computation.1 | async-start | bytes 524288 | tf_op jit(solution)/shard_map/all_to_all | solution.py:301
  50.3 4.3 %collective-permute-start.29 = (f32[1,1024]{1,0:T(1,128)S(1)}, f32[1,1024]{1,0:T(1,128)S(1)}, u32[]{:S(2)}, u32[]{:S(2)}) collective-permute-start(f32[1,1024]{1,0:T(1,128)S(1)} %get-tuple-element.24.refs_3_), channel_id=1, source_target_pairs={{0,15},{1,14},{2,13},{3,12},{4,11},{5,10},{6,9},{7,8},{8,7},{9,6},... | collective-permute-start | bytes 12296 | tf_op jit(solution)/shard_map/ppermute | solution.py:266
  54.9 3.2 %collective-permute-start.27 = (f32[1,1024]{1,0:T(1,128)S(1)}, f32[1,1024]{1,0:T(1,128)S(1)}, u32[]{:S(2)}, u32[]{:S(2)}) collective-permute-start(f32[1,1024]{1,0:T(1,128)S(1)} %get-tuple-element.24.refs_3_), channel_id=1, source_target_pairs={{0,13},{1,12},{2,15},{3,14},{4,9},{5,8},{6,11},{7,10},{8,5},{9,4},... | collective-permute-start | bytes 12296 | tf_op jit(solution)/shard_map/ppermute | solution.py:266
  58.5 1.4 %collective-permute-done.29.refs_18_ = f32[1,1024]{1,0:T(1,128)S(1)} collective-permute-done((f32[1,1024]{1,0:T(1,128)S(1)}, f32[1,1024]{1,0:T(1,128)S(1)}, u32[]{:S(2)}, u32[]{:S(2)}) %collective-permute-start.29) | collective-permute-done | bytes 4128 | tf_op jit(solution)/shard_map/ppermute | solution.py:266
  59.9 2.2 %collective-permute-start.24 = (f32[1,1024]{1,0:T(1,128)S(1)}, f32[1,1024]{1,0:T(1,128)S(1)}, u32[]{:S(2)}, u32[]{:S(2)}) collective-permute-start(f32[1,1024]{1,0:T(1,128)S(1)} %get-tuple-element.24.refs_3_), channel_id=1, source_target_pairs={{0,10},{1,11},{2,8},{3,9},{4,14},{5,15},{6,12},{7,13},{8,2},{9,3},... | collective-permute-start | bytes 12296 | tf_op jit(solution)/shard_map/ppermute | solution.py:266
  62.5 2.2 %collective-permute-start.22 = (f32[1,1024]{1,0:T(1,128)S(1)}, f32[1,1024]{1,0:T(1,128)S(1)}, u32[]{:S(2)}, u32[]{:S(2)}) collective-permute-start(f32[1,1024]{1,0:T(1,128)S(1)} %get-tuple-element.24.refs_3_), channel_id=1, source_target_pairs={{0,8},{1,9},{2,10},{3,11},{4,12},{5,13},{6,14},{7,15},{8,0},{9,1},... | collective-permute-start | bytes 12296 | tf_op jit(solution)/shard_map/ppermute | solution.py:266
  64.7 2.1 %collective-permute-start.21 = (f32[1,1024]{1,0:T(1,128)S(1)}, f32[1,1024]{1,0:T(1,128)S(1)}, u32[]{:S(2)}, u32[]{:S(2)}) collective-permute-start(f32[1,1024]{1,0:T(1,128)S(1)} %get-tuple-element.24.refs_3_), channel_id=1, source_target_pairs={{0,7},{1,6},{2,5},{3,4},{4,3},{5,2},{6,1},{7,0},{8,15},{9,14},{10,... | collective-permute-start | bytes 12296 | tf_op jit(solution)/shard_map/ppermute | solution.py:266
  66.8 0.6 collective-permute-start.20
  67.4 1.2 %collective-permute-start.19 = (f32[1,1024]{1,0:T(1,128)S(1)}, f32[1,1024]{1,0:T(1,128)S(1)}, u32[]{:S(2)}, u32[]{:S(2)}) collective-permute-start(f32[1,1024]{1,0:T(1,128)S(1)} %get-tuple-element.24.refs_3_), channel_id=1, source_target_pairs={{0,5},{1,4},{2,7},{3,6},{4,1},{5,0},{6,3},{7,2},{8,13},{9,12},{10,... | collective-permute-start | bytes 12296 | tf_op jit(solution)/shard_map/ppermute | solution.py:266
  69.1 1.4 %collective-permute-start.17 = (f32[1,1024]{1,0:T(1,128)S(1)}, f32[1,1024]{1,0:T(1,128)S(1)}, u32[]{:S(2)}, u32[]{:S(2)}) collective-permute-start(f32[1,1024]{1,0:T(1,128)S(1)} %get-tuple-element.24.refs_3_), channel_id=1, source_target_pairs={{0,3},{1,2},{2,1},{3,0},{4,7},{5,6},{6,5},{7,4},{8,11},{9,10},{10,... | collective-permute-start | bytes 12296 | tf_op jit(solution)/shard_map/ppermute | solution.py:266
  71.3 0.8 %collective-permute-done.18.refs_7_ = f32[1,1024]{1,0:T(1,128)S(1)} collective-permute-done((f32[1,1024]{1,0:T(1,128)S(1)}, f32[1,1024]{1,0:T(1,128)S(1)}, u32[]{:S(2)}, u32[]{:S(2)}) %collective-permute-start.18) | collective-permute-done | bytes 4128 | tf_op jit(solution)/shard_map/ppermute | solution.py:266
  72.2 1.9 %collective-permute-done.16.refs_5_ = f32[1,1024]{1,0:T(1,128)S(1)} collective-permute-done((f32[1,1024]{1,0:T(1,128)S(1)}, f32[1,1024]{1,0:T(1,128)S(1)}, u32[]{:S(2)}, u32[]{:S(2)}) %collective-permute-start.16) | collective-permute-done | bytes 4128 | tf_op jit(solution)/shard_map/ppermute | solution.py:266
  74.1 3.1 %shard_map.79 = f32[96,1024]{1,0:T(8,128)} custom-call(bf16[128,1024]{1,0:T(8,128)(2,1)S(1)} %get-tuple-element.21.refs_0_, bf16[1024,128]{1,0:T(8,128)(2,1)S(1)} %get-tuple-element.22.refs_1_, bf16[128,1024]{1,0:T(8,128)(2,1)S(1)} %get-tuple-element.23.refs_2_, f32[1,1024]{1,0:T(1,128)S(1)} %get-tuple-element.24.refs_3_, ...), custom_call_target="tpu_custom_call" | custom-call | tf_op jit(solution)/shard_map/pallas_call | solution.py:251
  77.2 0.9 %shard_map.78 = (f32[64,96]{1,0:T(8,128)}, f32[1,64]{1,0:T(1,128)}) custom-call(bf16[64,96]{1,0:T(8,128)(2,1)S(1)} %copy-done.3, bf16[1,64]{1,0:T(2,128)(2,1)S(1)} %bitcast.8, bf16[16,64,128]{2,1,0:T(8,128)(2,1)S(1)} %all-to-all-done.1.g_ref), custom_call_target="tpu_custom_call" | custom-call | tf_op jit(solution)/shard_map/pallas_call | solution.py:251
  (49 shorter events, 4.0 us)
Async XLA Ops:
  2.0 22.6 %copy-start.5 = (bf16[1024]{0:T(1024)(128)(2,1)S(1)}, bf16[1024]{0:T(1024)(128)(2,1)}, u32[]{:S(2)}) copy-start(bf16[1024]{0:T(1024)(128)(2,1)} %param.6) | copy-start | bytes 6148
  2.2 9.6 %collective-permute-start.14 = (bf16[64,128]{1,0:T(8,128)(2,1)S(1)}, bf16[64,128]{1,0:T(8,128)(2,1)S(1)}, u32[]{:S(2)}, u32[]{:S(2)}) collective-permute-start(bf16[64,128]{1,0:T(8,128)(2,1)S(1)} %shard_map.75.refs_2_), channel_id=1, source_target_pairs={{0,15},{1,14},{2,13},{3,12},{4,11},{5,10},{6,9},{7,8},{8,7},{9,6},... | collective-permute-start | bytes 49160 | tf_op jit(solution)/shard_map/ppermute | solution.py:266
  7.6 7.7 %collective-permute-start.13 = (bf16[64,128]{1,0:T(8,128)(2,1)S(1)}, bf16[64,128]{1,0:T(8,128)(2,1)S(1)}, u32[]{:S(2)}, u32[]{:S(2)}) collective-permute-start(bf16[64,128]{1,0:T(8,128)(2,1)S(1)} %shard_map.75.refs_2_), channel_id=1, source_target_pairs={{0,14},{1,15},{2,12},{3,13},{4,10},{5,11},{6,8},{7,9},{8,6},{9,7},... | collective-permute-start | bytes 49160 | tf_op jit(solution)/shard_map/ppermute | solution.py:266
  8.3 7.1 %collective-permute-start.12 = (bf16[64,128]{1,0:T(8,128)(2,1)S(1)}, bf16[64,128]{1,0:T(8,128)(2,1)S(1)}, u32[]{:S(2)}, u32[]{:S(2)}) collective-permute-start(bf16[64,128]{1,0:T(8,128)(2,1)S(1)} %shard_map.75.refs_2_), channel_id=1, source_target_pairs={{0,13},{1,12},{2,15},{3,14},{4,9},{5,8},{6,11},{7,10},{8,5},{9,4},... | collective-permute-start | bytes 49160 | tf_op jit(solution)/shard_map/ppermute | solution.py:266
  11.4 6.5 %collective-permute-start.11 = (bf16[64,128]{1,0:T(8,128)(2,1)S(1)}, bf16[64,128]{1,0:T(8,128)(2,1)S(1)}, u32[]{:S(2)}, u32[]{:S(2)}) collective-permute-start(bf16[64,128]{1,0:T(8,128)(2,1)S(1)} %shard_map.75.refs_2_), channel_id=1, source_target_pairs={{0,12},{1,13},{2,14},{3,15},{4,8},{5,9},{6,10},{7,11},{8,4},{9,5},... | collective-permute-start | bytes 49160 | tf_op jit(solution)/shard_map/ppermute | solution.py:266
  11.7 8.1 %collective-permute-start.10 = (bf16[64,128]{1,0:T(8,128)(2,1)S(1)}, bf16[64,128]{1,0:T(8,128)(2,1)S(1)}, u32[]{:S(2)}, u32[]{:S(2)}) collective-permute-start(bf16[64,128]{1,0:T(8,128)(2,1)S(1)} %shard_map.75.refs_2_), channel_id=1, source_target_pairs={{0,11},{1,10},{2,9},{3,8},{4,15},{5,14},{6,13},{7,12},{8,3},{9,2},... | collective-permute-start | bytes 49160 | tf_op jit(solution)/shard_map/ppermute | solution.py:266
  11.8 8.9 %collective-permute-start.9 = (bf16[64,128]{1,0:T(8,128)(2,1)S(1)}, bf16[64,128]{1,0:T(8,128)(2,1)S(1)}, u32[]{:S(2)}, u32[]{:S(2)}) collective-permute-start(bf16[64,128]{1,0:T(8,128)(2,1)S(1)} %shard_map.75.refs_2_), channel_id=1, source_target_pairs={{0,10},{1,11},{2,8},{3,9},{4,14},{5,15},{6,12},{7,13},{8,2},{9,3},... | collective-permute-start | bytes 49160 | tf_op jit(solution)/shard_map/ppermute | solution.py:266
  15.4 6.5 %collective-permute-start.8 = (bf16[64,128]{1,0:T(8,128)(2,1)S(1)}, bf16[64,128]{1,0:T(8,128)(2,1)S(1)}, u32[]{:S(2)}, u32[]{:S(2)}) collective-permute-start(bf16[64,128]{1,0:T(8,128)(2,1)S(1)} %shard_map.75.refs_2_), channel_id=1, source_target_pairs={{0,9},{1,8},{2,11},{3,10},{4,13},{5,12},{6,15},{7,14},{8,1},{9,0},... | collective-permute-start | bytes 49160 | tf_op jit(solution)/shard_map/ppermute | solution.py:266
  15.4 7.0 %collective-permute-start.7 = (bf16[64,128]{1,0:T(8,128)(2,1)S(1)}, bf16[64,128]{1,0:T(8,128)(2,1)S(1)}, u32[]{:S(2)}, u32[]{:S(2)}) collective-permute-start(bf16[64,128]{1,0:T(8,128)(2,1)S(1)} %shard_map.75.refs_2_), channel_id=1, source_target_pairs={{0,8},{1,9},{2,10},{3,11},{4,12},{5,13},{6,14},{7,15},{8,0},{9,1},... | collective-permute-start | bytes 49160 | tf_op jit(solution)/shard_map/ppermute | solution.py:266
  18.0 5.4 %collective-permute-start.6 = (bf16[64,128]{1,0:T(8,128)(2,1)S(1)}, bf16[64,128]{1,0:T(8,128)(2,1)S(1)}, u32[]{:S(2)}, u32[]{:S(2)}) collective-permute-start(bf16[64,128]{1,0:T(8,128)(2,1)S(1)} %shard_map.75.refs_2_), channel_id=1, source_target_pairs={{0,7},{1,6},{2,5},{3,4},{4,3},{5,2},{6,1},{7,0},{8,15},{9,14},{10,... | collective-permute-start | bytes 49160 | tf_op jit(solution)/shard_map/ppermute | solution.py:266
  19.9 4.8 %collective-permute-start.5 = (bf16[64,128]{1,0:T(8,128)(2,1)S(1)}, bf16[64,128]{1,0:T(8,128)(2,1)S(1)}, u32[]{:S(2)}, u32[]{:S(2)}) collective-permute-start(bf16[64,128]{1,0:T(8,128)(2,1)S(1)} %shard_map.75.refs_2_), channel_id=1, source_target_pairs={{0,6},{1,7},{2,4},{3,5},{4,2},{5,3},{6,0},{7,1},{8,14},{9,15},{10,... | collective-permute-start | bytes 49160 | tf_op jit(solution)/shard_map/ppermute | solution.py:266
  20.7 4.0 %collective-permute-start.4 = (bf16[64,128]{1,0:T(8,128)(2,1)S(1)}, bf16[64,128]{1,0:T(8,128)(2,1)S(1)}, u32[]{:S(2)}, u32[]{:S(2)}) collective-permute-start(bf16[64,128]{1,0:T(8,128)(2,1)S(1)} %shard_map.75.refs_2_), channel_id=1, source_target_pairs={{0,5},{1,4},{2,7},{3,6},{4,1},{5,0},{6,3},{7,2},{8,13},{9,12},{10,... | collective-permute-start | bytes 49160 | tf_op jit(solution)/shard_map/ppermute | solution.py:266
  21.9 3.7 %collective-permute-start.3 = (bf16[64,128]{1,0:T(8,128)(2,1)S(1)}, bf16[64,128]{1,0:T(8,128)(2,1)S(1)}, u32[]{:S(2)}, u32[]{:S(2)}) collective-permute-start(bf16[64,128]{1,0:T(8,128)(2,1)S(1)} %shard_map.75.refs_2_), channel_id=1, source_target_pairs={{0,4},{1,5},{2,6},{3,7},{4,0},{5,1},{6,2},{7,3},{8,12},{9,13},{10,... | collective-permute-start | bytes 49160 | tf_op jit(solution)/shard_map/ppermute | solution.py:266
  22.4 3.3 %collective-permute-start.2 = (bf16[64,128]{1,0:T(8,128)(2,1)S(1)}, bf16[64,128]{1,0:T(8,128)(2,1)S(1)}, u32[]{:S(2)}, u32[]{:S(2)}) collective-permute-start(bf16[64,128]{1,0:T(8,128)(2,1)S(1)} %shard_map.75.refs_2_), channel_id=1, source_target_pairs={{0,3},{1,2},{2,1},{3,0},{4,7},{5,6},{6,5},{7,4},{8,11},{9,10},{10,... | collective-permute-start | bytes 49160 | tf_op jit(solution)/shard_map/ppermute | solution.py:266
  23.3 3.7 %collective-permute-start.1 = (bf16[64,128]{1,0:T(8,128)(2,1)S(1)}, bf16[64,128]{1,0:T(8,128)(2,1)S(1)}, u32[]{:S(2)}, u32[]{:S(2)}) collective-permute-start(bf16[64,128]{1,0:T(8,128)(2,1)S(1)} %shard_map.75.refs_2_), channel_id=1, source_target_pairs={{0,2},{1,3},{2,0},{3,1},{4,6},{5,7},{6,4},{7,5},{8,10},{9,11},{10,... | collective-permute-start | bytes 49160 | tf_op jit(solution)/shard_map/ppermute | solution.py:266
  24.6 2.4 %collective-permute-start = (bf16[64,128]{1,0:T(8,128)(2,1)S(1)}, bf16[64,128]{1,0:T(8,128)(2,1)S(1)}, u32[]{:S(2)}, u32[]{:S(2)}) collective-permute-start(bf16[64,128]{1,0:T(8,128)(2,1)S(1)} %shard_map.75.refs_2_), channel_id=1, source_target_pairs={{0,1},{1,0},{2,3},{3,2},{4,5},{5,4},{6,7},{7,6},{8,9},{9,8},{10,11... | collective-permute-start | bytes 49160 | tf_op jit(solution)/shard_map/ppermute | solution.py:266
  46.7 30.4 %all-to-all-start.1 = ((bf16[16,64,128]{2,1,0:T(8,128)(2,1)}), bf16[16,64,128]{2,1,0:T(8,128)(2,1)S(1)}, u32[]{:S(2)}, u32[]{:S(2)}) async-start(bf16[16,64,128]{2,1,0:T(8,128)(2,1)} %get-tuple-element.19), calls=%async_computation.1 | async-start | bytes 524288 | tf_op jit(solution)/shard_map/all_to_all | solution.py:301
  50.3 9.6 %collective-permute-start.29 = (f32[1,1024]{1,0:T(1,128)S(1)}, f32[1,1024]{1,0:T(1,128)S(1)}, u32[]{:S(2)}, u32[]{:S(2)}) collective-permute-start(f32[1,1024]{1,0:T(1,128)S(1)} %get-tuple-element.24.refs_3_), channel_id=1, source_target_pairs={{0,15},{1,14},{2,13},{3,12},{4,11},{5,10},{6,9},{7,8},{8,7},{9,6},... | collective-permute-start | bytes 12296 | tf_op jit(solution)/shard_map/ppermute | solution.py:266
  54.6 7.4 %collective-permute-start.28 = (f32[1,1024]{1,0:T(1,128)S(1)}, f32[1,1024]{1,0:T(1,128)S(1)}, u32[]{:S(2)}, u32[]{:S(2)}) collective-permute-start(f32[1,1024]{1,0:T(1,128)S(1)} %get-tuple-element.24.refs_3_), channel_id=1, source_target_pairs={{0,14},{1,15},{2,12},{3,13},{4,10},{5,11},{6,8},{7,9},{8,6},{9,7},... | collective-permute-start | bytes 12296 | tf_op jit(solution)/shard_map/ppermute | solution.py:266
  54.9 7.5 %collective-permute-start.27 = (f32[1,1024]{1,0:T(1,128)S(1)}, f32[1,1024]{1,0:T(1,128)S(1)}, u32[]{:S(2)}, u32[]{:S(2)}) collective-permute-start(f32[1,1024]{1,0:T(1,128)S(1)} %get-tuple-element.24.refs_3_), channel_id=1, source_target_pairs={{0,13},{1,12},{2,15},{3,14},{4,9},{5,8},{6,11},{7,10},{8,5},{9,4},... | collective-permute-start | bytes 12296 | tf_op jit(solution)/shard_map/ppermute | solution.py:266
  58.1 6.6 %collective-permute-start.26 = (f32[1,1024]{1,0:T(1,128)S(1)}, f32[1,1024]{1,0:T(1,128)S(1)}, u32[]{:S(2)}, u32[]{:S(2)}) collective-permute-start(f32[1,1024]{1,0:T(1,128)S(1)} %get-tuple-element.24.refs_3_), channel_id=1, source_target_pairs={{0,12},{1,13},{2,14},{3,15},{4,8},{5,9},{6,10},{7,11},{8,4},{9,5},... | collective-permute-start | bytes 12296 | tf_op jit(solution)/shard_map/ppermute | solution.py:266
  58.5 8.3 %collective-permute-start.25 = (f32[1,1024]{1,0:T(1,128)S(1)}, f32[1,1024]{1,0:T(1,128)S(1)}, u32[]{:S(2)}, u32[]{:S(2)}) collective-permute-start(f32[1,1024]{1,0:T(1,128)S(1)} %get-tuple-element.24.refs_3_), channel_id=1, source_target_pairs={{0,11},{1,10},{2,9},{3,8},{4,15},{5,14},{6,13},{7,12},{8,3},{9,2},... | collective-permute-start | bytes 12296 | tf_op jit(solution)/shard_map/ppermute | solution.py:266
  59.9 7.5 %collective-permute-start.24 = (f32[1,1024]{1,0:T(1,128)S(1)}, f32[1,1024]{1,0:T(1,128)S(1)}, u32[]{:S(2)}, u32[]{:S(2)}) collective-permute-start(f32[1,1024]{1,0:T(1,128)S(1)} %get-tuple-element.24.refs_3_), channel_id=1, source_target_pairs={{0,10},{1,11},{2,8},{3,9},{4,14},{5,15},{6,12},{7,13},{8,2},{9,3},... | collective-permute-start | bytes 12296 | tf_op jit(solution)/shard_map/ppermute | solution.py:266
  62.1 6.5 %collective-permute-start.23 = (f32[1,1024]{1,0:T(1,128)S(1)}, f32[1,1024]{1,0:T(1,128)S(1)}, u32[]{:S(2)}, u32[]{:S(2)}) collective-permute-start(f32[1,1024]{1,0:T(1,128)S(1)} %get-tuple-element.24.refs_3_), channel_id=1, source_target_pairs={{0,9},{1,8},{2,11},{3,10},{4,13},{5,12},{6,15},{7,14},{8,1},{9,0},... | collective-permute-start | bytes 12296 | tf_op jit(solution)/shard_map/ppermute | solution.py:266
  62.5 6.6 %collective-permute-start.22 = (f32[1,1024]{1,0:T(1,128)S(1)}, f32[1,1024]{1,0:T(1,128)S(1)}, u32[]{:S(2)}, u32[]{:S(2)}) collective-permute-start(f32[1,1024]{1,0:T(1,128)S(1)} %get-tuple-element.24.refs_3_), channel_id=1, source_target_pairs={{0,8},{1,9},{2,10},{3,11},{4,12},{5,13},{6,14},{7,15},{8,0},{9,1},... | collective-permute-start | bytes 12296 | tf_op jit(solution)/shard_map/ppermute | solution.py:266
  64.7 5.8 %collective-permute-start.21 = (f32[1,1024]{1,0:T(1,128)S(1)}, f32[1,1024]{1,0:T(1,128)S(1)}, u32[]{:S(2)}, u32[]{:S(2)}) collective-permute-start(f32[1,1024]{1,0:T(1,128)S(1)} %get-tuple-element.24.refs_3_), channel_id=1, source_target_pairs={{0,7},{1,6},{2,5},{3,4},{4,3},{5,2},{6,1},{7,0},{8,15},{9,14},{10,... | collective-permute-start | bytes 12296 | tf_op jit(solution)/shard_map/ppermute | solution.py:266
  66.8 4.5 %collective-permute-start.20 = (f32[1,1024]{1,0:T(1,128)S(1)}, f32[1,1024]{1,0:T(1,128)S(1)}, u32[]{:S(2)}, u32[]{:S(2)}) collective-permute-start(f32[1,1024]{1,0:T(1,128)S(1)} %get-tuple-element.24.refs_3_), channel_id=1, source_target_pairs={{0,6},{1,7},{2,4},{3,5},{4,2},{5,3},{6,0},{7,1},{8,14},{9,15},{10,... | collective-permute-start | bytes 12296 | tf_op jit(solution)/shard_map/ppermute | solution.py:266
  67.4 3.9 %collective-permute-start.19 = (f32[1,1024]{1,0:T(1,128)S(1)}, f32[1,1024]{1,0:T(1,128)S(1)}, u32[]{:S(2)}, u32[]{:S(2)}) collective-permute-start(f32[1,1024]{1,0:T(1,128)S(1)} %get-tuple-element.24.refs_3_), channel_id=1, source_target_pairs={{0,5},{1,4},{2,7},{3,6},{4,1},{5,0},{6,3},{7,2},{8,13},{9,12},{10,... | collective-permute-start | bytes 12296 | tf_op jit(solution)/shard_map/ppermute | solution.py:266
  68.6 3.6 %collective-permute-start.18 = (f32[1,1024]{1,0:T(1,128)S(1)}, f32[1,1024]{1,0:T(1,128)S(1)}, u32[]{:S(2)}, u32[]{:S(2)}) collective-permute-start(f32[1,1024]{1,0:T(1,128)S(1)} %get-tuple-element.24.refs_3_), channel_id=1, source_target_pairs={{0,4},{1,5},{2,6},{3,7},{4,0},{5,1},{6,2},{7,3},{8,12},{9,13},{10,... | collective-permute-start | bytes 12296 | tf_op jit(solution)/shard_map/ppermute | solution.py:266
  69.1 3.1 %collective-permute-start.17 = (f32[1,1024]{1,0:T(1,128)S(1)}, f32[1,1024]{1,0:T(1,128)S(1)}, u32[]{:S(2)}, u32[]{:S(2)}) collective-permute-start(f32[1,1024]{1,0:T(1,128)S(1)} %get-tuple-element.24.refs_3_), channel_id=1, source_target_pairs={{0,3},{1,2},{2,1},{3,0},{4,7},{5,6},{6,5},{7,4},{8,11},{9,10},{10,... | collective-permute-start | bytes 12296 | tf_op jit(solution)/shard_map/ppermute | solution.py:266
  70.5 3.6 %collective-permute-start.16 = (f32[1,1024]{1,0:T(1,128)S(1)}, f32[1,1024]{1,0:T(1,128)S(1)}, u32[]{:S(2)}, u32[]{:S(2)}) collective-permute-start(f32[1,1024]{1,0:T(1,128)S(1)} %get-tuple-element.24.refs_3_), channel_id=1, source_target_pairs={{0,2},{1,3},{2,0},{3,1},{4,6},{5,7},{6,4},{7,5},{8,10},{9,11},{10,... | collective-permute-start | bytes 12296 | tf_op jit(solution)/shard_map/ppermute | solution.py:266
  71.3 2.7 %collective-permute-start.15 = (f32[1,1024]{1,0:T(1,128)S(1)}, f32[1,1024]{1,0:T(1,128)S(1)}, u32[]{:S(2)}, u32[]{:S(2)}) collective-permute-start(f32[1,1024]{1,0:T(1,128)S(1)} %get-tuple-element.24.refs_3_), channel_id=1, source_target_pairs={{0,1},{1,0},{2,3},{3,2},{4,5},{5,4},{6,7},{7,6},{8,9},{9,8},{10,11... | collective-permute-start | bytes 12296 | tf_op jit(solution)/shard_map/ppermute | solution.py:266
  (5 other events, 19.6 us)

commit v2 on v1

v2 whole, which is shorter than its diff:
```python
import functools
import math

import jax
import jax.numpy as jnp
from jax import lax
from jax.experimental import pallas as pl
from jax.experimental.pallas import tpu as pltpu
from jax.sharding import PartitionSpec as P

ITERS = 2
EPSILON = 0.02
LOG2E = math.log2(math.e)
AXES = ("row", "col")
TILE = 256
STEP = 32
EXT = 32
PAD = 16
F32 = jnp.float32
BF16 = jnp.bfloat16


def kappa_of(width):
    return 2.0 / (width * EPSILON)


def pieces(value):
    high = value.astype(BF16).astype(F32)
    rest = value - high
    mid = rest.astype(BF16).astype(F32)
    return high, mid, rest - mid


def select(index, values):
    out = jnp.zeros(index.shape, F32)
    for k, value in values.items():
        out = jnp.where(index == k, value, out)
    return out


def extras_y(index, c_term, mass):
    high, mid, low = pieces(c_term)
    return select(index, {0: high, 1: mid, 2: low, 3: 1.0, 4: 1.0, 5: 1.0, 6: mass})


def extras_x(index, b_term):
    high, mid, low = pieces(b_term)
    return select(index, {0: 1.0, 1: 1.0, 2: 1.0, 3: high, 4: mid, 5: low})


def rows_index(columns):
    return lax.broadcasted_iota(jnp.int32, (EXT, columns), 0)


def to_column(row):
    size = row.shape[1]
    eye = lax.broadcasted_iota(jnp.int32, (size, size), 0) == lax.broadcasted_iota(jnp.int32, (size, size), 1)
    return jnp.sum(jnp.where(eye, row, 0.0), axis=1, keepdims=True)


def to_row(column):
    size = column.shape[0]
    eye = lax.broadcasted_iota(jnp.int32, (size, size), 0) == lax.broadcasted_iota(jnp.int32, (size, size), 1)
    return jnp.sum(jnp.where(eye, column, 0.0), axis=0, keepdims=True)


def for_tiles(total, body):
    count = total // TILE
    if count <= 4:
        for t in range(count):
            body(pl.ds(t * TILE, TILE))
    else:

        @pl.loop(0, count)
        def _(t):
            body(pl.ds(pl.multiple_of(t * TILE, TILE), TILE))


def max_down(z_ref, rows):
    peak = z_ref[0:STEP, :]
    for r in range(STEP, rows, STEP):
        peak = jnp.maximum(peak, z_ref[r : r + STEP, :])
    return jnp.max(peak, axis=0, keepdims=True)


def exp_sum_down(z_ref, rows, scale, shift):
    total = jnp.zeros((STEP, TILE), F32)
    for r in range(0, rows, STEP):
        total = total + jnp.exp2((z_ref[r : r + STEP, :] - shift) * scale)
    return jnp.sum(total, axis=0, keepdims=True)


def prep_kernel(log_ny, y_ref, my_ref, out_ref):
    width = y_ref.shape[1]
    y = y_ref[...]
    yf = y.astype(F32)
    norm = jnp.sum(yf * yf, axis=1, keepdims=True)
    mass = to_column(my_ref[...].astype(F32))
    c_term = (mass - log_ny) / kappa_of(width) - 0.5 * norm
    index = lax.broadcasted_iota(jnp.int32, (y.shape[0], EXT), 1)
    ext = extras_y(index, c_term, mass).astype(BF16)
    for k in range(out_ref.shape[0]):
        out_ref[k, :, :width] = y
        out_ref[k, :, width:] = ext


def prep_x_kernel(xt_ref, xa_ref):
    width, n = xt_ref.shape
    xa_ref[:width, :] = xt_ref[...]
    xa_ref[width:, :] = extras_x(rows_index(n), jnp.zeros((1, n), F32)).astype(BF16)


def first_kernel(log_nx, xa0_ref, mx_ref, ya_ref, b_ref, l_ref, m_ref, rows_ref, xa_ref, z_ref, zc_ref):
    nd, yd, depth = ya_ref.shape
    n = mx_ref.shape[1]
    width = depth - EXT
    ny = nd * yd
    scale = kappa_of(width) * LOG2E
    la2 = (mx_ref[...].astype(F32) - log_nx) * LOG2E
    y_rows = ya_ref[...].reshape(ny, depth)

    def row_tile(t):
        z_ref[...] = jnp.dot(y_rows, xa0_ref[:, t], preferred_element_type=F32)
        peak = max_down(z_ref, ny)
        b_ref[:, t] = -peak - jnp.log(exp_sum_down(z_ref, ny, scale, peak)) * (LOG2E / scale)

    for_tiles(n, row_tile)
    b_term = b_ref[...] + la2 / scale
    b_ref[...] = b_term
    xa_ref[:width, :] = xa0_ref[:width, :]
    xa_ref[width:, :] = extras_x(rows_index(n), b_term).astype(BF16)
    rows_ref[...] = xa_ref[...].T
    y_tile = TILE // yd

    def col_tile(t):
        y_part = ya_ref[pl.ds(t.start // yd, y_tile)].reshape(TILE, depth)
        zc_ref[...] = lax.dot_general(
            rows_ref[...], y_part, (((1,), (1,)), ((), ())), preferred_element_type=F32
        )
        peak = max_down(zc_ref, n)
        m_ref[:, t] = peak
        lse = scale * peak + jnp.log(exp_sum_down(zc_ref, n, scale, peak)) * LOG2E
        l_ref[:, :, t] = jnp.broadcast_to(lse[None], (nd, 1, TILE))

    for_tiles(ny, col_tile)


def plan_kernel(rows_ref, ya_ref, m_ref, high_ref, low_ref, yt_ref, zc_ref):
    nd, yd, depth = ya_ref.shape
    n = rows_ref.shape[0]
    scale = kappa_of(depth - EXT) * LOG2E
    y_tile = TILE // yd

    def col_tile(t):
        y_part = ya_ref[pl.ds(t.start // yd, y_tile)].reshape(TILE, depth)
        yt_ref[:, t] = y_part.T
        zc_ref[...] = lax.dot_general(
            rows_ref[...], y_part, (((1,), (1,)), ((), ())), preferred_element_type=F32
        )
        peak = m_ref[:, t]
        for r in range(0, n, STEP):
            value = jnp.exp2((zc_ref[r : r + STEP, :] - peak) * scale)
            high = value.astype(BF16)
            high_ref[r : r + STEP, t] = high
            low_ref[r : r + STEP, t] = (value - high.astype(F32)).astype(BF16)

    for_tiles(nd * yd, col_tile)


def stack(out_ref, width, points, factor):
    moved = points.astype(F32) * factor
    high = moved.astype(BF16)
    out_ref[:width, :] = high
    out_ref[width : 2 * width, :] = (moved - high.astype(F32)).astype(BF16)
    one, two, three = pieces(factor)
    index = lax.broadcasted_iota(jnp.int32, (PAD, factor.shape[1]), 0)
    out_ref[2 * width :, :] = select(index, {0: one, 1: two, 2: three}).astype(BF16)


def unstack(product, width):
    ext = product[2 * width :]
    return product[:width] + product[width : 2 * width], (ext[0:1] + ext[1:2]) + ext[2:3]


def second_kernel(
    log_nx, log_ny, xt_ref, mx_ref, b_ref, l_ref, m_ref, yt_ref, high_ref, low_ref,
    f_ref, r_ref, v_ref, s_ref, g_ref, xs_ref, gt_ref,
):
    width, n = xt_ref.shape
    ny = m_ref.shape[1]
    nd, yd = g_ref.shape[:2]
    kappa = kappa_of(width)
    scale = kappa * LOG2E
    l_all = l_ref[...]
    peak = jnp.max(l_all, axis=0)
    lse2 = peak + jnp.log(jnp.sum(jnp.exp2(l_all - peak[None]), axis=0)) * LOG2E
    old = yt_ref[width:, :].astype(F32)
    c_old = (old[0:1] + old[1:2]) + old[2:3]
    lb2 = (old[6:7] - log_ny) * LOG2E
    c_term = c_old + (lb2 - lse2) / scale
    v = jnp.exp2(scale * m_ref[...] + (lb2 - lse2))
    v_ref[...] = v
    one, two, three = pieces(v)
    index = lax.broadcasted_iota(jnp.int32, (PAD, ny), 0)
    v_rows = select(index, {0: one, 1: two, 2: three}).astype(BF16)
    across = (((1,), (1,)), ((), ()))
    sums = lax.dot_general(v_rows, high_ref[...], across, preferred_element_type=F32) + lax.dot_general(
        v_rows, low_ref[...], across, preferred_element_type=F32
    )
    rowsum = (sums[0:1] + sums[1:2]) + sums[2:3]
    log_row = jnp.log(rowsum)
    xt = xt_ref[...]
    xf = xt.astype(F32)
    f_ref[...] = jnp.sum(xf * xf, axis=0, keepdims=True) / width + EPSILON * (kappa * b_ref[...] - log_row)
    r = jnp.exp(mx_ref[...].astype(F32) - log_nx - log_row)
    r_ref[...] = r
    stack(xs_ref, width, xt, r)
    high, mid, low = pieces(c_term)
    index = lax.broadcasted_iota(jnp.int32, (EXT, TILE), 0)
    for k in range(ny // TILE):
        t = slice(k * TILE, (k + 1) * TILE)
        product = jnp.dot(xs_ref[...], high_ref[:, t], preferred_element_type=F32) + jnp.dot(
            xs_ref[...], low_ref[:, t], preferred_element_type=F32
        )
        moment, total = unstack(product, width)
        total = total * v[:, t]
        s_ref[:, :, t] = jnp.broadcast_to(total[None], (nd, 1, TILE))
        gt_ref[:width, t] = yt_ref[:width, t].astype(F32) * total - moment * v[:, t]
        one, two, three = pieces(total)
        gt_ref[width:, t] = select(index, {0: one, 1: two, 2: three, 3: high[:, t], 4: mid[:, t], 5: low[:, t]})
    g_ref[...] = gt_ref[...].T.astype(BF16).reshape(nd, yd, width + EXT)


def grad_x_kernel(log_nx, log_ny, xt_ref, r_ref, v_ref, s_ref, yt_ref, high_ref, low_ref, out_ref, ys_ref):
    width, n = xt_ref.shape
    ny = v_ref.shape[1]
    mass = yt_ref[width:, :].astype(F32)[6:7]
    colsum = jnp.sum(s_ref[...], axis=0)
    q = v_ref[...] * jnp.exp(mass + log_nx - jnp.log(colsum))
    stack(ys_ref, width, yt_ref[:width, :], q)
    across = (((1,), (1,)), ((), ()))
    for k in range(n // TILE):
        t = slice(k * TILE, (k + 1) * TILE)
        product = lax.dot_general(
            ys_ref[...], high_ref[t, :], across, preferred_element_type=F32
        ) + lax.dot_general(ys_ref[...], low_ref[t, :], across, preferred_element_type=F32)
        moved, total = unstack(product, width)
        out_ref[:, t] = (xt_ref[:, t].astype(F32) * total - moved) * (r_ref[:, t] * (1.0 / ny))


def grad_y_kernel(y_ref, my_ref, g_ref, out_ref, pot_ref):
    yd, width = y_ref.shape
    nd = g_ref.shape[0]
    total = g_ref[0].astype(F32)
    for k in range(1, nd):
        total = total + g_ref[k].astype(F32)
    part = total[:, width:]
    colsum = (part[:, 0:1] + part[:, 1:2]) + part[:, 2:3]
    c_term = ((part[:, 3:4] + part[:, 4:5]) + part[:, 5:6]) * (1.0 / nd)
    mass = to_column(my_ref[...].astype(F32))
    out_ref[...] = total[:, :width] * (jnp.exp(mass) / colsum)
    yf = y_ref[...].astype(F32)
    norm = jnp.sum(yf * yf, axis=1, keepdims=True)
    pot = norm / width - EPSILON * (jnp.log(colsum) - kappa_of(width) * c_term)
    pot_ref[...] = to_row(pot)


def call(kernel, outs, scratch, limit, *args):
    return pl.pallas_call(
        kernel,
        out_shape=outs,
        in_specs=[pl.BlockSpec(memory_space=pltpu.VMEM)] * len(args),
        out_specs=jax.tree.map(lambda _: pl.BlockSpec(memory_space=pltpu.VMEM), outs),
        scratch_shapes=scratch,
        compiler_params=pltpu.CompilerParams(vmem_limit_bytes=limit),
    )(*args)


def shape(dims, dtype=F32):
    return jax.ShapeDtypeStruct(dims, dtype)


def on_device(points_x, points_y, mass_x, mass_y):
    n, width = points_x.shape
    yd = points_y.shape[0]
    nd = lax.axis_size("row") * lax.axis_size("col")
    ny = nd * yd
    log_nx, log_ny = math.log(n * nd), math.log(ny)
    depth = width + EXT
    limit = (8 + 24 * ny // 1024) * 1024 * 1024 if ny <= 1024 else 56 * 1024 * 1024
    run = functools.partial
    xt = points_x.T
    mx = mass_x.reshape(1, n)
    my = mass_y.reshape(1, yd)
    y_own = call(run(prep_kernel, log_ny), shape((nd, yd, depth), BF16), [], limit, points_y, my)
    ya = lax.all_to_all(y_own, AXES, 0, 0, tiled=True)
    xa = call(prep_x_kernel, shape((depth, n), BF16), [], limit, xt)
    b_term, lse, peak, rows = call(
        run(first_kernel, log_nx),
        (shape((1, n)), shape((nd, 1, ny)), shape((1, ny)), shape((n, depth), BF16)),
        [pltpu.VMEM((depth, n), BF16), pltpu.VMEM((ny, TILE), F32), pltpu.VMEM((n, TILE), F32)],
        limit, xa, mx, ya,
    )
    lse = lax.all_to_all(lse, AXES, 0, 0, tiled=True)
    high, low, yt = call(
        plan_kernel,
        (shape((n, ny), BF16), shape((n, ny), BF16), shape((depth, ny), BF16)),
        [pltpu.VMEM((n, TILE), F32)],
        limit, rows, ya, peak,
    )
    f_pot, r, v, sums, g_part = call(
        run(second_kernel, log_nx, log_ny),
        (shape((1, n)), shape((1, n)), shape((1, ny)), shape((nd, 1, ny)), shape((nd, yd, depth), BF16)),
        [pltpu.VMEM((2 * width + PAD, n), BF16), pltpu.VMEM((depth, ny), F32)],
        limit, xt, mx, b_term, lse, peak, yt, high, low,
    )
    sums = lax.all_to_all(sums, AXES, 0, 0, tiled=True)
    g_all = lax.all_to_all(g_part, AXES, 0, 0, tiled=True)
    grad_xt = call(
        run(grad_x_kernel, log_nx, log_ny),
        shape((width, n)),
        [pltpu.VMEM((2 * width + PAD, ny), BF16)],
        limit, xt, r, v, sums, yt, high, low,
    )
    grad_y, g_pot = call(
        grad_y_kernel, (shape((yd, width)), shape((1, yd))), [], limit, points_y, my, g_all
    )
    return f_pot.reshape(n), g_pot.reshape(yd), grad_xt.T, grad_y


def solution(mesh):
    in_specs = (
        P(("groups", "row", "col"), None),
        P(("groups", "col", "row"), None),
        P(("groups", "row", "col")),
        P(("groups", "col", "row")),
    )
    out_specs = (
        P(("groups", "row", "col")),
        P(("groups", "col", "row")),
        P(("groups", "row", "col"), None),
        P(("groups", "col", "row"), None),
    )
    return jax.shard_map(
        on_device, mesh=mesh, in_specs=in_specs, out_specs=out_specs, check_vma=False
    )
```

time: 78.5 us -> 63.2 us (0.81)
  starting transfers between devices: 44.7 us -> 14.4 us
  waiting for transfers between devices: 7.51 us -> 19 us
  local copies, waits for them, and re-layouts: 2.31 us -> 7.54 us
  blocking collectives: 11.7 us -> 9.47 us
    ppermute x30 -> x0, starting transfers between devices: 41.1 us -> none  [everyone(): lax.ppermute(value, AXES, [(s, s ^ k) for s in range(nd)])]
    all_to_all x0 -> x2, waiting for transfers between devices: none -> 12.8 us  [the longest x1 8.41 us: on_device(): ya = lax.all_to_all(y_own, AXES, 0, 0, tiled=True)]
    all_to_all x0 -> x2, starting transfers between devices: none -> 10.9 us  [the longest x1 7.39 us: on_device(): ya = lax.all_to_all(y_own, AXES, 0, 0, tiled=True)]
    ppermute x30 -> x0, waiting for transfers between devices: 7.51 us -> none  [everyone(): lax.ppermute(value, AXES, [(s, s ^ k) for s in range(nd)])]
    all_to_all x1, waiting for transfers between devices: 0.01 us -> 6.12 us  [on_device(): g_all = lax.all_to_all(g_part, AXES, 0, 0, tiled=True)]
    unnamed x12 -> x18, local copies, waits for them, and re-layouts: 2.3 us -> 6.85 us
    all_to_all x1, blocking collectives: 11.7 us -> 9.47 us  [on_device(): sums = lax.all_to_all(sums, AXES, 0, 0, tiled=True)]
    pallas_call x5 -> x7, Pallas kernels: 11.2 us -> 11.4 us  [call(): pl.pallas_call(kernel, out_shape=outs, in_specs=[pl.BlockSpec(memory_spac...]
  transfers between devices with their start and end apart: 31 -> 3, of which waited for: 7 -> 3; matrix products, arithmetic and copies ran while one was open for 0% -> 1% of each run, Pallas kernels for 4% -> 5%
where the time goes in v2:
time: 63.2 us; the launch traced here: 62.5 us
  waiting for transfers between devices  19 us (30%)
  starting transfers between devices  14.4 us (23%)
  Pallas kernels  11.4 us (18%)
  blocking collectives  9.47 us (15%)
  local copies, waits for them, and re-layouts  7.54 us (12%)
  between operations  0.71 us (1%)
    pallas_call x7, Pallas kernels, call(): pl.pallas_call(kernel, out_shape=outs, in_specs=[pl.BlockSpec(memory_spac...  11.4 us
    all_to_all x1, blocking collectives, on_device(): sums = lax.all_to_all(sums, AXES, 0, 0, tiled=True)  9.47 us
    all_to_all x1, waiting for transfers between devices, on_device(): ya = lax.all_to_all(y_own, AXES, 0, 0, tiled=True)  8.41 us
    all_to_all x1, starting transfers between devices, on_device(): ya = lax.all_to_all(y_own, AXES, 0, 0, tiled=True)  7.39 us
    unnamed x18, local copies, waits for them, and re-layouts  6.85 us
    all_to_all x1, waiting for transfers between devices, on_device(): g_all = lax.all_to_all(g_part, AXES, 0, 0, tiled=True)  6.12 us
    all_to_all x1, waiting for transfers between devices, on_device(): lse = lax.all_to_all(lse, AXES, 0, 0, tiled=True)  4.44 us
    all_to_all x1, starting transfers between devices, on_device(): g_all = lax.all_to_all(g_part, AXES, 0, 0, tiled=True)  3.53 us
  transfers between devices with their start and end apart: 3, of which 3 were waited for; matrix products, arithmetic and copies ran while one was open for 1% of the time, Pallas kernels for 5%

profile of v2, /device:TPU:0, one launch (start us, length us, event | category | flops | bytes accessed | tf_op | source)
XLA Modules:
  0.0 62.5 jit_solution(13721818982890825931)
XLA Ops:
  0.6 0.0 copy-start.4
  0.6 0.0 copy-start.5
  0.7 0.7 %copy-done.5 = bf16[64,96]{1,0:T(8,128)(2,1)S(1)} copy-done((bf16[64,96]{1,0:T(8,128)(2,1)S(1)}, bf16[64,96]{1,0:T(8,128)(2,1)}, u32[]{:S(2)}) %copy-start.5) | copy-done | bytes 12312
  1.4 0.0 copy-start.7
  1.4 0.7 %copy-done.7 = bf16[64]{0:T(256)(128)(2,1)S(1)} copy-done((bf16[64]{0:T(256)(128)(2,1)S(1)}, bf16[64]{0:T(256)(128)(2,1)}, u32[]{:S(2)}) %copy-start.7) | copy-done | bytes 152
  2.1 0.9 %shard_map.76 = bf16[16,64,128]{2,1,0:T(8,128)(2,1)} custom-call(bf16[64,96]{1,0:T(8,128)(2,1)S(1)} %copy-done.5, bf16[1,64]{1,0:T(2,128)(2,1)S(1)} %bitcast.8), custom_call_target="tpu_custom_call" | custom-call | tf_op jit(solution)/shard_map/pallas_call | solution.py:269
  3.0 7.4 %all-to-all-start = ((bf16[16,64,128]{2,1,0:T(8,128)(2,1)}), bf16[16,64,128]{2,1,0:T(8,128)(2,1)S(1)}, u32[]{:S(2)}, u32[]{:S(2)}) async-start(bf16[16,64,128]{2,1,0:T(8,128)(2,1)} %shard_map.76), calls=%async_computation | async-start | bytes 524288 | tf_op jit(solution)/shard_map/all_to_all | solution.py:296
  10.4 0.7 %reshape.20.mx_ref = bf16[1,1024]{1,0:T(2,128)(2,1)S(1)} reshape(bf16[1024]{0:T(1024)(128)(2,1)} %param.6) | data formatting | bytes 4096 | tf_op jit(solution)/shard_map/reshape | solution.py:293
  11.1 0.0 copy-start.3
  11.1 0.9 %copy-done.3 = bf16[1024,96]{0,1:T(8,128)(2,1)S(1)} copy-done((bf16[1024,96]{0,1:T(8,128)(2,1)S(1)}, bf16[1024,96]{0,1:T(8,128)(2,1)}, u32[]{:S(2)}) %copy-start.3) | copy-done | bytes 196632
  12.0 8.4 %all-to-all-done.ya_ref = bf16[16,64,128]{2,1,0:T(8,128)(2,1)S(1)} async-done(((bf16[16,64,128]{2,1,0:T(8,128)(2,1)}), bf16[16,64,128]{2,1,0:T(8,128)(2,1)S(1)}, u32[]{:S(2)}, u32[]{:S(2)}) %all-to-all-start) | async-done | bytes 262176 | tf_op jit(solution)/shard_map/all_to_all | solution.py:296
  20.4 3.1 %shard_map.77 = (f32[1,1024]{1,0:T(1,128)S(1)}, f32[16,1,1024]{2,1,0:T(1,128)}, f32[1,1024]{1,0:T(1,128)S(1)}, bf16[1024,128]{1,0:T(8,128)(2,1)S(1)}) custom-call(bf16[128,1024]{1,0:T(8,128)(2,1)S(1)} %shard_map.75.xa0_ref, bf16[1,1024]{1,0:T(2,128)(2,1)S(1)} %reshape.20.mx_ref, bf16[16,64,128]{2,1,0:T(8,128)(2,1)S(1)} %all-to-all-done.ya_ref), custom_call_target="tpu_custom_call" | custom-call | tf_op jit(solution)/shard_map/pallas_call | solution.py:269
  23.6 3.5 %all-to-all-start.1 = ((f32[16,1,1024]{2,1,0:T(1,128)}), f32[16,1,1024]{2,1,0:T(1,128)S(1)}, u32[]{:S(2)}, u32[]{:S(2)}) async-start(f32[16,1,1024]{2,1,0:T(1,128)} %get-tuple-element.19), calls=%async_computation.1 | async-start | bytes 131072 | tf_op jit(solution)/shard_map/all_to_all | solution.py:304
  27.1 1.1 %shard_map.78 = (bf16[1024,1024]{1,0:T(8,128)(2,1)S(1)}, bf16[1024,1024]{1,0:T(8,128)(2,1)S(1)}, bf16[128,1024]{1,0:T(8,128)(2,1)S(1)}) custom-call(bf16[1024,128]{1,0:T(8,128)(2,1)S(1)} %get-tuple-element.21.rows_ref, bf16[16,64,128]{2,1,0:T(8,128)(2,1)S(1)} %all-to-all-done.ya_ref, f32[1,1024]{1,0:T(1,128)S(1)} %get-tuple-element.20.m_ref), custom_call_target="tpu_custom_call" | custom-call | tf_op jit(solution)/shard_map/pallas_call | solution.py:269
  28.1 0.0 copy-start
  28.2 1.3 %copy-done = bf16[1024,1024]{1,0:T(8,128)(2,1)} copy-done((bf16[1024,1024]{1,0:T(8,128)(2,1)}, bf16[1024,1024]{1,0:T(8,128)(2,1)S(1)}, u32[]{:S(2)}) %copy-start) | copy-done | bytes 2097176
  29.5 4.4 %all-to-all-done.1.l_ref = f32[16,1,1024]{2,1,0:T(1,128)S(1)} async-done(((f32[16,1,1024]{2,1,0:T(1,128)}), f32[16,1,1024]{2,1,0:T(1,128)S(1)}, u32[]{:S(2)}, u32[]{:S(2)}) %all-to-all-start.1) | async-done | bytes 65568 | tf_op jit(solution)/shard_map/all_to_all | solution.py:304
  33.9 0.0 copy-done.4
  33.9 0.0 copy-start.1
  33.9 1.6 %copy-done.1 = bf16[1024,1024]{1,0:T(8,128)(2,1)S(1)} copy-done((bf16[1024,1024]{1,0:T(8,128)(2,1)S(1)}, bf16[1024,1024]{1,0:T(8,128)(2,1)}, u32[]{:S(2)}) %copy-start.1) | copy-done | bytes 2097176
  35.5 3.1 %shard_map.79 = (f32[1,1024]{1,0:T(1,128)}, f32[1,1024]{1,0:T(1,128)S(1)}, f32[1,1024]{1,0:T(1,128)S(1)}, f32[16,1,1024]{2,1,0:T(1,128)S(1)}, bf16[16,64,128]{2,1,0:T(8,128)(2,1)}) custom-call(bf16[96,1024]{1,0:T(8,128)(2,1)S(1)} %bitcast.6, bf16[1,1024]{1,0:T(2,128)(2,1)S(1)} %reshape.20.mx_ref, f32[1,1024]{1,0:T(1,128)S(1)} %get-tuple-element.18.b_ref, ...), custom_call_target="tpu_custom_call" | custom-call | tf_op jit(solution)/shard_map/pallas_call | solution.py:269
  38.6 9.5 %all_to_all.20.s_ref = f32[16,1,1024]{2,1,0:T(1,128)S(1)} all-to-all(f32[16,1,1024]{2,1,0:T(1,128)S(1)} %get-tuple-element.30), channel_id=1, replica_groups=mesh['groups'=2,'row'=8,'col'=2] {'row','col'}, dimensions={0} | all-to-all | bytes 131072 | tf_op jit(solution)/shard_map/all_to_all | solution.py:317
  48.1 3.5 %all-to-all-start.2 = ((bf16[16,64,128]{2,1,0:T(8,128)(2,1)}), bf16[16,64,128]{2,1,0:T(8,128)(2,1)S(1)}, u32[]{:S(2)}, u32[]{:S(2)}) async-start(bf16[16,64,128]{2,1,0:T(8,128)(2,1)} %get-tuple-element.26), calls=%async_computation.2 | async-start | bytes 524288 | tf_op jit(solution)/shard_map/all_to_all | solution.py:318
  51.6 0.0 copy-start.2
  51.6 1.6 %copy-done.2 = bf16[1024,1024]{1,0:T(8,128)(2,1)S(1)} copy-done((bf16[1024,1024]{1,0:T(8,128)(2,1)S(1)}, bf16[1024,1024]{1,0:T(8,128)(2,1)}, u32[]{:S(2)}) %copy-start.2) | copy-done | bytes 2097176
  53.2 0.0 copy-start.6
  53.2 0.0 copy-start.8
  53.2 2.3 %shard_map.81 = f32[96,1024]{1,0:T(8,128)} custom-call(bf16[96,1024]{1,0:T(8,128)(2,1)S(1)} %bitcast.7, f32[1,1024]{1,0:T(1,128)S(1)} %get-tuple-element.28.r_ref, f32[1,1024]{1,0:T(1,128)S(1)} %get-tuple-element.29.v_ref, f32[16,1,1024]{2,1,0:T(1,128)S(1)} %all_to_all.20.s_ref, bf16[128,1024]{1,0:T(8,128)(2,1)S(1)} %get-tuple-element.22.yt_ref, ...), custom_call_target="tpu_custom_call" | custom-call | tf_op jit(solution)/shard_map/pallas_call | solution.py:269
  55.5 6.1 %all-to-all-done.2.g_ref = bf16[16,64,128]{2,1,0:T(8,128)(2,1)S(1)} async-done(((bf16[16,64,128]{2,1,0:T(8,128)(2,1)}), bf16[16,64,128]{2,1,0:T(8,128)(2,1)S(1)}, u32[]{:S(2)}, u32[]{:S(2)}) %all-to-all-start.2) | async-done | bytes 262176 | tf_op jit(solution)/shard_map/all_to_all | solution.py:318
  61.6 0.0 copy-done.6
  61.6 0.0 copy-done.8
  61.6 0.9 %shard_map.80 = (f32[64,96]{1,0:T(8,128)}, f32[1,64]{1,0:T(1,128)}) custom-call(bf16[64,96]{1,0:T(8,128)(2,1)S(1)} %copy-done.6, bf16[1,64]{1,0:T(2,128)(2,1)S(1)} %bitcast.9, bf16[16,64,128]{2,1,0:T(8,128)(2,1)S(1)} %all-to-all-done.2.g_ref), custom_call_target="tpu_custom_call" | custom-call | tf_op jit(solution)/shard_map/pallas_call | solution.py:269
  (1 shorter events, 0.0 us)
Async XLA Ops:
  0.6 33.3 %copy-start.4 = (bf16[1024,96]{0,1:T(8,128)(2,1)S(1)}, bf16[1024,96]{0,1:T(8,128)(2,1)}, u32[]{:S(2)}) copy-start(bf16[1024,96]{0,1:T(8,128)(2,1)} %param.4) | copy-start | bytes 589828
  0.6 0.8 %copy-start.5 = (bf16[64,96]{1,0:T(8,128)(2,1)S(1)}, bf16[64,96]{1,0:T(8,128)(2,1)}, u32[]{:S(2)}) copy-start(bf16[64,96]{1,0:T(8,128)(2,1)} %y_ref.3) | copy-start | bytes 36868
  1.4 0.7 %copy-start.7 = (bf16[64]{0:T(256)(128)(2,1)S(1)}, bf16[64]{0:T(256)(128)(2,1)}, u32[]{:S(2)}) copy-start(bf16[64]{0:T(256)(128)(2,1)} %param.7) | copy-start | bytes 388
  3.0 17.4 %all-to-all-start = ((bf16[16,64,128]{2,1,0:T(8,128)(2,1)}), bf16[16,64,128]{2,1,0:T(8,128)(2,1)S(1)}, u32[]{:S(2)}, u32[]{:S(2)}) async-start(bf16[16,64,128]{2,1,0:T(8,128)(2,1)} %shard_map.76), calls=%async_computation | async-start | bytes 524288 | tf_op jit(solution)/shard_map/all_to_all | solution.py:296
  11.1 0.9 %copy-start.3 = (bf16[1024,96]{0,1:T(8,128)(2,1)S(1)}, bf16[1024,96]{0,1:T(8,128)(2,1)}, u32[]{:S(2)}) copy-start(bf16[1024,96]{0,1:T(8,128)(2,1)} %param.4) | copy-start | bytes 589828
  23.6 10.4 %all-to-all-start.1 = ((f32[16,1,1024]{2,1,0:T(1,128)}), f32[16,1,1024]{2,1,0:T(1,128)S(1)}, u32[]{:S(2)}, u32[]{:S(2)}) async-start(f32[16,1,1024]{2,1,0:T(1,128)} %get-tuple-element.19), calls=%async_computation.1 | async-start | bytes 131072 | tf_op jit(solution)/shard_map/all_to_all | solution.py:304
  28.1 1.3 %copy-start = (bf16[1024,1024]{1,0:T(8,128)(2,1)}, bf16[1024,1024]{1,0:T(8,128)(2,1)S(1)}, u32[]{:S(2)}) copy-start(bf16[1024,1024]{1,0:T(8,128)(2,1)S(1)} %get-tuple-element.24.low_ref) | copy-start | bytes 6291460
  33.9 1.6 %copy-start.1 = (bf16[1024,1024]{1,0:T(8,128)(2,1)S(1)}, bf16[1024,1024]{1,0:T(8,128)(2,1)}, u32[]{:S(2)}) copy-start(bf16[1024,1024]{1,0:T(8,128)(2,1)} %copy-done) | copy-start | bytes 6291460
  48.1 13.5 %all-to-all-start.2 = ((bf16[16,64,128]{2,1,0:T(8,128)(2,1)}), bf16[16,64,128]{2,1,0:T(8,128)(2,1)S(1)}, u32[]{:S(2)}, u32[]{:S(2)}) async-start(bf16[16,64,128]{2,1,0:T(8,128)(2,1)} %get-tuple-element.26), calls=%async_computation.2 | async-start | bytes 524288 | tf_op jit(solution)/shard_map/all_to_all | solution.py:318
  51.6 1.6 %copy-start.2 = (bf16[1024,1024]{1,0:T(8,128)(2,1)S(1)}, bf16[1024,1024]{1,0:T(8,128)(2,1)}, u32[]{:S(2)}) copy-start(bf16[1024,1024]{1,0:T(8,128)(2,1)} %copy-done) | copy-start | bytes 6291460
  53.2 8.4 %copy-start.6 = (bf16[64,96]{1,0:T(8,128)(2,1)S(1)}, bf16[64,96]{1,0:T(8,128)(2,1)}, u32[]{:S(2)}) copy-start(bf16[64,96]{1,0:T(8,128)(2,1)} %y_ref.3) | copy-start | bytes 36868
  53.2 8.4 %copy-start.8 = (bf16[64]{0:T(256)(128)(2,1)S(1)}, bf16[64]{0:T(256)(128)(2,1)}, u32[]{:S(2)}) copy-start(bf16[64]{0:T(256)(128)(2,1)} %param.7) | copy-start | bytes 388

commit v3 on v2

--- a/solution.py
+++ b/solution.py
@@ -11,11 +11,11 @@
 ITERS = 2
 EPSILON = 0.02
 LOG2E = math.log2(math.e)
-AXES = ("row", "col")
 TILE = 256
 STEP = 32
 EXT = 32
 PAD = 16
+LANES = 128
 F32 = jnp.float32
 BF16 = jnp.bfloat16
 
@@ -110,17 +110,22 @@
     xa_ref[width:, :] = extras_x(rows_index(n), jnp.zeros((1, n), F32)).astype(BF16)
 
 
-def first_kernel(log_nx, xa0_ref, mx_ref, ya_ref, b_ref, l_ref, m_ref, rows_ref, xa_ref, z_ref, zc_ref):
-    nd, yd, depth = ya_ref.shape
+def first_kernel(
+    log_nx, xa0_ref, mx_ref, mine_ref, other_ref, ya_ref, b_ref, l_ref, m_ref, rows_ref, xa_ref, z_ref, zc_ref
+):
+    rows, yd, depth = mine_ref.shape
     n = mx_ref.shape[1]
     width = depth - EXT
-    ny = nd * yd
+    half = rows * yd
+    ny = 2 * half
     scale = kappa_of(width) * LOG2E
     la2 = (mx_ref[...].astype(F32) - log_nx) * LOG2E
-    y_rows = ya_ref[...].reshape(ny, depth)
+    col = lax.axis_index("col")
+    ya_ref[pl.ds(pl.multiple_of(col * half, half), half), :] = mine_ref[...].reshape(half, depth)
+    ya_ref[pl.ds(pl.multiple_of((1 - col) * half, half), half), :] = other_ref[...].reshape(half, depth)
 
     def row_tile(t):
-        z_ref[...] = jnp.dot(y_rows, xa0_ref[:, t], preferred_element_type=F32)
+        z_ref[...] = jnp.dot(ya_ref[...], xa0_ref[:, t], preferred_element_type=F32)
         peak = max_down(z_ref, ny)
         b_ref[:, t] = -peak - jnp.log(exp_sum_down(z_ref, ny, scale, peak)) * (LOG2E / scale)
 
@@ -130,29 +135,26 @@
     xa_ref[:width, :] = xa0_ref[:width, :]
     xa_ref[width:, :] = extras_x(rows_index(n), b_term).astype(BF16)
     rows_ref[...] = xa_ref[...].T
-    y_tile = TILE // yd
 
     def col_tile(t):
-        y_part = ya_ref[pl.ds(t.start // yd, y_tile)].reshape(TILE, depth)
         zc_ref[...] = lax.dot_general(
-            rows_ref[...], y_part, (((1,), (1,)), ((), ())), preferred_element_type=F32
+            rows_ref[...], ya_ref[t, :], (((1,), (1,)), ((), ())), preferred_element_type=F32
         )
         peak = max_down(zc_ref, n)
         m_ref[:, t] = peak
         lse = scale * peak + jnp.log(exp_sum_down(zc_ref, n, scale, peak)) * LOG2E
-        l_ref[:, :, t] = jnp.broadcast_to(lse[None], (nd, 1, TILE))
+        l_ref[:, :, t] = jnp.broadcast_to(lse[None], (l_ref.shape[0], 1, TILE))
 
     for_tiles(ny, col_tile)
 
 
 def plan_kernel(rows_ref, ya_ref, m_ref, high_ref, low_ref, yt_ref, zc_ref):
-    nd, yd, depth = ya_ref.shape
+    ny, depth = ya_ref.shape
     n = rows_ref.shape[0]
     scale = kappa_of(depth - EXT) * LOG2E
-    y_tile = TILE // yd
 
     def col_tile(t):
-        y_part = ya_ref[pl.ds(t.start // yd, y_tile)].reshape(TILE, depth)
+        y_part = ya_ref[t, :]
         yt_ref[:, t] = y_part.T
         zc_ref[...] = lax.dot_general(
             rows_ref[...], y_part, (((1,), (1,)), ((), ())), preferred_element_type=F32
@@ -164,7 +166,7 @@
             high_ref[r : r + STEP, t] = high
             low_ref[r : r + STEP, t] = (value - high.astype(F32)).astype(BF16)
 
-    for_tiles(nd * yd, col_tile)
+    for_tiles(ny, col_tile)
 
 
 def stack(out_ref, width, points, factor):
@@ -182,22 +184,41 @@
     return product[:width] + product[width : 2 * width], (ext[0:1] + ext[1:2]) + ext[2:3]
 
 
+def to_lanes(row):
+    return jnp.concatenate([row[:, k : k + LANES] for k in range(0, row.shape[1], LANES)], axis=0)
+
+
+def from_lanes(block):
+    return jnp.concatenate([block[k : k + 1] for k in range(block.shape[0])], axis=1)
+
+
+def write_sums(ref, start, row):
+    count = row.shape[1] // LANES
+    for k, part in enumerate(pieces(row)):
+        ref[start + k * count : start + (k + 1) * count, :] = to_lanes(part)
+
+
+def sums_rows(ny):
+    return -(-3 * ny // LANES // 16) * 16
+
+
 def second_kernel(
-    log_nx, log_ny, xt_ref, mx_ref, b_ref, l_ref, m_ref, yt_ref, high_ref, low_ref,
-    f_ref, r_ref, v_ref, s_ref, g_ref, xs_ref, gt_ref,
+    log_nx, log_ny, xt_ref, mx_ref, b_ref, l_ref, other_ref, m_ref, yt_ref, high_ref, low_ref,
+    f_ref, r_ref, v_ref, c_ref, keep_ref, send_ref, xs_ref, gt_ref, sp_ref, part_ref,
 ):
     width, n = xt_ref.shape
     ny = m_ref.shape[1]
-    nd, yd = g_ref.shape[:2]
+    half = ny // 2
     kappa = kappa_of(width)
     scale = kappa * LOG2E
-    l_all = l_ref[...]
-    peak = jnp.max(l_all, axis=0)
-    lse2 = peak + jnp.log(jnp.sum(jnp.exp2(l_all - peak[None]), axis=0)) * LOG2E
+    l_mine, l_other = l_ref[...], other_ref[...]
+    peak = jnp.maximum(jnp.max(l_mine, axis=0), jnp.max(l_other, axis=0))
+    total = jnp.sum(jnp.exp2(l_mine - peak[None]), axis=0) + jnp.sum(jnp.exp2(l_other - peak[None]), axis=0)
+    lse2 = peak + jnp.log(total) * LOG2E
     old = yt_ref[width:, :].astype(F32)
     c_old = (old[0:1] + old[1:2]) + old[2:3]
     lb2 = (old[6:7] - log_ny) * LOG2E
-    c_term = c_old + (lb2 - lse2) / scale
+    c_ref[...] = to_lanes(c_old + (lb2 - lse2) / scale)
     v = jnp.exp2(scale * m_ref[...] + (lb2 - lse2))
     v_ref[...] = v
     one, two, three = pieces(v)
@@ -215,8 +236,7 @@
     r = jnp.exp(mx_ref[...].astype(F32) - log_nx - log_row)
     r_ref[...] = r
     stack(xs_ref, width, xt, r)
-    high, mid, low = pieces(c_term)
-    index = lax.broadcasted_iota(jnp.int32, (EXT, TILE), 0)
+    totals = []
     for k in range(ny // TILE):
         t = slice(k * TILE, (k + 1) * TILE)
         product = jnp.dot(xs_ref[...], high_ref[:, t], preferred_element_type=F32) + jnp.dot(
@@ -224,19 +244,63 @@
         )
         moment, total = unstack(product, width)
         total = total * v[:, t]
-        s_ref[:, :, t] = jnp.broadcast_to(total[None], (nd, 1, TILE))
+        totals.append(total)
         gt_ref[:width, t] = yt_ref[:width, t].astype(F32) * total - moment * v[:, t]
-        one, two, three = pieces(total)
-        gt_ref[width:, t] = select(index, {0: one, 1: two, 2: three, 3: high[:, t], 4: mid[:, t], 5: low[:, t]})
-    g_ref[...] = gt_ref[...].T.astype(BF16).reshape(nd, yd, width + EXT)
-
-
-def grad_x_kernel(log_nx, log_ny, xt_ref, r_ref, v_ref, s_ref, yt_ref, high_ref, low_ref, out_ref, ys_ref):
+    gt_ref[width:, :] = jnp.zeros((EXT, ny), F32)
+    sp_ref[...] = jnp.zeros(sp_ref.shape, F32)
+    write_sums(sp_ref, 0, jnp.concatenate(totals, axis=1))
+    part_ref[...] = gt_ref[...].T.astype(BF16)
+    col = lax.axis_index("col")
+    keep_ref[:half, :] = part_ref[pl.ds(pl.multiple_of(col * half, half), half), :]
+    send_ref[:half, :] = part_ref[pl.ds(pl.multiple_of((1 - col) * half, half), half), :]
+    sums = sp_ref[...].astype(BF16)
+    keep_ref[half:, :] = sums
+    send_ref[half:, :] = sums
+
+
+def add_kernel(mine_ref, other_ref, out_ref, sp_ref):
+    rows, block = out_ref.shape[:2]
+    extra = sp_ref.shape[0]
+    yd = block - extra
+    ny = 2 * rows * yd
+    count = ny // LANES
+    total = mine_ref[...].astype(F32) + other_ref[...].astype(F32)
+    ext = total[rows * yd :]
+    whole = (ext[:count] + ext[count : 2 * count]) + ext[2 * count : 3 * count]
+    sp_ref[...] = jnp.zeros(sp_ref.shape, F32)
+    for k, part in enumerate(pieces(whole)):
+        sp_ref[k * count : (k + 1) * count, :] = part
+    sums = sp_ref[...].astype(BF16)
+    for r in range(rows):
+        out_ref[r, :yd, :] = total[r * yd : (r + 1) * yd].astype(BF16)
+        out_ref[r, yd:, :] = sums
+
+
+def own_part(ref, yd):
+    block = lax.axis_index("col") * lax.axis_size("row") + lax.axis_index("row")
+    fit = LANES // yd
+    row = ref[pl.ds(block // fit, 1), :]
+    out = row[:, :yd]
+    for k in range(1, fit):
+        out = jnp.where(block % fit == k, row[:, k * yd : (k + 1) * yd], out)
+    return out
+
+
+def last_kernel(
+    log_nx, log_ny, xt_ref, r_ref, v_ref, c_ref, g_ref, yt_ref, high_ref, low_ref, y_ref, my_ref,
+    gx_ref, gy_ref, pot_ref, ys_ref, sum_ref,
+):
     width, n = xt_ref.shape
     ny = v_ref.shape[1]
+    yd = y_ref.shape[0]
+    count = ny // LANES
+    total = g_ref[0].astype(F32)
+    for k in range(1, g_ref.shape[0]):
+        total = total + g_ref[k].astype(F32)
+    ext = total[yd:]
+    sum_ref[...] = (ext[:count] + ext[count : 2 * count]) + ext[2 * count : 3 * count]
     mass = yt_ref[width:, :].astype(F32)[6:7]
-    colsum = jnp.sum(s_ref[...], axis=0)
-    q = v_ref[...] * jnp.exp(mass + log_nx - jnp.log(colsum))
+    q = v_ref[...] * jnp.exp(mass + log_nx - jnp.log(from_lanes(sum_ref[...])))
     stack(ys_ref, width, yt_ref[:width, :], q)
     across = (((1,), (1,)), ((), ()))
     for k in range(n // TILE):
@@ -244,25 +308,14 @@
         product = lax.dot_general(
             ys_ref[...], high_ref[t, :], across, preferred_element_type=F32
         ) + lax.dot_general(ys_ref[...], low_ref[t, :], across, preferred_element_type=F32)
-        moved, total = unstack(product, width)
-        out_ref[:, t] = (xt_ref[:, t].astype(F32) * total - moved) * (r_ref[:, t] * (1.0 / ny))
-
-
-def grad_y_kernel(y_ref, my_ref, g_ref, out_ref, pot_ref):
-    yd, width = y_ref.shape
-    nd = g_ref.shape[0]
-    total = g_ref[0].astype(F32)
-    for k in range(1, nd):
-        total = total + g_ref[k].astype(F32)
-    part = total[:, width:]
-    colsum = (part[:, 0:1] + part[:, 1:2]) + part[:, 2:3]
-    c_term = ((part[:, 3:4] + part[:, 4:5]) + part[:, 5:6]) * (1.0 / nd)
-    mass = to_column(my_ref[...].astype(F32))
-    out_ref[...] = total[:, :width] * (jnp.exp(mass) / colsum)
+        moved, weight = unstack(product, width)
+        gx_ref[:, t] = (xt_ref[:, t].astype(F32) * weight - moved) * (r_ref[:, t] * (1.0 / ny))
+    colsum = own_part(sum_ref, yd)
+    c_term = own_part(c_ref, yd)
+    gy_ref[...] = total[:yd, :width] * to_column(jnp.exp(my_ref[...].astype(F32)) / colsum)
     yf = y_ref[...].astype(F32)
-    norm = jnp.sum(yf * yf, axis=1, keepdims=True)
-    pot = norm / width - EPSILON * (jnp.log(colsum) - kappa_of(width) * c_term)
-    pot_ref[...] = to_row(pot)
+    norm = to_row(jnp.sum(yf * yf, axis=1, keepdims=True))
+    pot_ref[...] = norm / width - EPSILON * (jnp.log(colsum) - kappa_of(width) * c_term)
 
 
 def call(kernel, outs, scratch, limit, *args):
@@ -280,6 +333,10 @@
     return jax.ShapeDtypeStruct(dims, dtype)
 
 
+def swap(value):
+    return lax.ppermute(value, "col", [(0, 1), (1, 0)])
+
+
 def on_device(points_x, points_y, mass_x, mass_y):
     n, width = points_x.shape
     yd = points_y.shape[0]
@@ -287,43 +344,56 @@
     ny = nd * yd
     log_nx, log_ny = math.log(n * nd), math.log(ny)
     depth = width + EXT
-    limit = (8 + 24 * ny // 1024) * 1024 * 1024 if ny <= 1024 else 56 * 1024 * 1024
+    limit = (12 if ny <= 1024 else 56) * 1024 * 1024
+    rows = lax.axis_size("row")
+    extra = sums_rows(ny)
+    half = ny // 2
     run = functools.partial
     xt = points_x.T
     mx = mass_x.reshape(1, n)
     my = mass_y.reshape(1, yd)
-    y_own = call(run(prep_kernel, log_ny), shape((nd, yd, depth), BF16), [], limit, points_y, my)
-    ya = lax.all_to_all(y_own, AXES, 0, 0, tiled=True)
+    y_own = call(run(prep_kernel, log_ny), shape((rows, yd, depth), BF16), [], limit, points_y, my)
+    y_mine = lax.all_to_all(y_own, "row", 0, 0, tiled=True)
+    y_other = swap(y_mine)
     xa = call(prep_x_kernel, shape((depth, n), BF16), [], limit, xt)
-    b_term, lse, peak, rows = call(
+    ya, b_term, lse, peak, x_rows = call(
         run(first_kernel, log_nx),
-        (shape((1, n)), shape((nd, 1, ny)), shape((1, ny)), shape((n, depth), BF16)),
+        (
+            shape((ny, depth), BF16), shape((1, n)), shape((rows, 1, ny)), shape((1, ny)), shape((n, depth), BF16),
+        ),
         [pltpu.VMEM((depth, n), BF16), pltpu.VMEM((ny, TILE), F32), pltpu.VMEM((n, TILE), F32)],
-        limit, xa, mx, ya,
-    )
-    lse = lax.all_to_all(lse, AXES, 0, 0, tiled=True)
+        limit, xa, mx, y_mine, y_other,
+    )
+    lse = lax.all_to_all(lse, "row", 0, 0, tiled=True)
+    lse_other = swap(lse)
     high, low, yt = call(
         plan_kernel,
         (shape((n, ny), BF16), shape((n, ny), BF16), shape((depth, ny), BF16)),
         [pltpu.VMEM((n, TILE), F32)],
-        limit, rows, ya, peak,
-    )
-    f_pot, r, v, sums, g_part = call(
+        limit, x_rows, ya, peak,
+    )
+    f_pot, r, v, c_term, keep, send = call(
         run(second_kernel, log_nx, log_ny),
-        (shape((1, n)), shape((1, n)), shape((1, ny)), shape((nd, 1, ny)), shape((nd, yd, depth), BF16)),
-        [pltpu.VMEM((2 * width + PAD, n), BF16), pltpu.VMEM((depth, ny), F32)],
-        limit, xt, mx, b_term, lse, peak, yt, high, low,
-    )
-    sums = lax.all_to_all(sums, AXES, 0, 0, tiled=True)
-    g_all = lax.all_to_all(g_part, AXES, 0, 0, tiled=True)
-    grad_xt = call(
-        run(grad_x_kernel, log_nx, log_ny),
-        shape((width, n)),
-        [pltpu.VMEM((2 * width + PAD, ny), BF16)],
-        limit, xt, r, v, sums, yt, high, low,
-    )
-    grad_y, g_pot = call(
-        grad_y_kernel, (shape((yd, width)), shape((1, yd))), [], limit, points_y, my, g_all
+        (
+            shape((1, n)), shape((1, n)), shape((1, ny)), shape((ny // LANES, LANES)),
+            shape((half + extra, depth), BF16), shape((half + extra, depth), BF16),
+        ),
+        [
+            pltpu.VMEM((2 * width + PAD, n), BF16), pltpu.VMEM((depth, ny), F32), pltpu.VMEM((extra, LANES), F32),
+            pltpu.VMEM((ny, depth), BF16),
+        ],
+        limit, xt, mx, b_term, lse, lse_other, peak, yt, high, low,
+    )
+    part = call(
+        add_kernel, shape((rows, yd + extra, depth), BF16), [pltpu.VMEM((extra, LANES), F32)],
+        limit, keep, swap(send),
+    )
+    part = lax.all_to_all(part, "row", 0, 0, tiled=True)
+    grad_xt, grad_y, g_pot = call(
+        run(last_kernel, log_nx, log_ny),
+        (shape((width, n)), shape((yd, width)), shape((1, yd))),
+        [pltpu.VMEM((2 * width + PAD, ny), BF16), pltpu.VMEM((ny // LANES, LANES), F32)],
+        limit, xt, r, v, c_term, part, yt, high, low, points_y, my,
     )
     return f_pot.reshape(n), g_pot.reshape(yd), grad_xt.T, grad_y
 

time: 63.2 us -> 49.3 us (0.78)
  blocking collectives: 9.47 us -> 34.6 us
  waiting for transfers between devices: 19 us -> 1.12 us
  starting transfers between devices: 14.4 us -> 0.43 us
  local copies, waits for them, and re-layouts: 7.54 us -> 3.03 us
  Pallas kernels: 11.4 us -> 8.97 us
    all_to_all x1 -> x3, blocking collectives: 9.47 us -> 34.6 us  [the longest x1 14.4 us: on_device(): y_mine = lax.all_to_all(y_own, 'row', 0, 0, tiled=True)]
    all_to_all x3 -> x0, waiting for transfers between devices: 19 us -> none  [the longest x1 8.41 us: on_device(): ya = lax.all_to_all(y_own, AXES, 0, 0, tiled=True)]
    all_to_all x3 -> x0, starting transfers between devices: 14.4 us -> none  [the longest x1 7.39 us: on_device(): ya = lax.all_to_all(y_own, AXES, 0, 0, tiled=True)]
    unnamed x18 -> x12, local copies, waits for them, and re-layouts: 6.85 us -> 2.35 us
    pallas_call x7, Pallas kernels: 11.4 us -> 8.97 us  [call(): pl.pallas_call(kernel, out_shape=outs, in_specs=[pl.BlockSpec(memory_spac...]
    ppermute x0 -> x3, waiting for transfers between devices: none -> 1.12 us  [swap(): return lax.ppermute(value, 'col', [(0, 1), (1, 0)])]
  transfers between devices with their start and end apart: 3 -> 3, of which waited for: 3 -> 2; matrix products, arithmetic and copies ran while one was open for 1% -> 1% of each run, Pallas kernels for 5% -> 2%
where the time goes in v3:
time: 49.3 us; the launch traced here: 48.9 us
  blocking collectives  34.6 us (70%)
  Pallas kernels  8.97 us (18%)
  local copies, waits for them, and re-layouts  3.03 us (6%)
  waiting for transfers between devices  1.12 us (2%)
  between operations  0.69 us (1%)
    all_to_all x1, blocking collectives, on_device(): y_mine = lax.all_to_all(y_own, 'row', 0, 0, tiled=True)  14.4 us
    all_to_all x1, blocking collectives, on_device(): part = lax.all_to_all(part, 'row', 0, 0, tiled=True)  11.2 us
    all_to_all x1, blocking collectives, on_device(): lse = lax.all_to_all(lse, 'row', 0, 0, tiled=True)  9.06 us
    pallas_call x7, Pallas kernels, call(): pl.pallas_call(kernel, out_shape=outs, in_specs=[pl.BlockSpec(memory_spac...  8.97 us
    unnamed x12, local copies, waits for them, and re-layouts  2.35 us
    ppermute x3, waiting for transfers between devices, swap(): return lax.ppermute(value, 'col', [(0, 1), (1, 0)])  1.12 us
  transfers between devices with their start and end apart: 3, of which 2 were waited for; matrix products, arithmetic and copies ran while one was open for 1% of the time, Pallas kernels for 2%

profile of v3, /device:TPU:0, one launch (start us, length us, event | category | flops | bytes accessed | tf_op | source)
XLA Modules:
  0.0 48.9 jit_solution(6669732869367402922)
XLA Ops:
  0.6 0.0 copy-start.1
  0.6 0.0 copy-start.2
  0.7 0.7 %copy-done.2 = bf16[64,96]{1,0:T(8,128)(2,1)S(1)} copy-done((bf16[64,96]{1,0:T(8,128)(2,1)S(1)}, bf16[64,96]{1,0:T(8,128)(2,1)}, u32[]{:S(2)}) %copy-start.2) | copy-done | bytes 12312
  1.4 0.0 copy-start.4
  1.4 0.7 %copy-done.4 = bf16[64]{0:T(256)(128)(2,1)S(1)} copy-done((bf16[64]{0:T(256)(128)(2,1)S(1)}, bf16[64]{0:T(256)(128)(2,1)}, u32[]{:S(2)}) %copy-start.4) | copy-done | bytes 152
  2.1 0.2 shard_map.76
  2.2 14.4 %all_to_all.15.mine_ref = bf16[8,64,128]{2,1,0:T(8,128)(2,1)S(1)} all-to-all(bf16[8,64,128]{2,1,0:T(8,128)(2,1)S(1)} %shard_map.76), channel_id=1, replica_groups=mesh['groups'=2,'row'=8,'col'=2] {'row'}, dimensions={0} | all-to-all | bytes 262144 | tf_op jit(solution)/shard_map/all_to_all | solution.py:356
  16.7 0.0 collective-permute-start
  16.7 0.7 %reshape.20.mx_ref = bf16[1,1024]{1,0:T(2,128)(2,1)S(1)} reshape(bf16[1024]{0:T(1024)(128)(2,1)} %param.6) | data formatting | bytes 4096 | tf_op jit(solution)/shard_map/reshape | solution.py:353
  17.4 0.0 copy-start
  17.4 0.9 %copy-done = bf16[1024,96]{0,1:T(8,128)(2,1)S(1)} copy-done((bf16[1024,96]{0,1:T(8,128)(2,1)S(1)}, bf16[1024,96]{0,1:T(8,128)(2,1)}, u32[]{:S(2)}) %copy-start) | copy-done | bytes 196632
  18.3 0.0 collective-permute-done.other_ref
  18.3 2.6 %shard_map.77 = (bf16[1024,128]{1,0:T(8,128)(2,1)S(1)}, f32[1,1024]{1,0:T(1,128)S(1)}, f32[8,1,1024]{2,1,0:T(1,128)S(1)}, f32[1,1024]{1,0:T(1,128)S(1)}, bf16[1024,128]{1,0:T(8,128)(2,1)S(1)}) custom-call(bf16[128,1024]{1,0:T(8,128)(2,1)S(1)} %shard_map.75.xa0_ref, bf16[1,1024]{1,0:T(2,128)(2,1)S(1)} %reshape.20.mx_ref, ...), custom_call_target="tpu_custom_call" | custom-call | tf_op jit(solution)/shard_map/pallas_call | solution.py:322
  20.9 9.1 %all_to_all.16.l_ref = f32[8,1,1024]{2,1,0:T(1,128)S(1)} all-to-all(f32[8,1,1024]{2,1,0:T(1,128)S(1)} %get-tuple-element.22), channel_id=1, replica_groups=mesh['groups'=2,'row'=8,'col'=2] {'row'}, dimensions={0} | all-to-all | bytes 65536 | tf_op jit(solution)/shard_map/all_to_all | solution.py:367
  30.0 0.0 collective-permute-start.1
  30.0 1.1 %shard_map.78 = (bf16[1024,1024]{1,0:T(8,128)(2,1)S(1)}, bf16[1024,1024]{1,0:T(8,128)(2,1)S(1)}, bf16[128,1024]{1,0:T(8,128)(2,1)S(1)}) custom-call(bf16[1024,128]{1,0:T(8,128)(2,1)S(1)} %get-tuple-element.24.rows_ref, bf16[1024,128]{1,0:T(8,128)(2,1)S(1)} %get-tuple-element.25.ya_ref, f32[1,1024]{1,0:T(1,128)S(1)} %get-tuple-element.23.m_ref), custom_call_target="tpu_custom_call" | custom-call | tf_op jit(solution)/shard_map/pallas_call | solution.py:322
  31.1 0.1 collective-permute-done.1.other_ref
  31.2 0.0 copy-done.1
  31.2 0.0 copy-start.3
  31.2 0.0 copy-start.5
  31.2 2.8 %shard_map.79 = (f32[1,1024]{1,0:T(1,128)}, f32[1,1024]{1,0:T(1,128)S(1)}, f32[1,1024]{1,0:T(1,128)S(1)}, f32[8,128]{1,0:T(8,128)S(1)}, bf16[544,128]{1,0:T(8,128)(2,1)S(1)}, /*index=5*/bf16[544,128]{1,0:T(8,128)(2,1)S(1)}) custom-call(bf16[96,1024]{1,0:T(8,128)(2,1)S(1)} %bitcast.6, bf16[1,1024]{1,0:T(2,128)(2,1)S(1)} %reshape.20.mx_ref, ...), custom_call_target="tpu_custom_call" | custom-call | tf_op jit(solution)/shard_map/pallas_call | solution.py:322
  33.9 0.4 collective-permute-start.2
  34.4 1.0 %collective-permute-done.2.other_ref = bf16[544,128]{1,0:T(8,128)(2,1)S(1)} collective-permute-done((bf16[544,128]{1,0:T(8,128)(2,1)S(1)}, bf16[544,128]{1,0:T(8,128)(2,1)S(1)}, u32[]{:S(2)}, u32[]{:S(2)}) %collective-permute-start.2) | collective-permute-done | bytes 139296 | tf_op jit(solution)/shard_map/ppermute | solution.py:337
  35.4 11.2 %all_to_all.17.g_ref = bf16[8,96,128]{2,1,0:T(8,128)(2,1)S(1)} all-to-all(bf16[8,96,128]{2,1,0:T(8,128)(2,1)S(1)} %shard_map.80), channel_id=1, replica_groups=mesh['groups'=2,'row'=8,'col'=2] {'row'}, dimensions={0} | all-to-all | bytes 393216 | tf_op jit(solution)/shard_map/all_to_all | solution.py:391
  46.6 0.0 copy-done.3
  46.6 0.0 copy-done.5
  46.6 2.3 %shard_map.81 = (f32[96,1024]{1,0:T(8,128)}, f32[64,96]{1,0:T(8,128)}, f32[1,64]{1,0:T(1,128)}) custom-call(bf16[96,1024]{1,0:T(8,128)(2,1)S(1)} %bitcast.7, f32[1,1024]{1,0:T(1,128)S(1)} %get-tuple-element.30.r_ref, f32[1,1024]{1,0:T(1,128)S(1)} %get-tuple-element.31.v_ref, f32[8,128]{1,0:T(8,128)S(1)} %get-tuple-element.32.c_ref, ...), custom_call_target="tpu_custom_call" | custom-call | tf_op jit(solution)/shard_map/pallas_call | solution.py:322
  (2 shorter events, 0.1 us)
Async XLA Ops:
  0.6 30.6 %copy-start.1 = (bf16[1024,96]{0,1:T(8,128)(2,1)S(1)}, bf16[1024,96]{0,1:T(8,128)(2,1)}, u32[]{:S(2)}) copy-start(bf16[1024,96]{0,1:T(8,128)(2,1)} %param.4) | copy-start | bytes 589828
  0.6 0.8 %copy-start.2 = (bf16[64,96]{1,0:T(8,128)(2,1)S(1)}, bf16[64,96]{1,0:T(8,128)(2,1)}, u32[]{:S(2)}) copy-start(bf16[64,96]{1,0:T(8,128)(2,1)} %y_ref.3) | copy-start | bytes 36868
  1.4 0.7 %copy-start.4 = (bf16[64]{0:T(256)(128)(2,1)S(1)}, bf16[64]{0:T(256)(128)(2,1)}, u32[]{:S(2)}) copy-start(bf16[64]{0:T(256)(128)(2,1)} %param.7) | copy-start | bytes 388
  16.7 1.6 %collective-permute-start = (bf16[8,64,128]{2,1,0:T(8,128)(2,1)S(1)}, bf16[8,64,128]{2,1,0:T(8,128)(2,1)S(1)}, u32[]{:S(2)}, u32[]{:S(2)}) collective-permute-start(bf16[8,64,128]{2,1,0:T(8,128)(2,1)S(1)} %all_to_all.15.mine_ref), channel_id=1, source_target_pairs={{0,1},{1,0},{2,3},{3,2},{4,5},{5,4},{6,7},{7,6},{8,9},{9,8},{10,11... | collective-permute-start | bytes 393224 | tf_op jit(solution)/shard_map/ppermute | solution.py:337
  17.4 0.9 %copy-start = (bf16[1024,96]{0,1:T(8,128)(2,1)S(1)}, bf16[1024,96]{0,1:T(8,128)(2,1)}, u32[]{:S(2)}) copy-start(bf16[1024,96]{0,1:T(8,128)(2,1)} %param.4) | copy-start | bytes 589828
  30.0 1.2 %collective-permute-start.1 = (f32[8,1,1024]{2,1,0:T(1,128)S(1)}, f32[8,1,1024]{2,1,0:T(1,128)S(1)}, u32[]{:S(2)}, u32[]{:S(2)}) collective-permute-start(f32[8,1,1024]{2,1,0:T(1,128)S(1)} %all_to_all.16.l_ref), channel_id=1, source_target_pairs={{0,1},{1,0},{2,3},{3,2},{4,5},{5,4},{6,7},{7,6},{8,9},{9,8},{10,11... | collective-permute-start | bytes 98312 | tf_op jit(solution)/shard_map/ppermute | solution.py:337
  31.2 15.4 %copy-start.3 = (bf16[64,96]{1,0:T(8,128)(2,1)S(1)}, bf16[64,96]{1,0:T(8,128)(2,1)}, u32[]{:S(2)}) copy-start(bf16[64,96]{1,0:T(8,128)(2,1)} %y_ref.3) | copy-start | bytes 36868
  31.2 15.4 %copy-start.5 = (bf16[64]{0:T(256)(128)(2,1)S(1)}, bf16[64]{0:T(256)(128)(2,1)}, u32[]{:S(2)}) copy-start(bf16[64]{0:T(256)(128)(2,1)} %param.7) | copy-start | bytes 388
  33.9 1.4 %collective-permute-start.2 = (bf16[544,128]{1,0:T(8,128)(2,1)S(1)}, bf16[544,128]{1,0:T(8,128)(2,1)S(1)}, u32[]{:S(2)}, u32[]{:S(2)}) collective-permute-start(bf16[544,128]{1,0:T(8,128)(2,1)S(1)} %get-tuple-element.34), channel_id=1, source_target_pairs={{0,1},{1,0},{2,3},{3,2},{4,5},{5,4},{6,7},{7,6},{8,9},{9,8},{10,11... | collective-permute-start | bytes 417800 | tf_op jit(solution)/shard_map/ppermute | solution.py:337

commit v4 on v3

v4 whole, which is shorter than its diff:
```python
import functools
import math

import jax
import jax.numpy as jnp
from jax import lax
from jax.experimental import pallas as pl
from jax.experimental.pallas import tpu as pltpu
from jax.sharding import PartitionSpec as P

ITERS = 2
EPSILON = 0.02
LOG2E = math.log2(math.e)
TILE = 256
STEP = 32
EXT = 32
PAD = 16
LANES = 128
F32 = jnp.float32
BF16 = jnp.bfloat16


def kappa_of(width):
    return 2.0 / (width * EPSILON)


def pieces(value):
    high = value.astype(BF16).astype(F32)
    rest = value - high
    mid = rest.astype(BF16).astype(F32)
    return high, mid, rest - mid


def select(index, values):
    out = jnp.zeros(index.shape, F32)
    for k, value in values.items():
        out = jnp.where(index == k, value, out)
    return out


def extras_y(index, c_term, mass):
    high, mid, low = pieces(c_term)
    return select(index, {0: high, 1: mid, 2: low, 3: 1.0, 4: 1.0, 5: 1.0, 6: mass})


def extras_x(index, b_term):
    high, mid, low = pieces(b_term)
    return select(index, {0: 1.0, 1: 1.0, 2: 1.0, 3: high, 4: mid, 5: low})


def rows_index(columns):
    return lax.broadcasted_iota(jnp.int32, (EXT, columns), 0)


def to_column(row):
    size = row.shape[1]
    eye = lax.broadcasted_iota(jnp.int32, (size, size), 0) == lax.broadcasted_iota(jnp.int32, (size, size), 1)
    return jnp.sum(jnp.where(eye, row, 0.0), axis=1, keepdims=True)


def to_row(column):
    size = column.shape[0]
    eye = lax.broadcasted_iota(jnp.int32, (size, size), 0) == lax.broadcasted_iota(jnp.int32, (size, size), 1)
    return jnp.sum(jnp.where(eye, column, 0.0), axis=0, keepdims=True)


def for_tiles(total, body):
    count = total // TILE
    if count <= 4:
        for t in range(count):
            body(pl.ds(t * TILE, TILE))
    else:

        @pl.loop(0, count)
        def _(t):
            body(pl.ds(pl.multiple_of(t * TILE, TILE), TILE))


def max_down(z_ref, rows):
    peak = z_ref[0:STEP, :]
    for r in range(STEP, rows, STEP):
        peak = jnp.maximum(peak, z_ref[r : r + STEP, :])
    return jnp.max(peak, axis=0, keepdims=True)


def exp_sum_down(z_ref, rows, scale, shift):
    total = jnp.zeros((STEP, TILE), F32)
    for r in range(0, rows, STEP):
        total = total + jnp.exp2((z_ref[r : r + STEP, :] - shift) * scale)
    return jnp.sum(total, axis=0, keepdims=True)


def to_lanes(row):
    return jnp.concatenate([row[:, k : k + LANES] for k in range(0, row.shape[1], LANES)], axis=0)


def from_lanes(block):
    return jnp.concatenate([block[k : k + 1] for k in range(block.shape[0])], axis=1)


def write_sums(ref, start, row):
    count = row.shape[1] // LANES
    for k, part in enumerate(pieces(row)):
        ref[start + k * count : start + (k + 1) * count, :] = to_lanes(part)


def sums_rows(ny):
    return -(-3 * ny // LANES // 16) * 16


def copies(sems, *pairs):
    moves = [pltpu.make_async_copy(a, b, sems.at[k]) for k, (a, b) in enumerate(pairs)]
    for move in moves:
        move.start()
    for move in moves:
        move.wait()


def prep_y_kernel(log_ny, y_hbm, my_hbm, out_ref, y_ref, my_ref, sems):
    copies(sems, (y_hbm, y_ref), (my_hbm, my_ref))
    width = y_ref.shape[1]
    y = y_ref[...]
    yf = y.astype(F32)
    norm = jnp.sum(yf * yf, axis=1, keepdims=True)
    mass = to_column(my_ref[...].astype(F32))
    c_term = (mass - log_ny) / kappa_of(width) - 0.5 * norm
    index = lax.broadcasted_iota(jnp.int32, (y.shape[0], EXT), 1)
    out_ref[:, :width] = y
    out_ref[:, width:] = extras_y(index, c_term, mass).astype(BF16)


def prep_x_kernel(xt_hbm, mx_hbm, xa_ref, mx_ref, norm_ref, mx_in, sems):
    width, n = xt_hbm.shape
    copies(sems, (xt_hbm, xa_ref.at[:width, :]), (mx_hbm, mx_in))
    xa_ref[width:, :] = extras_x(rows_index(n), jnp.zeros((1, n), F32)).astype(BF16)
    mx_ref[...] = from_lanes(mx_in[...].astype(F32))
    xf = xa_ref[:width, :].astype(F32)
    norm_ref[...] = jnp.sum(xf * xf, axis=0, keepdims=True)


def join_kernel(mine_ref, other_ref, out_ref):
    rows = mine_ref.shape[0]
    out_ref[:rows, :] = mine_ref[...]
    out_ref[rows:, :] = other_ref[...]


def lse_kernel(mine_ref, other_ref, out_ref):
    mine, other = mine_ref[...], other_ref[...]
    peak = jnp.maximum(mine, other)
    out_ref[...] = peak + jnp.log(jnp.exp2(mine - peak) + jnp.exp2(other - peak)) * LOG2E


def reverse_bits(value, count):
    return sum(((value >> k) & 1) << (count - 1 - k) for k in range(count))


def first_kernel(
    log_nx, rows, xa0_ref, mx_ref, mine_ref, other_ref, ya_ref, b_ref, l_ref, m_ref, rows_ref, xa_ref, z_ref, zc_ref,
    b2_ref,
):
    half, depth = mine_ref.shape
    yd = half // rows
    n = mx_ref.shape[1]
    width = depth - EXT
    ny = 2 * half
    row, col = lax.axis_index("row"), lax.axis_index("col")
    for k in range(rows):
        place = (row ^ reverse_bits(k, rows.bit_length() - 1)) * yd
        ya_ref[pl.ds(pl.multiple_of(col * half + place, yd), yd), :] = mine_ref[k * yd : (k + 1) * yd, :]
        ya_ref[pl.ds(pl.multiple_of((1 - col) * half + place, yd), yd), :] = other_ref[k * yd : (k + 1) * yd, :]
    scale = kappa_of(width) * LOG2E
    la2 = (mx_ref[...] - log_nx) * LOG2E

    def row_tile(t):
        z_ref[...] = jnp.dot(ya_ref[...], xa0_ref[:, t], preferred_element_type=F32)
        peak = max_down(z_ref, ny)
        b_ref[:, t] = -peak - jnp.log(exp_sum_down(z_ref, ny, scale, peak)) * (LOG2E / scale)

    for_tiles(n, row_tile)
    b_term = b_ref[...] + la2 / scale
    b_ref[...] = b_term
    xa_ref[:width, :] = xa0_ref[:width, :]
    xa_ref[width:, :] = extras_x(rows_index(n), b_term).astype(BF16)
    rows_ref[...] = xa_ref[...].T

    def col_tile(t):
        zc_ref[...] = lax.dot_general(
            rows_ref[...], ya_ref[t, :], (((1,), (1,)), ((), ())), preferred_element_type=F32
        )
        peak = max_down(zc_ref, n)
        m_ref[:, t] = peak
        b2_ref[:, t] = scale * peak + jnp.log(exp_sum_down(zc_ref, n, scale, peak)) * LOG2E

    for_tiles(ny, col_tile)
    l_ref[...] = to_lanes(b2_ref[...])


def plan_kernel(rows_ref, ya_ref, m_ref, high_ref, low_ref, yt_ref, zc_ref):
    ny, depth = ya_ref.shape
    n = rows_ref.shape[0]
    scale = kappa_of(depth - EXT) * LOG2E

    def col_tile(t):
        y_part = ya_ref[t, :]
        yt_ref[:, t] = y_part.T
        zc_ref[...] = lax.dot_general(
            rows_ref[...], y_part, (((1,), (1,)), ((), ())), preferred_element_type=F32
        )
        peak = m_ref[:, t]
        for r in range(0, n, STEP):
            value = jnp.exp2((zc_ref[r : r + STEP, :] - peak) * scale)
            high = value.astype(BF16)
            high_ref[r : r + STEP, t] = high
            low_ref[r : r + STEP, t] = (value - high.astype(F32)).astype(BF16)

    for_tiles(ny, col_tile)


def stack(out_ref, width, points, factor):
    moved = points.astype(F32) * factor
    high = moved.astype(BF16)
    out_ref[:width, :] = high
    out_ref[width : 2 * width, :] = (moved - high.astype(F32)).astype(BF16)
    one, two, three = pieces(factor)
    index = lax.broadcasted_iota(jnp.int32, (PAD, factor.shape[1]), 0)
    out_ref[2 * width :, :] = select(index, {0: one, 1: two, 2: three}).astype(BF16)


def unstack(product, width):
    ext = product[2 * width :]
    return product[:width] + product[width : 2 * width], (ext[0:1] + ext[1:2]) + ext[2:3]


def second_kernel(
    log_nx, log_ny, xa_ref, mx_ref, norm_ref, b_ref, l_ref, m_ref, yt_ref, high_ref, low_ref,
    f_ref, r_ref, v_ref, c_ref, keep_ref, sum_ref, send_ref, xs_ref, gt_ref, part_ref,
):
    width = xa_ref.shape[0] - EXT
    ny = m_ref.shape[1]
    kappa = kappa_of(width)
    scale = kappa * LOG2E
    lse2 = from_lanes(l_ref[...])
    old = yt_ref[width:, :].astype(F32)
    c_old = (old[0:1] + old[1:2]) + old[2:3]
    lb2 = (old[6:7] - log_ny) * LOG2E
    c_ref[...] = to_lanes(c_old + (lb2 - lse2) / scale)
    v = jnp.exp2(scale * m_ref[...] + (lb2 - lse2))
    v_ref[...] = v
    one, two, three = pieces(v)
    index = lax.broadcasted_iota(jnp.int32, (PAD, ny), 0)
    v_rows = select(index, {0: one, 1: two, 2: three}).astype(BF16)
    across = (((1,), (1,)), ((), ()))
    sums = lax.dot_general(v_rows, high_ref[...], across, preferred_element_type=F32) + lax.dot_general(
        v_rows, low_ref[...], across, preferred_element_type=F32
    )
    rowsum = (sums[0:1] + sums[1:2]) + sums[2:3]
    log_row = jnp.log(rowsum)
    f_ref[...] = norm_ref[...] / width + EPSILON * (kappa * b_ref[...] - log_row)
    r = jnp.exp(mx_ref[...] - log_nx - log_row)
    r_ref[...] = r
    stack(xs_ref, width, xa_ref[:width, :], r)
    totals = []
    for k in range(ny // TILE):
        t = slice(k * TILE, (k + 1) * TILE)
        product = jnp.dot(xs_ref[...], high_ref[:, t], preferred_element_type=F32) + jnp.dot(
            xs_ref[...], low_ref[:, t], preferred_element_type=F32
        )
        moment, total = unstack(product, width)
        total = total * v[:, t]
        totals.append(total)
        gt_ref[:width, t] = yt_ref[:width, t].astype(F32) * total - moment * v[:, t]
    gt_ref[width:, :] = jnp.zeros((EXT, ny), F32)
    part_ref[...] = gt_ref[...].T
    sum_ref[...] = to_lanes(jnp.concatenate(totals, axis=1))
    split(lax.axis_index("col"), part_ref, sum_ref[...], keep_ref, send_ref)


def split(bit, part_ref, sums, keep_ref, send_ref):
    half = keep_ref.shape[0]
    keep_ref[...] = part_ref[pl.ds(pl.multiple_of(bit * half, half), half), :]
    send_ref[:half, :] = part_ref[pl.ds(pl.multiple_of((1 - bit) * half, half), half), :].astype(BF16)
    used = 3 * sums.shape[0]
    spare = send_ref.shape[0] - half - used
    parts = list(pieces(sums)) + ([jnp.zeros((spare, LANES), F32)] if spare else [])
    send_ref[half:, :] = jnp.concatenate(parts, axis=0).astype(BF16)


def add_received(keep_ref, sum_ref, got_ref):
    half = keep_ref.shape[0]
    count = sum_ref.shape[0]
    ext = got_ref[half:, :].astype(F32)
    sums = sum_ref[...] + ((ext[:count] + ext[count : 2 * count]) + ext[2 * count : 3 * count])
    return keep_ref[...] + got_ref[:half, :].astype(F32), sums


def add_kernel(shift, old_ref, sum0_ref, got_ref, keep_ref, sum_ref, send_ref, part_ref):
    total, sums = add_received(old_ref, sum0_ref, got_ref)
    part_ref[...] = total
    sum_ref[...] = sums
    split((lax.axis_index("row") >> shift) & 1, part_ref, sums, keep_ref, send_ref)


def own_part(ref, yd):
    block = lax.axis_index("col") * lax.axis_size("row") + lax.axis_index("row")
    fit = LANES // yd
    row = ref[pl.ds(block // fit, 1), :]
    out = row[:, :yd]
    for k in range(1, fit):
        out = jnp.where(block % fit == k, row[:, k * yd : (k + 1) * yd], out)
    return out


def last_kernel(
    log_nx, log_ny, xa_ref, r_ref, v_ref, c_ref, keep_ref, sum0_ref, got_ref, yt_ref, high_ref, low_ref, y_ref,
    gx_ref, gy_ref, pot_ref, ys_ref, sum_ref,
):
    width, n = gx_ref.shape
    ny = v_ref.shape[1]
    yd = y_ref.shape[0]
    total, sums = add_received(keep_ref, sum0_ref, got_ref)
    sum_ref[...] = sums
    mass = yt_ref[width:, :].astype(F32)[6:7]
    q = v_ref[...] * jnp.exp(mass + log_nx - jnp.log(from_lanes(sums)))
    stack(ys_ref, width, yt_ref[:width, :], q)
    across = (((1,), (1,)), ((), ()))
    for k in range(n // TILE):
        t = slice(k * TILE, (k + 1) * TILE)
        product = lax.dot_general(
            ys_ref[...], high_ref[t, :], across, preferred_element_type=F32
        ) + lax.dot_general(ys_ref[...], low_ref[t, :], across, preferred_element_type=F32)
        moved, weight = unstack(product, width)
        gx_ref[:, t] = (xa_ref[:width, t].astype(F32) * weight - moved) * (r_ref[:, t] * (1.0 / ny))
    colsum = own_part(sum_ref, yd)
    c_term = own_part(c_ref, yd)
    own = y_ref[...].astype(F32)
    gy_ref[...] = total[:, :width] * (jnp.exp(own[:, width + 6 : width + 7]) * to_column(1.0 / colsum))
    norm = to_row(jnp.sum(own[:, :width] * own[:, :width], axis=1, keepdims=True))
    pot_ref[...] = norm / width - EPSILON * (jnp.log(colsum) - kappa_of(width) * c_term)


def call(kernel, outs, scratch, limit, *args, space=pltpu.VMEM):
    return pl.pallas_call(
        kernel,
        out_shape=outs,
        in_specs=[pl.BlockSpec(memory_space=space)] * len(args),
        out_specs=jax.tree.map(lambda _: pl.BlockSpec(memory_space=pltpu.VMEM), outs),
        scratch_shapes=scratch,
        compiler_params=pltpu.CompilerParams(vmem_limit_bytes=limit),
    )(*args)


def shape(dims, dtype=F32):
    return jax.ShapeDtypeStruct(dims, dtype)


def swap(value, axis, size, step):
    return lax.ppermute(value, axis, [(k, k ^ step) for k in range(size)])


def on_device(points_x, points_y, mass_x, mass_y):
    n, width = points_x.shape
    yd = points_y.shape[0]
    rows = lax.axis_size("row")
    ny = 2 * rows * yd
    half = ny // 2
    count = ny // LANES
    levels = rows.bit_length() - 1
    log_nx, log_ny = math.log(n * 2 * rows), math.log(ny)
    depth = width + EXT
    limit = (12 if ny <= 1024 else 56) * 1024 * 1024
    extra = sums_rows(ny)
    run = functools.partial
    vmem = pltpu.VMEM
    two_sems = pltpu.SemaphoreType.DMA((2,))

    y_own = call(
        run(prep_y_kernel, log_ny), shape((yd, depth), BF16),
        [vmem((yd, width), BF16), vmem((1, yd), BF16), two_sems],
        limit, points_y, mass_y.reshape(1, yd), space=pl.ANY,
    )
    xa, mx, norm = call(
        prep_x_kernel, (shape((depth, n), BF16), shape((1, n)), shape((1, n))),
        [vmem((n // LANES, LANES), BF16), two_sems],
        limit, points_x.T, mass_x.reshape(n // LANES, LANES), space=pl.ANY,
    )
    y_mine = y_own
    for k in reversed(range(levels)):
        got = swap(y_mine, "row", rows, 1 << k)
        y_mine = call(join_kernel, shape((2 * got.shape[0], depth), BF16), [], limit, y_mine, got)
    y_other = swap(y_mine, "col", 2, 1)
    ya, b_term, lse, peak, x_rows = call(
        run(first_kernel, log_nx, rows),
        (shape((ny, depth), BF16), shape((1, n)), shape((count, LANES)), shape((1, ny)), shape((n, depth), BF16)),
        [vmem((depth, n), BF16), vmem((ny, TILE), F32), vmem((n, TILE), F32), vmem((1, ny), F32)],
        limit, xa, mx, y_mine, y_other,
    )
    high, low, yt = call(
        plan_kernel,
        (shape((n, ny), BF16), shape((n, ny), BF16), shape((depth, ny), BF16)),
        [vmem((n, TILE), F32)],
        limit, x_rows, ya, peak,
    )
    for k in reversed(range(levels)):
        lse = call(lse_kernel, shape((count, LANES)), [], limit, lse, swap(lse, "row", rows, 1 << k))
    lse = call(lse_kernel, shape((count, LANES)), [], limit, lse, swap(lse, "col", 2, 1))
    f_pot, r, v, c_term, keep, sums, send = call(
        run(second_kernel, log_nx, log_ny),
        (
            shape((1, n)), shape((1, n)), shape((1, ny)), shape((count, LANES)),
            shape((half, depth)), shape((count, LANES)), shape((half + extra, depth), BF16),
        ),
        [vmem((2 * width + PAD, n), BF16), vmem((depth, ny), F32), vmem((ny, depth), F32)],
        limit, xa, mx, norm, b_term, lse, peak, yt, high, low,
    )
    got = swap(send, "col", 2, 1)
    for k in reversed(range(levels)):
        half = half // 2
        keep, sums, send = call(
            run(add_kernel, k),
            (shape((half, depth)), shape((count, LANES)), shape((half + extra, depth), BF16)),
            [vmem((2 * half, depth), F32)],
            limit, keep, sums, got,
        )
        got = swap(send, "row", rows, 1 << k)
    grad_xt, grad_y, g_pot = call(
        run(last_kernel, log_nx, log_ny),
        (shape((width, n)), shape((yd, width)), shape((1, yd))),
        [vmem((2 * width + PAD, ny), BF16), vmem((count, LANES), F32)],
        limit, xa, r, v, c_term, keep, sums, got, yt, high, low, y_own,
    )
    return f_pot.reshape(n), g_pot.reshape(yd), grad_xt.T, grad_y


def solution(mesh):
    in_specs = (
        P(("groups", "row", "col"), None),
        P(("groups", "col", "row"), None),
        P(("groups", "row", "col")),
        P(("groups", "col", "row")),
    )
    out_specs = (
        P(("groups", "row", "col")),
        P(("groups", "col", "row")),
        P(("groups", "row", "col"), None),
        P(("groups", "col", "row"), None),
    )
    return jax.shard_map(
        on_device, mesh=mesh, in_specs=in_specs, out_specs=out_specs, check_vma=False
    )
```

time: 49.3 us -> 56 us (1.14)
  blocking collectives: 34.6 us -> 0 us
  waiting for transfers between devices: 1.12 us -> 22 us
  starting transfers between devices: 0.43 us -> 21 us
    all_to_all x3 -> x0, blocking collectives: 34.6 us -> none  [the longest x1 14.4 us: on_device(): y_mine = lax.all_to_all(y_own, 'row', 0, 0, tiled=True)]
    ppermute x3 -> x12, waiting for transfers between devices: 1.12 us -> 22 us  [swap(): return lax.ppermute(value, axis, [(k, k ^ step) for k in range(size)])]
    ppermute x3 -> x12, starting transfers between devices: 0.43 us -> 21 us  [swap(): return lax.ppermute(value, axis, [(k, k ^ step) for k in range(size)])]
    reshape x1 -> x0, local copies, waits for them, and re-layouts: 0.69 us -> none  [on_device(): mx = mass_x.reshape(1, n)]
    unnamed x12 -> x8, local copies, waits for them, and re-layouts: 2.35 us -> 2.97 us
    pallas_call x7 -> x16, Pallas kernels: 8.97 us -> 9.08 us  [call(): pl.pallas_call(kernel, out_shape=outs, in_specs=[pl.BlockSpec(memory_spac...]
  transfers between devices with their start and end apart: 3 -> 12, of which waited for: 2 -> 11; matrix products, arithmetic and copies ran while one was open for 1% -> 0% of each run, Pallas kernels for 2% -> 2%
where the time goes in v4:
time: 56 us; the launch traced here: 55.7 us
  waiting for transfers between devices  22 us (39%)
  starting transfers between devices  21 us (38%)
  Pallas kernels  9.08 us (16%)
  local copies, waits for them, and re-layouts  2.97 us (5%)
  between operations  0.73 us (1%)
    ppermute x12, waiting for transfers between devices, swap(): return lax.ppermute(value, axis, [(k, k ^ step) for k in range(size)])  22 us
    ppermute x12, starting transfers between devices, swap(): return lax.ppermute(value, axis, [(k, k ^ step) for k in range(size)])  21 us
    pallas_call x16, Pallas kernels, call(): pl.pallas_call(kernel, out_shape=outs, in_specs=[pl.BlockSpec(memory_spac...  9.08 us
    unnamed x8, local copies, waits for them, and re-layouts  2.97 us
  transfers between devices with their start and end apart: 12, of which 11 were waited for; matrix products, arithmetic and copies ran while one was open for 0% of the time, Pallas kernels for 2%

profile of v4, /device:TPU:0, one launch (start us, length us, event | category | flops | bytes accessed | tf_op | source)
XLA Modules:
  0.0 55.7 jit_solution(12903825538778491834)
XLA Ops:
  0.6 0.7 %copy-done.1 = bf16[64,96]{1,0:T(8,128)(2,1)S(1)} copy-done((bf16[64,96]{1,0:T(8,128)(2,1)S(1)}, bf16[64,96]{1,0:T(8,128)(2,1)}, u32[]{:S(2)}) %copy-start.1) | copy-done | bytes 12312
  1.4 0.7 %copy-done.3 = bf16[64]{0:T(256)(128)(2,1)S(1)} copy-done((bf16[64]{0:T(256)(128)(2,1)S(1)}, bf16[64]{0:T(256)(128)(2,1)}, u32[]{:S(2)}) %copy-start.3) | copy-done | bytes 152
  2.0 0.2 shard_map.76.mine_ref.y_ref
  2.2 4.1 %collective-permute-start = (bf16[64,128]{1,0:T(8,128)(2,1)S(1)}, bf16[64,128]{1,0:T(8,128)(2,1)S(1)}, u32[]{:S(2)}, u32[]{:S(2)}) collective-permute-start(bf16[64,128]{1,0:T(8,128)(2,1)S(1)} %shard_map.76.mine_ref.y_ref), channel_id=1, source_target_pairs={{0,8},{2,10},{4,12},{6,14},{8,0},{10,2},{12,4},{14,6},{1,9},{3,11}... | collective-permute-start | bytes 49160 | tf_op jit(solution)/shard_map/ppermute | solution.py:357
  6.3 1.7 %collective-permute-done.other_ref = bf16[64,128]{1,0:T(8,128)(2,1)S(1)} collective-permute-done((bf16[64,128]{1,0:T(8,128)(2,1)S(1)}, bf16[64,128]{1,0:T(8,128)(2,1)S(1)}, u32[]{:S(2)}, u32[]{:S(2)}) %collective-permute-start) | collective-permute-done | bytes 16416 | tf_op jit(solution)/shard_map/ppermute | solution.py:357
  8.0 1.9 %collective-permute-start.1 = (bf16[128,128]{1,0:T(8,128)(2,1)S(1)}, bf16[128,128]{1,0:T(8,128)(2,1)S(1)}, u32[]{:S(2)}, u32[]{:S(2)}) collective-permute-start(bf16[128,128]{1,0:T(8,128)(2,1)S(1)} %shard_map.77.mine_ref), channel_id=1, source_target_pairs={{0,4},{2,6},{4,0},{6,2},{8,12},{10,14},{12,8},{14,10},{1,5},{3,7},... | collective-permute-start | bytes 98312 | tf_op jit(solution)/shard_map/ppermute | solution.py:357
  10.0 2.0 %collective-permute-done.1.other_ref = bf16[128,128]{1,0:T(8,128)(2,1)S(1)} collective-permute-done((bf16[128,128]{1,0:T(8,128)(2,1)S(1)}, bf16[128,128]{1,0:T(8,128)(2,1)S(1)}, u32[]{:S(2)}, u32[]{:S(2)}) %collective-permute-start.1) | collective-permute-done | bytes 32800 | tf_op jit(solution)/shard_map/ppermute | solution.py:357
  12.0 1.9 %collective-permute-start.2 = (bf16[256,128]{1,0:T(8,128)(2,1)S(1)}, bf16[256,128]{1,0:T(8,128)(2,1)S(1)}, u32[]{:S(2)}, u32[]{:S(2)}) collective-permute-start(bf16[256,128]{1,0:T(8,128)(2,1)S(1)} %shard_map.78.mine_ref), channel_id=1, source_target_pairs={{0,2},{2,0},{4,6},{6,4},{8,10},{10,8},{12,14},{14,12},{1,3},{3,1},... | collective-permute-start | bytes 196616 | tf_op jit(solution)/shard_map/ppermute | solution.py:357
  13.9 2.4 %collective-permute-done.2.other_ref = bf16[256,128]{1,0:T(8,128)(2,1)S(1)} collective-permute-done((bf16[256,128]{1,0:T(8,128)(2,1)S(1)}, bf16[256,128]{1,0:T(8,128)(2,1)S(1)}, u32[]{:S(2)}, u32[]{:S(2)}) %collective-permute-start.2) | collective-permute-done | bytes 65568 | tf_op jit(solution)/shard_map/ppermute | solution.py:357
  16.2 0.1 collective-permute-start.3
  16.3 0.9 %copy-done = bf16[1024,96]{0,1:T(8,128)(2,1)S(1)} copy-done((bf16[1024,96]{0,1:T(8,128)(2,1)S(1)}, bf16[1024,96]{0,1:T(8,128)(2,1)}, u32[]{:S(2)}) %copy-start) | copy-done | bytes 196632
  17.3 0.7 %copy-done.2 = bf16[1024]{0:T(1024)(128)(2,1)S(1)} copy-done((bf16[1024]{0:T(1024)(128)(2,1)S(1)}, bf16[1024]{0:T(1024)(128)(2,1)}, u32[]{:S(2)}) %copy-start.2) | copy-done | bytes 2072
  17.9 0.3 shard_map.75
  18.2 2.6 %shard_map.80 = (bf16[1024,128]{1,0:T(8,128)(2,1)S(1)}, f32[1,1024]{1,0:T(1,128)S(1)}, f32[8,128]{1,0:T(8,128)S(1)}, f32[1,1024]{1,0:T(1,128)S(1)}, bf16[1024,128]{1,0:T(8,128)(2,1)S(1)}) custom-call(bf16[128,1024]{1,0:T(8,128)(2,1)S(1)} %get-tuple-element.34.xa0_ref.xa_ref, f32[1,1024]{1,0:T(1,128)S(1)} %get-tuple-element.35.mx_ref, ...), custom_call_target="tpu_custom_call" | custom-call | tf_op jit(solution)/shard_map/pallas_call | solution.py:342
  20.8 3.0 %collective-permute-start.4 = (f32[8,128]{1,0:T(8,128)S(1)}, f32[8,128]{1,0:T(8,128)S(1)}, u32[]{:S(2)}, u32[]{:S(2)}) collective-permute-start(f32[8,128]{1,0:T(8,128)S(1)} %get-tuple-element.38.mine_ref), channel_id=1, source_target_pairs={{0,8},{2,10},{4,12},{6,14},{8,0},{10,2},{12,4},{14,6},{1,9},{3,11}... | collective-permute-start | bytes 12296 | tf_op jit(solution)/shard_map/ppermute | solution.py:357
  23.8 1.6 %collective-permute-done.4.other_ref = f32[8,128]{1,0:T(8,128)S(1)} collective-permute-done((f32[8,128]{1,0:T(8,128)S(1)}, f32[8,128]{1,0:T(8,128)S(1)}, u32[]{:S(2)}, u32[]{:S(2)}) %collective-permute-start.4) | collective-permute-done | bytes 4128 | tf_op jit(solution)/shard_map/ppermute | solution.py:357
  25.4 2.0 %collective-permute-start.5 = (f32[8,128]{1,0:T(8,128)S(1)}, f32[8,128]{1,0:T(8,128)S(1)}, u32[]{:S(2)}, u32[]{:S(2)}) collective-permute-start(f32[8,128]{1,0:T(8,128)S(1)} %shard_map.81.mine_ref), channel_id=1, source_target_pairs={{0,4},{2,6},{4,0},{6,2},{8,12},{10,14},{12,8},{14,10},{1,5},{3,7},... | collective-permute-start | bytes 12296 | tf_op jit(solution)/shard_map/ppermute | solution.py:357
  27.4 1.7 %collective-permute-done.5.other_ref = f32[8,128]{1,0:T(8,128)S(1)} collective-permute-done((f32[8,128]{1,0:T(8,128)S(1)}, f32[8,128]{1,0:T(8,128)S(1)}, u32[]{:S(2)}, u32[]{:S(2)}) %collective-permute-start.5) | collective-permute-done | bytes 4128 | tf_op jit(solution)/shard_map/ppermute | solution.py:357
  29.1 2.0 %collective-permute-start.6 = (f32[8,128]{1,0:T(8,128)S(1)}, f32[8,128]{1,0:T(8,128)S(1)}, u32[]{:S(2)}, u32[]{:S(2)}) collective-permute-start(f32[8,128]{1,0:T(8,128)S(1)} %shard_map.82.mine_ref), channel_id=1, source_target_pairs={{0,2},{2,0},{4,6},{6,4},{8,10},{10,8},{12,14},{14,12},{1,3},{3,1},... | collective-permute-start | bytes 12296 | tf_op jit(solution)/shard_map/ppermute | solution.py:357
  31.0 1.7 %collective-permute-done.6.other_ref = f32[8,128]{1,0:T(8,128)S(1)} collective-permute-done((f32[8,128]{1,0:T(8,128)S(1)}, f32[8,128]{1,0:T(8,128)S(1)}, u32[]{:S(2)}, u32[]{:S(2)}) %collective-permute-start.6) | collective-permute-done | bytes 4128 | tf_op jit(solution)/shard_map/ppermute | solution.py:357
  32.8 1.1 %shard_map.85 = (bf16[1024,1024]{1,0:T(8,128)(2,1)S(1)}, bf16[1024,1024]{1,0:T(8,128)(2,1)S(1)}, bf16[128,1024]{1,0:T(8,128)(2,1)S(1)}) custom-call(bf16[1024,128]{1,0:T(8,128)(2,1)S(1)} %get-tuple-element.40.rows_ref, bf16[1024,128]{1,0:T(8,128)(2,1)S(1)} %get-tuple-element.41.ya_ref, f32[1,1024]{1,0:T(1,128)S(1)} %get-tuple-element.39.m_ref), custom_call_target="tpu_custom_call" | custom-call | tf_op jit(solution)/shard_map/pallas_call | solution.py:342
  33.9 0.1 collective-permute-done.7.other_ref
  34.0 2.5 %shard_map.86 = (f32[1,1024]{1,0:T(1,128)}, f32[1,1024]{1,0:T(1,128)S(1)}, f32[1,1024]{1,0:T(1,128)S(1)}, f32[8,128]{1,0:T(8,128)S(1)}, f32[512,128]{1,0:T(8,128...) custom-call(bf16[128,1024]{1,0:T(8,128)(2,1)S(1)} %get-tuple-element.34.xa0_ref.xa_ref, ...), custom_call_target="tpu_custom_call" | custom-call | tf_op jit(solution)/shard_map/pallas_call | solution.py:342
  36.5 0.5 collective-permute-start.8
  37.0 1.0 %collective-permute-done.8.got_ref = bf16[544,128]{1,0:T(8,128)(2,1)S(1)} collective-permute-done((bf16[544,128]{1,0:T(8,128)(2,1)S(1)}, bf16[544,128]{1,0:T(8,128)(2,1)S(1)}, u32[]{:S(2)}, u32[]{:S(2)}) %collective-permute-start.8) | collective-permute-done | bytes 139296 | tf_op jit(solution)/shard_map/ppermute | solution.py:357
  38.0 3.0 %collective-permute-start.9 = (bf16[288,128]{1,0:T(8,128)(2,1)S(1)}, bf16[288,128]{1,0:T(8,128)(2,1)S(1)}, u32[]{:S(2)}, u32[]{:S(2)}) collective-permute-start(bf16[288,128]{1,0:T(8,128)(2,1)S(1)} %get-tuple-element.54), channel_id=1, source_target_pairs={{0,8},{2,10},{4,12},{6,14},{8,0},{10,2},{12,4},{14,6},{1,9},{3,11}... | collective-permute-start | bytes 221192 | tf_op jit(solution)/shard_map/ppermute | solution.py:357
  41.0 4.4 %collective-permute-done.9.got_ref = bf16[288,128]{1,0:T(8,128)(2,1)S(1)} collective-permute-done((bf16[288,128]{1,0:T(8,128)(2,1)S(1)}, bf16[288,128]{1,0:T(8,128)(2,1)S(1)}, u32[]{:S(2)}, u32[]{:S(2)}) %collective-permute-start.9) | collective-permute-done | bytes 73760 | tf_op jit(solution)/shard_map/ppermute | solution.py:357
  45.4 0.8 %collective-permute-start.10 = (bf16[160,128]{1,0:T(8,128)(2,1)S(1)}, bf16[160,128]{1,0:T(8,128)(2,1)S(1)}, u32[]{:S(2)}, u32[]{:S(2)}) collective-permute-start(bf16[160,128]{1,0:T(8,128)(2,1)S(1)} %get-tuple-element.57), channel_id=1, source_target_pairs={{0,4},{2,6},{4,0},{6,2},{8,12},{10,14},{12,8},{14,10},{1,5},{3,7},... | collective-permute-start | bytes 122888 | tf_op jit(solution)/shard_map/ppermute | solution.py:357
  46.2 3.3 %collective-permute-done.10.got_ref = bf16[160,128]{1,0:T(8,128)(2,1)S(1)} collective-permute-done((bf16[160,128]{1,0:T(8,128)(2,1)S(1)}, bf16[160,128]{1,0:T(8,128)(2,1)S(1)}, u32[]{:S(2)}, u32[]{:S(2)}) %collective-permute-start.10) | collective-permute-done | bytes 40992 | tf_op jit(solution)/shard_map/ppermute | solution.py:357
  49.5 1.7 %collective-permute-start.11 = (bf16[96,128]{1,0:T(8,128)(2,1)S(1)}, bf16[96,128]{1,0:T(8,128)(2,1)S(1)}, u32[]{:S(2)}, u32[]{:S(2)}) collective-permute-start(bf16[96,128]{1,0:T(8,128)(2,1)S(1)} %get-tuple-element.60), channel_id=1, source_target_pairs={{0,2},{2,0},{4,6},{6,4},{8,10},{10,8},{12,14},{14,12},{1,3},{3,1},... | collective-permute-start | bytes 73736 | tf_op jit(solution)/shard_map/ppermute | solution.py:357
  51.2 2.2 %collective-permute-done.11.got_ref = bf16[96,128]{1,0:T(8,128)(2,1)S(1)} collective-permute-done((bf16[96,128]{1,0:T(8,128)(2,1)S(1)}, bf16[96,128]{1,0:T(8,128)(2,1)S(1)}, u32[]{:S(2)}, u32[]{:S(2)}) %collective-permute-start.11) | collective-permute-done | bytes 24608 | tf_op jit(solution)/shard_map/ppermute | solution.py:357
  53.4 2.3 %shard_map.90 = (f32[96,1024]{1,0:T(8,128)}, f32[64,96]{1,0:T(8,128)}, f32[1,64]{1,0:T(1,128)}) custom-call(bf16[128,1024]{1,0:T(8,128)(2,1)S(1)} %get-tuple-element.34.xa0_ref.xa_ref, f32[1,1024]{1,0:T(1,128)S(1)} %get-tuple-element.46.r_ref, f32[1,1024]{1,0:T(1,128)S(1)} %get-tuple-element.47.v_ref, f32[8,128]{1,0:T(8,128)S(1)} %get-tuple-element.48.c_ref, ...), custom_call_target="tpu_custom_call" | custom-call | tf_op jit(solution)/shard_map/pallas_call | solution.py:342
  (16 shorter events, 0.2 us)
Async XLA Ops:
  0.6 0.7 %copy-start.1 = (bf16[64,96]{1,0:T(8,128)(2,1)S(1)}, bf16[64,96]{1,0:T(8,128)(2,1)}, u32[]{:S(2)}) copy-start(bf16[64,96]{1,0:T(8,128)(2,1)} %y_hbm.1) | copy-start | bytes 36868
  1.3 0.7 %copy-start.3 = (bf16[64]{0:T(256)(128)(2,1)S(1)}, bf16[64]{0:T(256)(128)(2,1)}, u32[]{:S(2)}) copy-start(bf16[64]{0:T(256)(128)(2,1)} %param.7) | copy-start | bytes 388
  2.2 5.8 %collective-permute-start = (bf16[64,128]{1,0:T(8,128)(2,1)S(1)}, bf16[64,128]{1,0:T(8,128)(2,1)S(1)}, u32[]{:S(2)}, u32[]{:S(2)}) collective-permute-start(bf16[64,128]{1,0:T(8,128)(2,1)S(1)} %shard_map.76.mine_ref.y_ref), channel_id=1, source_target_pairs={{0,8},{2,10},{4,12},{6,14},{8,0},{10,2},{12,4},{14,6},{1,9},{3,11}... | collective-permute-start | bytes 49160 | tf_op jit(solution)/shard_map/ppermute | solution.py:357
  8.0 3.9 %collective-permute-start.1 = (bf16[128,128]{1,0:T(8,128)(2,1)S(1)}, bf16[128,128]{1,0:T(8,128)(2,1)S(1)}, u32[]{:S(2)}, u32[]{:S(2)}) collective-permute-start(bf16[128,128]{1,0:T(8,128)(2,1)S(1)} %shard_map.77.mine_ref), channel_id=1, source_target_pairs={{0,4},{2,6},{4,0},{6,2},{8,12},{10,14},{12,8},{14,10},{1,5},{3,7},... | collective-permute-start | bytes 98312 | tf_op jit(solution)/shard_map/ppermute | solution.py:357
  12.0 4.3 %collective-permute-start.2 = (bf16[256,128]{1,0:T(8,128)(2,1)S(1)}, bf16[256,128]{1,0:T(8,128)(2,1)S(1)}, u32[]{:S(2)}, u32[]{:S(2)}) collective-permute-start(bf16[256,128]{1,0:T(8,128)(2,1)S(1)} %shard_map.78.mine_ref), channel_id=1, source_target_pairs={{0,2},{2,0},{4,6},{6,4},{8,10},{10,8},{12,14},{14,12},{1,3},{3,1},... | collective-permute-start | bytes 196616 | tf_op jit(solution)/shard_map/ppermute | solution.py:357
  16.2 2.0 %collective-permute-start.3 = (bf16[512,128]{1,0:T(8,128)(2,1)S(1)}, bf16[512,128]{1,0:T(8,128)(2,1)S(1)}, u32[]{:S(2)}, u32[]{:S(2)}) collective-permute-start(bf16[512,128]{1,0:T(8,128)(2,1)S(1)} %shard_map.79.mine_ref), channel_id=1, source_target_pairs={{0,1},{1,0},{2,3},{3,2},{4,5},{5,4},{6,7},{7,6},{8,9},{9,8},{10,11... | collective-permute-start | bytes 393224 | tf_op jit(solution)/shard_map/ppermute | solution.py:357
  16.3 0.9 %copy-start = (bf16[1024,96]{0,1:T(8,128)(2,1)S(1)}, bf16[1024,96]{0,1:T(8,128)(2,1)}, u32[]{:S(2)}) copy-start(bf16[1024,96]{0,1:T(8,128)(2,1)} %param.4) | copy-start | bytes 589828
  17.3 0.7 %copy-start.2 = (bf16[1024]{0:T(1024)(128)(2,1)S(1)}, bf16[1024]{0:T(1024)(128)(2,1)}, u32[]{:S(2)}) copy-start(bf16[1024]{0:T(1024)(128)(2,1)} %param.6) | copy-start | bytes 6148
  20.8 4.6 %collective-permute-start.4 = (f32[8,128]{1,0:T(8,128)S(1)}, f32[8,128]{1,0:T(8,128)S(1)}, u32[]{:S(2)}, u32[]{:S(2)}) collective-permute-start(f32[8,128]{1,0:T(8,128)S(1)} %get-tuple-element.38.mine_ref), channel_id=1, source_target_pairs={{0,8},{2,10},{4,12},{6,14},{8,0},{10,2},{12,4},{14,6},{1,9},{3,11}... | collective-permute-start | bytes 12296 | tf_op jit(solution)/shard_map/ppermute | solution.py:357
  25.4 3.7 %collective-permute-start.5 = (f32[8,128]{1,0:T(8,128)S(1)}, f32[8,128]{1,0:T(8,128)S(1)}, u32[]{:S(2)}, u32[]{:S(2)}) collective-permute-start(f32[8,128]{1,0:T(8,128)S(1)} %shard_map.81.mine_ref), channel_id=1, source_target_pairs={{0,4},{2,6},{4,0},{6,2},{8,12},{10,14},{12,8},{14,10},{1,5},{3,7},... | collective-permute-start | bytes 12296 | tf_op jit(solution)/shard_map/ppermute | solution.py:357
  29.1 3.7 %collective-permute-start.6 = (f32[8,128]{1,0:T(8,128)S(1)}, f32[8,128]{1,0:T(8,128)S(1)}, u32[]{:S(2)}, u32[]{:S(2)}) collective-permute-start(f32[8,128]{1,0:T(8,128)S(1)} %shard_map.82.mine_ref), channel_id=1, source_target_pairs={{0,2},{2,0},{4,6},{6,4},{8,10},{10,8},{12,14},{14,12},{1,3},{3,1},... | collective-permute-start | bytes 12296 | tf_op jit(solution)/shard_map/ppermute | solution.py:357
  32.8 1.2 %collective-permute-start.7 = (f32[8,128]{1,0:T(8,128)S(1)}, f32[8,128]{1,0:T(8,128)S(1)}, u32[]{:S(2)}, u32[]{:S(2)}) collective-permute-start(f32[8,128]{1,0:T(8,128)S(1)} %shard_map.83.mine_ref), channel_id=1, source_target_pairs={{0,1},{1,0},{2,3},{3,2},{4,5},{5,4},{6,7},{7,6},{8,9},{9,8},{10,11... | collective-permute-start | bytes 12296 | tf_op jit(solution)/shard_map/ppermute | solution.py:357
  36.5 1.5 %collective-permute-start.8 = (bf16[544,128]{1,0:T(8,128)(2,1)S(1)}, bf16[544,128]{1,0:T(8,128)(2,1)S(1)}, u32[]{:S(2)}, u32[]{:S(2)}) collective-permute-start(bf16[544,128]{1,0:T(8,128)(2,1)S(1)} %get-tuple-element.51), channel_id=1, source_target_pairs={{0,1},{1,0},{2,3},{3,2},{4,5},{5,4},{6,7},{7,6},{8,9},{9,8},{10,11... | collective-permute-start | bytes 417800 | tf_op jit(solution)/shard_map/ppermute | solution.py:357
  38.0 7.4 %collective-permute-start.9 = (bf16[288,128]{1,0:T(8,128)(2,1)S(1)}, bf16[288,128]{1,0:T(8,128)(2,1)S(1)}, u32[]{:S(2)}, u32[]{:S(2)}) collective-permute-start(bf16[288,128]{1,0:T(8,128)(2,1)S(1)} %get-tuple-element.54), channel_id=1, source_target_pairs={{0,8},{2,10},{4,12},{6,14},{8,0},{10,2},{12,4},{14,6},{1,9},{3,11}... | collective-permute-start | bytes 221192 | tf_op jit(solution)/shard_map/ppermute | solution.py:357
  45.4 4.1 %collective-permute-start.10 = (bf16[160,128]{1,0:T(8,128)(2,1)S(1)}, bf16[160,128]{1,0:T(8,128)(2,1)S(1)}, u32[]{:S(2)}, u32[]{:S(2)}) collective-permute-start(bf16[160,128]{1,0:T(8,128)(2,1)S(1)} %get-tuple-element.57), channel_id=1, source_target_pairs={{0,4},{2,6},{4,0},{6,2},{8,12},{10,14},{12,8},{14,10},{1,5},{3,7},... | collective-permute-start | bytes 122888 | tf_op jit(solution)/shard_map/ppermute | solution.py:357
  49.5 3.9 %collective-permute-start.11 = (bf16[96,128]{1,0:T(8,128)(2,1)S(1)}, bf16[96,128]{1,0:T(8,128)(2,1)S(1)}, u32[]{:S(2)}, u32[]{:S(2)}) collective-permute-start(bf16[96,128]{1,0:T(8,128)(2,1)S(1)} %get-tuple-element.60), channel_id=1, source_target_pairs={{0,2},{2,0},{4,6},{6,4},{8,10},{10,8},{12,14},{14,12},{1,3},{3,1},... | collective-permute-start | bytes 73736 | tf_op jit(solution)/shard_map/ppermute | solution.py:357

commit v5 on v4

v5 whole, which is shorter than its diff:
```python
import functools
import math

import jax
import jax.numpy as jnp
from jax import lax
from jax.experimental import pallas as pl
from jax.experimental.pallas import tpu as pltpu
from jax.sharding import PartitionSpec as P

ITERS = 2
EPSILON = 0.02
LOG2E = math.log2(math.e)
TILE = 256
STEP = 32
EXT = 32
PAD = 16
LANES = 128
F32 = jnp.float32
BF16 = jnp.bfloat16


def kappa_of(width):
    return 2.0 / (width * EPSILON)


def pieces(value):
    high = value.astype(BF16).astype(F32)
    rest = value - high
    mid = rest.astype(BF16).astype(F32)
    return high, mid, rest - mid


def select(index, values):
    out = jnp.zeros(index.shape, F32)
    for k, value in values.items():
        out = jnp.where(index == k, value, out)
    return out


def extras_y(index, c_term, mass):
    high, mid, low = pieces(c_term)
    return select(index, {0: high, 1: mid, 2: low, 3: 1.0, 4: 1.0, 5: 1.0, 6: mass})


def extras_x(index, b_term):
    high, mid, low = pieces(b_term)
    return select(index, {0: 1.0, 1: 1.0, 2: 1.0, 3: high, 4: mid, 5: low})


def rows_index(columns):
    return lax.broadcasted_iota(jnp.int32, (EXT, columns), 0)


def to_column(row):
    size = row.shape[1]
    eye = lax.broadcasted_iota(jnp.int32, (size, size), 0) == lax.broadcasted_iota(jnp.int32, (size, size), 1)
    return jnp.sum(jnp.where(eye, row, 0.0), axis=1, keepdims=True)


def to_row(column):
    size = column.shape[0]
    eye = lax.broadcasted_iota(jnp.int32, (size, size), 0) == lax.broadcasted_iota(jnp.int32, (size, size), 1)
    return jnp.sum(jnp.where(eye, column, 0.0), axis=0, keepdims=True)


def for_tiles(total, body):
    count = total // TILE
    if count <= 4:
        for t in range(count):
            body(pl.ds(t * TILE, TILE))
    else:

        @pl.loop(0, count)
        def _(t):
            body(pl.ds(pl.multiple_of(t * TILE, TILE), TILE))


def max_down(z_ref, rows):
    peak = z_ref[0:STEP, :]
    for r in range(STEP, rows, STEP):
        peak = jnp.maximum(peak, z_ref[r : r + STEP, :])
    return jnp.max(peak, axis=0, keepdims=True)


def exp_sum_down(z_ref, rows, scale, shift):
    total = jnp.zeros((STEP, TILE), F32)
    for r in range(0, rows, STEP):
        total = total + jnp.exp2((z_ref[r : r + STEP, :] - shift) * scale)
    return jnp.sum(total, axis=0, keepdims=True)


def to_lanes(row):
    return jnp.concatenate([row[:, k : k + LANES] for k in range(0, row.shape[1], LANES)], axis=0)


def from_lanes(block):
    return jnp.concatenate([block[k : k + 1] for k in range(block.shape[0])], axis=1)


def sums_rows(ny):
    return -(-2 * ny // LANES // 16) * 16


def sums_out(sums):
    high = sums.astype(BF16).astype(F32)
    spare = sums_rows(sums.size) - 2 * sums.shape[0]
    return jnp.concatenate([high, sums - high] + [jnp.zeros((spare, LANES), F32)] * (spare > 0), axis=0)


def sums_in(ext, count):
    return ext[:count] + ext[count : 2 * count]


def pack(block):
    rows, width = block.shape
    base = rows * width // LANES
    spare = LANES - width
    side = [block[base:, k : k + spare] for k in range(0, width, spare)]
    return jnp.concatenate([block[:base], jnp.concatenate(side, axis=0)], axis=1)


def unpack(block, rows, width):
    base = block.shape[0]
    rest = rows - base
    side = [block[k : k + rest, width:] for k in range(0, base, rest)]
    return jnp.concatenate([block[:, :width], jnp.concatenate(side, axis=1)], axis=0)


def prep_kernel(
    log_ny, xt_hbm, y_hbm, mx_hbm, my_hbm, ya_ref, xa_ref, mx_ref, y_ref, my_ref, mx_in, sems
):
    width, n = xt_hbm.shape
    pairs = ((y_hbm, y_ref), (my_hbm, my_ref), (xt_hbm, xa_ref.at[:width, :]), (mx_hbm, mx_in))
    moves = [pltpu.make_async_copy(a, b, sems.at[k]) for k, (a, b) in enumerate(pairs)]
    for move in moves:
        move.start()
    xa_ref[width:, :] = extras_x(rows_index(n), jnp.zeros((1, n), F32)).astype(BF16)
    moves[0].wait()
    moves[1].wait()
    y = y_ref[...]
    yf = y.astype(F32)
    norm = jnp.sum(yf * yf, axis=1, keepdims=True)
    mass = to_column(my_ref[...].astype(F32))
    c_term = (mass - log_ny) / kappa_of(width) - 0.5 * norm
    ext = extras_y(lax.broadcasted_iota(jnp.int32, (y.shape[0], EXT), 1), c_term, mass).astype(BF16)
    for k in range(ya_ref.shape[0]):
        ya_ref[k, :, :width] = y
        ya_ref[k, :, width:] = ext
    moves[2].wait()
    moves[3].wait()
    mx_ref[...] = from_lanes(mx_in[...].astype(F32))


def half_kernel(xa_ref, mine_ref, peak_ref, total_ref, z_ref):
    rows, yd, depth = mine_ref.shape
    half = rows * yd
    scale = kappa_of(depth - EXT) * LOG2E
    y_rows = mine_ref[...].reshape(half, depth)

    def row_tile(t):
        z_ref[...] = jnp.dot(y_rows, xa_ref[:, t], preferred_element_type=F32)
        peak = max_down(z_ref, half)
        peak_ref[:, t] = peak
        total_ref[:, t] = exp_sum_down(z_ref, half, scale, peak)

    for_tiles(xa_ref.shape[1], row_tile)


def first_kernel(
    log_nx, xa0_ref, mx_ref, mine_ref, other_ref, peak_ref, total_ref,
    ya_ref, b_ref, l_ref, m_ref, rows_ref, xa_ref, z_ref, zc_ref, b2_ref,
):
    rows, yd, depth = mine_ref.shape
    n = mx_ref.shape[1]
    width = depth - EXT
    half = rows * yd
    ny = 2 * half
    col = lax.axis_index("col")
    scale = kappa_of(width) * LOG2E
    other = other_ref[...].reshape(half, depth)
    ya_ref[pl.ds(pl.multiple_of(col * half, half), half), :] = mine_ref[...].reshape(half, depth)
    ya_ref[pl.ds(pl.multiple_of((1 - col) * half, half), half), :] = other

    def row_tile(t):
        z_ref[...] = jnp.dot(other, xa0_ref[:, t], preferred_element_type=F32)
        old = peak_ref[:, t]
        peak = jnp.maximum(max_down(z_ref, half), old)
        total = exp_sum_down(z_ref, half, scale, peak) + total_ref[:, t] * jnp.exp2((old - peak) * scale)
        b_ref[:, t] = -peak - jnp.log(total) * (LOG2E / scale)

    for_tiles(n, row_tile)
    b_term = b_ref[...] + (mx_ref[...] - log_nx) * (LOG2E / scale)
    b_ref[...] = b_term
    xa_ref[:width, :] = xa0_ref[:width, :]
    xa_ref[width:, :] = extras_x(rows_index(n), b_term).astype(BF16)
    rows_ref[...] = xa_ref[...].T

    def col_tile(t):
        zc_ref[...] = lax.dot_general(
            rows_ref[...], ya_ref[t, :], (((1,), (1,)), ((), ())), preferred_element_type=F32
        )
        peak = max_down(zc_ref, n)
        m_ref[:, t] = peak
        b2_ref[:, t] = scale * peak + jnp.log(exp_sum_down(zc_ref, n, scale, peak)) * LOG2E

    for_tiles(ny, col_tile)
    lse = to_lanes(b2_ref[...])
    for k in range(rows):
        l_ref[k] = lse


def plan_kernel(xa_ref, rows_ref, ya_ref, m_ref, t_ref, yt_ref, norm_ref, zc_ref):
    ny, depth = ya_ref.shape
    n = rows_ref.shape[0]
    scale = kappa_of(depth - EXT) * LOG2E

    def col_tile(t):
        y_part = ya_ref[t, :]
        yt_ref[:, t] = y_part.T
        zc_ref[...] = lax.dot_general(
            rows_ref[...], y_part, (((1,), (1,)), ((), ())), preferred_element_type=F32
        )
        peak = m_ref[:, t]
        for r in range(0, n, STEP):
            t_ref[r : r + STEP, t] = jnp.exp2((zc_ref[r : r + STEP, :] - peak) * scale).astype(BF16)

    for_tiles(ny, col_tile)
    xf = xa_ref[: depth - EXT, :].astype(F32)
    norm_ref[...] = jnp.sum(xf * xf, axis=0, keepdims=True)


def stack(out_ref, width, points, factor):
    moved = points.astype(F32) * factor
    high = moved.astype(BF16)
    out_ref[:width, :] = high
    out_ref[width : 2 * width, :] = (moved - high.astype(F32)).astype(BF16)
    one, two, three = pieces(factor)
    index = lax.broadcasted_iota(jnp.int32, (PAD, factor.shape[1]), 0)
    out_ref[2 * width :, :] = select(index, {0: one, 1: two, 2: three}).astype(BF16)


def unstack(product, width):
    ext = product[2 * width :]
    return product[:width] + product[width : 2 * width], (ext[0:1] + ext[1:2]) + ext[2:3]


def second_kernel(
    log_nx, log_ny, xa_ref, mx_ref, norm_ref, b_ref, l_ref, other_ref, m_ref, yt_ref, t_ref,
    f_ref, r_ref, v_ref, c_ref, keep_ref, sum_ref, send_ref, xs_ref, gt_ref, part_ref,
):
    width = xa_ref.shape[0] - EXT
    ny = m_ref.shape[1]
    kappa = kappa_of(width)
    scale = kappa * LOG2E
    l_mine, l_other = l_ref[...], other_ref[...]
    peak = jnp.maximum(jnp.max(l_mine, axis=0), jnp.max(l_other, axis=0))
    total = jnp.sum(jnp.exp2(l_mine - peak[None]), axis=0) + jnp.sum(jnp.exp2(l_other - peak[None]), axis=0)
    lse2 = from_lanes(peak + jnp.log(total) * LOG2E)
    old = yt_ref[width:, :].astype(F32)
    c_old = (old[0:1] + old[1:2]) + old[2:3]
    lb2 = (old[6:7] - log_ny) * LOG2E
    c_ref[...] = to_lanes(c_old + (lb2 - lse2) / scale)
    v = jnp.exp2(scale * m_ref[...] + (lb2 - lse2))
    v_ref[...] = v
    one, two, three = pieces(v)
    index = lax.broadcasted_iota(jnp.int32, (PAD, ny), 0)
    v_rows = select(index, {0: one, 1: two, 2: three}).astype(BF16)
    across = (((1,), (1,)), ((), ()))
    sums = lax.dot_general(v_rows, t_ref[...], across, preferred_element_type=F32)
    rowsum = (sums[0:1] + sums[1:2]) + sums[2:3]
    log_row = jnp.log(rowsum)
    f_ref[...] = norm_ref[...] / width + EPSILON * (kappa * b_ref[...] - log_row)
    r = jnp.exp(mx_ref[...] - log_nx - log_row)
    r_ref[...] = r
    stack(xs_ref, width, xa_ref[:width, :], r)
    totals = []
    for k in range(ny // TILE):
        t = slice(k * TILE, (k + 1) * TILE)
        product = jnp.dot(xs_ref[...], t_ref[:, t], preferred_element_type=F32)
        moment, total = unstack(product, width)
        total = total * v[:, t]
        totals.append(total)
        gt_ref[:width, t] = yt_ref[:width, t].astype(F32) * total - moment * v[:, t]
    gt_ref[width:, :] = jnp.zeros((EXT, ny), F32)
    part_ref[...] = gt_ref[...].T
    sums = to_lanes(jnp.concatenate(totals, axis=1))
    sum_ref[...] = sums
    col = lax.axis_index("col")
    half = keep_ref.shape[0]
    keep_ref[...] = part_ref[pl.ds(pl.multiple_of(col * half, half), half), :]
    send_ref[:half, :] = part_ref[pl.ds(pl.multiple_of((1 - col) * half, half), half), :].astype(BF16)
    send_ref[half:, :] = sums_out(sums).astype(BF16)


def add_kernel(width, keep_ref, sum_ref, got_ref, out_ref):
    half = keep_ref.shape[0]
    rows = out_ref.shape[0]
    yd = half // rows
    base = yd * width // LANES
    count = sum_ref.shape[0]
    sums = sums_out(sum_ref[...] + sums_in(got_ref[half:, :].astype(F32), count)).astype(BF16)
    for r in range(rows):
        part = slice(r * yd, (r + 1) * yd)
        total = keep_ref[part, :] + got_ref[part, :].astype(F32)
        out_ref[r, :base, :] = pack(total[:, :width]).astype(BF16)
        out_ref[r, base:, :] = sums


def own_part(ref, yd):
    block = lax.axis_index("col") * lax.axis_size("row") + lax.axis_index("row")
    fit = LANES // yd
    row = ref[pl.ds(block // fit, 1), :]
    out = row[:, :yd]
    for k in range(1, fit):
        out = jnp.where(block % fit == k, row[:, k * yd : (k + 1) * yd], out)
    return out


def last_kernel(
    log_nx, log_ny, xa_ref, r_ref, v_ref, c_ref, got_ref, yt_ref, t_ref, y_ref,
    gx_ref, gy_ref, pot_ref, ys_ref, sum_ref,
):
    width, n = gx_ref.shape
    ny = v_ref.shape[1]
    yd = y_ref.shape[1]
    base = yd * width // LANES
    total = got_ref[0].astype(F32)
    for k in range(1, got_ref.shape[0]):
        total = total + got_ref[k].astype(F32)
    sums = sums_in(total[base:], ny // LANES)
    sum_ref[...] = sums
    mass = yt_ref[width:, :].astype(F32)[6:7]
    q = v_ref[...] * jnp.exp(mass + log_nx - jnp.log(from_lanes(sums)))
    stack(ys_ref, width, yt_ref[:width, :], q)
    across = (((1,), (1,)), ((), ()))
    for k in range(n // TILE):
        t = slice(k * TILE, (k + 1) * TILE)
        product = lax.dot_general(ys_ref[...], t_ref[t, :], across, preferred_element_type=F32)
        moved, weight = unstack(product, width)
        gx_ref[:, t] = (xa_ref[:width, t].astype(F32) * weight - moved) * (r_ref[:, t] * (1.0 / ny))
    colsum = own_part(sum_ref, yd)
    c_term = own_part(c_ref, yd)
    own = y_ref[0].astype(F32)
    gy_ref[...] = unpack(total[:base], yd, width) * (jnp.exp(own[:, width + 6 : width + 7]) * to_column(1.0 / colsum))
    norm = to_row(jnp.sum(own[:, :width] * own[:, :width], axis=1, keepdims=True))
    pot_ref[...] = norm / width - EPSILON * (jnp.log(colsum) - kappa_of(width) * c_term)


def call(kernel, outs, scratch, limit, *args, space=pltpu.VMEM):
    return pl.pallas_call(
        kernel,
        out_shape=outs,
        in_specs=[pl.BlockSpec(memory_space=space)] * len(args),
        out_specs=jax.tree.map(lambda _: pl.BlockSpec(memory_space=pltpu.VMEM), outs),
        scratch_shapes=scratch,
        compiler_params=pltpu.CompilerParams(vmem_limit_bytes=limit),
    )(*args)


def shape(dims, dtype=F32):
    return jax.ShapeDtypeStruct(dims, dtype)


def swap(value):
    return lax.ppermute(value, "col", [(0, 1), (1, 0)])


def on_device(points_x, points_y, mass_x, mass_y):
    n, width = points_x.shape
    yd = points_y.shape[0]
    rows = lax.axis_size("row")
    ny = 2 * rows * yd
    half = ny // 2
    count = ny // LANES
    log_nx, log_ny = math.log(n * 2 * rows), math.log(ny)
    depth = width + EXT
    limit = (12 if ny <= 1024 else 56) * 1024 * 1024
    extra = sums_rows(ny)
    run = functools.partial
    vmem = pltpu.VMEM
    y_own, xa, mx = call(
        run(prep_kernel, log_ny),
        (shape((rows, yd, depth), BF16), shape((depth, n), BF16), shape((1, n))),
        [
            vmem((yd, width), BF16), vmem((1, yd), BF16), vmem((n // LANES, LANES), BF16),
            pltpu.SemaphoreType.DMA((4,)),
        ],
        58 * 1024 * 1024,
        points_x.T, points_y, mass_x.reshape(n // LANES, LANES), mass_y.reshape(1, yd), space=pl.ANY,
    )
    y_mine = lax.all_to_all(y_own, "row", 0, 0, tiled=True)
    y_other = swap(y_mine)
    peak, total = call(
        half_kernel, (shape((1, n)), shape((1, n))), [vmem((half, TILE), F32)], limit, xa, y_mine
    )
    ya, b_term, lse, peak, x_rows = call(
        run(first_kernel, log_nx),
        (
            shape((ny, depth), BF16), shape((1, n)), shape((rows, count, LANES)), shape((1, ny)),
            shape((n, depth), BF16),
        ),
        [vmem((depth, n), BF16), vmem((half, TILE), F32), vmem((n, TILE), F32), vmem((1, ny), F32)],
        limit, xa, mx, y_mine, y_other, peak, total,
    )
    lse = lax.all_to_all(lse, "row", 0, 0, tiled=True)
    lse_other = swap(lse)
    plan, yt, norm = call(
        plan_kernel,
        (shape((n, ny), BF16), shape((depth, ny), BF16), shape((1, n))),
        [vmem((n, TILE), F32)],
        limit, xa, x_rows, ya, peak,
    )
    f_pot, r, v, c_term, keep, sums, send = call(
        run(second_kernel, log_nx, log_ny),
        (
            shape((1, n)), shape((1, n)), shape((1, ny)), shape((count, LANES)),
            shape((half, depth)), shape((count, LANES)), shape((half + extra, depth), BF16),
        ),
        [vmem((2 * width + PAD, n), BF16), vmem((depth, ny), F32), vmem((ny, depth), F32)],
        limit, xa, mx, norm, b_term, lse, lse_other, peak, yt, plan,
    )
    part = call(
        run(add_kernel, width), shape((rows, yd * width // LANES + extra, LANES), BF16), [],
        limit, keep, sums, swap(send),
    )
    part = lax.all_to_all(part, "row", 0, 0, tiled=True)
    grad_xt, grad_y, g_pot = call(
        run(last_kernel, log_nx, log_ny),
        (shape((width, n)), shape((yd, width)), shape((1, yd))),
        [vmem((2 * width + PAD, ny), BF16), vmem((count, LANES), F32)],
        limit, xa, r, v, c_term, part, yt, plan, y_own,
    )
    return f_pot.reshape(n), g_pot.reshape(yd), grad_xt.T, grad_y


def solution(mesh):
    in_specs = (
        P(("groups", "row", "col"), None),
        P(("groups", "col", "row"), None),
        P(("groups", "row", "col")),
        P(("groups", "col", "row")),
    )
    out_specs = (
        P(("groups", "row", "col")),
        P(("groups", "col", "row")),
        P(("groups", "row", "col"), None),
        P(("groups", "col", "row"), None),
    )
    return jax.shard_map(
        on_device, mesh=mesh, in_specs=in_specs, out_specs=out_specs, check_vma=False
    )
```

time: 56 us -> 47.5 us (0.85)
  blocking collectives: 0 us -> 33.7 us
  starting transfers between devices: 21 us -> 0.24 us
  waiting for transfers between devices: 22 us -> 1.64 us
  Pallas kernels: 9.08 us -> 8.44 us
  local copies, waits for them, and re-layouts: 2.97 us -> 2.33 us
    all_to_all x0 -> x3, blocking collectives: none -> 33.7 us  [the longest x1 14.6 us: on_device(): y_mine = lax.all_to_all(y_own, 'row', 0, 0, tiled=True)]
    ppermute x12 -> x3, starting transfers between devices: 21 us -> 0.24 us  [swap(): return lax.ppermute(value, 'col', [(0, 1), (1, 0)])]
    ppermute x12 -> x3, waiting for transfers between devices: 22 us -> 1.64 us  [swap(): return lax.ppermute(value, 'col', [(0, 1), (1, 0)])]
    unnamed x8 -> x10, local copies, waits for them, and re-layouts: 2.97 us -> 2.33 us
    pallas_call x16 -> x7, Pallas kernels: 9.08 us -> 8.44 us  [call(): pl.pallas_call(kernel, out_shape=outs, in_specs=[pl.BlockSpec(memory_spac...]
  transfers between devices with their start and end apart: 12 -> 3, of which waited for: 11 -> 2; matrix products, arithmetic and copies ran while one was open for 0% -> 0% of each run, Pallas kernels for 2% -> 3%
where the time goes in v5:
time: 47.5 us; the launch traced here: 47 us
  blocking collectives  33.7 us (71%)
  Pallas kernels  8.44 us (18%)
  local copies, waits for them, and re-layouts  2.33 us (5%)
  waiting for transfers between devices  1.64 us (3%)
  between operations  0.69 us (1%)
    all_to_all x1, blocking collectives, on_device(): y_mine = lax.all_to_all(y_own, 'row', 0, 0, tiled=True)  14.6 us
    all_to_all x1, blocking collectives, on_device(): part = lax.all_to_all(part, 'row', 0, 0, tiled=True)  9.99 us
    all_to_all x1, blocking collectives, on_device(): lse = lax.all_to_all(lse, 'row', 0, 0, tiled=True)  9.06 us
    pallas_call x7, Pallas kernels, call(): pl.pallas_call(kernel, out_shape=outs, in_specs=[pl.BlockSpec(memory_spac...  8.44 us
    unnamed x10, local copies, waits for them, and re-layouts  2.33 us
    ppermute x3, waiting for transfers between devices, swap(): return lax.ppermute(value, 'col', [(0, 1), (1, 0)])  1.64 us
  transfers between devices with their start and end apart: 3, of which 2 were waited for; matrix products, arithmetic and copies ran while one was open for 0% of the time, Pallas kernels for 3%

profile of v5, /device:TPU:0, one launch (start us, length us, event | category | flops | bytes accessed | tf_op | source)
XLA Modules:
  0.0 47.0 jit_solution(8671279409746885227)
XLA Ops:
  0.6 1.7 %shard_map.75 = (bf16[8,64,128]{2,1,0:T(8,128)(2,1)}, bf16[128,1024]{1,0:T(8,128)(2,1)}, f32[1,1024]{1,0:T(1,128)}) custom-call(bf16[96,1024]{1,0:T(8,128)(2,1)} %bitcast.6, bf16[64,96]{1,0:T(8,128)(2,1)} %y_hbm.1, bf16[8,128]{1,0:T(8,128)(2,1)} %bitcast.7, bf16[1,64]{1,0:T(2,128)(2,1)} %bitcast.8), custom_call_target="tpu_custom_call" | custom-call | tf_op jit(solution)/shard_map/pallas_call | solution.py:351
  2.4 14.6 %all_to_all.15.mine_ref = bf16[8,64,128]{2,1,0:T(8,128)(2,1)S(1)} all-to-all(bf16[8,64,128]{2,1,0:T(8,128)(2,1)} %get-tuple-element.29.y_ref), channel_id=1, replica_groups=mesh['groups'=2,'row'=8,'col'=2] {'row'}, dimensions={0} | all-to-all | bytes 262144 | tf_op jit(solution)/shard_map/all_to_all | solution.py:392
  17.0 0.0 collective-permute-start
  17.0 0.0 copy-start
  17.0 0.9 %copy-done = bf16[128,1024]{1,0:T(8,128)(2,1)S(1)} copy-done((bf16[128,1024]{1,0:T(8,128)(2,1)S(1)}, bf16[128,1024]{1,0:T(8,128)(2,1)}, u32[]{:S(2)}) %copy-start) | copy-done | bytes 262168
  18.0 0.7 %shard_map.76 = (f32[1,1024]{1,0:T(1,128)S(1)}, f32[1,1024]{1,0:T(1,128)S(1)}) custom-call(bf16[128,1024]{1,0:T(8,128)(2,1)S(1)} %copy-done, bf16[8,64,128]{2,1,0:T(8,128)(2,1)S(1)} %all_to_all.15.mine_ref), custom_call_target="tpu_custom_call" | custom-call | tf_op jit(solution)/shard_map/pallas_call | solution.py:351
  18.6 0.0 collective-permute-done.other_ref
  18.6 0.0 copy-start.3
  18.7 0.7 %copy-done.3 = f32[1,1024]{1,0:T(1,128)S(1)} copy-done((f32[1,1024]{1,0:T(1,128)S(1)}, f32[1,1024]{1,0:T(1,128)}, u32[]{:S(2)}) %copy-start.3) | copy-done | bytes 4120
  19.3 2.0 %shard_map.77 = (bf16[1024,128]{1,0:T(8,128)(2,1)S(1)}, f32[1,1024]{1,0:T(1,128)S(1)}, f32[8,8,128]{2,1,0:T(8,128)S(1)}, f32[1,1024]{1,0:T(1,128)S(1)}, bf16[1024,128]{1,0:T(8,128)(2,1)S(1)}) custom-call(bf16[128,1024]{1,0:T(8,128)(2,1)S(1)} %copy-done, f32[1,1024]{1,0:T(1,128)S(1)} %copy-done.3, bf16[8,64,128]{2,1,0:T(8,128)(2,1)S(1)} %all_to_all.15.mine_ref, ...), custom_call_target="tpu_custom_call" | custom-call | tf_op jit(solution)/shard_map/pallas_call | solution.py:351
  21.3 9.1 %all_to_all.16.l_ref = f32[8,8,128]{2,1,0:T(8,128)S(1)} all-to-all(f32[8,8,128]{2,1,0:T(8,128)S(1)} %get-tuple-element.37), channel_id=1, replica_groups=mesh['groups'=2,'row'=8,'col'=2] {'row'}, dimensions={0} | all-to-all | bytes 65536 | tf_op jit(solution)/shard_map/all_to_all | solution.py:406
  30.4 0.0 collective-permute-start.1
  30.4 0.0 copy-start.1
  30.4 0.0 copy-start.2
  30.4 0.7 %shard_map.78 = (bf16[1024,1024]{1,0:T(8,128)(2,1)S(1)}, bf16[128,1024]{1,0:T(8,128)(2,1)S(1)}, f32[1,1024]{1,0:T(1,128)S(1)}) custom-call(bf16[128,1024]{1,0:T(8,128)(2,1)S(1)} %copy-done, bf16[1024,128]{1,0:T(8,128)(2,1)S(1)} %get-tuple-element.32.rows_ref, bf16[1024,128]{1,0:T(8,128)(2,1)S(1)} %get-tuple-element.33.ya_ref, ...), custom_call_target="tpu_custom_call" | custom-call | tf_op jit(solution)/shard_map/pallas_call | solution.py:351
  31.1 0.5 collective-permute-done.1.other_ref
  31.6 0.0 copy-start.4
  31.6 0.7 %copy-done.4 = f32[1,1024]{1,0:T(1,128)S(1)} copy-done((f32[1,1024]{1,0:T(1,128)S(1)}, f32[1,1024]{1,0:T(1,128)}, u32[]{:S(2)}) %copy-start.4) | copy-done | bytes 4120
  32.3 1.5 %shard_map.79 = (f32[1,1024]{1,0:T(1,128)}, f32[1,1024]{1,0:T(1,128)S(1)}, f32[1,1024]{1,0:T(1,128)S(1)}, f32[8,128]{1,0:T(8,128)S(1)}, f32[512,128]{1,0:T(8,128...) custom-call(bf16[128,1024]{1,0:T(8,128)(2,1)S(1)} %copy-done, f32[1,1024]{1,0:T(1,128)S(1)} %copy-done.4, ...), custom_call_target="tpu_custom_call" | custom-call | tf_op jit(solution)/shard_map/pallas_call | solution.py:351
  33.8 0.2 collective-permute-start.2
  34.0 1.2 %collective-permute-done.2.got_ref = bf16[528,128]{1,0:T(8,128)(2,1)S(1)} collective-permute-done((bf16[528,128]{1,0:T(8,128)(2,1)S(1)}, bf16[528,128]{1,0:T(8,128)(2,1)S(1)}, u32[]{:S(2)}, u32[]{:S(2)}) %collective-permute-start.2) | collective-permute-done | bytes 135200 | tf_op jit(solution)/shard_map/ppermute | solution.py:366
  35.2 0.2 shard_map.80
  35.3 10.0 %all_to_all.17.got_ref = bf16[8,64,128]{2,1,0:T(8,128)(2,1)S(1)} all-to-all(bf16[8,64,128]{2,1,0:T(8,128)(2,1)S(1)} %shard_map.80), channel_id=1, replica_groups=mesh['groups'=2,'row'=8,'col'=2] {'row'}, dimensions={0} | all-to-all | bytes 262144 | tf_op jit(solution)/shard_map/all_to_all | solution.py:427
  45.3 0.0 copy-done.1
  45.3 0.0 copy-done.2
  45.3 1.7 %shard_map.81 = (f32[96,1024]{1,0:T(8,128)}, f32[64,96]{1,0:T(8,128)}, f32[1,64]{1,0:T(1,128)}) custom-call(bf16[128,1024]{1,0:T(8,128)(2,1)S(1)} %copy-done.1, f32[1,1024]{1,0:T(1,128)S(1)} %get-tuple-element.41.r_ref, f32[1,1024]{1,0:T(1,128)S(1)} %get-tuple-element.42.v_ref, f32[8,128]{1,0:T(8,128)S(1)} %get-tuple-element.43.c_ref, ...), custom_call_target="tpu_custom_call" | custom-call | tf_op jit(solution)/shard_map/pallas_call | solution.py:351
Async XLA Ops:
  17.0 1.6 %collective-permute-start = (bf16[8,64,128]{2,1,0:T(8,128)(2,1)S(1)}, bf16[8,64,128]{2,1,0:T(8,128)(2,1)S(1)}, u32[]{:S(2)}, u32[]{:S(2)}) collective-permute-start(bf16[8,64,128]{2,1,0:T(8,128)(2,1)S(1)} %all_to_all.15.mine_ref), channel_id=1, source_target_pairs={{0,1},{1,0},{2,3},{3,2},{4,5},{5,4},{6,7},{7,6},{8,9},{9,8},{10,11... | collective-permute-start | bytes 393224 | tf_op jit(solution)/shard_map/ppermute | solution.py:366
  17.0 1.0 %copy-start = (bf16[128,1024]{1,0:T(8,128)(2,1)S(1)}, bf16[128,1024]{1,0:T(8,128)(2,1)}, u32[]{:S(2)}) copy-start(bf16[128,1024]{1,0:T(8,128)(2,1)} %get-tuple-element.27.xa_ref.xa0_ref) | copy-start | bytes 786436
  18.6 0.7 %copy-start.3 = (f32[1,1024]{1,0:T(1,128)S(1)}, f32[1,1024]{1,0:T(1,128)}, u32[]{:S(2)}) copy-start(f32[1,1024]{1,0:T(1,128)} %get-tuple-element.28.mx_ref) | copy-start | bytes 12292
  30.4 1.2 %collective-permute-start.1 = (f32[8,8,128]{2,1,0:T(8,128)S(1)}, f32[8,8,128]{2,1,0:T(8,128)S(1)}, u32[]{:S(2)}, u32[]{:S(2)}) collective-permute-start(f32[8,8,128]{2,1,0:T(8,128)S(1)} %all_to_all.16.l_ref), channel_id=1, source_target_pairs={{0,1},{1,0},{2,3},{3,2},{4,5},{5,4},{6,7},{7,6},{8,9},{9,8},{10,11... | collective-permute-start | bytes 98312 | tf_op jit(solution)/shard_map/ppermute | solution.py:366
  30.4 15.0 %copy-start.1 = (bf16[128,1024]{1,0:T(8,128)(2,1)S(1)}, bf16[128,1024]{1,0:T(8,128)(2,1)}, u32[]{:S(2)}) copy-start(bf16[128,1024]{1,0:T(8,128)(2,1)} %get-tuple-element.27.xa_ref.xa0_ref) | copy-start | bytes 786436
  30.4 15.0 %copy-start.2 = (bf16[8,64,128]{2,1,0:T(8,128)(2,1)S(1)}, bf16[8,64,128]{2,1,0:T(8,128)(2,1)}, u32[]{:S(2)}) copy-start(bf16[8,64,128]{2,1,0:T(8,128)(2,1)} %get-tuple-element.29.y_ref) | copy-start | bytes 393220
  31.6 0.7 %copy-start.4 = (f32[1,1024]{1,0:T(1,128)S(1)}, f32[1,1024]{1,0:T(1,128)}, u32[]{:S(2)}) copy-start(f32[1,1024]{1,0:T(1,128)} %get-tuple-element.28.mx_ref) | copy-start | bytes 12292
  33.8 1.4 %collective-permute-start.2 = (bf16[528,128]{1,0:T(8,128)(2,1)S(1)}, bf16[528,128]{1,0:T(8,128)(2,1)S(1)}, u32[]{:S(2)}, u32[]{:S(2)}) collective-permute-start(bf16[528,128]{1,0:T(8,128)(2,1)S(1)} %get-tuple-element.46), channel_id=1, source_target_pairs={{0,1},{1,0},{2,3},{3,2},{4,5},{5,4},{6,7},{7,6},{8,9},{9,8},{10,11... | collective-permute-start | bytes 405512 | tf_op jit(solution)/shard_map/ppermute | solution.py:366

commit v6 on v5

--- a/solution.py
+++ b/solution.py
@@ -43,9 +43,9 @@
     return select(index, {0: high, 1: mid, 2: low, 3: 1.0, 4: 1.0, 5: 1.0, 6: mass})
 
 
-def extras_x(index, b_term):
+def extras_x(index, b_term, mass):
     high, mid, low = pieces(b_term)
-    return select(index, {0: 1.0, 1: 1.0, 2: 1.0, 3: high, 4: mid, 5: low})
+    return select(index, {0: 1.0, 1: 1.0, 2: 1.0, 3: high, 4: mid, 5: low, 7: mass})
 
 
 def rows_index(columns):
@@ -128,28 +128,38 @@
 
 
 def prep_kernel(
-    log_ny, xt_hbm, y_hbm, mx_hbm, my_hbm, ya_ref, xa_ref, mx_ref, y_ref, my_ref, mx_in, sems
+    log_ny, xt_hbm, y_hbm, mx_hbm, my_hbm, ya_hbm, xa_hbm, y_ref, my_ref, mx_ref, ya_ref, ext_ref, sems
 ):
     width, n = xt_hbm.shape
-    pairs = ((y_hbm, y_ref), (my_hbm, my_ref), (xt_hbm, xa_ref.at[:width, :]), (mx_hbm, mx_in))
-    moves = [pltpu.make_async_copy(a, b, sems.at[k]) for k, (a, b) in enumerate(pairs)]
-    for move in moves:
+    rows = ya_hbm.shape[0]
+    move_y = pltpu.make_async_copy(y_hbm, y_ref, sems.at[0])
+    move_my = pltpu.make_async_copy(my_hbm, my_ref, sems.at[1])
+    move_mx = pltpu.make_async_copy(mx_hbm, mx_ref, sems.at[2])
+    move_x = pltpu.make_async_copy(xt_hbm, xa_hbm.at[:width, :], sems.at[3])
+    for move in (move_y, move_my, move_mx, move_x):
         move.start()
-    xa_ref[width:, :] = extras_x(rows_index(n), jnp.zeros((1, n), F32)).astype(BF16)
-    moves[0].wait()
-    moves[1].wait()
+    move_y.wait()
     y = y_ref[...]
     yf = y.astype(F32)
     norm = jnp.sum(yf * yf, axis=1, keepdims=True)
+    move_my.wait()
     mass = to_column(my_ref[...].astype(F32))
     c_term = (mass - log_ny) / kappa_of(width) - 0.5 * norm
-    ext = extras_y(lax.broadcasted_iota(jnp.int32, (y.shape[0], EXT), 1), c_term, mass).astype(BF16)
-    for k in range(ya_ref.shape[0]):
-        ya_ref[k, :, :width] = y
-        ya_ref[k, :, width:] = ext
-    moves[2].wait()
-    moves[3].wait()
-    mx_ref[...] = from_lanes(mx_in[...].astype(F32))
+    index = lax.broadcasted_iota(jnp.int32, (y.shape[0], EXT), 1)
+    ya_ref[:, :width] = y
+    ya_ref[:, width:] = extras_y(index, c_term, mass).astype(BF16)
+    moves = [pltpu.make_async_copy(ya_ref, ya_hbm.at[k], sems.at[5 + k]) for k in range(rows)]
+    for move in moves:
+        move.start()
+    move_mx.wait()
+    mass = from_lanes(mx_ref[...].astype(F32))
+    ext_ref[...] = extras_x(rows_index(n), jnp.zeros((1, n), F32), mass).astype(BF16)
+    move_ext = pltpu.make_async_copy(ext_ref, xa_hbm.at[width:, :], sems.at[4])
+    move_ext.start()
+    for move in moves:
+        move.wait()
+    move_x.wait()
+    move_ext.wait()
 
 
 def half_kernel(xa_ref, mine_ref, peak_ref, total_ref, z_ref):
@@ -168,11 +178,11 @@
 
 
 def first_kernel(
-    log_nx, xa0_ref, mx_ref, mine_ref, other_ref, peak_ref, total_ref,
+    log_nx, xa0_ref, mine_ref, other_ref, peak_ref, total_ref,
     ya_ref, b_ref, l_ref, m_ref, rows_ref, xa_ref, z_ref, zc_ref, b2_ref,
 ):
     rows, yd, depth = mine_ref.shape
-    n = mx_ref.shape[1]
+    n = xa0_ref.shape[1]
     width = depth - EXT
     half = rows * yd
     ny = 2 * half
@@ -190,10 +200,11 @@
         b_ref[:, t] = -peak - jnp.log(total) * (LOG2E / scale)
 
     for_tiles(n, row_tile)
-    b_term = b_ref[...] + (mx_ref[...] - log_nx) * (LOG2E / scale)
+    mass = xa0_ref[width:, :].astype(F32)[7:8]
+    b_term = b_ref[...] + (mass - log_nx) * (LOG2E / scale)
     b_ref[...] = b_term
     xa_ref[:width, :] = xa0_ref[:width, :]
-    xa_ref[width:, :] = extras_x(rows_index(n), b_term).astype(BF16)
+    xa_ref[width:, :] = extras_x(rows_index(n), b_term, mass).astype(BF16)
     rows_ref[...] = xa_ref[...].T
 
     def col_tile(t):
@@ -246,7 +257,7 @@
 
 
 def second_kernel(
-    log_nx, log_ny, xa_ref, mx_ref, norm_ref, b_ref, l_ref, other_ref, m_ref, yt_ref, t_ref,
+    log_nx, log_ny, xa_ref, norm_ref, b_ref, l_ref, other_ref, m_ref, yt_ref, t_ref,
     f_ref, r_ref, v_ref, c_ref, keep_ref, sum_ref, send_ref, xs_ref, gt_ref, part_ref,
 ):
     width = xa_ref.shape[0] - EXT
@@ -271,7 +282,8 @@
     rowsum = (sums[0:1] + sums[1:2]) + sums[2:3]
     log_row = jnp.log(rowsum)
     f_ref[...] = norm_ref[...] / width + EPSILON * (kappa * b_ref[...] - log_row)
-    r = jnp.exp(mx_ref[...] - log_nx - log_row)
+    mass = xa_ref[width:, :].astype(F32)[7:8]
+    r = jnp.exp(mass - log_nx - log_row)
     r_ref[...] = r
     stack(xs_ref, width, xa_ref[:width, :], r)
     totals = []
@@ -332,13 +344,21 @@
     sum_ref[...] = sums
     mass = yt_ref[width:, :].astype(F32)[6:7]
     q = v_ref[...] * jnp.exp(mass + log_nx - jnp.log(from_lanes(sums)))
-    stack(ys_ref, width, yt_ref[:width, :], q)
-    across = (((1,), (1,)), ((), ()))
+    moved = yt_ref[:width, :].astype(F32) * q
+    high = moved.astype(BF16)
+    ys_ref[:width, :] = high
+    ys_ref[LANES : LANES + width, :] = (moved - high.astype(F32)).astype(BF16)
+    one, two, three = pieces(q)
+    ys_ref[width:LANES, :] = select(rows_index(ny), {0: one, 1: two, 2: three}).astype(BF16)
+    ys_ref[LANES + width :, :] = jnp.zeros((EXT, ny), BF16)
+    right = ys_ref[...].T
     for k in range(n // TILE):
         t = slice(k * TILE, (k + 1) * TILE)
-        product = lax.dot_general(ys_ref[...], t_ref[t, :], across, preferred_element_type=F32)
-        moved, weight = unstack(product, width)
-        gx_ref[:, t] = (xa_ref[:width, t].astype(F32) * weight - moved) * (r_ref[:, t] * (1.0 / ny))
+        product = jnp.dot(t_ref[t, :], right, preferred_element_type=F32)
+        product = (product[:, :LANES] + product[:, LANES:]).T
+        ext = product[width:]
+        weight = (ext[0:1] + ext[1:2]) + ext[2:3]
+        gx_ref[:, t] = (xa_ref[:width, t].astype(F32) * weight - product[:width]) * (r_ref[:, t] * (1.0 / ny))
     colsum = own_part(sum_ref, yd)
     c_term = own_part(c_ref, yd)
     own = y_ref[0].astype(F32)
@@ -352,7 +372,7 @@
         kernel,
         out_shape=outs,
         in_specs=[pl.BlockSpec(memory_space=space)] * len(args),
-        out_specs=jax.tree.map(lambda _: pl.BlockSpec(memory_space=pltpu.VMEM), outs),
+        out_specs=jax.tree.map(lambda _: pl.BlockSpec(memory_space=space), outs),
         scratch_shapes=scratch,
         compiler_params=pltpu.CompilerParams(vmem_limit_bytes=limit),
     )(*args)
@@ -379,12 +399,12 @@
     extra = sums_rows(ny)
     run = functools.partial
     vmem = pltpu.VMEM
-    y_own, xa, mx = call(
+    y_own, xa = call(
         run(prep_kernel, log_ny),
-        (shape((rows, yd, depth), BF16), shape((depth, n), BF16), shape((1, n))),
+        (shape((rows, yd, depth), BF16), shape((depth, n), BF16)),
         [
             vmem((yd, width), BF16), vmem((1, yd), BF16), vmem((n // LANES, LANES), BF16),
-            pltpu.SemaphoreType.DMA((4,)),
+            vmem((yd, depth), BF16), vmem((EXT, n), BF16), pltpu.SemaphoreType.DMA((5 + rows,)),
         ],
         58 * 1024 * 1024,
         points_x.T, points_y, mass_x.reshape(n // LANES, LANES), mass_y.reshape(1, yd), space=pl.ANY,
@@ -401,7 +421,7 @@
             shape((n, depth), BF16),
         ),
         [vmem((depth, n), BF16), vmem((half, TILE), F32), vmem((n, TILE), F32), vmem((1, ny), F32)],
-        limit, xa, mx, y_mine, y_other, peak, total,
+        limit, xa, y_mine, y_other, peak, total,
     )
     lse = lax.all_to_all(lse, "row", 0, 0, tiled=True)
     lse_other = swap(lse)
@@ -418,7 +438,7 @@
             shape((half, depth)), shape((count, LANES)), shape((half + extra, depth), BF16),
         ),
         [vmem((2 * width + PAD, n), BF16), vmem((depth, ny), F32), vmem((ny, depth), F32)],
-        limit, xa, mx, norm, b_term, lse, lse_other, peak, yt, plan,
+        limit, xa, norm, b_term, lse, lse_other, peak, yt, plan,
     )
     part = call(
         run(add_kernel, width), shape((rows, yd * width // LANES + extra, LANES), BF16), [],
@@ -428,7 +448,7 @@
     grad_xt, grad_y, g_pot = call(
         run(last_kernel, log_nx, log_ny),
         (shape((width, n)), shape((yd, width)), shape((1, yd))),
-        [vmem((2 * width + PAD, ny), BF16), vmem((count, LANES), F32)],
+        [vmem((2 * LANES, ny), BF16), vmem((count, LANES), F32)],
         limit, xa, r, v, c_term, part, yt, plan, y_own,
     )
     return f_pot.reshape(n), g_pot.reshape(yd), grad_xt.T, grad_y

time: 47.5 us -> 51.4 us (1.082)
  Pallas kernels: 8.44 us -> 13.8 us
  local copies, waits for them, and re-layouts: 2.33 us -> 0.96 us
    pallas_call x7, Pallas kernels: 8.44 us -> 13.8 us  [call(): pl.pallas_call(kernel, out_shape=outs, in_specs=[pl.BlockSpec(memory_spac...]
    unnamed x10 -> x6, local copies, waits for them, and re-layouts: 2.33 us -> 0.96 us
where the time goes in v6:
time: 51.4 us; the launch traced here: 51 us
  blocking collectives  33.7 us (66%)
  Pallas kernels  13.8 us (27%)
  waiting for transfers between devices  1.65 us (3%)
  local copies, waits for them, and re-layouts  0.96 us (2%)
  between operations  0.68 us (1%)
    all_to_all x1, blocking collectives, on_device(): y_mine = lax.all_to_all(y_own, 'row', 0, 0, tiled=True)  14.6 us
    pallas_call x7, Pallas kernels, call(): pl.pallas_call(kernel, out_shape=outs, in_specs=[pl.BlockSpec(memory_spac...  13.8 us
    all_to_all x1, blocking collectives, on_device(): part = lax.all_to_all(part, 'row', 0, 0, tiled=True)  9.99 us
    all_to_all x1, blocking collectives, on_device(): lse = lax.all_to_all(lse, 'row', 0, 0, tiled=True)  9.06 us
    ppermute x3, waiting for transfers between devices, swap(): return lax.ppermute(value, 'col', [(0, 1), (1, 0)])  1.65 us
  transfers between devices with their start and end apart: 3, of which 2 were waited for; matrix products, arithmetic and copies ran while one was open for 0% of the time, Pallas kernels for 3%

profile of v6, /device:TPU:0, one launch (start us, length us, event | category | flops | bytes accessed | tf_op | source)
XLA Modules:
  0.0 51.0 jit_solution(7881975226942363155)
XLA Ops:
  0.6 7.2 %shard_map.75 = (bf16[8,64,128]{2,1,0:T(8,128)(2,1)}, bf16[128,1024]{1,0:T(8,128)(2,1)}) custom-call(bf16[96,1024]{1,0:T(8,128)(2,1)} %bitcast.6, bf16[64,96]{1,0:T(8,128)(2,1)} %y_hbm.1, bf16[8,128]{1,0:T(8,128)(2,1)} %bitcast.7, bf16[1,64]{1,0:T(2,128)(2,1)} %bitcast.8), custom_call_target="tpu_custom_call" | custom-call | tf_op jit(solution)/shard_map/pallas_call | solution.py:371
  7.8 14.6 %all_to_all.15.mine_ref = bf16[8,64,128]{2,1,0:T(8,128)(2,1)S(1)} all-to-all(bf16[8,64,128]{2,1,0:T(8,128)(2,1)} %get-tuple-element.27.y_ref), channel_id=1, replica_groups=mesh['groups'=2,'row'=8,'col'=2] {'row'}, dimensions={0} | all-to-all | bytes 262144 | tf_op jit(solution)/shard_map/all_to_all | solution.py:412
  22.4 0.0 collective-permute-start
  22.5 0.0 copy-start
  22.5 0.9 %copy-done = bf16[128,1024]{1,0:T(8,128)(2,1)S(1)} copy-done((bf16[128,1024]{1,0:T(8,128)(2,1)S(1)}, bf16[128,1024]{1,0:T(8,128)(2,1)}, u32[]{:S(2)}) %copy-start) | copy-done | bytes 262168
  23.4 0.7 %shard_map.76 = (f32[1,1024]{1,0:T(1,128)S(1)}, f32[1,1024]{1,0:T(1,128)S(1)}) custom-call(bf16[128,1024]{1,0:T(8,128)(2,1)S(1)} %copy-done, bf16[8,64,128]{2,1,0:T(8,128)(2,1)S(1)} %all_to_all.15.mine_ref), custom_call_target="tpu_custom_call" | custom-call | tf_op jit(solution)/shard_map/pallas_call | solution.py:371
  24.1 0.0 collective-permute-done.other_ref
  24.1 2.0 %shard_map.77 = (bf16[1024,128]{1,0:T(8,128)(2,1)S(1)}, f32[1,1024]{1,0:T(1,128)S(1)}, f32[8,8,128]{2,1,0:T(8,128)S(1)}, f32[1,1024]{1,0:T(1,128)S(1)}, bf16[1024,128]{1,0:T(8,128)(2,1)S(1)}) custom-call(bf16[128,1024]{1,0:T(8,128)(2,1)S(1)} %copy-done, bf16[8,64,128]{2,1,0:T(8,128)(2,1)S(1)} %all_to_all.15.mine_ref, ...), custom_call_target="tpu_custom_call" | custom-call | tf_op jit(solution)/shard_map/pallas_call | solution.py:371
  26.1 9.1 %all_to_all.16.l_ref = f32[8,8,128]{2,1,0:T(8,128)S(1)} all-to-all(f32[8,8,128]{2,1,0:T(8,128)S(1)} %get-tuple-element.35), channel_id=1, replica_groups=mesh['groups'=2,'row'=8,'col'=2] {'row'}, dimensions={0} | all-to-all | bytes 65536 | tf_op jit(solution)/shard_map/all_to_all | solution.py:426
  35.1 0.0 collective-permute-start.1
  35.1 0.0 copy-start.1
  35.1 0.0 copy-start.2
  35.1 0.7 %shard_map.78 = (bf16[1024,1024]{1,0:T(8,128)(2,1)S(1)}, bf16[128,1024]{1,0:T(8,128)(2,1)S(1)}, f32[1,1024]{1,0:T(1,128)S(1)}) custom-call(bf16[128,1024]{1,0:T(8,128)(2,1)S(1)} %copy-done, bf16[1024,128]{1,0:T(8,128)(2,1)S(1)} %get-tuple-element.30.rows_ref, bf16[1024,128]{1,0:T(8,128)(2,1)S(1)} %get-tuple-element.31.ya_ref, ...), custom_call_target="tpu_custom_call" | custom-call | tf_op jit(solution)/shard_map/pallas_call | solution.py:371
  35.9 0.5 collective-permute-done.1.other_ref
  36.3 1.4 %shard_map.79 = (f32[1,1024]{1,0:T(1,128)}, f32[1,1024]{1,0:T(1,128)S(1)}, f32[1,1024]{1,0:T(1,128)S(1)}, f32[8,128]{1,0:T(8,128)S(1)}, f32[512,128]{1,0:T(8,128...) custom-call(bf16[128,1024]{1,0:T(8,128)(2,1)S(1)} %copy-done, f32[1,1024]{1,0:T(1,128)S(1)} %get-tuple-element.33.norm_ref, ...), custom_call_target="tpu_custom_call" | custom-call | tf_op jit(solution)/shard_map/pallas_call | solution.py:371
  37.7 0.2 collective-permute-start.2
  38.0 1.2 %collective-permute-done.2.got_ref = bf16[528,128]{1,0:T(8,128)(2,1)S(1)} collective-permute-done((bf16[528,128]{1,0:T(8,128)(2,1)S(1)}, bf16[528,128]{1,0:T(8,128)(2,1)S(1)}, u32[]{:S(2)}, u32[]{:S(2)}) %collective-permute-start.2) | collective-permute-done | bytes 135200 | tf_op jit(solution)/shard_map/ppermute | solution.py:386
  39.1 0.2 shard_map.80
  39.3 10.0 %all_to_all.17.got_ref = bf16[8,64,128]{2,1,0:T(8,128)(2,1)S(1)} all-to-all(bf16[8,64,128]{2,1,0:T(8,128)(2,1)S(1)} %shard_map.80), channel_id=1, replica_groups=mesh['groups'=2,'row'=8,'col'=2] {'row'}, dimensions={0} | all-to-all | bytes 262144 | tf_op jit(solution)/shard_map/all_to_all | solution.py:447
  49.3 0.0 copy-done.1
  49.3 0.0 copy-done.2
  49.3 1.7 %shard_map.81 = (f32[96,1024]{1,0:T(8,128)}, f32[64,96]{1,0:T(8,128)}, f32[1,64]{1,0:T(1,128)}) custom-call(bf16[128,1024]{1,0:T(8,128)(2,1)S(1)} %copy-done.1, f32[1,1024]{1,0:T(1,128)S(1)} %get-tuple-element.39.r_ref, f32[1,1024]{1,0:T(1,128)S(1)} %get-tuple-element.40.v_ref, f32[8,128]{1,0:T(8,128)S(1)} %get-tuple-element.41.c_ref, ...), custom_call_target="tpu_custom_call" | custom-call | tf_op jit(solution)/shard_map/pallas_call | solution.py:371
Async XLA Ops:
  22.4 1.6 %collective-permute-start = (bf16[8,64,128]{2,1,0:T(8,128)(2,1)S(1)}, bf16[8,64,128]{2,1,0:T(8,128)(2,1)S(1)}, u32[]{:S(2)}, u32[]{:S(2)}) collective-permute-start(bf16[8,64,128]{2,1,0:T(8,128)(2,1)S(1)} %all_to_all.15.mine_ref), channel_id=1, source_target_pairs={{0,1},{1,0},{2,3},{3,2},{4,5},{5,4},{6,7},{7,6},{8,9},{9,8},{10,11... | collective-permute-start | bytes 393224 | tf_op jit(solution)/shard_map/ppermute | solution.py:386
  22.5 1.0 %copy-start = (bf16[128,1024]{1,0:T(8,128)(2,1)S(1)}, bf16[128,1024]{1,0:T(8,128)(2,1)}, u32[]{:S(2)}) copy-start(bf16[128,1024]{1,0:T(8,128)(2,1)} %get-tuple-element.26.xa_ref.xa0_ref) | copy-start | bytes 786436
  35.1 1.2 %collective-permute-start.1 = (f32[8,8,128]{2,1,0:T(8,128)S(1)}, f32[8,8,128]{2,1,0:T(8,128)S(1)}, u32[]{:S(2)}, u32[]{:S(2)}) collective-permute-start(f32[8,8,128]{2,1,0:T(8,128)S(1)} %all_to_all.16.l_ref), channel_id=1, source_target_pairs={{0,1},{1,0},{2,3},{3,2},{4,5},{5,4},{6,7},{7,6},{8,9},{9,8},{10,11... | collective-permute-start | bytes 98312 | tf_op jit(solution)/shard_map/ppermute | solution.py:386
  35.1 14.2 %copy-start.1 = (bf16[128,1024]{1,0:T(8,128)(2,1)S(1)}, bf16[128,1024]{1,0:T(8,128)(2,1)}, u32[]{:S(2)}) copy-start(bf16[128,1024]{1,0:T(8,128)(2,1)} %get-tuple-element.26.xa_ref.xa0_ref) | copy-start | bytes 786436
  35.1 14.2 %copy-start.2 = (bf16[8,64,128]{2,1,0:T(8,128)(2,1)S(1)}, bf16[8,64,128]{2,1,0:T(8,128)(2,1)}, u32[]{:S(2)}) copy-start(bf16[8,64,128]{2,1,0:T(8,128)(2,1)} %get-tuple-element.27.y_ref) | copy-start | bytes 393220
  37.7 1.4 %collective-permute-start.2 = (bf16[528,128]{1,0:T(8,128)(2,1)S(1)}, bf16[528,128]{1,0:T(8,128)(2,1)S(1)}, u32[]{:S(2)}, u32[]{:S(2)}) collective-permute-start(bf16[528,128]{1,0:T(8,128)(2,1)S(1)} %get-tuple-element.44), channel_id=1, source_target_pairs={{0,1},{1,0},{2,3},{3,2},{4,5},{5,4},{6,7},{7,6},{8,9},{9,8},{10,11... | collective-permute-start | bytes 405512 | tf_op jit(solution)/shard_map/ppermute | solution.py:386

commit v7 on v6

--- a/solution.py
+++ b/solution.py
@@ -108,10 +108,6 @@
     return jnp.concatenate([high, sums - high] + [jnp.zeros((spare, LANES), F32)] * (spare > 0), axis=0)
 
 
-def sums_in(ext, count):
-    return ext[:count] + ext[count : 2 * count]
-
-
 def pack(block):
     rows, width = block.shape
     base = rows * width // LANES
@@ -128,15 +124,15 @@
 
 
 def prep_kernel(
-    log_ny, xt_hbm, y_hbm, mx_hbm, my_hbm, ya_hbm, xa_hbm, y_ref, my_ref, mx_ref, ya_ref, ext_ref, sems
+    log_ny, xt_hbm, y_hbm, mx_hbm, my_hbm, ya_hbm, xa_hbm, y_ref, my_ref, mx_ref, ya_ref, xa_ref, sems
 ):
     width, n = xt_hbm.shape
     rows = ya_hbm.shape[0]
     move_y = pltpu.make_async_copy(y_hbm, y_ref, sems.at[0])
     move_my = pltpu.make_async_copy(my_hbm, my_ref, sems.at[1])
     move_mx = pltpu.make_async_copy(mx_hbm, mx_ref, sems.at[2])
-    move_x = pltpu.make_async_copy(xt_hbm, xa_hbm.at[:width, :], sems.at[3])
-    for move in (move_y, move_my, move_mx, move_x):
+    move_x = pltpu.make_async_copy(xt_hbm, xa_ref.at[:width, :], sems.at[3])
+    for move in (move_y, move_my, move_x, move_mx):
         move.start()
     move_y.wait()
     y = y_ref[...]
@@ -153,13 +149,13 @@
         move.start()
     move_mx.wait()
     mass = from_lanes(mx_ref[...].astype(F32))
-    ext_ref[...] = extras_x(rows_index(n), jnp.zeros((1, n), F32), mass).astype(BF16)
-    move_ext = pltpu.make_async_copy(ext_ref, xa_hbm.at[width:, :], sems.at[4])
-    move_ext.start()
+    xa_ref[width:, :] = extras_x(rows_index(n), jnp.zeros((1, n), F32), mass).astype(BF16)
+    move_x.wait()
+    move_out = pltpu.make_async_copy(xa_ref, xa_hbm, sems.at[4])
+    move_out.start()
     for move in moves:
         move.wait()
-    move_x.wait()
-    move_ext.wait()
+    move_out.wait()
 
 
 def half_kernel(xa_ref, mine_ref, peak_ref, total_ref, z_ref):
@@ -257,11 +253,12 @@
 
 
 def second_kernel(
-    log_nx, log_ny, xa_ref, norm_ref, b_ref, l_ref, other_ref, m_ref, yt_ref, t_ref,
-    f_ref, r_ref, v_ref, c_ref, keep_ref, sum_ref, send_ref, xs_ref, gt_ref, part_ref,
+    log_nx, log_ny, xa_ref, b_ref, l_ref, other_ref, m_ref, yt_ref, t_ref,
+    r_ref, v_ref, c_ref, xs_ref, sum_ref, send_ref,
 ):
     width = xa_ref.shape[0] - EXT
     ny = m_ref.shape[1]
+    half = ny // 2
     kappa = kappa_of(width)
     scale = kappa * LOG2E
     l_mine, l_other = l_ref[...], other_ref[...]
@@ -280,42 +277,52 @@
     across = (((1,), (1,)), ((), ()))
     sums = lax.dot_general(v_rows, t_ref[...], across, preferred_element_type=F32)
     rowsum = (sums[0:1] + sums[1:2]) + sums[2:3]
-    log_row = jnp.log(rowsum)
-    f_ref[...] = norm_ref[...] / width + EPSILON * (kappa * b_ref[...] - log_row)
     mass = xa_ref[width:, :].astype(F32)[7:8]
-    r = jnp.exp(mass - log_nx - log_row)
+    r = jnp.exp(mass - log_nx) / rowsum
     r_ref[...] = r
     stack(xs_ref, width, xa_ref[:width, :], r)
-    totals = []
-    for k in range(ny // TILE):
-        t = slice(k * TILE, (k + 1) * TILE)
+    col = lax.axis_index("col")
+    for k in range(half // TILE):
+        t = pl.ds(pl.multiple_of((1 - col) * half + k * TILE, TILE), TILE)
         product = jnp.dot(xs_ref[...], t_ref[:, t], preferred_element_type=F32)
         moment, total = unstack(product, width)
-        total = total * v[:, t]
-        totals.append(total)
-        gt_ref[:width, t] = yt_ref[:width, t].astype(F32) * total - moment * v[:, t]
-    gt_ref[width:, :] = jnp.zeros((EXT, ny), F32)
-    part_ref[...] = gt_ref[...].T
-    sums = to_lanes(jnp.concatenate(totals, axis=1))
-    sum_ref[...] = sums
+        total = total * v_ref[:, t]
+        sum_ref[:, t] = total
+        part = yt_ref[:width, t].astype(F32) * total - moment * v_ref[:, t]
+        send_ref[:width, k * TILE : (k + 1) * TILE] = part.astype(BF16)
+        t = pl.ds(pl.multiple_of(col * half + k * TILE, TILE), TILE)
+        ext = jnp.dot(xs_ref[2 * width :, :], t_ref[:, t], preferred_element_type=F32)
+        sum_ref[:, t] = ((ext[0:1] + ext[1:2]) + ext[2:3]) * v_ref[:, t]
+    sums = sum_ref[...]
+    high = sums.astype(BF16).astype(F32)
+    low = sums - high
+    index = lax.broadcasted_iota(jnp.int32, (PAD, half), 0)
+    ext = select(index, {0: high[:, :half], 1: high[:, half:], 2: low[:, :half], 3: low[:, half:]})
+    send_ref[width:, :] = ext.astype(BF16)
+
+
+def keep_kernel(xs_ref, v_ref, sum_ref, yt_ref, t_ref, keep_ref):
+    width, half = keep_ref.shape
     col = lax.axis_index("col")
-    half = keep_ref.shape[0]
-    keep_ref[...] = part_ref[pl.ds(pl.multiple_of(col * half, half), half), :]
-    send_ref[:half, :] = part_ref[pl.ds(pl.multiple_of((1 - col) * half, half), half), :].astype(BF16)
-    send_ref[half:, :] = sums_out(sums).astype(BF16)
-
-
-def add_kernel(width, keep_ref, sum_ref, got_ref, out_ref):
-    half = keep_ref.shape[0]
+    for k in range(half // TILE):
+        t = pl.ds(pl.multiple_of(col * half + k * TILE, TILE), TILE)
+        product = jnp.dot(xs_ref[: 2 * width, :], t_ref[:, t], preferred_element_type=F32)
+        moment = product[:width] + product[width:]
+        part = yt_ref[:width, t].astype(F32) * sum_ref[:, t] - moment * v_ref[:, t]
+        keep_ref[:, k * TILE : (k + 1) * TILE] = part
+
+
+def add_kernel(keep_ref, sum_ref, got_ref, out_ref):
+    width, half = keep_ref.shape
     rows = out_ref.shape[0]
     yd = half // rows
     base = yd * width // LANES
-    count = sum_ref.shape[0]
-    sums = sums_out(sum_ref[...] + sums_in(got_ref[half:, :].astype(F32), count)).astype(BF16)
+    ext = got_ref[width:, :].astype(F32)
+    other = jnp.concatenate([ext[0:1] + ext[2:3], ext[1:2] + ext[3:4]], axis=1)
+    sums = sums_out(to_lanes(sum_ref[...] + other)).astype(BF16)
+    total = (keep_ref[...] + got_ref[:width, :].astype(F32)).T
     for r in range(rows):
-        part = slice(r * yd, (r + 1) * yd)
-        total = keep_ref[part, :] + got_ref[part, :].astype(F32)
-        out_ref[r, :base, :] = pack(total[:, :width]).astype(BF16)
+        out_ref[r, :base, :] = pack(total[r * yd : (r + 1) * yd, :]).astype(BF16)
         out_ref[r, base:, :] = sums
 
 
@@ -330,49 +337,61 @@
 
 
 def last_kernel(
-    log_nx, log_ny, xa_ref, r_ref, v_ref, c_ref, got_ref, yt_ref, t_ref, y_ref,
-    gx_ref, gy_ref, pot_ref, ys_ref, sum_ref,
+    log_nx, log_ny, xa_ref, norm_ref, b_ref, r_ref, v_ref, c_ref, got_ref, yt_ref, t_ref, y_ref,
+    f_hbm, pot_hbm, gx_hbm, gy_hbm, f_ref, pot_ref, gx_ref, gy_ref, ys_ref, sum_ref, sems,
 ):
     width, n = gx_ref.shape
     ny = v_ref.shape[1]
     yd = y_ref.shape[1]
     base = yd * width // LANES
+    count = ny // LANES
+    kappa = kappa_of(width)
+    moves = []
+
+    def leave(source, target):
+        move = pltpu.make_async_copy(source, target, sems.at[len(moves)])
+        move.start()
+        moves.append(move)
+
+    mass = xa_ref[width:, :].astype(F32)[7:8]
+    log_row = mass - log_nx - jnp.log(r_ref[...])
+    f_ref[...] = norm_ref[...] / width + EPSILON * (kappa * b_ref[...] - log_row)
+    leave(f_ref, f_hbm)
     total = got_ref[0].astype(F32)
     for k in range(1, got_ref.shape[0]):
         total = total + got_ref[k].astype(F32)
-    sums = sums_in(total[base:], ny // LANES)
+    sums = total[base : base + count] + total[base + count : base + 2 * count]
     sum_ref[...] = sums
-    mass = yt_ref[width:, :].astype(F32)[6:7]
-    q = v_ref[...] * jnp.exp(mass + log_nx - jnp.log(from_lanes(sums)))
-    moved = yt_ref[:width, :].astype(F32) * q
-    high = moved.astype(BF16)
-    ys_ref[:width, :] = high
-    ys_ref[LANES : LANES + width, :] = (moved - high.astype(F32)).astype(BF16)
-    one, two, three = pieces(q)
-    ys_ref[width:LANES, :] = select(rows_index(ny), {0: one, 1: two, 2: three}).astype(BF16)
-    ys_ref[LANES + width :, :] = jnp.zeros((EXT, ny), BF16)
-    right = ys_ref[...].T
-    for k in range(n // TILE):
-        t = slice(k * TILE, (k + 1) * TILE)
-        product = jnp.dot(t_ref[t, :], right, preferred_element_type=F32)
-        product = (product[:, :LANES] + product[:, LANES:]).T
-        ext = product[width:]
-        weight = (ext[0:1] + ext[1:2]) + ext[2:3]
-        gx_ref[:, t] = (xa_ref[:width, t].astype(F32) * weight - product[:width]) * (r_ref[:, t] * (1.0 / ny))
     colsum = own_part(sum_ref, yd)
     c_term = own_part(c_ref, yd)
     own = y_ref[0].astype(F32)
-    gy_ref[...] = unpack(total[:base], yd, width) * (jnp.exp(own[:, width + 6 : width + 7]) * to_column(1.0 / colsum))
+    gy_ref[...] = unpack(total[:base], yd, width) * (
+        jnp.exp(own[:, width + 6 : width + 7]) * to_column(1.0 / colsum)
+    )
+    leave(gy_ref, gy_hbm)
     norm = to_row(jnp.sum(own[:, :width] * own[:, :width], axis=1, keepdims=True))
-    pot_ref[...] = norm / width - EPSILON * (jnp.log(colsum) - kappa_of(width) * c_term)
-
-
-def call(kernel, outs, scratch, limit, *args, space=pltpu.VMEM):
+    pot_ref[...] = norm / width - EPSILON * (jnp.log(colsum) - kappa * c_term)
+    leave(pot_ref, pot_hbm)
+    mass = yt_ref[width:, :].astype(F32)[6:7]
+    q = v_ref[...] * jnp.exp(mass + log_nx - jnp.log(from_lanes(sums)))
+    stack(ys_ref, width, yt_ref[:width, :], q)
+    across = (((1,), (1,)), ((), ()))
+    for k in range(n // TILE):
+        t = slice(k * TILE, (k + 1) * TILE)
+        product = lax.dot_general(ys_ref[...], t_ref[t, :], across, preferred_element_type=F32)
+        moved, weight = unstack(product, width)
+        gx_ref[:, t] = (xa_ref[:width, t].astype(F32) * weight - moved) * (r_ref[:, t] * (1.0 / ny))
+        leave(gx_ref.at[:, t], gx_hbm.at[:, t])
+    for move in moves:
+        move.wait()
+
+
+def call(kernel, outs, scratch, limit, *args, space=pltpu.VMEM, out_space=pltpu.VMEM):
     return pl.pallas_call(
         kernel,
         out_shape=outs,
         in_specs=[pl.BlockSpec(memory_space=space)] * len(args),
-        out_specs=jax.tree.map(lambda _: pl.BlockSpec(memory_space=space), outs),
+        out_specs=jax.tree.map(lambda _: pl.BlockSpec(memory_space=out_space), outs),
         scratch_shapes=scratch,
         compiler_params=pltpu.CompilerParams(vmem_limit_bytes=limit),
     )(*args)
@@ -404,10 +423,10 @@
         (shape((rows, yd, depth), BF16), shape((depth, n), BF16)),
         [
             vmem((yd, width), BF16), vmem((1, yd), BF16), vmem((n // LANES, LANES), BF16),
-            vmem((yd, depth), BF16), vmem((EXT, n), BF16), pltpu.SemaphoreType.DMA((5 + rows,)),
+            vmem((yd, depth), BF16), vmem((depth, n), BF16), pltpu.SemaphoreType.DMA((5 + rows,)),
         ],
         58 * 1024 * 1024,
-        points_x.T, points_y, mass_x.reshape(n // LANES, LANES), mass_y.reshape(1, yd), space=pl.ANY,
+        points_x.T, points_y, mass_x.reshape(n // LANES, LANES), mass_y.reshape(1, yd), space=pl.ANY, out_space=pl.ANY,
     )
     y_mine = lax.all_to_all(y_own, "row", 0, 0, tiled=True)
     y_other = swap(y_mine)
@@ -431,25 +450,29 @@
         [vmem((n, TILE), F32)],
         limit, xa, x_rows, ya, peak,
     )
-    f_pot, r, v, c_term, keep, sums, send = call(
+    r, v, c_term, xs, sums, send = call(
         run(second_kernel, log_nx, log_ny),
         (
-            shape((1, n)), shape((1, n)), shape((1, ny)), shape((count, LANES)),
-            shape((half, depth)), shape((count, LANES)), shape((half + extra, depth), BF16),
+            shape((1, n)), shape((1, ny)), shape((count, LANES)), shape((2 * width + PAD, n), BF16),
+            shape((1, ny)), shape((width + PAD, half), BF16),
         ),
-        [vmem((2 * width + PAD, n), BF16), vmem((depth, ny), F32), vmem((ny, depth), F32)],
-        limit, xa, norm, b_term, lse, lse_other, peak, yt, plan,
-    )
+        [], limit, xa, b_term, lse, lse_other, peak, yt, plan,
+    )
+    got = swap(send)
+    keep = call(keep_kernel, shape((width, half)), [], limit, xs, v, sums, yt, plan)
     part = call(
-        run(add_kernel, width), shape((rows, yd * width // LANES + extra, LANES), BF16), [],
-        limit, keep, sums, swap(send),
+        add_kernel, shape((rows, yd * width // LANES + extra, LANES), BF16), [], limit, keep, sums, got
     )
     part = lax.all_to_all(part, "row", 0, 0, tiled=True)
-    grad_xt, grad_y, g_pot = call(
+    f_pot, g_pot, grad_xt, grad_y = call(
         run(last_kernel, log_nx, log_ny),
-        (shape((width, n)), shape((yd, width)), shape((1, yd))),
-        [vmem((2 * LANES, ny), BF16), vmem((count, LANES), F32)],
-        limit, xa, r, v, c_term, part, yt, plan, y_own,
+        (shape((1, n)), shape((1, yd)), shape((width, n)), shape((yd, width))),
+        [
+            vmem((1, n), F32), vmem((1, yd), F32), vmem((width, n), F32), vmem((yd, width), F32),
+            vmem((2 * width + PAD, ny), BF16), vmem((count, LANES), F32),
+            pltpu.SemaphoreType.DMA((3 + n // TILE,)),
+        ],
+        limit, xa, norm, b_term, r, v, c_term, part, yt, plan, y_own, out_space=pl.ANY,
     )
     return f_pot.reshape(n), g_pot.reshape(yd), grad_xt.T, grad_y
 

time: 51.4 us -> 45.8 us (0.89)
  Pallas kernels: 13.8 us -> 8.64 us
    pallas_call x7 -> x8, Pallas kernels: 13.8 us -> 8.64 us  [call(): pl.pallas_call(kernel, out_shape=outs, in_specs=[pl.BlockSpec(memory_spac...]
  transfers between devices with their start and end apart: 3 -> 3, of which waited for: 2 -> 2; matrix products, arithmetic and copies ran while one was open for 0% -> 0% of each run, Pallas kernels for 3% -> 4%
where the time goes in v7:
time: 45.8 us; the launch traced here: 45.4 us
  blocking collectives  33.7 us (74%)
  Pallas kernels  8.64 us (19%)
  waiting for transfers between devices  1.23 us (3%)
  local copies, waits for them, and re-layouts  0.96 us (2%)
  between operations  0.71 us (2%)
    all_to_all x1, blocking collectives, on_device(): y_mine = lax.all_to_all(y_own, 'row', 0, 0, tiled=True)  14.6 us
    all_to_all x1, blocking collectives, on_device(): part = lax.all_to_all(part, 'row', 0, 0, tiled=True)  9.98 us
    all_to_all x1, blocking collectives, on_device(): lse = lax.all_to_all(lse, 'row', 0, 0, tiled=True)  9.06 us
    pallas_call x8, Pallas kernels, call(): pl.pallas_call(kernel, out_shape=outs, in_specs=[pl.BlockSpec(memory_spac...  8.64 us
    ppermute x3, waiting for transfers between devices, swap(): return lax.ppermute(value, 'col', [(0, 1), (1, 0)])  1.23 us
    unnamed x6, local copies, waits for them, and re-layouts  0.96 us
  transfers between devices with their start and end apart: 3, of which 2 were waited for; matrix products, arithmetic and copies ran while one was open for 0% of the time, Pallas kernels for 4%

profile of v7, /device:TPU:0, one launch (start us, length us, event | category | flops | bytes accessed | tf_op | source)
XLA Modules:
  0.0 45.4 jit_solution(17172170117542859302)
XLA Ops:
  0.6 1.8 %shard_map.75 = (bf16[8,64,128]{2,1,0:T(8,128)(2,1)}, bf16[128,1024]{1,0:T(8,128)(2,1)}) custom-call(bf16[96,1024]{1,0:T(8,128)(2,1)} %bitcast.6, bf16[64,96]{1,0:T(8,128)(2,1)} %y_hbm.1, bf16[8,128]{1,0:T(8,128)(2,1)} %bitcast.7, bf16[1,64]{1,0:T(2,128)(2,1)} %bitcast.8), custom_call_target="tpu_custom_call" | custom-call | tf_op jit(solution)/shard_map/pallas_call | solution.py:390
  2.5 14.6 %all_to_all.15.mine_ref = bf16[8,64,128]{2,1,0:T(8,128)(2,1)S(1)} all-to-all(bf16[8,64,128]{2,1,0:T(8,128)(2,1)} %get-tuple-element.27.y_ref), channel_id=1, replica_groups=mesh['groups'=2,'row'=8,'col'=2] {'row'}, dimensions={0} | all-to-all | bytes 262144 | tf_op jit(solution)/shard_map/all_to_all | solution.py:431
  17.1 0.0 collective-permute-start
  17.1 0.0 copy-start
  17.1 0.9 %copy-done = bf16[128,1024]{1,0:T(8,128)(2,1)S(1)} copy-done((bf16[128,1024]{1,0:T(8,128)(2,1)S(1)}, bf16[128,1024]{1,0:T(8,128)(2,1)}, u32[]{:S(2)}) %copy-start) | copy-done | bytes 262168
  18.1 0.7 %shard_map.76 = (f32[1,1024]{1,0:T(1,128)S(1)}, f32[1,1024]{1,0:T(1,128)S(1)}) custom-call(bf16[128,1024]{1,0:T(8,128)(2,1)S(1)} %copy-done, bf16[8,64,128]{2,1,0:T(8,128)(2,1)S(1)} %all_to_all.15.mine_ref), custom_call_target="tpu_custom_call" | custom-call | tf_op jit(solution)/shard_map/pallas_call | solution.py:390
  18.7 0.0 collective-permute-done.other_ref
  18.7 2.0 %shard_map.77 = (bf16[1024,128]{1,0:T(8,128)(2,1)S(1)}, f32[1,1024]{1,0:T(1,128)S(1)}, f32[8,8,128]{2,1,0:T(8,128)S(1)}, f32[1,1024]{1,0:T(1,128)S(1)}, bf16[1024,128]{1,0:T(8,128)(2,1)S(1)}) custom-call(bf16[128,1024]{1,0:T(8,128)(2,1)S(1)} %copy-done, bf16[8,64,128]{2,1,0:T(8,128)(2,1)S(1)} %all_to_all.15.mine_ref, ...), custom_call_target="tpu_custom_call" | custom-call | tf_op jit(solution)/shard_map/pallas_call | solution.py:390
  20.7 9.1 %all_to_all.16.l_ref = f32[8,8,128]{2,1,0:T(8,128)S(1)} all-to-all(f32[8,8,128]{2,1,0:T(8,128)S(1)} %get-tuple-element.35), channel_id=1, replica_groups=mesh['groups'=2,'row'=8,'col'=2] {'row'}, dimensions={0} | all-to-all | bytes 65536 | tf_op jit(solution)/shard_map/all_to_all | solution.py:445
  29.8 0.0 collective-permute-start.1
  29.8 0.7 %shard_map.78 = (bf16[1024,1024]{1,0:T(8,128)(2,1)S(1)}, bf16[128,1024]{1,0:T(8,128)(2,1)S(1)}, f32[1,1024]{1,0:T(1,128)S(1)}) custom-call(bf16[128,1024]{1,0:T(8,128)(2,1)S(1)} %copy-done, bf16[1024,128]{1,0:T(8,128)(2,1)S(1)} %get-tuple-element.30.rows_ref, bf16[1024,128]{1,0:T(8,128)(2,1)S(1)} %get-tuple-element.31.ya_ref, ...), custom_call_target="tpu_custom_call" | custom-call | tf_op jit(solution)/shard_map/pallas_call | solution.py:390
  30.5 0.5 %collective-permute-done.1.other_ref = f32[8,8,128]{2,1,0:T(8,128)S(1)} collective-permute-done((f32[8,8,128]{2,1,0:T(8,128)S(1)}, f32[8,8,128]{2,1,0:T(8,128)S(1)}, u32[]{:S(2)}, u32[]{:S(2)}) %collective-permute-start.1) | collective-permute-done | bytes 32800 | tf_op jit(solution)/shard_map/ppermute | solution.py:405
  31.0 1.2 %shard_map.79 = (f32[1,1024]{1,0:T(1,128)S(1)}, f32[1,1024]{1,0:T(1,128)S(1)}, f32[8,128]{1,0:T(8,128)S(1)}, bf16[208,1024]{1,0:T(8,128)(2,1)S(1)}, f32[1,1024]{1,0:T(1,128)S(1)}, /*index=5*/bf16[112,512]{1,0:T(8,128)(2,1)S(1)}) custom-call(bf16[128,1024]{1,0:T(8,128)(2,1)S(1)} %copy-done, f32[1,1024]{1,0:T(1,128)S(1)} %get-tuple-element.34.b_ref, ...), custom_call_target="tpu_custom_call" | custom-call | tf_op jit(solution)/shard_map/pallas_call | solution.py:390
  32.2 0.0 copy-start.1
  32.2 0.0 copy-start.2
  32.2 0.2 collective-permute-start.2
  32.4 0.4 shard_map.80.keep_ref
  32.8 0.8 %collective-permute-done.2.got_ref = bf16[112,512]{1,0:T(8,128)(2,1)S(1)} collective-permute-done((bf16[112,512]{1,0:T(8,128)(2,1)S(1)}, bf16[112,512]{1,0:T(8,128)(2,1)S(1)}, u32[]{:S(2)}, u32[]{:S(2)}) %collective-permute-start.2) | collective-permute-done | bytes 114720 | tf_op jit(solution)/shard_map/ppermute | solution.py:405
  33.6 0.3 shard_map.81
  33.8 10.0 %all_to_all.17.got_ref = bf16[8,64,128]{2,1,0:T(8,128)(2,1)S(1)} all-to-all(bf16[8,64,128]{2,1,0:T(8,128)(2,1)S(1)} %shard_map.81), channel_id=1, replica_groups=mesh['groups'=2,'row'=8,'col'=2] {'row'}, dimensions={0} | all-to-all | bytes 262144 | tf_op jit(solution)/shard_map/all_to_all | solution.py:466
  43.8 0.0 copy-done.1
  43.8 0.0 copy-done.2
  43.8 1.6 %shard_map.82 = (f32[1,1024]{1,0:T(1,128)}, f32[1,64]{1,0:T(1,128)}, f32[96,1024]{1,0:T(8,128)}, f32[64,96]{1,0:T(8,128)}) custom-call(bf16[128,1024]{1,0:T(8,128)(2,1)S(1)} %copy-done.1, f32[1,1024]{1,0:T(1,128)S(1)} %get-tuple-element.33.norm_ref, f32[1,1024]{1,0:T(1,128)S(1)} %get-tuple-element.34.b_ref, f32[1,1024]{1,0:T(1,128)S(1)} %get-tuple-element.38.r_ref, ...), custom_call_target="tpu_custom_call" | custom-call | tf_op jit(solution)/shard_map/pallas_call | solution.py:390
Async XLA Ops:
  17.1 1.6 %collective-permute-start = (bf16[8,64,128]{2,1,0:T(8,128)(2,1)S(1)}, bf16[8,64,128]{2,1,0:T(8,128)(2,1)S(1)}, u32[]{:S(2)}, u32[]{:S(2)}) collective-permute-start(bf16[8,64,128]{2,1,0:T(8,128)(2,1)S(1)} %all_to_all.15.mine_ref), channel_id=1, source_target_pairs={{0,1},{1,0},{2,3},{3,2},{4,5},{5,4},{6,7},{7,6},{8,9},{9,8},{10,11... | collective-permute-start | bytes 393224 | tf_op jit(solution)/shard_map/ppermute | solution.py:405
  17.1 1.0 %copy-start = (bf16[128,1024]{1,0:T(8,128)(2,1)S(1)}, bf16[128,1024]{1,0:T(8,128)(2,1)}, u32[]{:S(2)}) copy-start(bf16[128,1024]{1,0:T(8,128)(2,1)} %get-tuple-element.26.xa_ref.xa0_ref) | copy-start | bytes 786436
  29.8 1.2 %collective-permute-start.1 = (f32[8,8,128]{2,1,0:T(8,128)S(1)}, f32[8,8,128]{2,1,0:T(8,128)S(1)}, u32[]{:S(2)}, u32[]{:S(2)}) collective-permute-start(f32[8,8,128]{2,1,0:T(8,128)S(1)} %all_to_all.16.l_ref), channel_id=1, source_target_pairs={{0,1},{1,0},{2,3},{3,2},{4,5},{5,4},{6,7},{7,6},{8,9},{9,8},{10,11... | collective-permute-start | bytes 98312 | tf_op jit(solution)/shard_map/ppermute | solution.py:405
  32.2 11.7 %copy-start.1 = (bf16[128,1024]{1,0:T(8,128)(2,1)S(1)}, bf16[128,1024]{1,0:T(8,128)(2,1)}, u32[]{:S(2)}) copy-start(bf16[128,1024]{1,0:T(8,128)(2,1)} %get-tuple-element.26.xa_ref.xa0_ref) | copy-start | bytes 786436
  32.2 11.6 %copy-start.2 = (bf16[8,64,128]{2,1,0:T(8,128)(2,1)S(1)}, bf16[8,64,128]{2,1,0:T(8,128)(2,1)}, u32[]{:S(2)}) copy-start(bf16[8,64,128]{2,1,0:T(8,128)(2,1)} %get-tuple-element.27.y_ref) | copy-start | bytes 393220
  32.2 1.4 %collective-permute-start.2 = (bf16[112,512]{1,0:T(8,128)(2,1)S(1)}, bf16[112,512]{1,0:T(8,128)(2,1)S(1)}, u32[]{:S(2)}, u32[]{:S(2)}) collective-permute-start(bf16[112,512]{1,0:T(8,128)(2,1)S(1)} %get-tuple-element.43), channel_id=1, source_target_pairs={{0,1},{1,0},{2,3},{3,2},{4,5},{5,4},{6,7},{7,6},{8,9},{9,8},{10,11... | collective-permute-start | bytes 344072 | tf_op jit(solution)/shard_map/ppermute | solution.py:405

commit v8 on v7

--- a/solution.py
+++ b/solution.py
@@ -16,6 +16,7 @@
 EXT = 32
 PAD = 16
 LANES = 128
+AXES = ("row", "col")
 F32 = jnp.float32
 BF16 = jnp.bfloat16
 
@@ -38,11 +39,6 @@
     return out
 
 
-def extras_y(index, c_term, mass):
-    high, mid, low = pieces(c_term)
-    return select(index, {0: high, 1: mid, 2: low, 3: 1.0, 4: 1.0, 5: 1.0, 6: mass})
-
-
 def extras_x(index, b_term, mass):
     high, mid, low = pieces(b_term)
     return select(index, {0: 1.0, 1: 1.0, 2: 1.0, 3: high, 4: mid, 5: low, 7: mass})
@@ -64,16 +60,21 @@
     return jnp.sum(jnp.where(eye, column, 0.0), axis=0, keepdims=True)
 
 
-def for_tiles(total, body):
+def for_tiles(total, product, z_ref, use):
     count = total // TILE
-    if count <= 4:
+    slots = z_ref.shape[0]
+    if count <= slots:
         for t in range(count):
-            body(pl.ds(t * TILE, TILE))
+            z_ref[t] = product(pl.ds(t * TILE, TILE))
+        for t in range(count):
+            use(pl.ds(t * TILE, TILE), z_ref.at[t])
     else:
 
         @pl.loop(0, count)
         def _(t):
-            body(pl.ds(pl.multiple_of(t * TILE, TILE), TILE))
+            tile = pl.ds(pl.multiple_of(t * TILE, TILE), TILE)
+            z_ref[0] = product(tile)
+            use(tile, z_ref.at[0])
 
 
 def max_down(z_ref, rows):
@@ -83,10 +84,13 @@
     return jnp.max(peak, axis=0, keepdims=True)
 
 
-def exp_sum_down(z_ref, rows, scale, shift):
+def exp_sum_down(z_ref, rows, scale, shift, keep=None):
     total = jnp.zeros((STEP, TILE), F32)
     for r in range(0, rows, STEP):
-        total = total + jnp.exp2((z_ref[r : r + STEP, :] - shift) * scale)
+        value = jnp.exp2((z_ref[r : r + STEP, :] - shift) * scale)
+        total = total + value
+        if keep is not None:
+            keep(r, value.astype(BF16))
     return jnp.sum(total, axis=0, keepdims=True)
 
 
@@ -123,59 +127,50 @@
     return jnp.concatenate([block[:, :width], jnp.concatenate(side, axis=1)], axis=0)
 
 
-def prep_kernel(
-    log_ny, xt_hbm, y_hbm, mx_hbm, my_hbm, ya_hbm, xa_hbm, y_ref, my_ref, mx_ref, ya_ref, xa_ref, sems
-):
-    width, n = xt_hbm.shape
-    rows = ya_hbm.shape[0]
-    move_y = pltpu.make_async_copy(y_hbm, y_ref, sems.at[0])
-    move_my = pltpu.make_async_copy(my_hbm, my_ref, sems.at[1])
-    move_mx = pltpu.make_async_copy(mx_hbm, mx_ref, sems.at[2])
-    move_x = pltpu.make_async_copy(xt_hbm, xa_ref.at[:width, :], sems.at[3])
-    for move in (move_y, move_my, move_x, move_mx):
-        move.start()
-    move_y.wait()
+def ones_kernel(ext_ref):
+    index = lax.broadcasted_iota(jnp.int32, ext_ref.shape, 1)
+    ext_ref[...] = select(index, {3: 1.0, 4: 1.0, 5: 1.0})
+
+
+def prep_kernel(log_ny, y_ref, my_ref, ones_ref, ya_ref):
+    width = y_ref.shape[1]
     y = y_ref[...]
     yf = y.astype(F32)
     norm = jnp.sum(yf * yf, axis=1, keepdims=True)
-    move_my.wait()
     mass = to_column(my_ref[...].astype(F32))
     c_term = (mass - log_ny) / kappa_of(width) - 0.5 * norm
-    index = lax.broadcasted_iota(jnp.int32, (y.shape[0], EXT), 1)
-    ya_ref[:, :width] = y
-    ya_ref[:, width:] = extras_y(index, c_term, mass).astype(BF16)
-    moves = [pltpu.make_async_copy(ya_ref, ya_hbm.at[k], sems.at[5 + k]) for k in range(rows)]
-    for move in moves:
-        move.start()
-    move_mx.wait()
+    high, mid, low = pieces(c_term)
+    index = lax.broadcasted_iota(jnp.int32, ones_ref.shape, 1)
+    ext = (ones_ref[...] + select(index, {0: high, 1: mid, 2: low, 6: mass})).astype(BF16)
+    for k in range(ya_ref.shape[0]):
+        ya_ref[k, :, :width] = y
+        ya_ref[k, :, width:] = ext
+
+
+def half_kernel(xt_ref, mx_ref, mine_ref, xa_ref, peak_ref, total_ref, z_ref):
+    rows, yd, depth = mine_ref.shape
+    width, n = xt_ref.shape
+    half = rows * yd
+    scale = kappa_of(width) * LOG2E
     mass = from_lanes(mx_ref[...].astype(F32))
+    xa_ref[:width, :] = xt_ref[...]
     xa_ref[width:, :] = extras_x(rows_index(n), jnp.zeros((1, n), F32), mass).astype(BF16)
-    move_x.wait()
-    move_out = pltpu.make_async_copy(xa_ref, xa_hbm, sems.at[4])
-    move_out.start()
-    for move in moves:
-        move.wait()
-    move_out.wait()
-
-
-def half_kernel(xa_ref, mine_ref, peak_ref, total_ref, z_ref):
-    rows, yd, depth = mine_ref.shape
-    half = rows * yd
-    scale = kappa_of(depth - EXT) * LOG2E
     y_rows = mine_ref[...].reshape(half, depth)
 
-    def row_tile(t):
-        z_ref[...] = jnp.dot(y_rows, xa_ref[:, t], preferred_element_type=F32)
-        peak = max_down(z_ref, half)
+    def product(t):
+        return jnp.dot(y_rows, xa_ref[:, t], preferred_element_type=F32)
+
+    def use(t, z):
+        peak = max_down(z, half)
         peak_ref[:, t] = peak
-        total_ref[:, t] = exp_sum_down(z_ref, half, scale, peak)
-
-    for_tiles(xa_ref.shape[1], row_tile)
+        total_ref[:, t] = exp_sum_down(z, half, scale, peak)
+
+    for_tiles(n, product, z_ref, use)
 
 
 def first_kernel(
     log_nx, xa0_ref, mine_ref, other_ref, peak_ref, total_ref,
-    ya_ref, b_ref, l_ref, m_ref, rows_ref, xa_ref, z_ref, zc_ref, b2_ref,
+    yt_ref, b_ref, l_ref, m_ref, t_ref, xa_ref, ya_ref, z_ref, zc_ref, b2_ref,
 ):
     rows, yd, depth = mine_ref.shape
     n = xa0_ref.shape[1]
@@ -185,56 +180,42 @@
     col = lax.axis_index("col")
     scale = kappa_of(width) * LOG2E
     other = other_ref[...].reshape(half, depth)
+
+    def product(t):
+        return jnp.dot(other, xa0_ref[:, t], preferred_element_type=F32)
+
+    def use(t, z):
+        old = peak_ref[:, t]
+        peak = jnp.maximum(max_down(z, half), old)
+        total = exp_sum_down(z, half, scale, peak) + total_ref[:, t] * jnp.exp2((old - peak) * scale)
+        b_ref[:, t] = -peak - jnp.log(total) * (LOG2E / scale)
+
+    for_tiles(n, product, z_ref, use)
     ya_ref[pl.ds(pl.multiple_of(col * half, half), half), :] = mine_ref[...].reshape(half, depth)
     ya_ref[pl.ds(pl.multiple_of((1 - col) * half, half), half), :] = other
-
-    def row_tile(t):
-        z_ref[...] = jnp.dot(other, xa0_ref[:, t], preferred_element_type=F32)
-        old = peak_ref[:, t]
-        peak = jnp.maximum(max_down(z_ref, half), old)
-        total = exp_sum_down(z_ref, half, scale, peak) + total_ref[:, t] * jnp.exp2((old - peak) * scale)
-        b_ref[:, t] = -peak - jnp.log(total) * (LOG2E / scale)
-
-    for_tiles(n, row_tile)
+    yt_ref[...] = ya_ref[...].T
     mass = xa0_ref[width:, :].astype(F32)[7:8]
     b_term = b_ref[...] + (mass - log_nx) * (LOG2E / scale)
     b_ref[...] = b_term
     xa_ref[:width, :] = xa0_ref[:width, :]
     xa_ref[width:, :] = extras_x(rows_index(n), b_term, mass).astype(BF16)
-    rows_ref[...] = xa_ref[...].T
-
-    def col_tile(t):
-        zc_ref[...] = lax.dot_general(
-            rows_ref[...], ya_ref[t, :], (((1,), (1,)), ((), ())), preferred_element_type=F32
-        )
-        peak = max_down(zc_ref, n)
+    x_rows = xa_ref[...].T
+
+    def product(t):
+        return jnp.dot(x_rows, yt_ref[:, t], preferred_element_type=F32)
+
+    def use(t, z):
+        def keep(r, value):
+            t_ref[r : r + STEP, t] = value
+
+        peak = max_down(z, n)
         m_ref[:, t] = peak
-        b2_ref[:, t] = scale * peak + jnp.log(exp_sum_down(zc_ref, n, scale, peak)) * LOG2E
-
-    for_tiles(ny, col_tile)
+        b2_ref[:, t] = scale * peak + jnp.log(exp_sum_down(z, n, scale, peak, keep)) * LOG2E
+
+    for_tiles(ny, product, zc_ref, use)
     lse = to_lanes(b2_ref[...])
-    for k in range(rows):
+    for k in range(2 * rows):
         l_ref[k] = lse
-
-
-def plan_kernel(xa_ref, rows_ref, ya_ref, m_ref, t_ref, yt_ref, norm_ref, zc_ref):
-    ny, depth = ya_ref.shape
-    n = rows_ref.shape[0]
-    scale = kappa_of(depth - EXT) * LOG2E
-
-    def col_tile(t):
-        y_part = ya_ref[t, :]
-        yt_ref[:, t] = y_part.T
-        zc_ref[...] = lax.dot_general(
-            rows_ref[...], y_part, (((1,), (1,)), ((), ())), preferred_element_type=F32
-        )
-        peak = m_ref[:, t]
-        for r in range(0, n, STEP):
-            t_ref[r : r + STEP, t] = jnp.exp2((zc_ref[r : r + STEP, :] - peak) * scale).astype(BF16)
-
-    for_tiles(ny, col_tile)
-    xf = xa_ref[: depth - EXT, :].astype(F32)
-    norm_ref[...] = jnp.sum(xf * xf, axis=0, keepdims=True)
 
 
 def stack(out_ref, width, points, factor):
@@ -253,7 +234,7 @@
 
 
 def second_kernel(
-    log_nx, log_ny, xa_ref, b_ref, l_ref, other_ref, m_ref, yt_ref, t_ref,
+    log_nx, log_ny, xa_ref, b_ref, l_ref, m_ref, yt_ref, t_ref,
     r_ref, v_ref, c_ref, xs_ref, sum_ref, send_ref,
 ):
     width = xa_ref.shape[0] - EXT
@@ -261,9 +242,9 @@
     half = ny // 2
     kappa = kappa_of(width)
     scale = kappa * LOG2E
-    l_mine, l_other = l_ref[...], other_ref[...]
-    peak = jnp.maximum(jnp.max(l_mine, axis=0), jnp.max(l_other, axis=0))
-    total = jnp.sum(jnp.exp2(l_mine - peak[None]), axis=0) + jnp.sum(jnp.exp2(l_other - peak[None]), axis=0)
+    l_all = l_ref[...]
+    peak = jnp.max(l_all, axis=0)
+    total = jnp.sum(jnp.exp2(l_all - peak[None]), axis=0)
     lse2 = from_lanes(peak + jnp.log(total) * LOG2E)
     old = yt_ref[width:, :].astype(F32)
     c_old = (old[0:1] + old[1:2]) + old[2:3]
@@ -301,7 +282,7 @@
     send_ref[width:, :] = ext.astype(BF16)
 
 
-def keep_kernel(xs_ref, v_ref, sum_ref, yt_ref, t_ref, keep_ref):
+def keep_kernel(xa_ref, xs_ref, v_ref, sum_ref, yt_ref, t_ref, keep_ref, norm_ref):
     width, half = keep_ref.shape
     col = lax.axis_index("col")
     for k in range(half // TILE):
@@ -310,6 +291,8 @@
         moment = product[:width] + product[width:]
         part = yt_ref[:width, t].astype(F32) * sum_ref[:, t] - moment * v_ref[:, t]
         keep_ref[:, k * TILE : (k + 1) * TILE] = part
+    xf = xa_ref[:width, :].astype(F32)
+    norm_ref[...] = jnp.sum(xf * xf, axis=0, keepdims=True)
 
 
 def add_kernel(keep_ref, sum_ref, got_ref, out_ref):
@@ -386,13 +369,14 @@
         move.wait()
 
 
-def call(kernel, outs, scratch, limit, *args, space=pltpu.VMEM, out_space=pltpu.VMEM):
+def call(kernel, outs, scratch, limit, *args, space=pltpu.VMEM, out_space=pltpu.VMEM, cost=None):
     return pl.pallas_call(
         kernel,
         out_shape=outs,
         in_specs=[pl.BlockSpec(memory_space=space)] * len(args),
         out_specs=jax.tree.map(lambda _: pl.BlockSpec(memory_space=out_space), outs),
         scratch_shapes=scratch,
+        cost_estimate=cost,
         compiler_params=pltpu.CompilerParams(vmem_limit_bytes=limit),
     )(*args)
 
@@ -414,52 +398,50 @@
     count = ny // LANES
     log_nx, log_ny = math.log(n * 2 * rows), math.log(ny)
     depth = width + EXT
-    limit = (12 if ny <= 1024 else 56) * 1024 * 1024
+    limit = (20 if ny <= 1024 else 56) * 1024 * 1024
     extra = sums_rows(ny)
     run = functools.partial
     vmem = pltpu.VMEM
-    y_own, xa = call(
-        run(prep_kernel, log_ny),
-        (shape((rows, yd, depth), BF16), shape((depth, n), BF16)),
-        [
-            vmem((yd, width), BF16), vmem((1, yd), BF16), vmem((n // LANES, LANES), BF16),
-            vmem((yd, depth), BF16), vmem((depth, n), BF16), pltpu.SemaphoreType.DMA((5 + rows,)),
-        ],
-        58 * 1024 * 1024,
-        points_x.T, points_y, mass_x.reshape(n // LANES, LANES), mass_y.reshape(1, yd), space=pl.ANY, out_space=pl.ANY,
+    slots = 4 if ny <= 1024 else 1
+    ones = call(
+        ones_kernel, shape((yd, EXT)), [], limit,
+        cost=pl.CostEstimate(flops=4 * 10**9, bytes_accessed=10000, transcendentals=0),
+    )
+    y_own = call(
+        run(prep_kernel, log_ny), shape((rows, yd, depth), BF16), [], limit, points_y, mass_y.reshape(1, yd), ones,
+        cost=pl.CostEstimate(flops=4 * 10**9, bytes_accessed=400000, transcendentals=0),
     )
     y_mine = lax.all_to_all(y_own, "row", 0, 0, tiled=True)
     y_other = swap(y_mine)
-    peak, total = call(
-        half_kernel, (shape((1, n)), shape((1, n))), [vmem((half, TILE), F32)], limit, xa, y_mine
-    )
-    ya, b_term, lse, peak, x_rows = call(
+    xa, peak, total = call(
+        half_kernel, (shape((depth, n), BF16), shape((1, n)), shape((1, n))), [vmem((slots, half, TILE), F32)],
+        limit, points_x.T, mass_x.reshape(n // LANES, LANES), y_mine,
+    )
+    yt, b_term, lse, peak, plan = call(
         run(first_kernel, log_nx),
         (
-            shape((ny, depth), BF16), shape((1, n)), shape((rows, count, LANES)), shape((1, ny)),
-            shape((n, depth), BF16),
+            shape((depth, ny), BF16), shape((1, n)), shape((2 * rows, count, LANES)), shape((1, ny)),
+            shape((n, ny), BF16),
         ),
-        [vmem((depth, n), BF16), vmem((half, TILE), F32), vmem((n, TILE), F32), vmem((1, ny), F32)],
+        [
+            vmem((depth, n), BF16), vmem((ny, depth), BF16), vmem((slots, half, TILE), F32),
+            vmem((slots, n, TILE), F32), vmem((1, ny), F32),
+        ],
         limit, xa, y_mine, y_other, peak, total,
     )
-    lse = lax.all_to_all(lse, "row", 0, 0, tiled=True)
-    lse_other = swap(lse)
-    plan, yt, norm = call(
-        plan_kernel,
-        (shape((n, ny), BF16), shape((depth, ny), BF16), shape((1, n))),
-        [vmem((n, TILE), F32)],
-        limit, xa, x_rows, ya, peak,
-    )
+    lse = lax.all_to_all(lse, AXES, 0, 0, tiled=True)
     r, v, c_term, xs, sums, send = call(
         run(second_kernel, log_nx, log_ny),
         (
             shape((1, n)), shape((1, ny)), shape((count, LANES)), shape((2 * width + PAD, n), BF16),
             shape((1, ny)), shape((width + PAD, half), BF16),
         ),
-        [], limit, xa, b_term, lse, lse_other, peak, yt, plan,
+        [], limit, xa, b_term, lse, peak, yt, plan,
     )
     got = swap(send)
-    keep = call(keep_kernel, shape((width, half)), [], limit, xs, v, sums, yt, plan)
+    keep, norm = call(
+        keep_kernel, (shape((width, half)), shape((1, n))), [], limit, xa, xs, v, sums, yt, plan
+    )
     part = call(
         add_kernel, shape((rows, yd * width // LANES + extra, LANES), BF16), [], limit, keep, sums, got
     )

time: 45.8 us -> 43.5 us (0.950)
  Pallas kernels: 8.64 us -> 6.31 us
    pallas_call x8, Pallas kernels: 8.64 us -> 6.31 us  [call(): pl.pallas_call(kernel, out_shape=outs, in_specs=[pl.BlockSpec(memory_spac...]
    ppermute x3 -> x2, waiting for transfers between devices: 1.23 us -> 1.57 us  [swap(): return lax.ppermute(value, 'col', [(0, 1), (1, 0)])]
    unnamed x6 -> x8, local copies, waits for them, and re-layouts: 0.96 us -> 0.71 us
  transfers between devices with their start and end apart: 3 -> 2, of which waited for: 2 -> 2; matrix products, arithmetic and copies ran while one was open for 0% -> 0% of each run, Pallas kernels for 4% -> 2%
where the time goes in v8:
time: 43.5 us; the launch traced here: 43.2 us
  blocking collectives  33.9 us (78%)
  Pallas kernels  6.31 us (15%)
  waiting for transfers between devices  1.57 us (4%)
  local copies, waits for them, and re-layouts  0.71 us (2%)
  between operations  0.71 us (2%)
    all_to_all x1, blocking collectives, on_device(): y_mine = lax.all_to_all(y_own, 'row', 0, 0, tiled=True)  14.4 us
    all_to_all x1, blocking collectives, on_device(): part = lax.all_to_all(part, 'row', 0, 0, tiled=True)  9.97 us
    all_to_all x1, blocking collectives, on_device(): lse = lax.all_to_all(lse, AXES, 0, 0, tiled=True)  9.48 us
    pallas_call x8, Pallas kernels, call(): pl.pallas_call(kernel, out_shape=outs, in_specs=[pl.BlockSpec(memory_spac...  6.31 us
    ppermute x2, waiting for transfers between devices, swap(): return lax.ppermute(value, 'col', [(0, 1), (1, 0)])  1.57 us
  transfers between devices with their start and end apart: 2, of which 2 were waited for; matrix products, arithmetic and copies ran while one was open for 0% of the time, Pallas kernels for 2%

profile of v8, /device:TPU:0, one launch (start us, length us, event | category | flops | bytes accessed | tf_op | source)
XLA Modules:
  0.0 43.2 jit_solution(11320706135419409864)
XLA Ops:
  0.6 0.0 copy-start.3
  0.6 0.0 copy-start.2
  0.7 0.6 %copy-done.3 = bf16[64]{0:T(256)(128)(2,1)S(1)} copy-done((bf16[64]{0:T(256)(128)(2,1)S(1)}, bf16[64]{0:T(256)(128)(2,1)}, u32[]{:S(2)}) %copy-start.3) | copy-done | bytes 152
  1.3 0.1 copy-done.2
  1.4 0.0 copy-start
  1.4 0.0 copy-start.1
  1.4 0.2 shard_map.76.y_ref
  1.6 14.4 %all_to_all.15.mine_ref = bf16[8,64,128]{2,1,0:T(8,128)(2,1)S(1)} all-to-all(bf16[8,64,128]{2,1,0:T(8,128)(2,1)S(1)} %shard_map.76.y_ref), channel_id=1, replica_groups=mesh['groups'=2,'row'=8,'col'=2] {'row'}, dimensions={0} | all-to-all | bytes 262144 | tf_op jit(solution)/shard_map/all_to_all | solution.py:414
  16.0 0.0 collective-permute-start
  16.0 0.0 copy-done
  16.0 0.0 copy-done.1
  16.0 0.7 %shard_map.77 = (bf16[128,1024]{1,0:T(8,128)(2,1)S(1)}, f32[1,1024]{1,0:T(1,128)S(1)}, f32[1,1024]{1,0:T(1,128)S(1)}) custom-call(bf16[96,1024]{1,0:T(8,128)(2,1)S(1)} %bitcast.6, bf16[8,128]{1,0:T(8,128)(2,1)S(1)} %bitcast.7, bf16[8,64,128]{2,1,0:T(8,128)(2,1)S(1)} %all_to_all.15.mine_ref), custom_call_target="tpu_custom_call" | custom-call | tf_op jit(solution)/shard_map/pallas_call | solution.py:373
  16.7 0.7 %collective-permute-done.other_ref = bf16[8,64,128]{2,1,0:T(8,128)(2,1)S(1)} collective-permute-done((bf16[8,64,128]{2,1,0:T(8,128)(2,1)S(1)}, bf16[8,64,128]{2,1,0:T(8,128)(2,1)S(1)}, u32[]{:S(2)}, u32[]{:S(2)}) %collective-permute-start) | collective-permute-done | bytes 131104 | tf_op jit(solution)/shard_map/ppermute | solution.py:389
  17.3 2.0 %shard_map.78 = (bf16[128,1024]{1,0:T(8,128)(2,1)S(1)}, f32[1,1024]{1,0:T(1,128)S(1)}, f32[16,8,128]{2,1,0:T(8,128)S(1)}, f32[1,1024]{1,0:T(1,128)S(1)}, bf16[1024,1024]{1,0:T(8,128)(2,1)S(1)}) custom-call(bf16[128,1024]{1,0:T(8,128)(2,1)S(1)} %get-tuple-element.24.xa0_ref.xa_ref, bf16[8,64,128]{2,1,0:T(8,128)(2,1)S(1)} %all_to_all.15.mine_ref, ...), custom_call_target="tpu_custom_call" | custom-call | tf_op jit(solution)/shard_map/pallas_call | solution.py:373
  19.3 9.5 %all_to_all.16.l_ref = f32[16,8,128]{2,1,0:T(8,128)S(1)} all-to-all(f32[16,8,128]{2,1,0:T(8,128)S(1)} %get-tuple-element.28), channel_id=1, replica_groups=mesh['groups'=2,'row'=8,'col'=2] {'row','col'}, dimensions={0} | all-to-all | bytes 131072 | tf_op jit(solution)/shard_map/all_to_all | solution.py:432
  28.8 1.2 %shard_map.79 = (f32[1,1024]{1,0:T(1,128)S(1)}, f32[1,1024]{1,0:T(1,128)S(1)}, f32[8,128]{1,0:T(8,128)S(1)}, bf16[208,1024]{1,0:T(8,128)(2,1)S(1)}, f32[1,1024]{1,0:T(1,128)S(1)}, /*index=5*/bf16[112,512]{1,0:T(8,128)(2,1)S(1)}) custom-call(bf16[128,1024]{1,0:T(8,128)(2,1)S(1)} %get-tuple-element.24.xa0_ref.xa_ref, f32[1,1024]{1,0:T(1,128)S(1)} %get-tuple-element.27.b_ref, ...), custom_call_target="tpu_custom_call" | custom-call | tf_op jit(solution)/shard_map/pallas_call | solution.py:373
  30.0 0.1 collective-permute-start.1
  30.1 0.4 shard_map.80
  30.5 0.9 %collective-permute-done.1.got_ref = bf16[112,512]{1,0:T(8,128)(2,1)S(1)} collective-permute-done((bf16[112,512]{1,0:T(8,128)(2,1)S(1)}, bf16[112,512]{1,0:T(8,128)(2,1)S(1)}, u32[]{:S(2)}, u32[]{:S(2)}) %collective-permute-start.1) | collective-permute-done | bytes 114720 | tf_op jit(solution)/shard_map/ppermute | solution.py:389
  31.4 0.3 shard_map.81
  31.6 10.0 %all_to_all.17.got_ref = bf16[8,64,128]{2,1,0:T(8,128)(2,1)S(1)} all-to-all(bf16[8,64,128]{2,1,0:T(8,128)(2,1)S(1)} %shard_map.81), channel_id=1, replica_groups=mesh['groups'=2,'row'=8,'col'=2] {'row'}, dimensions={0} | all-to-all | bytes 262144 | tf_op jit(solution)/shard_map/all_to_all | solution.py:448
  41.6 1.6 %shard_map.82 = (f32[1,1024]{1,0:T(1,128)}, f32[1,64]{1,0:T(1,128)}, f32[96,1024]{1,0:T(8,128)}, f32[64,96]{1,0:T(8,128)}) custom-call(bf16[128,1024]{1,0:T(8,128)(2,1)S(1)} %get-tuple-element.24.xa0_ref.xa_ref, f32[1,1024]{1,0:T(1,128)S(1)} %get-tuple-element.35.norm_ref, f32[1,1024]{1,0:T(1,128)S(1)} %get-tuple-element.27.b_ref, ...), custom_call_target="tpu_custom_call" | custom-call | tf_op jit(solution)/shard_map/pallas_call | solution.py:373
  (1 shorter events, 0.0 us)
Async XLA Ops:
  0.6 0.7 %copy-start.3 = (bf16[64]{0:T(256)(128)(2,1)S(1)}, bf16[64]{0:T(256)(128)(2,1)}, u32[]{:S(2)}) copy-start(bf16[64]{0:T(256)(128)(2,1)} %param.7) | copy-start | bytes 388
  0.6 0.7 %copy-start.2 = (bf16[64,96]{1,0:T(8,128)(2,1)S(1)}, bf16[64,96]{1,0:T(8,128)(2,1)}, u32[]{:S(2)}) copy-start(bf16[64,96]{1,0:T(8,128)(2,1)} %y_ref.1) | copy-start | bytes 36868
  1.4 14.6 %copy-start = (bf16[1024,96]{0,1:T(8,128)(2,1)S(1)}, bf16[1024,96]{0,1:T(8,128)(2,1)}, u32[]{:S(2)}) copy-start(bf16[1024,96]{0,1:T(8,128)(2,1)} %param.4) | copy-start | bytes 589828
  1.4 14.6 %copy-start.1 = (bf16[1024]{0:T(1024)(128)(2,1)S(1)}, bf16[1024]{0:T(1024)(128)(2,1)}, u32[]{:S(2)}) copy-start(bf16[1024]{0:T(1024)(128)(2,1)} %param.6) | copy-start | bytes 6148
  16.0 1.3 %collective-permute-start = (bf16[8,64,128]{2,1,0:T(8,128)(2,1)S(1)}, bf16[8,64,128]{2,1,0:T(8,128)(2,1)S(1)}, u32[]{:S(2)}, u32[]{:S(2)}) collective-permute-start(bf16[8,64,128]{2,1,0:T(8,128)(2,1)S(1)} %all_to_all.15.mine_ref), channel_id=1, source_target_pairs={{0,1},{1,0},{2,3},{3,2},{4,5},{5,4},{6,7},{7,6},{8,9},{9,8},{10,11... | collective-permute-start | bytes 393224 | tf_op jit(solution)/shard_map/ppermute | solution.py:389
  30.0 1.4 %collective-permute-start.1 = (bf16[112,512]{1,0:T(8,128)(2,1)S(1)}, bf16[112,512]{1,0:T(8,128)(2,1)S(1)}, u32[]{:S(2)}, u32[]{:S(2)}) collective-permute-start(bf16[112,512]{1,0:T(8,128)(2,1)S(1)} %get-tuple-element.39), channel_id=1, source_target_pairs={{0,1},{1,0},{2,3},{3,2},{4,5},{5,4},{6,7},{7,6},{8,9},{9,8},{10,11... | collective-permute-start | bytes 344072 | tf_op jit(solution)/shard_map/ppermute | solution.py:389

commit v9 on v8

--- a/solution.py
+++ b/solution.py
@@ -12,7 +12,8 @@
 EPSILON = 0.02
 LOG2E = math.log2(math.e)
 TILE = 256
-STEP = 32
+STEP = 8
+WIDE = 1024
 EXT = 32
 PAD = 16
 LANES = 128
@@ -60,37 +61,19 @@
     return jnp.sum(jnp.where(eye, column, 0.0), axis=0, keepdims=True)
 
 
-def for_tiles(total, product, z_ref, use):
-    count = total // TILE
-    slots = z_ref.shape[0]
-    if count <= slots:
-        for t in range(count):
-            z_ref[t] = product(pl.ds(t * TILE, TILE))
-        for t in range(count):
-            use(pl.ds(t * TILE, TILE), z_ref.at[t])
-    else:
-
-        @pl.loop(0, count)
-        def _(t):
-            tile = pl.ds(pl.multiple_of(t * TILE, TILE), TILE)
-            z_ref[0] = product(tile)
-            use(tile, z_ref.at[0])
-
-
-def max_down(z_ref, rows):
+def max_down(z_ref):
+    rows, columns = z_ref.shape
     peak = z_ref[0:STEP, :]
     for r in range(STEP, rows, STEP):
         peak = jnp.maximum(peak, z_ref[r : r + STEP, :])
     return jnp.max(peak, axis=0, keepdims=True)
 
 
-def exp_sum_down(z_ref, rows, scale, shift, keep=None):
-    total = jnp.zeros((STEP, TILE), F32)
+def exp_sum_down(z_ref, scale, shift):
+    rows, columns = z_ref.shape
+    total = jnp.zeros((STEP, columns), F32)
     for r in range(0, rows, STEP):
-        value = jnp.exp2((z_ref[r : r + STEP, :] - shift) * scale)
-        total = total + value
-        if keep is not None:
-            keep(r, value.astype(BF16))
+        total = total + jnp.exp2((z_ref[r : r + STEP, :] - shift) * scale)
     return jnp.sum(total, axis=0, keepdims=True)
 
 
@@ -147,7 +130,7 @@
         ya_ref[k, :, width:] = ext
 
 
-def half_kernel(xt_ref, mx_ref, mine_ref, xa_ref, peak_ref, total_ref, z_ref):
+def half_kernel(xt_ref, mx_ref, mine_ref, xa_ref, rows_ref, yt_ref, peak_ref, total_ref, z_ref):
     rows, yd, depth = mine_ref.shape
     width, n = xt_ref.shape
     half = rows * yd
@@ -155,24 +138,20 @@
     mass = from_lanes(mx_ref[...].astype(F32))
     xa_ref[:width, :] = xt_ref[...]
     xa_ref[width:, :] = extras_x(rows_index(n), jnp.zeros((1, n), F32), mass).astype(BF16)
-    y_rows = mine_ref[...].reshape(half, depth)
-
-    def product(t):
-        return jnp.dot(y_rows, xa_ref[:, t], preferred_element_type=F32)
-
-    def use(t, z):
-        peak = max_down(z, half)
-        peak_ref[:, t] = peak
-        total_ref[:, t] = exp_sum_down(z, half, scale, peak)
-
-    for_tiles(n, product, z_ref, use)
+    mine = mine_ref[...].reshape(half, depth)
+    z_ref[...] = jnp.dot(mine, xa_ref[...], preferred_element_type=F32)
+    peak = max_down(z_ref)
+    peak_ref[...] = peak
+    total_ref[...] = exp_sum_down(z_ref, scale, peak)
+    rows_ref[...] = xa_ref[...].T
+    yt_ref[...] = mine.T
 
 
 def first_kernel(
-    log_nx, xa0_ref, mine_ref, other_ref, peak_ref, total_ref,
-    yt_ref, b_ref, l_ref, m_ref, t_ref, xa_ref, ya_ref, z_ref, zc_ref, b2_ref,
+    log_nx, xa0_ref, rows0_ref, mine_ref, other_ref, peak_ref, total_ref,
+    yt_ref, b_ref, l_ref, m_ref, t_ref, z_ref, zc_ref, b2_ref,
 ):
-    rows, yd, depth = mine_ref.shape
+    rows, yd, depth = other_ref.shape
     n = xa0_ref.shape[1]
     width = depth - EXT
     half = rows * yd
@@ -180,39 +159,39 @@
     col = lax.axis_index("col")
     scale = kappa_of(width) * LOG2E
     other = other_ref[...].reshape(half, depth)
-
-    def product(t):
-        return jnp.dot(other, xa0_ref[:, t], preferred_element_type=F32)
-
-    def use(t, z):
-        old = peak_ref[:, t]
-        peak = jnp.maximum(max_down(z, half), old)
-        total = exp_sum_down(z, half, scale, peak) + total_ref[:, t] * jnp.exp2((old - peak) * scale)
-        b_ref[:, t] = -peak - jnp.log(total) * (LOG2E / scale)
-
-    for_tiles(n, product, z_ref, use)
-    ya_ref[pl.ds(pl.multiple_of(col * half, half), half), :] = mine_ref[...].reshape(half, depth)
-    ya_ref[pl.ds(pl.multiple_of((1 - col) * half, half), half), :] = other
-    yt_ref[...] = ya_ref[...].T
+    z_ref[...] = jnp.dot(other, xa0_ref[...], preferred_element_type=F32)
+    yt_ref[:, pl.ds(pl.multiple_of(col * half, half), half)] = mine_ref[...]
+    yt_ref[:, pl.ds(pl.multiple_of((1 - col) * half, half), half)] = other.T
+    old = peak_ref[...]
+    peak = jnp.maximum(max_down(z_ref), old)
+    total = exp_sum_down(z_ref, scale, peak) + total_ref[...] * jnp.exp2((old - peak) * scale)
     mass = xa0_ref[width:, :].astype(F32)[7:8]
-    b_term = b_ref[...] + (mass - log_nx) * (LOG2E / scale)
+    b_term = -peak + (mass - log_nx - jnp.log(total)) * (LOG2E / scale)
     b_ref[...] = b_term
-    xa_ref[:width, :] = xa0_ref[:width, :]
-    xa_ref[width:, :] = extras_x(rows_index(n), b_term, mass).astype(BF16)
-    x_rows = xa_ref[...].T
-
-    def product(t):
-        return jnp.dot(x_rows, yt_ref[:, t], preferred_element_type=F32)
-
-    def use(t, z):
-        def keep(r, value):
-            t_ref[r : r + STEP, t] = value
-
-        peak = max_down(z, n)
+    ext = extras_x(rows_index(n), b_term, mass).T.astype(BF16)
+    x_rows = jnp.concatenate([rows0_ref[:, :width], ext], axis=1)
+    wide = min(WIDE, ny)
+
+    def columns(t):
+        zc_ref[...] = jnp.dot(x_rows, yt_ref[:, t], preferred_element_type=F32)
+        peak = max_down(zc_ref)
         m_ref[:, t] = peak
-        b2_ref[:, t] = scale * peak + jnp.log(exp_sum_down(z, n, scale, peak, keep)) * LOG2E
-
-    for_tiles(ny, product, zc_ref, use)
+        total = jnp.zeros((2 * STEP, wide), F32)
+        for r in range(0, n, 2 * STEP):
+            value = jnp.exp2((zc_ref[r : r + 2 * STEP, :] - peak) * scale)
+            total = total + value
+            t_ref[r : r + 2 * STEP, t] = value.astype(BF16)
+        total = jnp.sum(total, axis=0, keepdims=True)
+        b2_ref[:, t] = scale * peak + jnp.log(total) * LOG2E
+
+    if ny == wide:
+        columns(slice(0, ny))
+    else:
+
+        @pl.loop(0, ny // wide)
+        def _(t):
+            columns(pl.ds(pl.multiple_of(t * wide, wide), wide))
+
     lse = to_lanes(b2_ref[...])
     for k in range(2 * rows):
         l_ref[k] = lse
@@ -402,7 +381,6 @@
     extra = sums_rows(ny)
     run = functools.partial
     vmem = pltpu.VMEM
-    slots = 4 if ny <= 1024 else 1
     ones = call(
         ones_kernel, shape((yd, EXT)), [], limit,
         cost=pl.CostEstimate(flops=4 * 10**9, bytes_accessed=10000, transcendentals=0),
@@ -413,8 +391,13 @@
     )
     y_mine = lax.all_to_all(y_own, "row", 0, 0, tiled=True)
     y_other = swap(y_mine)
-    xa, peak, total = call(
-        half_kernel, (shape((depth, n), BF16), shape((1, n)), shape((1, n))), [vmem((slots, half, TILE), F32)],
+    xa, x_rows, yt_mine, peak, total = call(
+        half_kernel,
+        (
+            shape((depth, n), BF16), shape((n, depth), BF16), shape((depth, half), BF16), shape((1, n)),
+            shape((1, n)),
+        ),
+        [vmem((half, n), F32)],
         limit, points_x.T, mass_x.reshape(n // LANES, LANES), y_mine,
     )
     yt, b_term, lse, peak, plan = call(
@@ -423,11 +406,8 @@
             shape((depth, ny), BF16), shape((1, n)), shape((2 * rows, count, LANES)), shape((1, ny)),
             shape((n, ny), BF16),
         ),
-        [
-            vmem((depth, n), BF16), vmem((ny, depth), BF16), vmem((slots, half, TILE), F32),
-            vmem((slots, n, TILE), F32), vmem((1, ny), F32),
-        ],
-        limit, xa, y_mine, y_other, peak, total,
+        [vmem((half, n), F32), vmem((n, min(WIDE, ny)), F32), vmem((1, ny), F32)],
+        limit, xa, x_rows, yt_mine, y_other, peak, total,
     )
     lse = lax.all_to_all(lse, AXES, 0, 0, tiled=True)
     r, v, c_term, xs, sums, send = call(

time: 43.5 us -> 43.9 us (level)
  transfers between devices with their start and end apart: 2 -> 2, of which waited for: 2 -> 2; matrix products, arithmetic and copies ran while one was open for 0% -> 0% of each run, Pallas kernels for 2% -> 3%
where the time goes in v9:
time: 43.9 us; the launch traced here: 43.6 us
  blocking collectives  33.9 us (77%)
  Pallas kernels  6.71 us (15%)
  waiting for transfers between devices  1.52 us (3%)
  local copies, waits for them, and re-layouts  0.71 us (2%)
  between operations  0.71 us (2%)
    all_to_all x1, blocking collectives, on_device(): y_mine = lax.all_to_all(y_own, 'row', 0, 0, tiled=True)  14.4 us
    all_to_all x1, blocking collectives, on_device(): part = lax.all_to_all(part, 'row', 0, 0, tiled=True)  9.97 us
    all_to_all x1, blocking collectives, on_device(): lse = lax.all_to_all(lse, AXES, 0, 0, tiled=True)  9.48 us
    pallas_call x8, Pallas kernels, call(): pl.pallas_call(kernel, out_shape=outs, in_specs=[pl.BlockSpec(memory_spac...  6.71 us
    ppermute x2, waiting for transfers between devices, swap(): return lax.ppermute(value, 'col', [(0, 1), (1, 0)])  1.52 us
  transfers between devices with their start and end apart: 2, of which 2 were waited for; matrix products, arithmetic and copies ran while one was open for 0% of the time, Pallas kernels for 3%

profile of v9, /device:TPU:0, one launch (start us, length us, event | category | flops | bytes accessed | tf_op | source)
XLA Modules:
  0.0 43.6 jit_solution(8453871854026102634)
XLA Ops:
  0.6 0.0 copy-start.3
  0.6 0.0 copy-start.2
  0.7 0.6 %copy-done.3 = bf16[64]{0:T(256)(128)(2,1)S(1)} copy-done((bf16[64]{0:T(256)(128)(2,1)S(1)}, bf16[64]{0:T(256)(128)(2,1)}, u32[]{:S(2)}) %copy-start.3) | copy-done | bytes 152
  1.3 0.1 copy-done.2
  1.4 0.0 copy-start
  1.4 0.0 copy-start.1
  1.4 0.2 shard_map.76.y_ref
  1.6 14.4 %all_to_all.15.mine_ref = bf16[8,64,128]{2,1,0:T(8,128)(2,1)S(1)} all-to-all(bf16[8,64,128]{2,1,0:T(8,128)(2,1)S(1)} %shard_map.76.y_ref), channel_id=1, replica_groups=mesh['groups'=2,'row'=8,'col'=2] {'row'}, dimensions={0} | all-to-all | bytes 262144 | tf_op jit(solution)/shard_map/all_to_all | solution.py:392
  16.0 0.0 collective-permute-start
  16.0 0.0 copy-done
  16.0 0.0 copy-done.1
  16.0 0.7 %shard_map.77 = (bf16[128,1024]{1,0:T(8,128)(2,1)S(1)}, bf16[1024,128]{1,0:T(8,128)(2,1)S(1)}, bf16[128,512]{1,0:T(8,128)(2,1)S(1)}, f32[1,1024]{1,0:T(1,128)S(1)}, f32[1,1024]{1,0:T(1,128)S(1)}) custom-call(bf16[96,1024]{1,0:T(8,128)(2,1)S(1)} %bitcast.6, bf16[8,128]{1,0:T(8,128)(2,1)S(1)} %bitcast.7, bf16[8,64,128]{2,1,0:T(8,128)(2,1)S(1)} %all_to_all.15.mine_ref), custom_call_target="tpu_custom_call" | custom-call | tf_op jit(solution)/shard_map/pallas_call | solution.py:352
  16.7 0.6 %collective-permute-done.other_ref = bf16[8,64,128]{2,1,0:T(8,128)(2,1)S(1)} collective-permute-done((bf16[8,64,128]{2,1,0:T(8,128)(2,1)S(1)}, bf16[8,64,128]{2,1,0:T(8,128)(2,1)S(1)}, u32[]{:S(2)}, u32[]{:S(2)}) %collective-permute-start) | collective-permute-done | bytes 131104 | tf_op jit(solution)/shard_map/ppermute | solution.py:368
  17.3 2.4 %shard_map.78 = (bf16[128,1024]{1,0:T(8,128)(2,1)S(1)}, f32[1,1024]{1,0:T(1,128)S(1)}, f32[16,8,128]{2,1,0:T(8,128)S(1)}, f32[1,1024]{1,0:T(1,128)S(1)}, bf16[1024,1024]{1,0:T(8,128)(2,1)S(1)}) custom-call(bf16[128,1024]{1,0:T(8,128)(2,1)S(1)} %get-tuple-element.26.xa0_ref.xa_ref, bf16[1024,128]{1,0:T(8,128)(2,1)S(1)} %get-tuple-element.27.rows0_ref, ...), custom_call_target="tpu_custom_call" | custom-call | tf_op jit(solution)/shard_map/pallas_call | solution.py:352
  19.7 9.5 %all_to_all.16.l_ref = f32[16,8,128]{2,1,0:T(8,128)S(1)} all-to-all(f32[16,8,128]{2,1,0:T(8,128)S(1)} %get-tuple-element.32), channel_id=1, replica_groups=mesh['groups'=2,'row'=8,'col'=2] {'row','col'}, dimensions={0} | all-to-all | bytes 131072 | tf_op jit(solution)/shard_map/all_to_all | solution.py:412
  29.2 1.2 %shard_map.79 = (f32[1,1024]{1,0:T(1,128)S(1)}, f32[1,1024]{1,0:T(1,128)S(1)}, f32[8,128]{1,0:T(8,128)S(1)}, bf16[208,1024]{1,0:T(8,128)(2,1)S(1)}, f32[1,1024]{1,0:T(1,128)S(1)}, /*index=5*/bf16[112,512]{1,0:T(8,128)(2,1)S(1)}) custom-call(bf16[128,1024]{1,0:T(8,128)(2,1)S(1)} %get-tuple-element.26.xa0_ref.xa_ref, f32[1,1024]{1,0:T(1,128)S(1)} %get-tuple-element.31.b_ref, ...), custom_call_target="tpu_custom_call" | custom-call | tf_op jit(solution)/shard_map/pallas_call | solution.py:352
  30.3 0.1 collective-permute-start.1
  30.4 0.4 shard_map.80
  30.8 0.9 %collective-permute-done.1.got_ref = bf16[112,512]{1,0:T(8,128)(2,1)S(1)} collective-permute-done((bf16[112,512]{1,0:T(8,128)(2,1)S(1)}, bf16[112,512]{1,0:T(8,128)(2,1)S(1)}, u32[]{:S(2)}, u32[]{:S(2)}) %collective-permute-start.1) | collective-permute-done | bytes 114720 | tf_op jit(solution)/shard_map/ppermute | solution.py:368
  31.7 0.3 shard_map.81
  32.0 10.0 %all_to_all.17.got_ref = bf16[8,64,128]{2,1,0:T(8,128)(2,1)S(1)} all-to-all(bf16[8,64,128]{2,1,0:T(8,128)(2,1)S(1)} %shard_map.81), channel_id=1, replica_groups=mesh['groups'=2,'row'=8,'col'=2] {'row'}, dimensions={0} | all-to-all | bytes 262144 | tf_op jit(solution)/shard_map/all_to_all | solution.py:428
  42.0 1.6 %shard_map.82 = (f32[1,1024]{1,0:T(1,128)}, f32[1,64]{1,0:T(1,128)}, f32[96,1024]{1,0:T(8,128)}, f32[64,96]{1,0:T(8,128)}) custom-call(bf16[128,1024]{1,0:T(8,128)(2,1)S(1)} %get-tuple-element.26.xa0_ref.xa_ref, f32[1,1024]{1,0:T(1,128)S(1)} %get-tuple-element.39.norm_ref, f32[1,1024]{1,0:T(1,128)S(1)} %get-tuple-element.31.b_ref, ...), custom_call_target="tpu_custom_call" | custom-call | tf_op jit(solution)/shard_map/pallas_call | solution.py:352
  (1 shorter events, 0.0 us)
Async XLA Ops:
  0.6 0.7 %copy-start.3 = (bf16[64]{0:T(256)(128)(2,1)S(1)}, bf16[64]{0:T(256)(128)(2,1)}, u32[]{:S(2)}) copy-start(bf16[64]{0:T(256)(128)(2,1)} %param.7) | copy-start | bytes 388
  0.6 0.7 %copy-start.2 = (bf16[64,96]{1,0:T(8,128)(2,1)S(1)}, bf16[64,96]{1,0:T(8,128)(2,1)}, u32[]{:S(2)}) copy-start(bf16[64,96]{1,0:T(8,128)(2,1)} %y_ref.1) | copy-start | bytes 36868
  1.4 14.6 %copy-start = (bf16[1024,96]{0,1:T(8,128)(2,1)S(1)}, bf16[1024,96]{0,1:T(8,128)(2,1)}, u32[]{:S(2)}) copy-start(bf16[1024,96]{0,1:T(8,128)(2,1)} %param.4) | copy-start | bytes 589828
  1.4 14.6 %copy-start.1 = (bf16[1024]{0:T(1024)(128)(2,1)S(1)}, bf16[1024]{0:T(1024)(128)(2,1)}, u32[]{:S(2)}) copy-start(bf16[1024]{0:T(1024)(128)(2,1)} %param.6) | copy-start | bytes 6148
  16.0 1.3 %collective-permute-start = (bf16[8,64,128]{2,1,0:T(8,128)(2,1)S(1)}, bf16[8,64,128]{2,1,0:T(8,128)(2,1)S(1)}, u32[]{:S(2)}, u32[]{:S(2)}) collective-permute-start(bf16[8,64,128]{2,1,0:T(8,128)(2,1)S(1)} %all_to_all.15.mine_ref), channel_id=1, source_target_pairs={{0,1},{1,0},{2,3},{3,2},{4,5},{5,4},{6,7},{7,6},{8,9},{9,8},{10,11... | collective-permute-start | bytes 393224 | tf_op jit(solution)/shard_map/ppermute | solution.py:368
  30.3 1.4 %collective-permute-start.1 = (bf16[112,512]{1,0:T(8,128)(2,1)S(1)}, bf16[112,512]{1,0:T(8,128)(2,1)S(1)}, u32[]{:S(2)}, u32[]{:S(2)}) collective-permute-start(bf16[112,512]{1,0:T(8,128)(2,1)S(1)} %get-tuple-element.43), channel_id=1, source_target_pairs={{0,1},{1,0},{2,3},{3,2},{4,5},{5,4},{6,7},{7,6},{8,9},{9,8},{10,11... | collective-permute-start | bytes 344072 | tf_op jit(solution)/shard_map/ppermute | solution.py:368

commit v10 on v8

--- a/solution.py
+++ b/solution.py
@@ -64,10 +64,11 @@
     count = total // TILE
     slots = z_ref.shape[0]
     if count <= slots:
-        for t in range(count):
-            z_ref[t] = product(pl.ds(t * TILE, TILE))
-        for t in range(count):
-            use(pl.ds(t * TILE, TILE), z_ref.at[t])
+        for t in range(count + 1):
+            if t < count:
+                z_ref[t] = product(pl.ds(t * TILE, TILE))
+            if t > 0:
+                use(pl.ds((t - 1) * TILE, TILE), z_ref.at[t - 1])
     else:
 
         @pl.loop(0, count)
@@ -77,16 +78,16 @@
             use(tile, z_ref.at[0])
 
 
-def max_down(z_ref, rows):
+def max_down(z_ref):
     peak = z_ref[0:STEP, :]
-    for r in range(STEP, rows, STEP):
+    for r in range(STEP, z_ref.shape[0], STEP):
         peak = jnp.maximum(peak, z_ref[r : r + STEP, :])
     return jnp.max(peak, axis=0, keepdims=True)
 
 
-def exp_sum_down(z_ref, rows, scale, shift, keep=None):
+def exp_sum_down(z_ref, scale, shift, keep=None):
     total = jnp.zeros((STEP, TILE), F32)
-    for r in range(0, rows, STEP):
+    for r in range(0, z_ref.shape[0], STEP):
         value = jnp.exp2((z_ref[r : r + STEP, :] - shift) * scale)
         total = total + value
         if keep is not None:
@@ -147,7 +148,7 @@
         ya_ref[k, :, width:] = ext
 
 
-def half_kernel(xt_ref, mx_ref, mine_ref, xa_ref, peak_ref, total_ref, z_ref):
+def half_kernel(xt_ref, mx_ref, mine_ref, xa_ref, rows_ref, yt_ref, peak_ref, total_ref, z_ref):
     rows, yd, depth = mine_ref.shape
     width, n = xt_ref.shape
     half = rows * yd
@@ -155,24 +156,26 @@
     mass = from_lanes(mx_ref[...].astype(F32))
     xa_ref[:width, :] = xt_ref[...]
     xa_ref[width:, :] = extras_x(rows_index(n), jnp.zeros((1, n), F32), mass).astype(BF16)
-    y_rows = mine_ref[...].reshape(half, depth)
+    mine = mine_ref[...].reshape(half, depth)
 
     def product(t):
-        return jnp.dot(y_rows, xa_ref[:, t], preferred_element_type=F32)
+        return jnp.dot(mine, xa_ref[:, t], preferred_element_type=F32)
 
     def use(t, z):
-        peak = max_down(z, half)
+        peak = max_down(z)
         peak_ref[:, t] = peak
-        total_ref[:, t] = exp_sum_down(z, half, scale, peak)
+        total_ref[:, t] = exp_sum_down(z, scale, peak)
 
     for_tiles(n, product, z_ref, use)
+    rows_ref[...] = xa_ref[...].T
+    yt_ref[...] = mine.T
 
 
 def first_kernel(
-    log_nx, xa0_ref, mine_ref, other_ref, peak_ref, total_ref,
-    yt_ref, b_ref, l_ref, m_ref, t_ref, xa_ref, ya_ref, z_ref, zc_ref, b2_ref,
+    log_nx, xa0_ref, rows0_ref, mine_ref, other_ref, peak_ref, total_ref,
+    yt_ref, b_ref, l_ref, m_ref, t_ref, z_ref, zc_ref, b2_ref,
 ):
-    rows, yd, depth = mine_ref.shape
+    rows, yd, depth = other_ref.shape
     n = xa0_ref.shape[1]
     width = depth - EXT
     half = rows * yd
@@ -180,26 +183,24 @@
     col = lax.axis_index("col")
     scale = kappa_of(width) * LOG2E
     other = other_ref[...].reshape(half, depth)
+    yt_ref[:, pl.ds(pl.multiple_of(col * half, half), half)] = mine_ref[...]
+    yt_ref[:, pl.ds(pl.multiple_of((1 - col) * half, half), half)] = other.T
 
     def product(t):
         return jnp.dot(other, xa0_ref[:, t], preferred_element_type=F32)
 
     def use(t, z):
         old = peak_ref[:, t]
-        peak = jnp.maximum(max_down(z, half), old)
-        total = exp_sum_down(z, half, scale, peak) + total_ref[:, t] * jnp.exp2((old - peak) * scale)
+        peak = jnp.maximum(max_down(z), old)
+        total = exp_sum_down(z, scale, peak) + total_ref[:, t] * jnp.exp2((old - peak) * scale)
         b_ref[:, t] = -peak - jnp.log(total) * (LOG2E / scale)
 
     for_tiles(n, product, z_ref, use)
-    ya_ref[pl.ds(pl.multiple_of(col * half, half), half), :] = mine_ref[...].reshape(half, depth)
-    ya_ref[pl.ds(pl.multiple_of((1 - col) * half, half), half), :] = other
-    yt_ref[...] = ya_ref[...].T
     mass = xa0_ref[width:, :].astype(F32)[7:8]
     b_term = b_ref[...] + (mass - log_nx) * (LOG2E / scale)
     b_ref[...] = b_term
-    xa_ref[:width, :] = xa0_ref[:width, :]
-    xa_ref[width:, :] = extras_x(rows_index(n), b_term, mass).astype(BF16)
-    x_rows = xa_ref[...].T
+    ext = extras_x(rows_index(n), b_term, mass).T.astype(BF16)
+    x_rows = jnp.concatenate([rows0_ref[:, :width], ext], axis=1)
 
     def product(t):
         return jnp.dot(x_rows, yt_ref[:, t], preferred_element_type=F32)
@@ -208,9 +209,9 @@
         def keep(r, value):
             t_ref[r : r + STEP, t] = value
 
-        peak = max_down(z, n)
+        peak = max_down(z)
         m_ref[:, t] = peak
-        b2_ref[:, t] = scale * peak + jnp.log(exp_sum_down(z, n, scale, peak, keep)) * LOG2E
+        b2_ref[:, t] = scale * peak + jnp.log(exp_sum_down(z, scale, peak, keep)) * LOG2E
 
     for_tiles(ny, product, zc_ref, use)
     lse = to_lanes(b2_ref[...])
@@ -413,8 +414,13 @@
     )
     y_mine = lax.all_to_all(y_own, "row", 0, 0, tiled=True)
     y_other = swap(y_mine)
-    xa, peak, total = call(
-        half_kernel, (shape((depth, n), BF16), shape((1, n)), shape((1, n))), [vmem((slots, half, TILE), F32)],
+    xa, x_rows, yt_mine, peak, total = call(
+        half_kernel,
+        (
+            shape((depth, n), BF16), shape((n, depth), BF16), shape((depth, half), BF16), shape((1, n)),
+            shape((1, n)),
+        ),
+        [vmem((slots, half, TILE), F32)],
         limit, points_x.T, mass_x.reshape(n // LANES, LANES), y_mine,
     )
     yt, b_term, lse, peak, plan = call(
@@ -423,11 +429,8 @@
             shape((depth, ny), BF16), shape((1, n)), shape((2 * rows, count, LANES)), shape((1, ny)),
             shape((n, ny), BF16),
         ),
-        [
-            vmem((depth, n), BF16), vmem((ny, depth), BF16), vmem((slots, half, TILE), F32),
-            vmem((slots, n, TILE), F32), vmem((1, ny), F32),
-        ],
-        limit, xa, y_mine, y_other, peak, total,
+        [vmem((slots, half, TILE), F32), vmem((slots, n, TILE), F32), vmem((1, ny), F32)],
+        limit, xa, x_rows, yt_mine, y_other, peak, total,
     )
     lse = lax.all_to_all(lse, AXES, 0, 0, tiled=True)
     r, v, c_term, xs, sums, send = call(

time: 43.5 us -> 43.9 us (level)
  transfers between devices with their start and end apart: 2 -> 2, of which waited for: 2 -> 2; matrix products, arithmetic and copies ran while one was open for 0% -> 0% of each run, Pallas kernels for 2% -> 3%
where the time goes in v10:
time: 43.9 us; the launch traced here: 43.6 us
  blocking collectives  33.9 us (77%)
  Pallas kernels  6.71 us (15%)
  waiting for transfers between devices  1.54 us (4%)
  local copies, waits for them, and re-layouts  0.71 us (2%)
  between operations  0.71 us (2%)
    all_to_all x1, blocking collectives, on_device(): y_mine = lax.all_to_all(y_own, 'row', 0, 0, tiled=True)  14.4 us
    all_to_all x1, blocking collectives, on_device(): part = lax.all_to_all(part, 'row', 0, 0, tiled=True)  9.97 us
    all_to_all x1, blocking collectives, on_device(): lse = lax.all_to_all(lse, AXES, 0, 0, tiled=True)  9.48 us
    pallas_call x8, Pallas kernels, call(): pl.pallas_call(kernel, out_shape=outs, in_specs=[pl.BlockSpec(memory_spac...  6.71 us
    ppermute x2, waiting for transfers between devices, swap(): return lax.ppermute(value, 'col', [(0, 1), (1, 0)])  1.54 us
  transfers between devices with their start and end apart: 2, of which 2 were waited for; matrix products, arithmetic and copies ran while one was open for 0% of the time, Pallas kernels for 3%

profile of v10, /device:TPU:0, one launch (start us, length us, event | category | flops | bytes accessed | tf_op | source)
XLA Modules:
  0.0 43.6 jit_solution(11610734541727244992)
XLA Ops:
  0.6 0.0 copy-start.3
  0.6 0.0 copy-start.2
  0.7 0.6 %copy-done.3 = bf16[64]{0:T(256)(128)(2,1)S(1)} copy-done((bf16[64]{0:T(256)(128)(2,1)S(1)}, bf16[64]{0:T(256)(128)(2,1)}, u32[]{:S(2)}) %copy-start.3) | copy-done | bytes 152
  1.3 0.1 copy-done.2
  1.4 0.0 copy-start
  1.4 0.0 copy-start.1
  1.4 0.2 shard_map.76.y_ref
  1.6 14.4 %all_to_all.15.mine_ref = bf16[8,64,128]{2,1,0:T(8,128)(2,1)S(1)} all-to-all(bf16[8,64,128]{2,1,0:T(8,128)(2,1)S(1)} %shard_map.76.y_ref), channel_id=1, replica_groups=mesh['groups'=2,'row'=8,'col'=2] {'row'}, dimensions={0} | all-to-all | bytes 262144 | tf_op jit(solution)/shard_map/all_to_all | solution.py:415
  16.0 0.0 collective-permute-start
  16.0 0.0 copy-done
  16.0 0.0 copy-done.1
  16.0 0.7 %shard_map.77 = (bf16[128,1024]{1,0:T(8,128)(2,1)S(1)}, bf16[1024,128]{1,0:T(8,128)(2,1)S(1)}, bf16[128,512]{1,0:T(8,128)(2,1)S(1)}, f32[1,1024]{1,0:T(1,128)S(1)}, f32[1,1024]{1,0:T(1,128)S(1)}) custom-call(bf16[96,1024]{1,0:T(8,128)(2,1)S(1)} %bitcast.6, bf16[8,128]{1,0:T(8,128)(2,1)S(1)} %bitcast.7, bf16[8,64,128]{2,1,0:T(8,128)(2,1)S(1)} %all_to_all.15.mine_ref), custom_call_target="tpu_custom_call" | custom-call | tf_op jit(solution)/shard_map/pallas_call | solution.py:374
  16.7 0.6 %collective-permute-done.other_ref = bf16[8,64,128]{2,1,0:T(8,128)(2,1)S(1)} collective-permute-done((bf16[8,64,128]{2,1,0:T(8,128)(2,1)S(1)}, bf16[8,64,128]{2,1,0:T(8,128)(2,1)S(1)}, u32[]{:S(2)}, u32[]{:S(2)}) %collective-permute-start) | collective-permute-done | bytes 131104 | tf_op jit(solution)/shard_map/ppermute | solution.py:390
  17.3 2.4 %shard_map.78 = (bf16[128,1024]{1,0:T(8,128)(2,1)S(1)}, f32[1,1024]{1,0:T(1,128)S(1)}, f32[16,8,128]{2,1,0:T(8,128)S(1)}, f32[1,1024]{1,0:T(1,128)S(1)}, bf16[1024,1024]{1,0:T(8,128)(2,1)S(1)}) custom-call(bf16[128,1024]{1,0:T(8,128)(2,1)S(1)} %get-tuple-element.26.xa0_ref.xa_ref, bf16[1024,128]{1,0:T(8,128)(2,1)S(1)} %get-tuple-element.27.rows0_ref, ...), custom_call_target="tpu_custom_call" | custom-call | tf_op jit(solution)/shard_map/pallas_call | solution.py:374
  19.7 9.5 %all_to_all.16.l_ref = f32[16,8,128]{2,1,0:T(8,128)S(1)} all-to-all(f32[16,8,128]{2,1,0:T(8,128)S(1)} %get-tuple-element.32), channel_id=1, replica_groups=mesh['groups'=2,'row'=8,'col'=2] {'row','col'}, dimensions={0} | all-to-all | bytes 131072 | tf_op jit(solution)/shard_map/all_to_all | solution.py:435
  29.2 1.2 %shard_map.79 = (f32[1,1024]{1,0:T(1,128)S(1)}, f32[1,1024]{1,0:T(1,128)S(1)}, f32[8,128]{1,0:T(8,128)S(1)}, bf16[208,1024]{1,0:T(8,128)(2,1)S(1)}, f32[1,1024]{1,0:T(1,128)S(1)}, /*index=5*/bf16[112,512]{1,0:T(8,128)(2,1)S(1)}) custom-call(bf16[128,1024]{1,0:T(8,128)(2,1)S(1)} %get-tuple-element.26.xa0_ref.xa_ref, f32[1,1024]{1,0:T(1,128)S(1)} %get-tuple-element.31.b_ref, ...), custom_call_target="tpu_custom_call" | custom-call | tf_op jit(solution)/shard_map/pallas_call | solution.py:374
  30.4 0.1 collective-permute-start.1
  30.4 0.4 shard_map.80
  30.9 0.9 %collective-permute-done.1.got_ref = bf16[112,512]{1,0:T(8,128)(2,1)S(1)} collective-permute-done((bf16[112,512]{1,0:T(8,128)(2,1)S(1)}, bf16[112,512]{1,0:T(8,128)(2,1)S(1)}, u32[]{:S(2)}, u32[]{:S(2)}) %collective-permute-start.1) | collective-permute-done | bytes 114720 | tf_op jit(solution)/shard_map/ppermute | solution.py:390
  31.8 0.3 shard_map.81
  32.0 10.0 %all_to_all.17.got_ref = bf16[8,64,128]{2,1,0:T(8,128)(2,1)S(1)} all-to-all(bf16[8,64,128]{2,1,0:T(8,128)(2,1)S(1)} %shard_map.81), channel_id=1, replica_groups=mesh['groups'=2,'row'=8,'col'=2] {'row'}, dimensions={0} | all-to-all | bytes 262144 | tf_op jit(solution)/shard_map/all_to_all | solution.py:451
  42.0 1.6 %shard_map.82 = (f32[1,1024]{1,0:T(1,128)}, f32[1,64]{1,0:T(1,128)}, f32[96,1024]{1,0:T(8,128)}, f32[64,96]{1,0:T(8,128)}) custom-call(bf16[128,1024]{1,0:T(8,128)(2,1)S(1)} %get-tuple-element.26.xa0_ref.xa_ref, f32[1,1024]{1,0:T(1,128)S(1)} %get-tuple-element.39.norm_ref, f32[1,1024]{1,0:T(1,128)S(1)} %get-tuple-element.31.b_ref, ...), custom_call_target="tpu_custom_call" | custom-call | tf_op jit(solution)/shard_map/pallas_call | solution.py:374
  (1 shorter events, 0.0 us)
Async XLA Ops:
  0.6 0.7 %copy-start.3 = (bf16[64]{0:T(256)(128)(2,1)S(1)}, bf16[64]{0:T(256)(128)(2,1)}, u32[]{:S(2)}) copy-start(bf16[64]{0:T(256)(128)(2,1)} %param.7) | copy-start | bytes 388
  0.6 0.7 %copy-start.2 = (bf16[64,96]{1,0:T(8,128)(2,1)S(1)}, bf16[64,96]{1,0:T(8,128)(2,1)}, u32[]{:S(2)}) copy-start(bf16[64,96]{1,0:T(8,128)(2,1)} %y_ref.1) | copy-start | bytes 36868
  1.4 14.6 %copy-start = (bf16[1024,96]{0,1:T(8,128)(2,1)S(1)}, bf16[1024,96]{0,1:T(8,128)(2,1)}, u32[]{:S(2)}) copy-start(bf16[1024,96]{0,1:T(8,128)(2,1)} %param.4) | copy-start | bytes 589828
  1.4 14.6 %copy-start.1 = (bf16[1024]{0:T(1024)(128)(2,1)S(1)}, bf16[1024]{0:T(1024)(128)(2,1)}, u32[]{:S(2)}) copy-start(bf16[1024]{0:T(1024)(128)(2,1)} %param.6) | copy-start | bytes 6148
  16.0 1.3 %collective-permute-start = (bf16[8,64,128]{2,1,0:T(8,128)(2,1)S(1)}, bf16[8,64,128]{2,1,0:T(8,128)(2,1)S(1)}, u32[]{:S(2)}, u32[]{:S(2)}) collective-permute-start(bf16[8,64,128]{2,1,0:T(8,128)(2,1)S(1)} %all_to_all.15.mine_ref), channel_id=1, source_target_pairs={{0,1},{1,0},{2,3},{3,2},{4,5},{5,4},{6,7},{7,6},{8,9},{9,8},{10,11... | collective-permute-start | bytes 393224 | tf_op jit(solution)/shard_map/ppermute | solution.py:390
  30.4 1.4 %collective-permute-start.1 = (bf16[112,512]{1,0:T(8,128)(2,1)S(1)}, bf16[112,512]{1,0:T(8,128)(2,1)S(1)}, u32[]{:S(2)}, u32[]{:S(2)}) collective-permute-start(bf16[112,512]{1,0:T(8,128)(2,1)S(1)} %get-tuple-element.43), channel_id=1, source_target_pairs={{0,1},{1,0},{2,3},{3,2},{4,5},{5,4},{6,7},{7,6},{8,9},{9,8},{10,11... | collective-permute-start | bytes 344072 | tf_op jit(solution)/shard_map/ppermute | solution.py:390

commit v11 on v9

--- a/solution.py
+++ b/solution.py
@@ -12,8 +12,6 @@
 EPSILON = 0.02
 LOG2E = math.log2(math.e)
 TILE = 256
-STEP = 8
-WIDE = 1024
 EXT = 32
 PAD = 16
 LANES = 128
@@ -61,20 +59,16 @@
     return jnp.sum(jnp.where(eye, column, 0.0), axis=0, keepdims=True)
 
 
-def max_down(z_ref):
-    rows, columns = z_ref.shape
-    peak = z_ref[0:STEP, :]
-    for r in range(STEP, rows, STEP):
-        peak = jnp.maximum(peak, z_ref[r : r + STEP, :])
-    return jnp.max(peak, axis=0, keepdims=True)
-
-
-def exp_sum_down(z_ref, scale, shift):
-    rows, columns = z_ref.shape
-    total = jnp.zeros((STEP, columns), F32)
-    for r in range(0, rows, STEP):
-        total = total + jnp.exp2((z_ref[r : r + STEP, :] - shift) * scale)
-    return jnp.sum(total, axis=0, keepdims=True)
+def for_tiles(total, body):
+    count = total // TILE
+    if count <= 4:
+        for t in range(count):
+            body(pl.ds(t * TILE, TILE))
+    else:
+
+        @pl.loop(0, count)
+        def _(t):
+            body(pl.ds(pl.multiple_of(t * TILE, TILE), TILE))
 
 
 def to_lanes(row):
@@ -130,7 +124,7 @@
         ya_ref[k, :, width:] = ext
 
 
-def half_kernel(xt_ref, mx_ref, mine_ref, xa_ref, rows_ref, yt_ref, peak_ref, total_ref, z_ref):
+def half_kernel(xt_ref, mx_ref, mine_ref, xa_ref, yt_ref, peak_ref, total_ref):
     rows, yd, depth = mine_ref.shape
     width, n = xt_ref.shape
     half = rows * yd
@@ -139,17 +133,20 @@
     xa_ref[:width, :] = xt_ref[...]
     xa_ref[width:, :] = extras_x(rows_index(n), jnp.zeros((1, n), F32), mass).astype(BF16)
     mine = mine_ref[...].reshape(half, depth)
-    z_ref[...] = jnp.dot(mine, xa_ref[...], preferred_element_type=F32)
-    peak = max_down(z_ref)
-    peak_ref[...] = peak
-    total_ref[...] = exp_sum_down(z_ref, scale, peak)
-    rows_ref[...] = xa_ref[...].T
+
+    def row_tile(t):
+        z = jnp.dot(mine, xa_ref[:, t], preferred_element_type=F32)
+        peak = jnp.max(z, axis=0, keepdims=True)
+        peak_ref[:, t] = peak
+        total_ref[:, t] = jnp.sum(jnp.exp2((z - peak) * scale), axis=0, keepdims=True)
+
+    for_tiles(n, row_tile)
     yt_ref[...] = mine.T
 
 
 def first_kernel(
-    log_nx, xa0_ref, rows0_ref, mine_ref, other_ref, peak_ref, total_ref,
-    yt_ref, b_ref, l_ref, m_ref, t_ref, z_ref, zc_ref, b2_ref,
+    log_nx, xa0_ref, mine_ref, other_ref, peak_ref, total_ref,
+    yt_ref, b_ref, l_ref, m_ref, t_ref, xa_ref, b2_ref,
 ):
     rows, yd, depth = other_ref.shape
     n = xa0_ref.shape[1]
@@ -159,39 +156,34 @@
     col = lax.axis_index("col")
     scale = kappa_of(width) * LOG2E
     other = other_ref[...].reshape(half, depth)
-    z_ref[...] = jnp.dot(other, xa0_ref[...], preferred_element_type=F32)
     yt_ref[:, pl.ds(pl.multiple_of(col * half, half), half)] = mine_ref[...]
     yt_ref[:, pl.ds(pl.multiple_of((1 - col) * half, half), half)] = other.T
-    old = peak_ref[...]
-    peak = jnp.maximum(max_down(z_ref), old)
-    total = exp_sum_down(z_ref, scale, peak) + total_ref[...] * jnp.exp2((old - peak) * scale)
+
+    def row_tile(t):
+        z = jnp.dot(other, xa0_ref[:, t], preferred_element_type=F32)
+        old = peak_ref[:, t]
+        peak = jnp.maximum(jnp.max(z, axis=0, keepdims=True), old)
+        total = jnp.sum(jnp.exp2((z - peak) * scale), axis=0, keepdims=True)
+        total = total + total_ref[:, t] * jnp.exp2((old - peak) * scale)
+        b_ref[:, t] = -peak - jnp.log(total) * (LOG2E / scale)
+
+    for_tiles(n, row_tile)
     mass = xa0_ref[width:, :].astype(F32)[7:8]
-    b_term = -peak + (mass - log_nx - jnp.log(total)) * (LOG2E / scale)
+    b_term = b_ref[...] + (mass - log_nx) * (LOG2E / scale)
     b_ref[...] = b_term
-    ext = extras_x(rows_index(n), b_term, mass).T.astype(BF16)
-    x_rows = jnp.concatenate([rows0_ref[:, :width], ext], axis=1)
-    wide = min(WIDE, ny)
-
-    def columns(t):
-        zc_ref[...] = jnp.dot(x_rows, yt_ref[:, t], preferred_element_type=F32)
-        peak = max_down(zc_ref)
+    xa_ref[:width, :] = xa0_ref[:width, :]
+    xa_ref[width:, :] = extras_x(rows_index(n), b_term, mass).astype(BF16)
+    x_rows = xa_ref[...].T
+
+    def col_tile(t):
+        z = jnp.dot(x_rows, yt_ref[:, t], preferred_element_type=F32)
+        peak = jnp.max(z, axis=0, keepdims=True)
         m_ref[:, t] = peak
-        total = jnp.zeros((2 * STEP, wide), F32)
-        for r in range(0, n, 2 * STEP):
-            value = jnp.exp2((zc_ref[r : r + 2 * STEP, :] - peak) * scale)
-            total = total + value
-            t_ref[r : r + 2 * STEP, t] = value.astype(BF16)
-        total = jnp.sum(total, axis=0, keepdims=True)
-        b2_ref[:, t] = scale * peak + jnp.log(total) * LOG2E
-
-    if ny == wide:
-        columns(slice(0, ny))
-    else:
-
-        @pl.loop(0, ny // wide)
-        def _(t):
-            columns(pl.ds(pl.multiple_of(t * wide, wide), wide))
-
+        value = jnp.exp2((z - peak) * scale)
+        t_ref[:, t] = value.astype(BF16)
+        b2_ref[:, t] = scale * peak + jnp.log(jnp.sum(value, axis=0, keepdims=True)) * LOG2E
+
+    for_tiles(ny, col_tile)
     lse = to_lanes(b2_ref[...])
     for k in range(2 * rows):
         l_ref[k] = lse
@@ -391,13 +383,12 @@
     )
     y_mine = lax.all_to_all(y_own, "row", 0, 0, tiled=True)
     y_other = swap(y_mine)
-    xa, x_rows, yt_mine, peak, total = call(
+    xa, yt_mine, peak, total = call(
         half_kernel,
         (
-            shape((depth, n), BF16), shape((n, depth), BF16), shape((depth, half), BF16), shape((1, n)),
-            shape((1, n)),
+            shape((depth, n), BF16), shape((depth, half), BF16), shape((1, n)), shape((1, n)),
         ),
-        [vmem((half, n), F32)],
+        [],
         limit, points_x.T, mass_x.reshape(n // LANES, LANES), y_mine,
     )
     yt, b_term, lse, peak, plan = call(
@@ -406,8 +397,8 @@
             shape((depth, ny), BF16), shape((1, n)), shape((2 * rows, count, LANES)), shape((1, ny)),
             shape((n, ny), BF16),
         ),
-        [vmem((half, n), F32), vmem((n, min(WIDE, ny)), F32), vmem((1, ny), F32)],
-        limit, xa, x_rows, yt_mine, y_other, peak, total,
+        [vmem((depth, n), BF16), vmem((1, ny), F32)],
+        limit, xa, yt_mine, y_other, peak, total,
     )
     lse = lax.all_to_all(lse, AXES, 0, 0, tiled=True)
     r, v, c_term, xs, sums, send = call(

time: 43.9 us -> 44 us (level)
  no operation moved by 1% of the time
where the time goes in v11:
time: 44 us; the launch traced here: 43.7 us
  blocking collectives  33.9 us (77%)
  Pallas kernels  6.81 us (15%)
  waiting for transfers between devices  1.5 us (3%)
  local copies, waits for them, and re-layouts  0.71 us (2%)
  between operations  0.71 us (2%)
    all_to_all x1, blocking collectives, on_device(): y_mine = lax.all_to_all(y_own, 'row', 0, 0, tiled=True)  14.4 us
    all_to_all x1, blocking collectives, on_device(): part = lax.all_to_all(part, 'row', 0, 0, tiled=True)  9.97 us
    all_to_all x1, blocking collectives, on_device(): lse = lax.all_to_all(lse, AXES, 0, 0, tiled=True)  9.48 us
    pallas_call x8, Pallas kernels, call(): pl.pallas_call(kernel, out_shape=outs, in_specs=[pl.BlockSpec(memory_spac...  6.81 us
    ppermute x2, waiting for transfers between devices, swap(): return lax.ppermute(value, 'col', [(0, 1), (1, 0)])  1.5 us
  transfers between devices with their start and end apart: 2, of which 2 were waited for; matrix products, arithmetic and copies ran while one was open for 0% of the time, Pallas kernels for 3%

profile of v11, /device:TPU:0, one launch (start us, length us, event | category | flops | bytes accessed | tf_op | source)
XLA Modules:
  0.0 43.7 jit_solution(1908303521962843)
XLA Ops:
  0.6 0.0 copy-start.3
  0.6 0.0 copy-start.2
  0.7 0.6 %copy-done.3 = bf16[64]{0:T(256)(128)(2,1)S(1)} copy-done((bf16[64]{0:T(256)(128)(2,1)S(1)}, bf16[64]{0:T(256)(128)(2,1)}, u32[]{:S(2)}) %copy-start.3) | copy-done | bytes 152
  1.3 0.1 copy-done.2
  1.4 0.0 copy-start
  1.4 0.0 copy-start.1
  1.4 0.2 shard_map.76.y_ref
  1.6 14.4 %all_to_all.15.mine_ref = bf16[8,64,128]{2,1,0:T(8,128)(2,1)S(1)} all-to-all(bf16[8,64,128]{2,1,0:T(8,128)(2,1)S(1)} %shard_map.76.y_ref), channel_id=1, replica_groups=mesh['groups'=2,'row'=8,'col'=2] {'row'}, dimensions={0} | all-to-all | bytes 262144 | tf_op jit(solution)/shard_map/all_to_all | solution.py:384
  16.0 0.0 collective-permute-start
  16.0 0.0 copy-done
  16.0 0.0 copy-done.1
  16.0 0.7 %shard_map.77 = (bf16[128,1024]{1,0:T(8,128)(2,1)S(1)}, bf16[128,512]{1,0:T(8,128)(2,1)S(1)}, f32[1,1024]{1,0:T(1,128)S(1)}, f32[1,1024]{1,0:T(1,128)S(1)}) custom-call(bf16[96,1024]{1,0:T(8,128)(2,1)S(1)} %bitcast.6, bf16[8,128]{1,0:T(8,128)(2,1)S(1)} %bitcast.7, bf16[8,64,128]{2,1,0:T(8,128)(2,1)S(1)} %all_to_all.15.mine_ref), custom_call_target="tpu_custom_call" | custom-call | tf_op jit(solution)/shard_map/pallas_call | solution.py:344
  16.7 0.6 %collective-permute-done.other_ref = bf16[8,64,128]{2,1,0:T(8,128)(2,1)S(1)} collective-permute-done((bf16[8,64,128]{2,1,0:T(8,128)(2,1)S(1)}, bf16[8,64,128]{2,1,0:T(8,128)(2,1)S(1)}, u32[]{:S(2)}, u32[]{:S(2)}) %collective-permute-start) | collective-permute-done | bytes 131104 | tf_op jit(solution)/shard_map/ppermute | solution.py:360
  17.3 2.4 %shard_map.78 = (bf16[128,1024]{1,0:T(8,128)(2,1)S(1)}, f32[1,1024]{1,0:T(1,128)S(1)}, f32[16,8,128]{2,1,0:T(8,128)S(1)}, f32[1,1024]{1,0:T(1,128)S(1)}, bf16[1024,1024]{1,0:T(8,128)(2,1)S(1)}) custom-call(bf16[128,1024]{1,0:T(8,128)(2,1)S(1)} %get-tuple-element.25.xa0_ref.xa_ref, bf16[128,512]{1,0:T(8,128)(2,1)S(1)} %get-tuple-element.26.mine_ref, ...), custom_call_target="tpu_custom_call" | custom-call | tf_op jit(solution)/shard_map/pallas_call | solution.py:344
  19.8 9.5 %all_to_all.16.l_ref = f32[16,8,128]{2,1,0:T(8,128)S(1)} all-to-all(f32[16,8,128]{2,1,0:T(8,128)S(1)} %get-tuple-element.30), channel_id=1, replica_groups=mesh['groups'=2,'row'=8,'col'=2] {'row','col'}, dimensions={0} | all-to-all | bytes 131072 | tf_op jit(solution)/shard_map/all_to_all | solution.py:403
  29.2 1.2 %shard_map.79 = (f32[1,1024]{1,0:T(1,128)S(1)}, f32[1,1024]{1,0:T(1,128)S(1)}, f32[8,128]{1,0:T(8,128)S(1)}, bf16[208,1024]{1,0:T(8,128)(2,1)S(1)}, f32[1,1024]{1,0:T(1,128)S(1)}, /*index=5*/bf16[112,512]{1,0:T(8,128)(2,1)S(1)}) custom-call(bf16[128,1024]{1,0:T(8,128)(2,1)S(1)} %get-tuple-element.25.xa0_ref.xa_ref, f32[1,1024]{1,0:T(1,128)S(1)} %get-tuple-element.29.b_ref, ...), custom_call_target="tpu_custom_call" | custom-call | tf_op jit(solution)/shard_map/pallas_call | solution.py:344
  30.4 0.1 collective-permute-start.1
  30.5 0.4 shard_map.80
  30.9 0.9 %collective-permute-done.1.got_ref = bf16[112,512]{1,0:T(8,128)(2,1)S(1)} collective-permute-done((bf16[112,512]{1,0:T(8,128)(2,1)S(1)}, bf16[112,512]{1,0:T(8,128)(2,1)S(1)}, u32[]{:S(2)}, u32[]{:S(2)}) %collective-permute-start.1) | collective-permute-done | bytes 114720 | tf_op jit(solution)/shard_map/ppermute | solution.py:360
  31.8 0.3 shard_map.81
  32.1 10.0 %all_to_all.17.got_ref = bf16[8,64,128]{2,1,0:T(8,128)(2,1)S(1)} all-to-all(bf16[8,64,128]{2,1,0:T(8,128)(2,1)S(1)} %shard_map.81), channel_id=1, replica_groups=mesh['groups'=2,'row'=8,'col'=2] {'row'}, dimensions={0} | all-to-all | bytes 262144 | tf_op jit(solution)/shard_map/all_to_all | solution.py:419
  42.0 1.6 %shard_map.82 = (f32[1,1024]{1,0:T(1,128)}, f32[1,64]{1,0:T(1,128)}, f32[96,1024]{1,0:T(8,128)}, f32[64,96]{1,0:T(8,128)}) custom-call(bf16[128,1024]{1,0:T(8,128)(2,1)S(1)} %get-tuple-element.25.xa0_ref.xa_ref, f32[1,1024]{1,0:T(1,128)S(1)} %get-tuple-element.37.norm_ref, f32[1,1024]{1,0:T(1,128)S(1)} %get-tuple-element.29.b_ref, ...), custom_call_target="tpu_custom_call" | custom-call | tf_op jit(solution)/shard_map/pallas_call | solution.py:344
  (1 shorter events, 0.0 us)
Async XLA Ops:
  0.6 0.7 %copy-start.3 = (bf16[64]{0:T(256)(128)(2,1)S(1)}, bf16[64]{0:T(256)(128)(2,1)}, u32[]{:S(2)}) copy-start(bf16[64]{0:T(256)(128)(2,1)} %param.7) | copy-start | bytes 388
  0.6 0.7 %copy-start.2 = (bf16[64,96]{1,0:T(8,128)(2,1)S(1)}, bf16[64,96]{1,0:T(8,128)(2,1)}, u32[]{:S(2)}) copy-start(bf16[64,96]{1,0:T(8,128)(2,1)} %y_ref.1) | copy-start | bytes 36868
  1.4 14.6 %copy-start = (bf16[1024,96]{0,1:T(8,128)(2,1)S(1)}, bf16[1024,96]{0,1:T(8,128)(2,1)}, u32[]{:S(2)}) copy-start(bf16[1024,96]{0,1:T(8,128)(2,1)} %param.4) | copy-start | bytes 589828
  1.4 14.6 %copy-start.1 = (bf16[1024]{0:T(1024)(128)(2,1)S(1)}, bf16[1024]{0:T(1024)(128)(2,1)}, u32[]{:S(2)}) copy-start(bf16[1024]{0:T(1024)(128)(2,1)} %param.6) | copy-start | bytes 6148
  16.0 1.3 %collective-permute-start = (bf16[8,64,128]{2,1,0:T(8,128)(2,1)S(1)}, bf16[8,64,128]{2,1,0:T(8,128)(2,1)S(1)}, u32[]{:S(2)}, u32[]{:S(2)}) collective-permute-start(bf16[8,64,128]{2,1,0:T(8,128)(2,1)S(1)} %all_to_all.15.mine_ref), channel_id=1, source_target_pairs={{0,1},{1,0},{2,3},{3,2},{4,5},{5,4},{6,7},{7,6},{8,9},{9,8},{10,11... | collective-permute-start | bytes 393224 | tf_op jit(solution)/shard_map/ppermute | solution.py:360
  30.4 1.4 %collective-permute-start.1 = (bf16[112,512]{1,0:T(8,128)(2,1)S(1)}, bf16[112,512]{1,0:T(8,128)(2,1)S(1)}, u32[]{:S(2)}, u32[]{:S(2)}) collective-permute-start(bf16[112,512]{1,0:T(8,128)(2,1)S(1)} %get-tuple-element.41), channel_id=1, source_target_pairs={{0,1},{1,0},{2,3},{3,2},{4,5},{5,4},{6,7},{7,6},{8,9},{9,8},{10,11... | collective-permute-start | bytes 344072 | tf_op jit(solution)/shard_map/ppermute | solution.py:360

commit v12 on v9

--- a/solution.py
+++ b/solution.py
@@ -130,7 +130,7 @@
         ya_ref[k, :, width:] = ext
 
 
-def half_kernel(xt_ref, mx_ref, mine_ref, xa_ref, rows_ref, yt_ref, peak_ref, total_ref, z_ref):
+def half_kernel(xt_ref, mx_ref, mine_ref, xa_ref, yt_ref, peak_ref, total_ref, z_ref):
     rows, yd, depth = mine_ref.shape
     width, n = xt_ref.shape
     half = rows * yd
@@ -143,33 +143,53 @@
     peak = max_down(z_ref)
     peak_ref[...] = peak
     total_ref[...] = exp_sum_down(z_ref, scale, peak)
-    rows_ref[...] = xa_ref[...].T
     yt_ref[...] = mine.T
 
 
+def by_core(half, body):
+    halves = (slice(0, half), slice(half, 2 * half))
+    col = lax.axis_index("col")
+
+    @pl.when(col == 0)
+    def _():
+        body(halves[0], halves[1])
+
+    @pl.when(col == 1)
+    def _():
+        body(halves[1], halves[0])
+
+
+def tiles_of(part):
+    return [slice(k, k + TILE) for k in range(part.start, part.stop, TILE)]
+
+
 def first_kernel(
-    log_nx, xa0_ref, rows0_ref, mine_ref, other_ref, peak_ref, total_ref,
-    yt_ref, b_ref, l_ref, m_ref, t_ref, z_ref, zc_ref, b2_ref,
+    log_nx, xa0_ref, mine_ref, other_ref, peak_ref, total_ref,
+    yt_ref, b_ref, l_ref, m_ref, t_ref, xa_ref, z_ref, zc_ref, b2_ref,
 ):
     rows, yd, depth = other_ref.shape
     n = xa0_ref.shape[1]
     width = depth - EXT
     half = rows * yd
     ny = 2 * half
-    col = lax.axis_index("col")
     scale = kappa_of(width) * LOG2E
     other = other_ref[...].reshape(half, depth)
     z_ref[...] = jnp.dot(other, xa0_ref[...], preferred_element_type=F32)
-    yt_ref[:, pl.ds(pl.multiple_of(col * half, half), half)] = mine_ref[...]
-    yt_ref[:, pl.ds(pl.multiple_of((1 - col) * half, half), half)] = other.T
+
+    def place(mine, theirs):
+        yt_ref[:, mine] = mine_ref[...]
+        yt_ref[:, theirs] = other.T
+
+    by_core(half, place)
     old = peak_ref[...]
     peak = jnp.maximum(max_down(z_ref), old)
     total = exp_sum_down(z_ref, scale, peak) + total_ref[...] * jnp.exp2((old - peak) * scale)
     mass = xa0_ref[width:, :].astype(F32)[7:8]
     b_term = -peak + (mass - log_nx - jnp.log(total)) * (LOG2E / scale)
     b_ref[...] = b_term
-    ext = extras_x(rows_index(n), b_term, mass).T.astype(BF16)
-    x_rows = jnp.concatenate([rows0_ref[:, :width], ext], axis=1)
+    xa_ref[:width, :] = xa0_ref[:width, :]
+    xa_ref[width:, :] = extras_x(rows_index(n), b_term, mass).astype(BF16)
+    x_rows = xa_ref[...].T
     wide = min(WIDE, ny)
 
     def columns(t):
@@ -241,18 +261,20 @@
     r = jnp.exp(mass - log_nx) / rowsum
     r_ref[...] = r
     stack(xs_ref, width, xa_ref[:width, :], r)
-    col = lax.axis_index("col")
-    for k in range(half // TILE):
-        t = pl.ds(pl.multiple_of((1 - col) * half + k * TILE, TILE), TILE)
-        product = jnp.dot(xs_ref[...], t_ref[:, t], preferred_element_type=F32)
-        moment, total = unstack(product, width)
-        total = total * v_ref[:, t]
-        sum_ref[:, t] = total
-        part = yt_ref[:width, t].astype(F32) * total - moment * v_ref[:, t]
-        send_ref[:width, k * TILE : (k + 1) * TILE] = part.astype(BF16)
-        t = pl.ds(pl.multiple_of(col * half + k * TILE, TILE), TILE)
-        ext = jnp.dot(xs_ref[2 * width :, :], t_ref[:, t], preferred_element_type=F32)
-        sum_ref[:, t] = ((ext[0:1] + ext[1:2]) + ext[2:3]) * v_ref[:, t]
+
+    def products(mine, theirs):
+        for t in tiles_of(theirs):
+            product = jnp.dot(xs_ref[...], t_ref[:, t], preferred_element_type=F32)
+            moment, total = unstack(product, width)
+            total = total * v[:, t]
+            sum_ref[:, t] = total
+            part = yt_ref[:width, t].astype(F32) * total - moment * v[:, t]
+            send_ref[:width, t.start - theirs.start : t.stop - theirs.start] = part.astype(BF16)
+        for t in tiles_of(mine):
+            ext = jnp.dot(xs_ref[2 * width :, :], t_ref[:, t], preferred_element_type=F32)
+            sum_ref[:, t] = ((ext[0:1] + ext[1:2]) + ext[2:3]) * v[:, t]
+
+    by_core(half, products)
     sums = sum_ref[...]
     high = sums.astype(BF16).astype(F32)
     low = sums - high
@@ -263,13 +285,15 @@
 
 def keep_kernel(xa_ref, xs_ref, v_ref, sum_ref, yt_ref, t_ref, keep_ref, norm_ref):
     width, half = keep_ref.shape
-    col = lax.axis_index("col")
-    for k in range(half // TILE):
-        t = pl.ds(pl.multiple_of(col * half + k * TILE, TILE), TILE)
-        product = jnp.dot(xs_ref[: 2 * width, :], t_ref[:, t], preferred_element_type=F32)
-        moment = product[:width] + product[width:]
-        part = yt_ref[:width, t].astype(F32) * sum_ref[:, t] - moment * v_ref[:, t]
-        keep_ref[:, k * TILE : (k + 1) * TILE] = part
+
+    def products(mine, theirs):
+        for t in tiles_of(mine):
+            product = jnp.dot(xs_ref[: 2 * width, :], t_ref[:, t], preferred_element_type=F32)
+            moment = product[:width] + product[width:]
+            part = yt_ref[:width, t].astype(F32) * sum_ref[:, t] - moment * v_ref[:, t]
+            keep_ref[:, t.start - mine.start : t.stop - mine.start] = part
+
+    by_core(half, products)
     xf = xa_ref[:width, :].astype(F32)
     norm_ref[...] = jnp.sum(xf * xf, axis=0, keepdims=True)
 
@@ -391,11 +415,10 @@
     )
     y_mine = lax.all_to_all(y_own, "row", 0, 0, tiled=True)
     y_other = swap(y_mine)
-    xa, x_rows, yt_mine, peak, total = call(
+    xa, yt_mine, peak, total = call(
         half_kernel,
         (
-            shape((depth, n), BF16), shape((n, depth), BF16), shape((depth, half), BF16), shape((1, n)),
-            shape((1, n)),
+            shape((depth, n), BF16), shape((depth, half), BF16), shape((1, n)), shape((1, n)),
         ),
         [vmem((half, n), F32)],
         limit, points_x.T, mass_x.reshape(n // LANES, LANES), y_mine,
@@ -406,8 +429,8 @@
             shape((depth, ny), BF16), shape((1, n)), shape((2 * rows, count, LANES)), shape((1, ny)),
             shape((n, ny), BF16),
         ),
-        [vmem((half, n), F32), vmem((n, min(WIDE, ny)), F32), vmem((1, ny), F32)],
-        limit, xa, x_rows, yt_mine, y_other, peak, total,
+        [vmem((depth, n), BF16), vmem((half, n), F32), vmem((n, min(WIDE, ny)), F32), vmem((1, ny), F32)],
+        limit, xa, yt_mine, y_other, peak, total,
     )
     lse = lax.all_to_all(lse, AXES, 0, 0, tiled=True)
     r, v, c_term, xs, sums, send = call(

time: 43.9 us -> 43.7 us (level)
  no operation moved by 1% of the time
where the time goes in v12:
time: 43.7 us; the launch traced here: 43.5 us
  blocking collectives  33.9 us (78%)
  Pallas kernels  6.58 us (15%)
  waiting for transfers between devices  1.51 us (3%)
  local copies, waits for them, and re-layouts  0.71 us (2%)
  between operations  0.71 us (2%)
    all_to_all x1, blocking collectives, on_device(): y_mine = lax.all_to_all(y_own, 'row', 0, 0, tiled=True)  14.4 us
    all_to_all x1, blocking collectives, on_device(): part = lax.all_to_all(part, 'row', 0, 0, tiled=True)  9.97 us
    all_to_all x1, blocking collectives, on_device(): lse = lax.all_to_all(lse, AXES, 0, 0, tiled=True)  9.48 us
    pallas_call x8, Pallas kernels, call(): pl.pallas_call(kernel, out_shape=outs, in_specs=[pl.BlockSpec(memory_spac...  6.58 us
    ppermute x2, waiting for transfers between devices, swap(): return lax.ppermute(value, 'col', [(0, 1), (1, 0)])  1.51 us
  transfers between devices with their start and end apart: 2, of which 2 were waited for; matrix products, arithmetic and copies ran while one was open for 0% of the time, Pallas kernels for 3%

profile of v12, /device:TPU:0, one launch (start us, length us, event | category | flops | bytes accessed | tf_op | source)
XLA Modules:
  0.0 43.5 jit_solution(2929443622982916436)
XLA Ops:
  0.6 0.0 copy-start.3
  0.6 0.0 copy-start.2
  0.7 0.6 %copy-done.3 = bf16[64]{0:T(256)(128)(2,1)S(1)} copy-done((bf16[64]{0:T(256)(128)(2,1)S(1)}, bf16[64]{0:T(256)(128)(2,1)}, u32[]{:S(2)}) %copy-start.3) | copy-done | bytes 152
  1.3 0.1 copy-done.2
  1.4 0.0 copy-start
  1.4 0.0 copy-start.1
  1.4 0.2 shard_map.76.y_ref
  1.6 14.4 %all_to_all.15.mine_ref = bf16[8,64,128]{2,1,0:T(8,128)(2,1)S(1)} all-to-all(bf16[8,64,128]{2,1,0:T(8,128)(2,1)S(1)} %shard_map.76.y_ref), channel_id=1, replica_groups=mesh['groups'=2,'row'=8,'col'=2] {'row'}, dimensions={0} | all-to-all | bytes 262144 | tf_op jit(solution)/shard_map/all_to_all | solution.py:416
  16.0 0.0 collective-permute-start
  16.0 0.0 copy-done
  16.0 0.0 copy-done.1
  16.0 0.7 %shard_map.77 = (bf16[128,1024]{1,0:T(8,128)(2,1)S(1)}, bf16[128,512]{1,0:T(8,128)(2,1)S(1)}, f32[1,1024]{1,0:T(1,128)S(1)}, f32[1,1024]{1,0:T(1,128)S(1)}) custom-call(bf16[96,1024]{1,0:T(8,128)(2,1)S(1)} %bitcast.6, bf16[8,128]{1,0:T(8,128)(2,1)S(1)} %bitcast.7, bf16[8,64,128]{2,1,0:T(8,128)(2,1)S(1)} %all_to_all.15.mine_ref), custom_call_target="tpu_custom_call" | custom-call | tf_op jit(solution)/shard_map/pallas_call | solution.py:376
  16.7 0.6 %collective-permute-done.other_ref = bf16[8,64,128]{2,1,0:T(8,128)(2,1)S(1)} collective-permute-done((bf16[8,64,128]{2,1,0:T(8,128)(2,1)S(1)}, bf16[8,64,128]{2,1,0:T(8,128)(2,1)S(1)}, u32[]{:S(2)}, u32[]{:S(2)}) %collective-permute-start) | collective-permute-done | bytes 131104 | tf_op jit(solution)/shard_map/ppermute | solution.py:392
  17.3 2.1 %shard_map.78 = (bf16[128,1024]{1,0:T(8,128)(2,1)S(1)}, f32[1,1024]{1,0:T(1,128)S(1)}, f32[16,8,128]{2,1,0:T(8,128)S(1)}, f32[1,1024]{1,0:T(1,128)S(1)}, bf16[1024,1024]{1,0:T(8,128)(2,1)S(1)}) custom-call(bf16[128,1024]{1,0:T(8,128)(2,1)S(1)} %get-tuple-element.25.xa0_ref.xa_ref, bf16[128,512]{1,0:T(8,128)(2,1)S(1)} %get-tuple-element.26.mine_ref, ...), custom_call_target="tpu_custom_call" | custom-call | tf_op jit(solution)/shard_map/pallas_call | solution.py:376
  19.4 9.5 %all_to_all.16.l_ref = f32[16,8,128]{2,1,0:T(8,128)S(1)} all-to-all(f32[16,8,128]{2,1,0:T(8,128)S(1)} %get-tuple-element.30), channel_id=1, replica_groups=mesh['groups'=2,'row'=8,'col'=2] {'row','col'}, dimensions={0} | all-to-all | bytes 131072 | tf_op jit(solution)/shard_map/all_to_all | solution.py:435
  28.9 1.3 %shard_map.79 = (f32[1,1024]{1,0:T(1,128)S(1)}, f32[1,1024]{1,0:T(1,128)S(1)}, f32[8,128]{1,0:T(8,128)S(1)}, bf16[208,1024]{1,0:T(8,128)(2,1)S(1)}, f32[1,1024]{1,0:T(1,128)S(1)}, /*index=5*/bf16[112,512]{1,0:T(8,128)(2,1)S(1)}) custom-call(bf16[128,1024]{1,0:T(8,128)(2,1)S(1)} %get-tuple-element.25.xa0_ref.xa_ref, f32[1,1024]{1,0:T(1,128)S(1)} %get-tuple-element.29.b_ref, ...), custom_call_target="tpu_custom_call" | custom-call | tf_op jit(solution)/shard_map/pallas_call | solution.py:376
  30.2 0.1 collective-permute-start.1
  30.3 0.4 shard_map.80
  30.7 0.9 %collective-permute-done.1.got_ref = bf16[112,512]{1,0:T(8,128)(2,1)S(1)} collective-permute-done((bf16[112,512]{1,0:T(8,128)(2,1)S(1)}, bf16[112,512]{1,0:T(8,128)(2,1)S(1)}, u32[]{:S(2)}, u32[]{:S(2)}) %collective-permute-start.1) | collective-permute-done | bytes 114720 | tf_op jit(solution)/shard_map/ppermute | solution.py:392
  31.6 0.3 shard_map.81
  31.9 10.0 %all_to_all.17.got_ref = bf16[8,64,128]{2,1,0:T(8,128)(2,1)S(1)} all-to-all(bf16[8,64,128]{2,1,0:T(8,128)(2,1)S(1)} %shard_map.81), channel_id=1, replica_groups=mesh['groups'=2,'row'=8,'col'=2] {'row'}, dimensions={0} | all-to-all | bytes 262144 | tf_op jit(solution)/shard_map/all_to_all | solution.py:451
  41.8 1.6 %shard_map.82 = (f32[1,1024]{1,0:T(1,128)}, f32[1,64]{1,0:T(1,128)}, f32[96,1024]{1,0:T(8,128)}, f32[64,96]{1,0:T(8,128)}) custom-call(bf16[128,1024]{1,0:T(8,128)(2,1)S(1)} %get-tuple-element.25.xa0_ref.xa_ref, f32[1,1024]{1,0:T(1,128)S(1)} %get-tuple-element.37.norm_ref, f32[1,1024]{1,0:T(1,128)S(1)} %get-tuple-element.29.b_ref, ...), custom_call_target="tpu_custom_call" | custom-call | tf_op jit(solution)/shard_map/pallas_call | solution.py:376
  (1 shorter events, 0.0 us)
Async XLA Ops:
  0.6 0.7 %copy-start.3 = (bf16[64]{0:T(256)(128)(2,1)S(1)}, bf16[64]{0:T(256)(128)(2,1)}, u32[]{:S(2)}) copy-start(bf16[64]{0:T(256)(128)(2,1)} %param.7) | copy-start | bytes 388
  0.6 0.7 %copy-start.2 = (bf16[64,96]{1,0:T(8,128)(2,1)S(1)}, bf16[64,96]{1,0:T(8,128)(2,1)}, u32[]{:S(2)}) copy-start(bf16[64,96]{1,0:T(8,128)(2,1)} %y_ref.1) | copy-start | bytes 36868
  1.4 14.6 %copy-start = (bf16[1024,96]{0,1:T(8,128)(2,1)S(1)}, bf16[1024,96]{0,1:T(8,128)(2,1)}, u32[]{:S(2)}) copy-start(bf16[1024,96]{0,1:T(8,128)(2,1)} %param.4) | copy-start | bytes 589828
  1.4 14.6 %copy-start.1 = (bf16[1024]{0:T(1024)(128)(2,1)S(1)}, bf16[1024]{0:T(1024)(128)(2,1)}, u32[]{:S(2)}) copy-start(bf16[1024]{0:T(1024)(128)(2,1)} %param.6) | copy-start | bytes 6148
  16.0 1.3 %collective-permute-start = (bf16[8,64,128]{2,1,0:T(8,128)(2,1)S(1)}, bf16[8,64,128]{2,1,0:T(8,128)(2,1)S(1)}, u32[]{:S(2)}, u32[]{:S(2)}) collective-permute-start(bf16[8,64,128]{2,1,0:T(8,128)(2,1)S(1)} %all_to_all.15.mine_ref), channel_id=1, source_target_pairs={{0,1},{1,0},{2,3},{3,2},{4,5},{5,4},{6,7},{7,6},{8,9},{9,8},{10,11... | collective-permute-start | bytes 393224 | tf_op jit(solution)/shard_map/ppermute | solution.py:392
  30.2 1.4 %collective-permute-start.1 = (bf16[112,512]{1,0:T(8,128)(2,1)S(1)}, bf16[112,512]{1,0:T(8,128)(2,1)S(1)}, u32[]{:S(2)}, u32[]{:S(2)}) collective-permute-start(bf16[112,512]{1,0:T(8,128)(2,1)S(1)} %get-tuple-element.41), channel_id=1, source_target_pairs={{0,1},{1,0},{2,3},{3,2},{4,5},{5,4},{6,7},{7,6},{8,9},{9,8},{10,11... | collective-permute-start | bytes 344072 | tf_op jit(solution)/shard_map/ppermute | solution.py:392

commit v13 on v8

--- a/solution.py
+++ b/solution.py
@@ -16,6 +16,8 @@
 EXT = 32
 PAD = 16
 LANES = 128
+TINY = 1e-25
+ACROSS = (((1,), (1,)), ((), ()))
 AXES = ("row", "col")
 F32 = jnp.float32
 BF16 = jnp.bfloat16
@@ -90,7 +92,7 @@
         value = jnp.exp2((z_ref[r : r + STEP, :] - shift) * scale)
         total = total + value
         if keep is not None:
-            keep(r, value.astype(BF16))
+            keep(r, value)
     return jnp.sum(total, axis=0, keepdims=True)
 
 
@@ -147,7 +149,27 @@
         ya_ref[k, :, width:] = ext
 
 
-def half_kernel(xt_ref, mx_ref, mine_ref, xa_ref, peak_ref, total_ref, z_ref):
+def halves(row):
+    half = row.shape[1] // 2
+    return row[:, :half], row[:, half:]
+
+
+def other_order(row):
+    mine, other = halves(row)
+    return jnp.where(lax.axis_index("col") == 0, row, jnp.concatenate([other, mine], axis=1))
+
+
+def piece_rows(row):
+    one, two, three = pieces(row)
+    index = lax.broadcasted_iota(jnp.int32, (PAD, row.shape[1]), 0)
+    return select(index, {0: one, 1: two, 2: three}).astype(BF16)
+
+
+def sum_pieces(block):
+    return (block[0:1] + block[1:2]) + block[2:3]
+
+
+def half_kernel(xt_ref, mx_ref, mine_ref, xa_ref, yt_ref, peak_ref, total_ref, e_ref, z_ref):
     rows, yd, depth = mine_ref.shape
     width, n = xt_ref.shape
     half = rows * yd
@@ -155,65 +177,87 @@
     mass = from_lanes(mx_ref[...].astype(F32))
     xa_ref[:width, :] = xt_ref[...]
     xa_ref[width:, :] = extras_x(rows_index(n), jnp.zeros((1, n), F32), mass).astype(BF16)
-    y_rows = mine_ref[...].reshape(half, depth)
+    mine = mine_ref[...].reshape(half, depth)
 
     def product(t):
-        return jnp.dot(y_rows, xa_ref[:, t], preferred_element_type=F32)
+        return jnp.dot(mine, xa_ref[:, t], preferred_element_type=F32)
 
     def use(t, z):
+        def keep(r, value):
+            e_ref[r : r + STEP, t] = value
+
         peak = max_down(z, half)
         peak_ref[:, t] = peak
-        total_ref[:, t] = exp_sum_down(z, half, scale, peak)
+        total_ref[:, t] = exp_sum_down(z, half, scale, peak, keep)
 
     for_tiles(n, product, z_ref, use)
+    yt_ref[...] = mine.T
 
 
 def first_kernel(
-    log_nx, xa0_ref, mine_ref, other_ref, peak_ref, total_ref,
-    yt_ref, b_ref, l_ref, m_ref, t_ref, xa_ref, ya_ref, z_ref, zc_ref, b2_ref,
+    log_nx, xa_ref, mine_ref, other_ref, peak_ref, total_ref, e_ref,
+    yt_ref, km_ref, ko_ref, b_ref, omega_ref, mu_ref, l_ref, xb_ref, z_ref, sum_ref, lse_ref,
 ):
-    rows, yd, depth = mine_ref.shape
-    n = xa0_ref.shape[1]
+    rows, yd, depth = other_ref.shape
+    n = xa_ref.shape[1]
     width = depth - EXT
     half = rows * yd
-    ny = 2 * half
-    col = lax.axis_index("col")
     scale = kappa_of(width) * LOG2E
     other = other_ref[...].reshape(half, depth)
 
     def product(t):
-        return jnp.dot(other, xa0_ref[:, t], preferred_element_type=F32)
+        return jnp.dot(other, xa_ref[:, t], preferred_element_type=F32)
 
     def use(t, z):
+        def keep(r, value):
+            ko_ref[r : r + STEP, t] = value.astype(BF16)
+
         old = peak_ref[:, t]
         peak = jnp.maximum(max_down(z, half), old)
-        total = exp_sum_down(z, half, scale, peak) + total_ref[:, t] * jnp.exp2((old - peak) * scale)
+        down = jnp.exp2((old - peak) * scale)
+        total = exp_sum_down(z, half, scale, peak, keep) + total_ref[:, t] * down
+        sum_ref[:, t] = total
         b_ref[:, t] = -peak - jnp.log(total) * (LOG2E / scale)
+        for r in range(0, half, STEP):
+            km_ref[r : r + STEP, t] = (e_ref[r : r + STEP, t] * down).astype(BF16)
 
     for_tiles(n, product, z_ref, use)
-    ya_ref[pl.ds(pl.multiple_of(col * half, half), half), :] = mine_ref[...].reshape(half, depth)
-    ya_ref[pl.ds(pl.multiple_of((1 - col) * half, half), half), :] = other
-    yt_ref[...] = ya_ref[...].T
-    mass = xa0_ref[width:, :].astype(F32)[7:8]
-    b_term = b_ref[...] + (mass - log_nx) * (LOG2E / scale)
-    b_ref[...] = b_term
-    xa_ref[:width, :] = xa0_ref[:width, :]
-    xa_ref[width:, :] = extras_x(rows_index(n), b_term, mass).astype(BF16)
-    x_rows = xa_ref[...].T
-
-    def product(t):
-        return jnp.dot(x_rows, yt_ref[:, t], preferred_element_type=F32)
-
-    def use(t, z):
-        def keep(r, value):
-            t_ref[r : r + STEP, t] = value
-
-        peak = max_down(z, n)
-        m_ref[:, t] = peak
-        b2_ref[:, t] = scale * peak + jnp.log(exp_sum_down(z, n, scale, peak, keep)) * LOG2E
-
-    for_tiles(ny, product, zc_ref, use)
-    lse = to_lanes(b2_ref[...])
+    yt_ref[...] = other.T
+    mass = xa_ref[width:, :].astype(F32)[7:8]
+    b_ref[...] = b_ref[...] + (mass - log_nx) * (LOG2E / scale)
+    omega = jnp.exp(mass - log_nx) / sum_ref[...]
+    omega_ref[...] = omega
+    left = piece_rows(omega)
+    sums = jnp.concatenate(
+        [
+            sum_pieces(lax.dot_general(left, ref[...], ACROSS, preferred_element_type=F32))
+            for ref in (km_ref, ko_ref)
+        ],
+        axis=1,
+    )
+    lse_ref[...] = jnp.log(sums) * LOG2E
+    mu_ref[...] = jnp.zeros(mu_ref.shape, F32)
+
+    @pl.when(jnp.min(sums) < TINY)
+    def _():
+        xb_ref[:width, :] = xa_ref[:width, :]
+        xb_ref[width:, :] = extras_x(rows_index(n), b_ref[...], mass).astype(BF16)
+        omega_ref[...] = jnp.ones((1, n), F32)
+        step = LANES // yd
+        for k, (y_ref, k_ref) in enumerate(((mine_ref, km_ref), (other_ref, ko_ref))):
+
+            @pl.loop(0, rows // step)
+            def _(t):
+                y = y_ref[pl.ds(t * step, step)].reshape(LANES, depth)
+                z = jnp.dot(y, xb_ref[...], preferred_element_type=F32)
+                peak = jnp.max(z, axis=1, keepdims=True)
+                value = jnp.exp2((z - peak) * scale)
+                k_ref[pl.ds(pl.multiple_of(t * LANES, LANES), LANES), :] = value.astype(BF16)
+                place = pl.ds(pl.multiple_of(k * half + t * LANES, LANES), LANES)
+                mu_ref[:, place] = to_row(scale * peak)
+                lse_ref[:, place] = to_row(scale * peak + jnp.log(jnp.sum(value, axis=1, keepdims=True)) * LOG2E)
+
+    lse = to_lanes(other_order(lse_ref[...]))
     for k in range(2 * rows):
         l_ref[k] = lse
 
@@ -234,63 +278,60 @@
 
 
 def second_kernel(
-    log_nx, log_ny, xa_ref, b_ref, l_ref, m_ref, yt_ref, t_ref,
-    r_ref, v_ref, c_ref, xs_ref, sum_ref, send_ref,
+    log_nx, log_ny, xa_ref, omega_ref, mu_ref, l_ref, ym_ref, yo_ref, km_ref, ko_ref,
+    r_ref, wr_ref, v_ref, c_ref, xs_ref, sum_ref, send_ref,
 ):
     width = xa_ref.shape[0] - EXT
-    ny = m_ref.shape[1]
-    half = ny // 2
+    half = ym_ref.shape[1]
     kappa = kappa_of(width)
     scale = kappa * LOG2E
     l_all = l_ref[...]
     peak = jnp.max(l_all, axis=0)
     total = jnp.sum(jnp.exp2(l_all - peak[None]), axis=0)
-    lse2 = from_lanes(peak + jnp.log(total) * LOG2E)
-    old = yt_ref[width:, :].astype(F32)
-    c_old = (old[0:1] + old[1:2]) + old[2:3]
+    lse2 = other_order(from_lanes(peak + jnp.log(total) * LOG2E))
+    old = jnp.concatenate([ym_ref[width:, :], yo_ref[width:, :]], axis=1).astype(F32)
     lb2 = (old[6:7] - log_ny) * LOG2E
-    c_ref[...] = to_lanes(c_old + (lb2 - lse2) / scale)
-    v = jnp.exp2(scale * m_ref[...] + (lb2 - lse2))
+    c_ref[...] = to_lanes(sum_pieces(old) + (lb2 - lse2) / scale)
+    v = jnp.exp2(mu_ref[...] + (lb2 - lse2))
     v_ref[...] = v
-    one, two, three = pieces(v)
-    index = lax.broadcasted_iota(jnp.int32, (PAD, ny), 0)
-    v_rows = select(index, {0: one, 1: two, 2: three}).astype(BF16)
-    across = (((1,), (1,)), ((), ()))
-    sums = lax.dot_general(v_rows, t_ref[...], across, preferred_element_type=F32)
-    rowsum = (sums[0:1] + sums[1:2]) + sums[2:3]
+    v_mine, v_other = halves(v)
+    left = piece_rows(v)
+    rowsum = jnp.dot(left[:, :half], km_ref[...], preferred_element_type=F32) + jnp.dot(
+        left[:, half:], ko_ref[...], preferred_element_type=F32
+    )
+    omega = omega_ref[...]
+    rowsum = sum_pieces(rowsum) * omega
     mass = xa_ref[width:, :].astype(F32)[7:8]
     r = jnp.exp(mass - log_nx) / rowsum
     r_ref[...] = r
-    stack(xs_ref, width, xa_ref[:width, :], r)
-    col = lax.axis_index("col")
+    wr_ref[...] = r * omega
+    stack(xs_ref, width, xa_ref[:width, :], r * omega)
+    totals = []
     for k in range(half // TILE):
-        t = pl.ds(pl.multiple_of((1 - col) * half + k * TILE, TILE), TILE)
-        product = jnp.dot(xs_ref[...], t_ref[:, t], preferred_element_type=F32)
+        t = slice(k * TILE, (k + 1) * TILE)
+        product = lax.dot_general(xs_ref[...], ko_ref[t, :], ACROSS, preferred_element_type=F32)
         moment, total = unstack(product, width)
-        total = total * v_ref[:, t]
-        sum_ref[:, t] = total
-        part = yt_ref[:width, t].astype(F32) * total - moment * v_ref[:, t]
-        send_ref[:width, k * TILE : (k + 1) * TILE] = part.astype(BF16)
-        t = pl.ds(pl.multiple_of(col * half + k * TILE, TILE), TILE)
-        ext = jnp.dot(xs_ref[2 * width :, :], t_ref[:, t], preferred_element_type=F32)
-        sum_ref[:, t] = ((ext[0:1] + ext[1:2]) + ext[2:3]) * v_ref[:, t]
-    sums = sum_ref[...]
-    high = sums.astype(BF16).astype(F32)
-    low = sums - high
+        total = total * v_other[:, t]
+        totals.append(total)
+        part = yo_ref[:width, t].astype(F32) * total - moment * v_other[:, t]
+        send_ref[:width, t] = part.astype(BF16)
+    s_other = jnp.concatenate(totals, axis=1)
+    ext = lax.dot_general(xs_ref[2 * width :, :], km_ref[...], ACROSS, preferred_element_type=F32)
+    s_mine = sum_pieces(ext) * v_mine
+    sum_ref[...] = jnp.concatenate([s_mine, s_other], axis=1)
+    high_m, high_o = s_mine.astype(BF16).astype(F32), s_other.astype(BF16).astype(F32)
     index = lax.broadcasted_iota(jnp.int32, (PAD, half), 0)
-    ext = select(index, {0: high[:, :half], 1: high[:, half:], 2: low[:, :half], 3: low[:, half:]})
+    ext = select(index, {0: high_m, 1: high_o, 2: s_mine - high_m, 3: s_other - high_o})
     send_ref[width:, :] = ext.astype(BF16)
 
 
-def keep_kernel(xa_ref, xs_ref, v_ref, sum_ref, yt_ref, t_ref, keep_ref, norm_ref):
+def keep_kernel(xa_ref, xs_ref, v_ref, sum_ref, ym_ref, km_ref, keep_ref, norm_ref):
     width, half = keep_ref.shape
-    col = lax.axis_index("col")
     for k in range(half // TILE):
-        t = pl.ds(pl.multiple_of(col * half + k * TILE, TILE), TILE)
-        product = jnp.dot(xs_ref[: 2 * width, :], t_ref[:, t], preferred_element_type=F32)
+        t = slice(k * TILE, (k + 1) * TILE)
+        product = lax.dot_general(xs_ref[: 2 * width, :], km_ref[t, :], ACROSS, preferred_element_type=F32)
         moment = product[:width] + product[width:]
-        part = yt_ref[:width, t].astype(F32) * sum_ref[:, t] - moment * v_ref[:, t]
-        keep_ref[:, k * TILE : (k + 1) * TILE] = part
+        keep_ref[:, t] = ym_ref[:width, t].astype(F32) * sum_ref[:, t] - moment * v_ref[:, t]
     xf = xa_ref[:width, :].astype(F32)
     norm_ref[...] = jnp.sum(xf * xf, axis=0, keepdims=True)
 
@@ -301,7 +342,7 @@
     yd = half // rows
     base = yd * width // LANES
     ext = got_ref[width:, :].astype(F32)
-    other = jnp.concatenate([ext[0:1] + ext[2:3], ext[1:2] + ext[3:4]], axis=1)
+    other = jnp.concatenate([ext[1:2] + ext[3:4], ext[0:1] + ext[2:3]], axis=1)
     sums = sums_out(to_lanes(sum_ref[...] + other)).astype(BF16)
     total = (keep_ref[...] + got_ref[:width, :].astype(F32)).T
     for r in range(rows):
@@ -310,7 +351,7 @@
 
 
 def own_part(ref, yd):
-    block = lax.axis_index("col") * lax.axis_size("row") + lax.axis_index("row")
+    block = lax.axis_index("row")
     fit = LANES // yd
     row = ref[pl.ds(block // fit, 1), :]
     out = row[:, :yd]
@@ -320,7 +361,7 @@
 
 
 def last_kernel(
-    log_nx, log_ny, xa_ref, norm_ref, b_ref, r_ref, v_ref, c_ref, got_ref, yt_ref, t_ref, y_ref,
+    log_nx, log_ny, xa_ref, norm_ref, b_ref, r_ref, wr_ref, v_ref, c_ref, got_ref, ym_ref, yo_ref, km_ref, ko_ref, y_ref,
     f_hbm, pot_hbm, gx_hbm, gy_hbm, f_ref, pot_ref, gx_ref, gy_ref, ys_ref, sum_ref, sems,
 ):
     width, n = gx_ref.shape
@@ -355,15 +396,18 @@
     norm = to_row(jnp.sum(own[:, :width] * own[:, :width], axis=1, keepdims=True))
     pot_ref[...] = norm / width - EPSILON * (jnp.log(colsum) - kappa * c_term)
     leave(pot_ref, pot_hbm)
-    mass = yt_ref[width:, :].astype(F32)[6:7]
+    half = ny // 2
+    yt = jnp.concatenate([ym_ref[...], yo_ref[...]], axis=1)
+    mass = yt[width:].astype(F32)[6:7]
     q = v_ref[...] * jnp.exp(mass + log_nx - jnp.log(from_lanes(sums)))
-    stack(ys_ref, width, yt_ref[:width, :], q)
-    across = (((1,), (1,)), ((), ()))
+    stack(ys_ref, width, yt[:width], q)
     for k in range(n // TILE):
         t = slice(k * TILE, (k + 1) * TILE)
-        product = lax.dot_general(ys_ref[...], t_ref[t, :], across, preferred_element_type=F32)
+        product = jnp.dot(ys_ref[:, :half], km_ref[:, t], preferred_element_type=F32) + jnp.dot(
+            ys_ref[:, half:], ko_ref[:, t], preferred_element_type=F32
+        )
         moved, weight = unstack(product, width)
-        gx_ref[:, t] = (xa_ref[:width, t].astype(F32) * weight - moved) * (r_ref[:, t] * (1.0 / ny))
+        gx_ref[:, t] = (xa_ref[:width, t].astype(F32) * weight - moved) * (wr_ref[:, t] * (1.0 / ny))
         leave(gx_ref.at[:, t], gx_hbm.at[:, t])
     for move in moves:
         move.wait()
@@ -413,34 +457,35 @@
     )
     y_mine = lax.all_to_all(y_own, "row", 0, 0, tiled=True)
     y_other = swap(y_mine)
-    xa, peak, total = call(
-        half_kernel, (shape((depth, n), BF16), shape((1, n)), shape((1, n))), [vmem((slots, half, TILE), F32)],
+    xa, yt_mine, peak, total, exps = call(
+        half_kernel,
+        (
+            shape((depth, n), BF16), shape((depth, half), BF16), shape((1, n)), shape((1, n)), shape((half, n)),
+        ),
+        [vmem((slots, half, TILE), F32)],
         limit, points_x.T, mass_x.reshape(n // LANES, LANES), y_mine,
     )
-    yt, b_term, lse, peak, plan = call(
+    yt_other, kept_mine, kept_other, b_term, omega, mu, lse = call(
         run(first_kernel, log_nx),
         (
-            shape((depth, ny), BF16), shape((1, n)), shape((2 * rows, count, LANES)), shape((1, ny)),
-            shape((n, ny), BF16),
+            shape((depth, half), BF16), shape((half, n), BF16), shape((half, n), BF16), shape((1, n)),
+            shape((1, n)), shape((1, ny)), shape((2 * rows, count, LANES)),
         ),
-        [
-            vmem((depth, n), BF16), vmem((ny, depth), BF16), vmem((slots, half, TILE), F32),
-            vmem((slots, n, TILE), F32), vmem((1, ny), F32),
-        ],
-        limit, xa, y_mine, y_other, peak, total,
+        [vmem((depth, n), BF16), vmem((slots, half, TILE), F32), vmem((1, n), F32), vmem((1, ny), F32)],
+        limit, xa, y_mine, y_other, peak, total, exps,
     )
     lse = lax.all_to_all(lse, AXES, 0, 0, tiled=True)
-    r, v, c_term, xs, sums, send = call(
+    r, wr, v, c_term, xs, sums, send = call(
         run(second_kernel, log_nx, log_ny),
         (
-            shape((1, n)), shape((1, ny)), shape((count, LANES)), shape((2 * width + PAD, n), BF16),
-            shape((1, ny)), shape((width + PAD, half), BF16),
+            shape((1, n)), shape((1, n)), shape((1, ny)), shape((count, LANES)),
+            shape((2 * width + PAD, n), BF16), shape((1, ny)), shape((width + PAD, half), BF16),
         ),
-        [], limit, xa, b_term, lse, peak, yt, plan,
+        [], limit, xa, omega, mu, lse, yt_mine, yt_other, kept_mine, kept_other,
     )
     got = swap(send)
     keep, norm = call(
-        keep_kernel, (shape((width, half)), shape((1, n))), [], limit, xa, xs, v, sums, yt, plan
+        keep_kernel, (shape((width, half)), shape((1, n))), [], limit, xa, xs, v, sums, yt_mine, kept_mine
     )
     part = call(
         add_kernel, shape((rows, yd * width // LANES + extra, LANES), BF16), [], limit, keep, sums, got
@@ -454,7 +499,8 @@
             vmem((2 * width + PAD, ny), BF16), vmem((count, LANES), F32),
             pltpu.SemaphoreType.DMA((3 + n // TILE,)),
         ],
-        limit, xa, norm, b_term, r, v, c_term, part, yt, plan, y_own, out_space=pl.ANY,
+        limit, xa, norm, b_term, r, wr, v, c_term, part, yt_mine, yt_other, kept_mine, kept_other, y_own,
+        out_space=pl.ANY,
     )
     return f_pot.reshape(n), g_pot.reshape(yd), grad_xt.T, grad_y
 

time: 43.5 us -> 46.5 us (1.069)
  Pallas kernels: 6.31 us -> 9.44 us
    pallas_call x8, Pallas kernels: 6.31 us -> 9.44 us  [call(): pl.pallas_call(kernel, out_shape=outs, in_specs=[pl.BlockSpec(memory_spac...]
  transfers between devices with their start and end apart: 2 -> 2, of which waited for: 2 -> 2; matrix products, arithmetic and copies ran while one was open for 0% -> 0% of each run, Pallas kernels for 2% -> 3%
where the time goes in v13:
time: 46.5 us; the launch traced here: 46.2 us
  blocking collectives  33.9 us (73%)
  Pallas kernels  9.44 us (20%)
  waiting for transfers between devices  1.4 us (3%)
  local copies, waits for them, and re-layouts  0.71 us (2%)
  between operations  0.71 us (2%)
    all_to_all x1, blocking collectives, on_device(): y_mine = lax.all_to_all(y_own, 'row', 0, 0, tiled=True)  14.4 us
    all_to_all x1, blocking collectives, on_device(): part = lax.all_to_all(part, 'row', 0, 0, tiled=True)  9.97 us
    all_to_all x1, blocking collectives, on_device(): lse = lax.all_to_all(lse, AXES, 0, 0, tiled=True)  9.48 us
    pallas_call x8, Pallas kernels, call(): pl.pallas_call(kernel, out_shape=outs, in_specs=[pl.BlockSpec(memory_spac...  9.44 us
    ppermute x2, waiting for transfers between devices, swap(): return lax.ppermute(value, 'col', [(0, 1), (1, 0)])  1.4 us
  transfers between devices with their start and end apart: 2, of which 2 were waited for; matrix products, arithmetic and copies ran while one was open for 0% of the time, Pallas kernels for 3%

profile of v13, /device:TPU:0, one launch (start us, length us, event | category | flops | bytes accessed | tf_op | source)
XLA Modules:
  0.0 46.2 jit_solution(5545788922459708553)
XLA Ops:
  0.6 0.0 copy-start.3
  0.6 0.0 copy-start.2
  0.7 0.6 %copy-done.3 = bf16[64]{0:T(256)(128)(2,1)S(1)} copy-done((bf16[64]{0:T(256)(128)(2,1)S(1)}, bf16[64]{0:T(256)(128)(2,1)}, u32[]{:S(2)}) %copy-start.3) | copy-done | bytes 152
  1.3 0.1 copy-done.2
  1.4 0.0 copy-start
  1.4 0.0 copy-start.1
  1.4 0.2 shard_map.76.y_ref
  1.6 14.4 %all_to_all.15.mine_ref = bf16[8,64,128]{2,1,0:T(8,128)(2,1)S(1)} all-to-all(bf16[8,64,128]{2,1,0:T(8,128)(2,1)S(1)} %shard_map.76.y_ref), channel_id=1, replica_groups=mesh['groups'=2,'row'=8,'col'=2] {'row'}, dimensions={0} | all-to-all | bytes 262144 | tf_op jit(solution)/shard_map/all_to_all | solution.py:458
  16.0 0.0 collective-permute-start
  16.0 0.0 copy-done
  16.0 0.0 copy-done.1
  16.0 0.7 %shard_map.77 = (bf16[128,1024]{1,0:T(8,128)(2,1)S(1)}, bf16[128,512]{1,0:T(8,128)(2,1)S(1)}, f32[1,1024]{1,0:T(1,128)S(1)}, f32[1,1024]{1,0:T(1,128)S(1)}, f32[512,1024]{1,0:T(8,128)S(1)}) custom-call(bf16[96,1024]{1,0:T(8,128)(2,1)S(1)} %bitcast.6, bf16[8,128]{1,0:T(8,128)(2,1)S(1)} %bitcast.7, bf16[8,64,128]{2,1,0:T(8,128)(2,1)S(1)} %all_to_all.15.mine_ref), custom_call_target="tpu_custom_call" | custom-call | tf_op jit(solution)/shard_map/pallas_call | solution.py:417
  16.7 0.6 %collective-permute-done.other_ref = bf16[8,64,128]{2,1,0:T(8,128)(2,1)S(1)} collective-permute-done((bf16[8,64,128]{2,1,0:T(8,128)(2,1)S(1)}, bf16[8,64,128]{2,1,0:T(8,128)(2,1)S(1)}, u32[]{:S(2)}, u32[]{:S(2)}) %collective-permute-start) | collective-permute-done | bytes 131104 | tf_op jit(solution)/shard_map/ppermute | solution.py:433
  17.3 5.2 %shard_map.78 = (bf16[128,512]{1,0:T(8,128)(2,1)S(1)}, bf16[512,1024]{1,0:T(8,128)(2,1)S(1)}, bf16[512,1024]{1,0:T(8,128)(2,1)S(1)}, f32[1,1024]{1,0:T(1,128)S(1...) custom-call(bf16[128,1024]{1,0:T(8,128)(2,1)S(1)} %get-tuple-element.29.xa_ref, ...), custom_call_target="tpu_custom_call" | custom-call | tf_op jit(solution)/shard_map/pallas_call | solution.py:417
  22.6 9.5 %all_to_all.16.l_ref = f32[16,8,128]{2,1,0:T(8,128)S(1)} all-to-all(f32[16,8,128]{2,1,0:T(8,128)S(1)} %get-tuple-element.35), channel_id=1, replica_groups=mesh['groups'=2,'row'=8,'col'=2] {'row','col'}, dimensions={0} | all-to-all | bytes 131072 | tf_op jit(solution)/shard_map/all_to_all | solution.py:477
  32.0 1.1 %shard_map.79 = (f32[1,1024]{1,0:T(1,128)S(1)}, f32[1,1024]{1,0:T(1,128)S(1)}, f32[1,1024]{1,0:T(1,128)S(1)}, f32[8,128]{1,0:T(8,128)S(1)}, bf16[208,1024]{1,0:T...) custom-call(bf16[128,1024]{1,0:T(8,128)(2,1)S(1)} %get-tuple-element.29.xa_ref, ...), custom_call_target="tpu_custom_call" | custom-call | tf_op jit(solution)/shard_map/pallas_call | solution.py:417
  33.1 0.1 collective-permute-start.1
  33.2 0.5 %shard_map.80 = (f32[96,512]{1,0:T(8,128)S(1)}, f32[1,1024]{1,0:T(1,128)S(1)}) custom-call(bf16[128,1024]{1,0:T(8,128)(2,1)S(1)} %get-tuple-element.29.xa_ref, bf16[208,1024]{1,0:T(8,128)(2,1)S(1)} %get-tuple-element.40.xs_ref, f32[1,1024]{1,0:T(1,128)S(1)} %get-tuple-element.41.v_ref, f32[1,1024]{1,0:T(1,128)S(1)} %get-tuple-element.42.sum_ref, ...), custom_call_target="tpu_custom_call" | custom-call | tf_op jit(solution)/shard_map/pallas_call | solution.py:417
  33.7 0.8 %collective-permute-done.1.got_ref = bf16[112,512]{1,0:T(8,128)(2,1)S(1)} collective-permute-done((bf16[112,512]{1,0:T(8,128)(2,1)S(1)}, bf16[112,512]{1,0:T(8,128)(2,1)S(1)}, u32[]{:S(2)}, u32[]{:S(2)}) %collective-permute-start.1) | collective-permute-done | bytes 114720 | tf_op jit(solution)/shard_map/ppermute | solution.py:433
  34.5 0.3 shard_map.81
  34.8 10.0 %all_to_all.17.got_ref = bf16[8,64,128]{2,1,0:T(8,128)(2,1)S(1)} all-to-all(bf16[8,64,128]{2,1,0:T(8,128)(2,1)S(1)} %shard_map.81), channel_id=1, replica_groups=mesh['groups'=2,'row'=8,'col'=2] {'row'}, dimensions={0} | all-to-all | bytes 262144 | tf_op jit(solution)/shard_map/all_to_all | solution.py:493
  44.8 1.4 %shard_map.82 = (f32[1,1024]{1,0:T(1,128)}, f32[1,64]{1,0:T(1,128)}, f32[96,1024]{1,0:T(8,128)}, f32[64,96]{1,0:T(8,128)}) custom-call(bf16[128,1024]{1,0:T(8,128)(2,1)S(1)} %get-tuple-element.29.xa_ref, f32[1,1024]{1,0:T(1,128)S(1)} %get-tuple-element.43.norm_ref, f32[1,1024]{1,0:T(1,128)S(1)} %get-tuple-element.44.b_ref, ...), custom_call_target="tpu_custom_call" | custom-call | tf_op jit(solution)/shard_map/pallas_call | solution.py:417
  (1 shorter events, 0.0 us)
Async XLA Ops:
  0.6 0.7 %copy-start.3 = (bf16[64]{0:T(256)(128)(2,1)S(1)}, bf16[64]{0:T(256)(128)(2,1)}, u32[]{:S(2)}) copy-start(bf16[64]{0:T(256)(128)(2,1)} %param.7) | copy-start | bytes 388
  0.6 0.7 %copy-start.2 = (bf16[64,96]{1,0:T(8,128)(2,1)S(1)}, bf16[64,96]{1,0:T(8,128)(2,1)}, u32[]{:S(2)}) copy-start(bf16[64,96]{1,0:T(8,128)(2,1)} %y_ref.1) | copy-start | bytes 36868
  1.4 14.6 %copy-start = (bf16[1024,96]{0,1:T(8,128)(2,1)S(1)}, bf16[1024,96]{0,1:T(8,128)(2,1)}, u32[]{:S(2)}) copy-start(bf16[1024,96]{0,1:T(8,128)(2,1)} %param.4) | copy-start | bytes 589828
  1.4 14.6 %copy-start.1 = (bf16[1024]{0:T(1024)(128)(2,1)S(1)}, bf16[1024]{0:T(1024)(128)(2,1)}, u32[]{:S(2)}) copy-start(bf16[1024]{0:T(1024)(128)(2,1)} %param.6) | copy-start | bytes 6148
  16.0 1.3 %collective-permute-start = (bf16[8,64,128]{2,1,0:T(8,128)(2,1)S(1)}, bf16[8,64,128]{2,1,0:T(8,128)(2,1)S(1)}, u32[]{:S(2)}, u32[]{:S(2)}) collective-permute-start(bf16[8,64,128]{2,1,0:T(8,128)(2,1)S(1)} %all_to_all.15.mine_ref), channel_id=1, source_target_pairs={{0,1},{1,0},{2,3},{3,2},{4,5},{5,4},{6,7},{7,6},{8,9},{9,8},{10,11... | collective-permute-start | bytes 393224 | tf_op jit(solution)/shard_map/ppermute | solution.py:433
  33.1 1.4 %collective-permute-start.1 = (bf16[112,512]{1,0:T(8,128)(2,1)S(1)}, bf16[112,512]{1,0:T(8,128)(2,1)S(1)}, u32[]{:S(2)}, u32[]{:S(2)}) collective-permute-start(bf16[112,512]{1,0:T(8,128)(2,1)S(1)} %get-tuple-element.49), channel_id=1, source_target_pairs={{0,1},{1,0},{2,3},{3,2},{4,5},{5,4},{6,7},{7,6},{8,9},{9,8},{10,11... | collective-permute-start | bytes 344072 | tf_op jit(solution)/shard_map/ppermute | solution.py:433

commit v14 on v13

--- a/solution.py
+++ b/solution.py
@@ -16,7 +16,9 @@
 EXT = 32
 PAD = 16
 LANES = 128
-TINY = 1e-25
+LIFT = 40.0
+TINY = 1e-31
+HUGE = 1e35
 ACROSS = (((1,), (1,)), ((), ()))
 AXES = ("row", "col")
 F32 = jnp.float32
@@ -169,7 +171,7 @@
     return (block[0:1] + block[1:2]) + block[2:3]
 
 
-def half_kernel(xt_ref, mx_ref, mine_ref, xa_ref, yt_ref, peak_ref, total_ref, e_ref, z_ref):
+def half_kernel(xt_ref, mx_ref, mine_ref, xa_ref, yt_ref, base_ref, total_ref, k_ref, z_ref):
     rows, yd, depth = mine_ref.shape
     width, n = xt_ref.shape
     half = rows * yd
@@ -184,19 +186,19 @@
 
     def use(t, z):
         def keep(r, value):
-            e_ref[r : r + STEP, t] = value
-
-        peak = max_down(z, half)
-        peak_ref[:, t] = peak
-        total_ref[:, t] = exp_sum_down(z, half, scale, peak, keep)
+            k_ref[r : r + STEP, t] = value.astype(BF16)
+
+        base = max_down(z, half) - LIFT / scale
+        base_ref[:, t] = base
+        total_ref[:, t] = exp_sum_down(z, half, scale, base, keep)
 
     for_tiles(n, product, z_ref, use)
     yt_ref[...] = mine.T
 
 
 def first_kernel(
-    log_nx, xa_ref, mine_ref, other_ref, peak_ref, total_ref, e_ref,
-    yt_ref, km_ref, ko_ref, b_ref, omega_ref, mu_ref, l_ref, xb_ref, z_ref, sum_ref, lse_ref,
+    log_nx, xa_ref, mine_ref, other_ref, base_ref, total_ref, km0_ref,
+    yt_ref, km_ref, ko_ref, b_ref, omega_ref, mu_ref, l_ref, xb_ref, z_ref, sum_ref, lse_ref, sem,
 ):
     rows, yd, depth = other_ref.shape
     n = xa_ref.shape[1]
@@ -204,6 +206,8 @@
     half = rows * yd
     scale = kappa_of(width) * LOG2E
     other = other_ref[...].reshape(half, depth)
+    move = pltpu.make_async_copy(km0_ref, km_ref, sem)
+    move.start()
 
     def product(t):
         return jnp.dot(other, xa_ref[:, t], preferred_element_type=F32)
@@ -212,22 +216,17 @@
         def keep(r, value):
             ko_ref[r : r + STEP, t] = value.astype(BF16)
 
-        old = peak_ref[:, t]
-        peak = jnp.maximum(max_down(z, half), old)
-        down = jnp.exp2((old - peak) * scale)
-        total = exp_sum_down(z, half, scale, peak, keep) + total_ref[:, t] * down
-        sum_ref[:, t] = total
-        b_ref[:, t] = -peak - jnp.log(total) * (LOG2E / scale)
-        for r in range(0, half, STEP):
-            km_ref[r : r + STEP, t] = (e_ref[r : r + STEP, t] * down).astype(BF16)
+        sum_ref[:, t] = exp_sum_down(z, half, scale, base_ref[:, t], keep) + total_ref[:, t]
 
     for_tiles(n, product, z_ref, use)
     yt_ref[...] = other.T
     mass = xa_ref[width:, :].astype(F32)[7:8]
-    b_ref[...] = b_ref[...] + (mass - log_nx) * (LOG2E / scale)
-    omega = jnp.exp(mass - log_nx) / sum_ref[...]
+    total = sum_ref[...]
+    b_ref[...] = (mass - log_nx - jnp.log(total)) * (LOG2E / scale) - base_ref[...]
+    omega = jnp.exp(mass - log_nx) * (2.0**LIFT / total)
     omega_ref[...] = omega
     left = piece_rows(omega)
+    move.wait()
     sums = jnp.concatenate(
         [
             sum_pieces(lax.dot_general(left, ref[...], ACROSS, preferred_element_type=F32))
@@ -235,21 +234,42 @@
         ],
         axis=1,
     )
-    lse_ref[...] = jnp.log(sums) * LOG2E
-    mu_ref[...] = jnp.zeros(mu_ref.shape, F32)
-
-    @pl.when(jnp.min(sums) < TINY)
+    lse_ref[...] = jnp.log(sums) * LOG2E - LIFT
+    mu_ref[...] = jnp.full(mu_ref.shape, -LIFT, F32)
+
+    @pl.when(jnp.logical_not((jnp.max(total) < HUGE) & (jnp.min(sums) > TINY)))
     def _():
+        step = LANES // yd
+        sides = ((0, mine_ref, km_ref), (1, other_ref, ko_ref))
+
+        def scores(y_ref, x_ref, t):
+            y = y_ref[pl.ds(t * step, step)].reshape(LANES, depth)
+            return jnp.dot(y, x_ref[...], preferred_element_type=F32)
+
+        b_ref[...] = jnp.full((1, n), -jnp.inf, F32)
+        for k, y_ref, k_ref in sides:
+
+            @pl.loop(0, rows // step)
+            def _(t):
+                b_ref[...] = jnp.maximum(b_ref[...], jnp.max(scores(y_ref, xa_ref, t), axis=0, keepdims=True))
+
+        sum_ref[...] = jnp.zeros((1, n), F32)
+        for k, y_ref, k_ref in sides:
+
+            @pl.loop(0, rows // step)
+            def _(t):
+                value = jnp.exp2((scores(y_ref, xa_ref, t) - b_ref[...]) * scale)
+                sum_ref[...] = sum_ref[...] + jnp.sum(value, axis=0, keepdims=True)
+
+        b_ref[...] = (mass - log_nx - jnp.log(sum_ref[...])) * (LOG2E / scale) - b_ref[...]
         xb_ref[:width, :] = xa_ref[:width, :]
         xb_ref[width:, :] = extras_x(rows_index(n), b_ref[...], mass).astype(BF16)
         omega_ref[...] = jnp.ones((1, n), F32)
-        step = LANES // yd
-        for k, (y_ref, k_ref) in enumerate(((mine_ref, km_ref), (other_ref, ko_ref))):
+        for k, y_ref, k_ref in sides:
 
             @pl.loop(0, rows // step)
             def _(t):
-                y = y_ref[pl.ds(t * step, step)].reshape(LANES, depth)
-                z = jnp.dot(y, xb_ref[...], preferred_element_type=F32)
+                z = scores(y_ref, xb_ref, t)
                 peak = jnp.max(z, axis=1, keepdims=True)
                 value = jnp.exp2((z - peak) * scale)
                 k_ref[pl.ds(pl.multiple_of(t * LANES, LANES), LANES), :] = value.astype(BF16)
@@ -457,10 +477,11 @@
     )
     y_mine = lax.all_to_all(y_own, "row", 0, 0, tiled=True)
     y_other = swap(y_mine)
-    xa, yt_mine, peak, total, exps = call(
+    xa, yt_mine, base, total, kept_mine = call(
         half_kernel,
         (
-            shape((depth, n), BF16), shape((depth, half), BF16), shape((1, n)), shape((1, n)), shape((half, n)),
+            shape((depth, n), BF16), shape((depth, half), BF16), shape((1, n)), shape((1, n)),
+            shape((half, n), BF16),
         ),
         [vmem((slots, half, TILE), F32)],
         limit, points_x.T, mass_x.reshape(n // LANES, LANES), y_mine,
@@ -471,8 +492,8 @@
             shape((depth, half), BF16), shape((half, n), BF16), shape((half, n), BF16), shape((1, n)),
             shape((1, n)), shape((1, ny)), shape((2 * rows, count, LANES)),
         ),
-        [vmem((depth, n), BF16), vmem((slots, half, TILE), F32), vmem((1, n), F32), vmem((1, ny), F32)],
-        limit, xa, y_mine, y_other, peak, total, exps,
+        [vmem((depth, n), BF16), vmem((slots, half, TILE), F32), vmem((1, n), F32), vmem((1, ny), F32), pltpu.SemaphoreType.DMA],
+        limit, xa, y_mine, y_other, base, total, kept_mine,
     )
     lse = lax.all_to_all(lse, AXES, 0, 0, tiled=True)
     r, wr, v, c_term, xs, sums, send = call(

time: 46.5 us -> 50.4 us (1.084)
  Pallas kernels: 9.44 us -> 13 us
  local copies, waits for them, and re-layouts: 0.71 us -> 1.37 us
  waiting for transfers between devices: 1.4 us -> 0.8 us
    pallas_call x8, Pallas kernels: 9.44 us -> 13 us  [call(): pl.pallas_call(kernel, out_shape=outs, in_specs=[pl.BlockSpec(memory_spac...]
    unnamed x8, local copies, waits for them, and re-layouts: 0.71 us -> 1.37 us
    ppermute x2, waiting for transfers between devices: 1.4 us -> 0.8 us  [swap(): return lax.ppermute(value, 'col', [(0, 1), (1, 0)])]
  transfers between devices with their start and end apart: 2 -> 2, of which waited for: 2 -> 1; matrix products, arithmetic and copies ran while one was open for 0% -> 0% of each run, Pallas kernels for 3% -> 3%
where the time goes in v14:
time: 50.4 us; the launch traced here: 50 us
  blocking collectives  34 us (67%)
  Pallas kernels  13 us (26%)
  local copies, waits for them, and re-layouts  1.37 us (3%)
  waiting for transfers between devices  0.8 us (2%)
  between operations  0.72 us (1%)
    all_to_all x1, blocking collectives, on_device(): y_mine = lax.all_to_all(y_own, 'row', 0, 0, tiled=True)  14.6 us
    pallas_call x8, Pallas kernels, call(): pl.pallas_call(kernel, out_shape=outs, in_specs=[pl.BlockSpec(memory_spac...  13 us
    all_to_all x1, blocking collectives, on_device(): part = lax.all_to_all(part, 'row', 0, 0, tiled=True)  9.97 us
    all_to_all x1, blocking collectives, on_device(): lse = lax.all_to_all(lse, AXES, 0, 0, tiled=True)  9.48 us
    unnamed x8, local copies, waits for them, and re-layouts  1.37 us
  transfers between devices with their start and end apart: 2, of which 1 were waited for; matrix products, arithmetic and copies ran while one was open for 0% of the time, Pallas kernels for 3%

profile of v14, /device:TPU:0, one launch (start us, length us, event | category | flops | bytes accessed | tf_op | source)
XLA Modules:
  0.0 50.0 jit_solution(9185068877674044297)
XLA Ops:
  0.6 0.0 copy-start.2
  0.7 0.0 copy-start.3
  0.7 0.7 %copy-done.2 = bf16[64,96]{1,0:T(8,128)(2,1)S(1)} copy-done((bf16[64,96]{1,0:T(8,128)(2,1)S(1)}, bf16[64,96]{1,0:T(8,128)(2,1)}, u32[]{:S(2)}) %copy-start.2) | copy-done | bytes 12312
  1.3 0.0 copy-done.3
  1.4 0.2 shard_map.76.y_ref
  1.5 0.0 copy-start
  1.6 14.6 %all_to_all.15.mine_ref = bf16[8,64,128]{2,1,0:T(8,128)(2,1)S(1)} all-to-all(bf16[8,64,128]{2,1,0:T(8,128)(2,1)S(1)} %shard_map.76.y_ref), channel_id=1, replica_groups=mesh['groups'=2,'row'=8,'col'=2] {'row'}, dimensions={0} | all-to-all | bytes 262144 | tf_op jit(solution)/shard_map/all_to_all | solution.py:478
  16.1 0.0 copy-start.1
  16.1 0.0 collective-permute-start
  16.1 0.0 copy-done
  16.1 0.7 %copy-done.1 = bf16[1024]{0:T(1024)(128)(2,1)S(1)} copy-done((bf16[1024]{0:T(1024)(128)(2,1)S(1)}, bf16[1024]{0:T(1024)(128)(2,1)}, u32[]{:S(2)}) %copy-start.1) | copy-done | bytes 2072
  16.8 0.8 %shard_map.77 = (bf16[128,1024]{1,0:T(8,128)(2,1)S(1)}, bf16[128,512]{1,0:T(8,128)(2,1)S(1)}, f32[1,1024]{1,0:T(1,128)S(1)}, f32[1,1024]{1,0:T(1,128)S(1)}, bf16[512,1024]{1,0:T(8,128)(2,1)S(1)}) custom-call(bf16[96,1024]{1,0:T(8,128)(2,1)S(1)} %bitcast.6, bf16[8,128]{1,0:T(8,128)(2,1)S(1)} %bitcast.7, bf16[8,64,128]{2,1,0:T(8,128)(2,1)S(1)} %all_to_all.15.mine_ref), custom_call_target="tpu_custom_call" | custom-call | tf_op jit(solution)/shard_map/pallas_call | solution.py:437
  17.6 0.0 collective-permute-done.other_ref
  17.6 8.7 %shard_map.78 = (bf16[128,512]{1,0:T(8,128)(2,1)S(1)}, bf16[512,1024]{1,0:T(8,128)(2,1)S(1)}, bf16[512,1024]{1,0:T(8,128)(2,1)S(1)}, f32[1,1024]{1,0:T(1,128)S(1...) custom-call(bf16[128,1024]{1,0:T(8,128)(2,1)S(1)} %get-tuple-element.29.xa_ref, ...), custom_call_target="tpu_custom_call" | custom-call | tf_op jit(solution)/shard_map/pallas_call | solution.py:437
  26.3 9.5 %all_to_all.16.l_ref = f32[16,8,128]{2,1,0:T(8,128)S(1)} all-to-all(f32[16,8,128]{2,1,0:T(8,128)S(1)} %get-tuple-element.35), channel_id=1, replica_groups=mesh['groups'=2,'row'=8,'col'=2] {'row','col'}, dimensions={0} | all-to-all | bytes 131072 | tf_op jit(solution)/shard_map/all_to_all | solution.py:498
  35.8 1.1 %shard_map.79 = (f32[1,1024]{1,0:T(1,128)S(1)}, f32[1,1024]{1,0:T(1,128)S(1)}, f32[1,1024]{1,0:T(1,128)S(1)}, f32[8,128]{1,0:T(8,128)S(1)}, bf16[208,1024]{1,0:T...) custom-call(bf16[128,1024]{1,0:T(8,128)(2,1)S(1)} %get-tuple-element.29.xa_ref, ...), custom_call_target="tpu_custom_call" | custom-call | tf_op jit(solution)/shard_map/pallas_call | solution.py:437
  36.9 0.1 collective-permute-start.1
  37.0 0.5 %shard_map.80 = (f32[96,512]{1,0:T(8,128)S(1)}, f32[1,1024]{1,0:T(1,128)S(1)}) custom-call(bf16[128,1024]{1,0:T(8,128)(2,1)S(1)} %get-tuple-element.29.xa_ref, bf16[208,1024]{1,0:T(8,128)(2,1)S(1)} %get-tuple-element.40.xs_ref, f32[1,1024]{1,0:T(1,128)S(1)} %get-tuple-element.41.v_ref, f32[1,1024]{1,0:T(1,128)S(1)} %get-tuple-element.42.sum_ref, ...), custom_call_target="tpu_custom_call" | custom-call | tf_op jit(solution)/shard_map/pallas_call | solution.py:437
  37.5 0.8 %collective-permute-done.1.got_ref = bf16[112,512]{1,0:T(8,128)(2,1)S(1)} collective-permute-done((bf16[112,512]{1,0:T(8,128)(2,1)S(1)}, bf16[112,512]{1,0:T(8,128)(2,1)S(1)}, u32[]{:S(2)}, u32[]{:S(2)}) %collective-permute-start.1) | collective-permute-done | bytes 114720 | tf_op jit(solution)/shard_map/ppermute | solution.py:453
  38.3 0.3 shard_map.81
  38.6 10.0 %all_to_all.17.got_ref = bf16[8,64,128]{2,1,0:T(8,128)(2,1)S(1)} all-to-all(bf16[8,64,128]{2,1,0:T(8,128)(2,1)S(1)} %shard_map.81), channel_id=1, replica_groups=mesh['groups'=2,'row'=8,'col'=2] {'row'}, dimensions={0} | all-to-all | bytes 262144 | tf_op jit(solution)/shard_map/all_to_all | solution.py:514
  48.5 1.4 %shard_map.82 = (f32[1,1024]{1,0:T(1,128)}, f32[1,64]{1,0:T(1,128)}, f32[96,1024]{1,0:T(8,128)}, f32[64,96]{1,0:T(8,128)}) custom-call(bf16[128,1024]{1,0:T(8,128)(2,1)S(1)} %get-tuple-element.29.xa_ref, f32[1,1024]{1,0:T(1,128)S(1)} %get-tuple-element.43.norm_ref, f32[1,1024]{1,0:T(1,128)S(1)} %get-tuple-element.44.b_ref, ...), custom_call_target="tpu_custom_call" | custom-call | tf_op jit(solution)/shard_map/pallas_call | solution.py:437
  (1 shorter events, 0.0 us)
Async XLA Ops:
  0.6 0.7 %copy-start.2 = (bf16[64,96]{1,0:T(8,128)(2,1)S(1)}, bf16[64,96]{1,0:T(8,128)(2,1)}, u32[]{:S(2)}) copy-start(bf16[64,96]{1,0:T(8,128)(2,1)} %y_ref.1) | copy-start | bytes 36868
  0.7 0.7 %copy-start.3 = (bf16[64]{0:T(256)(128)(2,1)S(1)}, bf16[64]{0:T(256)(128)(2,1)}, u32[]{:S(2)}) copy-start(bf16[64]{0:T(256)(128)(2,1)} %param.7) | copy-start | bytes 388
  1.5 14.6 %copy-start = (bf16[1024,96]{0,1:T(8,128)(2,1)S(1)}, bf16[1024,96]{0,1:T(8,128)(2,1)}, u32[]{:S(2)}) copy-start(bf16[1024,96]{0,1:T(8,128)(2,1)} %param.4) | copy-start | bytes 589828
  16.1 0.7 %copy-start.1 = (bf16[1024]{0:T(1024)(128)(2,1)S(1)}, bf16[1024]{0:T(1024)(128)(2,1)}, u32[]{:S(2)}) copy-start(bf16[1024]{0:T(1024)(128)(2,1)} %param.6) | copy-start | bytes 6148
  16.1 1.5 %collective-permute-start = (bf16[8,64,128]{2,1,0:T(8,128)(2,1)S(1)}, bf16[8,64,128]{2,1,0:T(8,128)(2,1)S(1)}, u32[]{:S(2)}, u32[]{:S(2)}) collective-permute-start(bf16[8,64,128]{2,1,0:T(8,128)(2,1)S(1)} %all_to_all.15.mine_ref), channel_id=1, source_target_pairs={{0,1},{1,0},{2,3},{3,2},{4,5},{5,4},{6,7},{7,6},{8,9},{9,8},{10,11... | collective-permute-start | bytes 393224 | tf_op jit(solution)/shard_map/ppermute | solution.py:453
  36.9 1.4 %collective-permute-start.1 = (bf16[112,512]{1,0:T(8,128)(2,1)S(1)}, bf16[112,512]{1,0:T(8,128)(2,1)S(1)}, u32[]{:S(2)}, u32[]{:S(2)}) collective-permute-start(bf16[112,512]{1,0:T(8,128)(2,1)S(1)} %get-tuple-element.49), channel_id=1, source_target_pairs={{0,1},{1,0},{2,3},{3,2},{4,5},{5,4},{6,7},{7,6},{8,9},{9,8},{10,11... | collective-permute-start | bytes 344072 | tf_op jit(solution)/shard_map/ppermute | solution.py:453

commit v15 on v14

--- a/solution.py
+++ b/solution.py
@@ -43,9 +43,9 @@
     return out
 
 
-def extras_x(index, b_term, mass):
+def extras_x(index, b_term):
     high, mid, low = pieces(b_term)
-    return select(index, {0: 1.0, 1: 1.0, 2: 1.0, 3: high, 4: mid, 5: low, 7: mass})
+    return select(index, {0: 1.0, 1: 1.0, 2: 1.0, 3: high, 4: mid, 5: low})
 
 
 def rows_index(columns):
@@ -136,7 +136,8 @@
     ext_ref[...] = select(index, {3: 1.0, 4: 1.0, 5: 1.0})
 
 
-def prep_kernel(log_ny, y_ref, my_ref, ones_ref, ya_ref):
+def prep_kernel(log_nx, log_ny, y_ref, my_ref, mx_ref, ones_ref, ya_ref, la_ref):
+    la_ref[...] = from_lanes(mx_ref[...].astype(F32)) - log_nx
     width = y_ref.shape[1]
     y = y_ref[...]
     yf = y.astype(F32)
@@ -171,14 +172,13 @@
     return (block[0:1] + block[1:2]) + block[2:3]
 
 
-def half_kernel(xt_ref, mx_ref, mine_ref, xa_ref, yt_ref, base_ref, total_ref, k_ref, z_ref):
+def half_kernel(xt_ref, mine_ref, xa_ref, yt_ref, base_ref, total_ref, k_ref, z_ref):
     rows, yd, depth = mine_ref.shape
     width, n = xt_ref.shape
     half = rows * yd
     scale = kappa_of(width) * LOG2E
-    mass = from_lanes(mx_ref[...].astype(F32))
     xa_ref[:width, :] = xt_ref[...]
-    xa_ref[width:, :] = extras_x(rows_index(n), jnp.zeros((1, n), F32), mass).astype(BF16)
+    xa_ref[width:, :] = extras_x(rows_index(n), jnp.zeros((1, n), F32)).astype(BF16)
     mine = mine_ref[...].reshape(half, depth)
 
     def product(t):
@@ -197,7 +197,7 @@
 
 
 def first_kernel(
-    log_nx, xa_ref, mine_ref, other_ref, base_ref, total_ref, km0_ref,
+    xa_ref, la_ref, mine_ref, other_ref, base_ref, total_ref, km0_ref,
     yt_ref, km_ref, ko_ref, b_ref, omega_ref, mu_ref, l_ref, xb_ref, z_ref, sum_ref, lse_ref, sem,
 ):
     rows, yd, depth = other_ref.shape
@@ -220,10 +220,10 @@
 
     for_tiles(n, product, z_ref, use)
     yt_ref[...] = other.T
-    mass = xa_ref[width:, :].astype(F32)[7:8]
+    log_a = la_ref[...]
     total = sum_ref[...]
-    b_ref[...] = (mass - log_nx - jnp.log(total)) * (LOG2E / scale) - base_ref[...]
-    omega = jnp.exp(mass - log_nx) * (2.0**LIFT / total)
+    b_ref[...] = (log_a - jnp.log(total)) * (LOG2E / scale) - base_ref[...]
+    omega = jnp.exp(log_a) * (2.0**LIFT / total)
     omega_ref[...] = omega
     left = piece_rows(omega)
     move.wait()
@@ -261,9 +261,9 @@
                 value = jnp.exp2((scores(y_ref, xa_ref, t) - b_ref[...]) * scale)
                 sum_ref[...] = sum_ref[...] + jnp.sum(value, axis=0, keepdims=True)
 
-        b_ref[...] = (mass - log_nx - jnp.log(sum_ref[...])) * (LOG2E / scale) - b_ref[...]
+        b_ref[...] = (log_a - jnp.log(sum_ref[...])) * (LOG2E / scale) - b_ref[...]
         xb_ref[:width, :] = xa_ref[:width, :]
-        xb_ref[width:, :] = extras_x(rows_index(n), b_ref[...], mass).astype(BF16)
+        xb_ref[width:, :] = extras_x(rows_index(n), b_ref[...]).astype(BF16)
         omega_ref[...] = jnp.ones((1, n), F32)
         for k, y_ref, k_ref in sides:
 
@@ -298,7 +298,7 @@
 
 
 def second_kernel(
-    log_nx, log_ny, xa_ref, omega_ref, mu_ref, l_ref, ym_ref, yo_ref, km_ref, ko_ref,
+    log_ny, xa_ref, la_ref, omega_ref, mu_ref, l_ref, ym_ref, yo_ref, km_ref, ko_ref,
     r_ref, wr_ref, v_ref, c_ref, xs_ref, sum_ref, send_ref,
 ):
     width = xa_ref.shape[0] - EXT
@@ -321,8 +321,7 @@
     )
     omega = omega_ref[...]
     rowsum = sum_pieces(rowsum) * omega
-    mass = xa_ref[width:, :].astype(F32)[7:8]
-    r = jnp.exp(mass - log_nx) / rowsum
+    r = jnp.exp(la_ref[...]) / rowsum
     r_ref[...] = r
     wr_ref[...] = r * omega
     stack(xs_ref, width, xa_ref[:width, :], r * omega)
@@ -381,7 +380,7 @@
 
 
 def last_kernel(
-    log_nx, log_ny, xa_ref, norm_ref, b_ref, r_ref, wr_ref, v_ref, c_ref, got_ref, ym_ref, yo_ref, km_ref, ko_ref, y_ref,
+    log_nx, xa_ref, la_ref, norm_ref, b_ref, r_ref, wr_ref, v_ref, c_ref, got_ref, ym_ref, yo_ref, km_ref, ko_ref, y_ref,
     f_hbm, pot_hbm, gx_hbm, gy_hbm, f_ref, pot_ref, gx_ref, gy_ref, ys_ref, sum_ref, sems,
 ):
     width, n = gx_ref.shape
@@ -397,8 +396,7 @@
         move.start()
         moves.append(move)
 
-    mass = xa_ref[width:, :].astype(F32)[7:8]
-    log_row = mass - log_nx - jnp.log(r_ref[...])
+    log_row = la_ref[...] - jnp.log(r_ref[...])
     f_ref[...] = norm_ref[...] / width + EPSILON * (kappa * b_ref[...] - log_row)
     leave(f_ref, f_hbm)
     total = got_ref[0].astype(F32)
@@ -471,8 +469,9 @@
         ones_kernel, shape((yd, EXT)), [], limit,
         cost=pl.CostEstimate(flops=4 * 10**9, bytes_accessed=10000, transcendentals=0),
     )
-    y_own = call(
-        run(prep_kernel, log_ny), shape((rows, yd, depth), BF16), [], limit, points_y, mass_y.reshape(1, yd), ones,
+    y_own, log_a = call(
+        run(prep_kernel, log_nx, log_ny), (shape((rows, yd, depth), BF16), shape((1, n))), [], limit,
+        points_y, mass_y.reshape(1, yd), mass_x.reshape(n // LANES, LANES), ones,
         cost=pl.CostEstimate(flops=4 * 10**9, bytes_accessed=400000, transcendentals=0),
     )
     y_mine = lax.all_to_all(y_own, "row", 0, 0, tiled=True)
@@ -484,25 +483,25 @@
             shape((half, n), BF16),
         ),
         [vmem((slots, half, TILE), F32)],
-        limit, points_x.T, mass_x.reshape(n // LANES, LANES), y_mine,
+        limit, points_x.T, y_mine,
     )
     yt_other, kept_mine, kept_other, b_term, omega, mu, lse = call(
-        run(first_kernel, log_nx),
+        first_kernel,
         (
             shape((depth, half), BF16), shape((half, n), BF16), shape((half, n), BF16), shape((1, n)),
             shape((1, n)), shape((1, ny)), shape((2 * rows, count, LANES)),
         ),
         [vmem((depth, n), BF16), vmem((slots, half, TILE), F32), vmem((1, n), F32), vmem((1, ny), F32), pltpu.SemaphoreType.DMA],
-        limit, xa, y_mine, y_other, base, total, kept_mine,
+        limit, xa, log_a, y_mine, y_other, base, total, kept_mine,
     )
     lse = lax.all_to_all(lse, AXES, 0, 0, tiled=True)
     r, wr, v, c_term, xs, sums, send = call(
-        run(second_kernel, log_nx, log_ny),
+        run(second_kernel, log_ny),
         (
             shape((1, n)), shape((1, n)), shape((1, ny)), shape((count, LANES)),
             shape((2 * width + PAD, n), BF16), shape((1, ny)), shape((width + PAD, half), BF16),
         ),
-        [], limit, xa, omega, mu, lse, yt_mine, yt_other, kept_mine, kept_other,
+        [], limit, xa, log_a, omega, mu, lse, yt_mine, yt_other, kept_mine, kept_other,
     )
     got = swap(send)
     keep, norm = call(
@@ -513,14 +512,14 @@
     )
     part = lax.all_to_all(part, "row", 0, 0, tiled=True)
     f_pot, g_pot, grad_xt, grad_y = call(
-        run(last_kernel, log_nx, log_ny),
+        run(last_kernel, log_nx),
         (shape((1, n)), shape((1, yd)), shape((width, n)), shape((yd, width))),
         [
             vmem((1, n), F32), vmem((1, yd), F32), vmem((width, n), F32), vmem((yd, width), F32),
             vmem((2 * width + PAD, ny), BF16), vmem((count, LANES), F32),
             pltpu.SemaphoreType.DMA((3 + n // TILE,)),
         ],
-        limit, xa, norm, b_term, r, wr, v, c_term, part, yt_mine, yt_other, kept_mine, kept_other, y_own,
+        limit, xa, log_a, norm, b_term, r, wr, v, c_term, part, yt_mine, yt_other, kept_mine, kept_other, y_own,
         out_space=pl.ANY,
     )
     return f_pot.reshape(n), g_pot.reshape(yd), grad_xt.T, grad_y

time: 50.4 us -> 50.3 us (level)
  local copies, waits for them, and re-layouts: 1.37 us -> 0.69 us
  waiting for transfers between devices: 0.8 us -> 1.36 us
    unnamed x8, local copies, waits for them, and re-layouts: 1.37 us -> 0.69 us
    ppermute x2, waiting for transfers between devices: 0.8 us -> 1.36 us  [swap(): return lax.ppermute(value, 'col', [(0, 1), (1, 0)])]
  transfers between devices with their start and end apart: 2 -> 2, of which waited for: 1 -> 2; matrix products, arithmetic and copies ran while one was open for 0% -> 0% of each run, Pallas kernels for 3% -> 3%
where the time goes in v15:
time: 50.3 us; the launch traced here: 49.9 us
  blocking collectives  34 us (68%)
  Pallas kernels  13.1 us (26%)
  waiting for transfers between devices  1.36 us (3%)
  between operations  0.72 us (1%)
  local copies, waits for them, and re-layouts  0.69 us (1%)
    all_to_all x1, blocking collectives, on_device(): y_mine = lax.all_to_all(y_own, 'row', 0, 0, tiled=True)  14.6 us
    pallas_call x8, Pallas kernels, call(): pl.pallas_call(kernel, out_shape=outs, in_specs=[pl.BlockSpec(memory_spac...  13.1 us
    all_to_all x1, blocking collectives, on_device(): part = lax.all_to_all(part, 'row', 0, 0, tiled=True)  9.97 us
    all_to_all x1, blocking collectives, on_device(): lse = lax.all_to_all(lse, AXES, 0, 0, tiled=True)  9.48 us
    ppermute x2, waiting for transfers between devices, swap(): return lax.ppermute(value, 'col', [(0, 1), (1, 0)])  1.36 us
  transfers between devices with their start and end apart: 2, of which 2 were waited for; matrix products, arithmetic and copies ran while one was open for 0% of the time, Pallas kernels for 3%

profile of v15, /device:TPU:0, one launch (start us, length us, event | category | flops | bytes accessed | tf_op | source)
XLA Modules:
  0.0 49.9 jit_solution(16560087143767634971)
XLA Ops:
  0.6 0.0 copy-start.1
  0.7 0.0 copy-start.2
  0.7 0.0 copy-start.3
  0.7 0.7 %copy-done.1 = bf16[64,96]{1,0:T(8,128)(2,1)S(1)} copy-done((bf16[64,96]{1,0:T(8,128)(2,1)S(1)}, bf16[64,96]{1,0:T(8,128)(2,1)}, u32[]{:S(2)}) %copy-start.1) | copy-done | bytes 12312
  1.3 0.0 copy-done.2
  1.4 0.0 copy-done.3
  1.4 0.2 shard_map.76
  1.5 0.0 copy-start
  1.6 14.6 %all_to_all.15.mine_ref = bf16[8,64,128]{2,1,0:T(8,128)(2,1)S(1)} all-to-all(bf16[8,64,128]{2,1,0:T(8,128)(2,1)S(1)} %get-tuple-element.31.y_ref), channel_id=1, replica_groups=mesh['groups'=2,'row'=8,'col'=2] {'row'}, dimensions={0} | all-to-all | bytes 262144 | tf_op jit(solution)/shard_map/all_to_all | solution.py:477
  16.1 0.0 collective-permute-start
  16.1 0.0 copy-done
  16.1 0.8 %shard_map.77 = (bf16[128,1024]{1,0:T(8,128)(2,1)S(1)}, bf16[128,512]{1,0:T(8,128)(2,1)S(1)}, f32[1,1024]{1,0:T(1,128)S(1)}, f32[1,1024]{1,0:T(1,128)S(1)}, bf16[512,1024]{1,0:T(8,128)(2,1)S(1)}) custom-call(bf16[96,1024]{1,0:T(8,128)(2,1)S(1)} %bitcast.6, bf16[8,64,128]{2,1,0:T(8,128)(2,1)S(1)} %all_to_all.15.mine_ref), custom_call_target="tpu_custom_call" | custom-call | tf_op jit(solution)/shard_map/pallas_call | solution.py:435
  16.9 0.6 %collective-permute-done.other_ref = bf16[8,64,128]{2,1,0:T(8,128)(2,1)S(1)} collective-permute-done((bf16[8,64,128]{2,1,0:T(8,128)(2,1)S(1)}, bf16[8,64,128]{2,1,0:T(8,128)(2,1)S(1)}, u32[]{:S(2)}, u32[]{:S(2)}) %collective-permute-start) | collective-permute-done | bytes 131104 | tf_op jit(solution)/shard_map/ppermute | solution.py:451
  17.5 8.7 %shard_map.78 = (bf16[128,512]{1,0:T(8,128)(2,1)S(1)}, bf16[512,1024]{1,0:T(8,128)(2,1)S(1)}, bf16[512,1024]{1,0:T(8,128)(2,1)S(1)}, f32[1,1024]{1,0:T(1,128)S(1...) custom-call(bf16[128,1024]{1,0:T(8,128)(2,1)S(1)} %get-tuple-element.32.xa_ref, ...), custom_call_target="tpu_custom_call" | custom-call | tf_op jit(solution)/shard_map/pallas_call | solution.py:435
  26.2 9.5 %all_to_all.16.l_ref = f32[16,8,128]{2,1,0:T(8,128)S(1)} all-to-all(f32[16,8,128]{2,1,0:T(8,128)S(1)} %get-tuple-element.39), channel_id=1, replica_groups=mesh['groups'=2,'row'=8,'col'=2] {'row','col'}, dimensions={0} | all-to-all | bytes 131072 | tf_op jit(solution)/shard_map/all_to_all | solution.py:497
  35.7 1.2 %shard_map.79 = (f32[1,1024]{1,0:T(1,128)S(1)}, f32[1,1024]{1,0:T(1,128)S(1)}, f32[1,1024]{1,0:T(1,128)S(1)}, f32[8,128]{1,0:T(8,128)S(1)}, bf16[208,1024]{1,0:T...) custom-call(bf16[128,1024]{1,0:T(8,128)(2,1)S(1)} %get-tuple-element.32.xa_ref, ...), custom_call_target="tpu_custom_call" | custom-call | tf_op jit(solution)/shard_map/pallas_call | solution.py:435
  36.9 0.1 collective-permute-start.1
  36.9 0.5 %shard_map.80 = (f32[96,512]{1,0:T(8,128)S(1)}, f32[1,1024]{1,0:T(1,128)S(1)}) custom-call(bf16[128,1024]{1,0:T(8,128)(2,1)S(1)} %get-tuple-element.32.xa_ref, bf16[208,1024]{1,0:T(8,128)(2,1)S(1)} %get-tuple-element.44.xs_ref, f32[1,1024]{1,0:T(1,128)S(1)} %get-tuple-element.45.v_ref, f32[1,1024]{1,0:T(1,128)S(1)} %get-tuple-element.46.sum_ref, ...), custom_call_target="tpu_custom_call" | custom-call | tf_op jit(solution)/shard_map/pallas_call | solution.py:435
  37.5 0.8 %collective-permute-done.1.got_ref = bf16[112,512]{1,0:T(8,128)(2,1)S(1)} collective-permute-done((bf16[112,512]{1,0:T(8,128)(2,1)S(1)}, bf16[112,512]{1,0:T(8,128)(2,1)S(1)}, u32[]{:S(2)}, u32[]{:S(2)}) %collective-permute-start.1) | collective-permute-done | bytes 114720 | tf_op jit(solution)/shard_map/ppermute | solution.py:451
  38.3 0.3 shard_map.81
  38.5 10.0 %all_to_all.17.got_ref = bf16[8,64,128]{2,1,0:T(8,128)(2,1)S(1)} all-to-all(bf16[8,64,128]{2,1,0:T(8,128)(2,1)S(1)} %shard_map.81), channel_id=1, replica_groups=mesh['groups'=2,'row'=8,'col'=2] {'row'}, dimensions={0} | all-to-all | bytes 262144 | tf_op jit(solution)/shard_map/all_to_all | solution.py:513
  48.5 1.4 %shard_map.82 = (f32[1,1024]{1,0:T(1,128)}, f32[1,64]{1,0:T(1,128)}, f32[96,1024]{1,0:T(8,128)}, f32[64,96]{1,0:T(8,128)}) custom-call(bf16[128,1024]{1,0:T(8,128)(2,1)S(1)} %get-tuple-element.32.xa_ref, f32[1,1024]{1,0:T(1,128)S(1)} %get-tuple-element.33.la_ref, f32[1,1024]{1,0:T(1,128)S(1)} %get-tuple-element.47.norm_ref, ...), custom_call_target="tpu_custom_call" | custom-call | tf_op jit(solution)/shard_map/pallas_call | solution.py:435
  (1 shorter events, 0.0 us)
Async XLA Ops:
  0.6 0.7 %copy-start.1 = (bf16[64,96]{1,0:T(8,128)(2,1)S(1)}, bf16[64,96]{1,0:T(8,128)(2,1)}, u32[]{:S(2)}) copy-start(bf16[64,96]{1,0:T(8,128)(2,1)} %y_ref.1) | copy-start | bytes 36868
  0.7 0.7 %copy-start.2 = (bf16[1024]{0:T(1024)(128)(2,1)S(1)}, bf16[1024]{0:T(1024)(128)(2,1)}, u32[]{:S(2)}) copy-start(bf16[1024]{0:T(1024)(128)(2,1)} %param.6) | copy-start | bytes 6148
  0.7 0.7 %copy-start.3 = (bf16[64]{0:T(256)(128)(2,1)S(1)}, bf16[64]{0:T(256)(128)(2,1)}, u32[]{:S(2)}) copy-start(bf16[64]{0:T(256)(128)(2,1)} %param.7) | copy-start | bytes 388
  1.5 14.6 %copy-start = (bf16[1024,96]{0,1:T(8,128)(2,1)S(1)}, bf16[1024,96]{0,1:T(8,128)(2,1)}, u32[]{:S(2)}) copy-start(bf16[1024,96]{0,1:T(8,128)(2,1)} %param.4) | copy-start | bytes 589828
  16.1 1.3 %collective-permute-start = (bf16[8,64,128]{2,1,0:T(8,128)(2,1)S(1)}, bf16[8,64,128]{2,1,0:T(8,128)(2,1)S(1)}, u32[]{:S(2)}, u32[]{:S(2)}) collective-permute-start(bf16[8,64,128]{2,1,0:T(8,128)(2,1)S(1)} %all_to_all.15.mine_ref), channel_id=1, source_target_pairs={{0,1},{1,0},{2,3},{3,2},{4,5},{5,4},{6,7},{7,6},{8,9},{9,8},{10,11... | collective-permute-start | bytes 393224 | tf_op jit(solution)/shard_map/ppermute | solution.py:451
  36.9 1.4 %collective-permute-start.1 = (bf16[112,512]{1,0:T(8,128)(2,1)S(1)}, bf16[112,512]{1,0:T(8,128)(2,1)S(1)}, u32[]{:S(2)}, u32[]{:S(2)}) collective-permute-start(bf16[112,512]{1,0:T(8,128)(2,1)S(1)} %get-tuple-element.53), channel_id=1, source_target_pairs={{0,1},{1,0},{2,3},{3,2},{4,5},{5,4},{6,7},{7,6},{8,9},{9,8},{10,11... | collective-permute-start | bytes 344072 | tf_op jit(solution)/shard_map/ppermute | solution.py:451

commit v16 on v15

--- a/solution.py
+++ b/solution.py
@@ -16,9 +16,9 @@
 EXT = 32
 PAD = 16
 LANES = 128
-LIFT = 40.0
-TINY = 1e-31
-HUGE = 1e35
+LIFT = 52.0
+TINY = 1e-24
+HUGE = 5e33
 ACROSS = (((1,), (1,)), ((), ()))
 AXES = ("row", "col")
 F32 = jnp.float32
@@ -117,18 +117,13 @@
 
 
 def pack(block):
-    rows, width = block.shape
-    base = rows * width // LANES
-    spare = LANES - width
-    side = [block[base:, k : k + spare] for k in range(0, width, spare)]
-    return jnp.concatenate([block[:base], jnp.concatenate(side, axis=0)], axis=1)
-
-
-def unpack(block, rows, width):
-    base = block.shape[0]
-    rest = rows - base
-    side = [block[k : k + rest, width:] for k in range(0, base, rest)]
-    return jnp.concatenate([block[:, :width], jnp.concatenate(side, axis=1)], axis=0)
+    width, yd = block.shape
+    base = width * yd // LANES
+    return jnp.concatenate([block[k : k + base] for k in range(0, width, base)], axis=1)
+
+
+def unpack(block, yd):
+    return jnp.concatenate([block[:, k : k + yd] for k in range(0, LANES, yd)], axis=0)
 
 
 def ones_kernel(ext_ref):
@@ -344,7 +339,7 @@
     send_ref[width:, :] = ext.astype(BF16)
 
 
-def keep_kernel(xa_ref, xs_ref, v_ref, sum_ref, ym_ref, km_ref, keep_ref, norm_ref):
+def keep_kernel(log_nx, xa_ref, xs_ref, v_ref, sum_ref, ym_ref, yo_ref, km_ref, keep_ref, norm_ref, q_ref):
     width, half = keep_ref.shape
     for k in range(half // TILE):
         t = slice(k * TILE, (k + 1) * TILE)
@@ -353,6 +348,8 @@
         keep_ref[:, t] = ym_ref[:width, t].astype(F32) * sum_ref[:, t] - moment * v_ref[:, t]
     xf = xa_ref[:width, :].astype(F32)
     norm_ref[...] = jnp.sum(xf * xf, axis=0, keepdims=True)
+    mass = jnp.concatenate([ym_ref[width:, :], yo_ref[width:, :]], axis=1).astype(F32)[6:7]
+    q_ref[...] = v_ref[...] * jnp.exp(mass + log_nx)
 
 
 def add_kernel(keep_ref, sum_ref, got_ref, out_ref):
@@ -363,9 +360,9 @@
     ext = got_ref[width:, :].astype(F32)
     other = jnp.concatenate([ext[1:2] + ext[3:4], ext[0:1] + ext[2:3]], axis=1)
     sums = sums_out(to_lanes(sum_ref[...] + other)).astype(BF16)
-    total = (keep_ref[...] + got_ref[:width, :].astype(F32)).T
+    total = keep_ref[...] + got_ref[:width, :].astype(F32)
     for r in range(rows):
-        out_ref[r, :base, :] = pack(total[r * yd : (r + 1) * yd, :]).astype(BF16)
+        out_ref[r, :base, :] = pack(total[:, r * yd : (r + 1) * yd]).astype(BF16)
         out_ref[r, base:, :] = sums
 
 
@@ -380,11 +377,11 @@
 
 
 def last_kernel(
-    log_nx, xa_ref, la_ref, norm_ref, b_ref, r_ref, wr_ref, v_ref, c_ref, got_ref, ym_ref, yo_ref, km_ref, ko_ref, y_ref,
+    xa_ref, la_ref, norm_ref, b_ref, r_ref, wr_ref, q_ref, c_ref, got_ref, ym_ref, yo_ref, km_ref, ko_ref, y_ref,
     f_hbm, pot_hbm, gx_hbm, gy_hbm, f_ref, pot_ref, gx_ref, gy_ref, ys_ref, sum_ref, sems,
 ):
     width, n = gx_ref.shape
-    ny = v_ref.shape[1]
+    ny = q_ref.shape[1]
     yd = y_ref.shape[1]
     base = yd * width // LANES
     count = ny // LANES
@@ -407,7 +404,7 @@
     colsum = own_part(sum_ref, yd)
     c_term = own_part(c_ref, yd)
     own = y_ref[0].astype(F32)
-    gy_ref[...] = unpack(total[:base], yd, width) * (
+    gy_ref[...] = unpack(total[:base], yd).T * (
         jnp.exp(own[:, width + 6 : width + 7]) * to_column(1.0 / colsum)
     )
     leave(gy_ref, gy_hbm)
@@ -415,10 +412,8 @@
     pot_ref[...] = norm / width - EPSILON * (jnp.log(colsum) - kappa * c_term)
     leave(pot_ref, pot_hbm)
     half = ny // 2
-    yt = jnp.concatenate([ym_ref[...], yo_ref[...]], axis=1)
-    mass = yt[width:].astype(F32)[6:7]
-    q = v_ref[...] * jnp.exp(mass + log_nx - jnp.log(from_lanes(sums)))
-    stack(ys_ref, width, yt[:width], q)
+    yt = jnp.concatenate([ym_ref[:width, :], yo_ref[:width, :]], axis=1)
+    stack(ys_ref, width, yt, q_ref[...] / from_lanes(sums))
     for k in range(n // TILE):
         t = slice(k * TILE, (k + 1) * TILE)
         product = jnp.dot(ys_ref[:, :half], km_ref[:, t], preferred_element_type=F32) + jnp.dot(
@@ -504,22 +499,23 @@
         [], limit, xa, log_a, omega, mu, lse, yt_mine, yt_other, kept_mine, kept_other,
     )
     got = swap(send)
-    keep, norm = call(
-        keep_kernel, (shape((width, half)), shape((1, n))), [], limit, xa, xs, v, sums, yt_mine, kept_mine
+    keep, norm, q = call(
+        run(keep_kernel, log_nx), (shape((width, half)), shape((1, n)), shape((1, ny))), [],
+        limit, xa, xs, v, sums, yt_mine, yt_other, kept_mine,
     )
     part = call(
         add_kernel, shape((rows, yd * width // LANES + extra, LANES), BF16), [], limit, keep, sums, got
     )
     part = lax.all_to_all(part, "row", 0, 0, tiled=True)
     f_pot, g_pot, grad_xt, grad_y = call(
-        run(last_kernel, log_nx),
+        last_kernel,
         (shape((1, n)), shape((1, yd)), shape((width, n)), shape((yd, width))),
         [
             vmem((1, n), F32), vmem((1, yd), F32), vmem((width, n), F32), vmem((yd, width), F32),
             vmem((2 * width + PAD, ny), BF16), vmem((count, LANES), F32),
             pltpu.SemaphoreType.DMA((3 + n // TILE,)),
         ],
-        limit, xa, log_a, norm, b_term, r, wr, v, c_term, part, yt_mine, yt_other, kept_mine, kept_other, y_own,
+        limit, xa, log_a, norm, b_term, r, wr, q, c_term, part, yt_mine, yt_other, kept_mine, kept_other, y_own,
         out_space=pl.ANY,
     )
     return f_pot.reshape(n), g_pot.reshape(yd), grad_xt.T, grad_y

time: 50.3 us -> 50.2 us (level)
  no operation moved by 1% of the time
where the time goes in v16:
time: 50.2 us; the launch traced here: 49.8 us
  blocking collectives  34 us (68%)
  Pallas kernels  13 us (26%)
  waiting for transfers between devices  1.38 us (3%)
  between operations  0.72 us (1%)
  local copies, waits for them, and re-layouts  0.69 us (1%)
    all_to_all x1, blocking collectives, on_device(): y_mine = lax.all_to_all(y_own, 'row', 0, 0, tiled=True)  14.6 us
    pallas_call x8, Pallas kernels, call(): pl.pallas_call(kernel, out_shape=outs, in_specs=[pl.BlockSpec(memory_spac...  13 us
    all_to_all x1, blocking collectives, on_device(): part = lax.all_to_all(part, 'row', 0, 0, tiled=True)  9.97 us
    all_to_all x1, blocking collectives, on_device(): lse = lax.all_to_all(lse, AXES, 0, 0, tiled=True)  9.48 us
    ppermute x2, waiting for transfers between devices, swap(): return lax.ppermute(value, 'col', [(0, 1), (1, 0)])  1.38 us
  transfers between devices with their start and end apart: 2, of which 2 were waited for; matrix products, arithmetic and copies ran while one was open for 0% of the time, Pallas kernels for 3%

profile of v16, /device:TPU:0, one launch (start us, length us, event | category | flops | bytes accessed | tf_op | source)
XLA Modules:
  0.0 49.8 jit_solution(11675598357136460251)
XLA Ops:
  0.6 0.0 copy-start.1
  0.7 0.0 copy-start.2
  0.7 0.0 copy-start.3
  0.7 0.7 %copy-done.1 = bf16[64,96]{1,0:T(8,128)(2,1)S(1)} copy-done((bf16[64,96]{1,0:T(8,128)(2,1)S(1)}, bf16[64,96]{1,0:T(8,128)(2,1)}, u32[]{:S(2)}) %copy-start.1) | copy-done | bytes 12312
  1.3 0.0 copy-done.2
  1.4 0.0 copy-done.3
  1.4 0.2 shard_map.76
  1.5 0.0 copy-start
  1.6 14.6 %all_to_all.15.mine_ref = bf16[8,64,128]{2,1,0:T(8,128)(2,1)S(1)} all-to-all(bf16[8,64,128]{2,1,0:T(8,128)(2,1)S(1)} %get-tuple-element.32.y_ref), channel_id=1, replica_groups=mesh['groups'=2,'row'=8,'col'=2] {'row'}, dimensions={0} | all-to-all | bytes 262144 | tf_op jit(solution)/shard_map/all_to_all | solution.py:472
  16.1 0.0 collective-permute-start
  16.1 0.0 copy-done
  16.1 0.8 %shard_map.77 = (bf16[128,1024]{1,0:T(8,128)(2,1)S(1)}, bf16[128,512]{1,0:T(8,128)(2,1)S(1)}, f32[1,1024]{1,0:T(1,128)S(1)}, f32[1,1024]{1,0:T(1,128)S(1)}, bf16[512,1024]{1,0:T(8,128)(2,1)S(1)}) custom-call(bf16[96,1024]{1,0:T(8,128)(2,1)S(1)} %bitcast.6, bf16[8,64,128]{2,1,0:T(8,128)(2,1)S(1)} %all_to_all.15.mine_ref), custom_call_target="tpu_custom_call" | custom-call | tf_op jit(solution)/shard_map/pallas_call | solution.py:430
  16.9 0.6 %collective-permute-done.other_ref = bf16[8,64,128]{2,1,0:T(8,128)(2,1)S(1)} collective-permute-done((bf16[8,64,128]{2,1,0:T(8,128)(2,1)S(1)}, bf16[8,64,128]{2,1,0:T(8,128)(2,1)S(1)}, u32[]{:S(2)}, u32[]{:S(2)}) %collective-permute-start) | collective-permute-done | bytes 131104 | tf_op jit(solution)/shard_map/ppermute | solution.py:446
  17.5 8.8 %shard_map.78 = (bf16[128,512]{1,0:T(8,128)(2,1)S(1)}, bf16[512,1024]{1,0:T(8,128)(2,1)S(1)}, bf16[512,1024]{1,0:T(8,128)(2,1)S(1)}, f32[1,1024]{1,0:T(1,128)S(1...) custom-call(bf16[128,1024]{1,0:T(8,128)(2,1)S(1)} %get-tuple-element.33.xa_ref, ...), custom_call_target="tpu_custom_call" | custom-call | tf_op jit(solution)/shard_map/pallas_call | solution.py:430
  26.2 9.5 %all_to_all.16.l_ref = f32[16,8,128]{2,1,0:T(8,128)S(1)} all-to-all(f32[16,8,128]{2,1,0:T(8,128)S(1)} %get-tuple-element.40), channel_id=1, replica_groups=mesh['groups'=2,'row'=8,'col'=2] {'row','col'}, dimensions={0} | all-to-all | bytes 131072 | tf_op jit(solution)/shard_map/all_to_all | solution.py:492
  35.7 1.2 %shard_map.79 = (f32[1,1024]{1,0:T(1,128)S(1)}, f32[1,1024]{1,0:T(1,128)S(1)}, f32[1,1024]{1,0:T(1,128)S(1)}, f32[8,128]{1,0:T(8,128)S(1)}, bf16[208,1024]{1,0:T...) custom-call(bf16[128,1024]{1,0:T(8,128)(2,1)S(1)} %get-tuple-element.33.xa_ref, ...), custom_call_target="tpu_custom_call" | custom-call | tf_op jit(solution)/shard_map/pallas_call | solution.py:430
  36.9 0.1 collective-permute-start.1
  37.0 0.5 %shard_map.80 = (f32[96,512]{1,0:T(8,128)S(1)}, f32[1,1024]{1,0:T(1,128)S(1)}, f32[1,1024]{1,0:T(1,128)S(1)}) custom-call(bf16[128,1024]{1,0:T(8,128)(2,1)S(1)} %get-tuple-element.33.xa_ref, bf16[208,1024]{1,0:T(8,128)(2,1)S(1)} %get-tuple-element.45.xs_ref, f32[1,1024]{1,0:T(1,128)S(1)} %get-tuple-element.46.v_ref, ...), custom_call_target="tpu_custom_call" | custom-call | tf_op jit(solution)/shard_map/pallas_call | solution.py:430
  37.5 0.8 %collective-permute-done.1.got_ref = bf16[112,512]{1,0:T(8,128)(2,1)S(1)} collective-permute-done((bf16[112,512]{1,0:T(8,128)(2,1)S(1)}, bf16[112,512]{1,0:T(8,128)(2,1)S(1)}, u32[]{:S(2)}, u32[]{:S(2)}) %collective-permute-start.1) | collective-permute-done | bytes 114720 | tf_op jit(solution)/shard_map/ppermute | solution.py:446
  38.3 0.1 shard_map.81
  38.4 10.0 %all_to_all.17.got_ref = bf16[8,64,128]{2,1,0:T(8,128)(2,1)S(1)} all-to-all(bf16[8,64,128]{2,1,0:T(8,128)(2,1)S(1)} %shard_map.81), channel_id=1, replica_groups=mesh['groups'=2,'row'=8,'col'=2] {'row'}, dimensions={0} | all-to-all | bytes 262144 | tf_op jit(solution)/shard_map/all_to_all | solution.py:509
  48.4 1.5 %shard_map.82 = (f32[1,1024]{1,0:T(1,128)}, f32[1,64]{1,0:T(1,128)}, f32[96,1024]{1,0:T(8,128)}, f32[64,96]{1,0:T(8,128)}) custom-call(bf16[128,1024]{1,0:T(8,128)(2,1)S(1)} %get-tuple-element.33.xa_ref, f32[1,1024]{1,0:T(1,128)S(1)} %get-tuple-element.34.la_ref, f32[1,1024]{1,0:T(1,128)S(1)} %get-tuple-element.48.norm_ref, ...), custom_call_target="tpu_custom_call" | custom-call | tf_op jit(solution)/shard_map/pallas_call | solution.py:430
  (1 shorter events, 0.0 us)
Async XLA Ops:
  0.6 0.7 %copy-start.1 = (bf16[64,96]{1,0:T(8,128)(2,1)S(1)}, bf16[64,96]{1,0:T(8,128)(2,1)}, u32[]{:S(2)}) copy-start(bf16[64,96]{1,0:T(8,128)(2,1)} %y_ref.1) | copy-start | bytes 36868
  0.7 0.7 %copy-start.2 = (bf16[1024]{0:T(1024)(128)(2,1)S(1)}, bf16[1024]{0:T(1024)(128)(2,1)}, u32[]{:S(2)}) copy-start(bf16[1024]{0:T(1024)(128)(2,1)} %param.6) | copy-start | bytes 6148
  0.7 0.7 %copy-start.3 = (bf16[64]{0:T(256)(128)(2,1)S(1)}, bf16[64]{0:T(256)(128)(2,1)}, u32[]{:S(2)}) copy-start(bf16[64]{0:T(256)(128)(2,1)} %param.7) | copy-start | bytes 388
  1.5 14.6 %copy-start = (bf16[1024,96]{0,1:T(8,128)(2,1)S(1)}, bf16[1024,96]{0,1:T(8,128)(2,1)}, u32[]{:S(2)}) copy-start(bf16[1024,96]{0,1:T(8,128)(2,1)} %param.4) | copy-start | bytes 589828
  16.1 1.3 %collective-permute-start = (bf16[8,64,128]{2,1,0:T(8,128)(2,1)S(1)}, bf16[8,64,128]{2,1,0:T(8,128)(2,1)S(1)}, u32[]{:S(2)}, u32[]{:S(2)}) collective-permute-start(bf16[8,64,128]{2,1,0:T(8,128)(2,1)S(1)} %all_to_all.15.mine_ref), channel_id=1, source_target_pairs={{0,1},{1,0},{2,3},{3,2},{4,5},{5,4},{6,7},{7,6},{8,9},{9,8},{10,11... | collective-permute-start | bytes 393224 | tf_op jit(solution)/shard_map/ppermute | solution.py:446
  36.9 1.4 %collective-permute-start.1 = (bf16[112,512]{1,0:T(8,128)(2,1)S(1)}, bf16[112,512]{1,0:T(8,128)(2,1)S(1)}, u32[]{:S(2)}, u32[]{:S(2)}) collective-permute-start(bf16[112,512]{1,0:T(8,128)(2,1)S(1)} %get-tuple-element.55), channel_id=1, source_target_pairs={{0,1},{1,0},{2,3},{3,2},{4,5},{5,4},{6,7},{7,6},{8,9},{9,8},{10,11... | collective-permute-start | bytes 344072 | tf_op jit(solution)/shard_map/ppermute | solution.py:446

commit v17 on v16

--- a/solution.py
+++ b/solution.py
@@ -11,8 +11,8 @@
 ITERS = 2
 EPSILON = 0.02
 LOG2E = math.log2(math.e)
-TILE = 256
-STEP = 32
+TILE = 512
+STEP = 16
 EXT = 32
 PAD = 16
 LANES = 128

time: 50.2 us -> 50.2 us (level)
  no operation moved by 1% of the time
where the time goes in v17:
time: 50.2 us; the launch traced here: 49.8 us
  blocking collectives  34 us (68%)
  Pallas kernels  13 us (26%)
  waiting for transfers between devices  1.4 us (3%)
  between operations  0.72 us (1%)
  local copies, waits for them, and re-layouts  0.69 us (1%)
    all_to_all x1, blocking collectives, on_device(): y_mine = lax.all_to_all(y_own, 'row', 0, 0, tiled=True)  14.6 us
    pallas_call x8, Pallas kernels, call(): pl.pallas_call(kernel, out_shape=outs, in_specs=[pl.BlockSpec(memory_spac...  13 us
    all_to_all x1, blocking collectives, on_device(): part = lax.all_to_all(part, 'row', 0, 0, tiled=True)  9.97 us
    all_to_all x1, blocking collectives, on_device(): lse = lax.all_to_all(lse, AXES, 0, 0, tiled=True)  9.48 us
    ppermute x2, waiting for transfers between devices, swap(): return lax.ppermute(value, 'col', [(0, 1), (1, 0)])  1.4 us
  transfers between devices with their start and end apart: 2, of which 2 were waited for; matrix products, arithmetic and copies ran while one was open for 0% of the time, Pallas kernels for 3%

profile of v17, /device:TPU:0, one launch (start us, length us, event | category | flops | bytes accessed | tf_op | source)
XLA Modules:
  0.0 49.8 jit_solution(10885135980162686069)
XLA Ops:
  0.6 0.0 copy-start.1
  0.7 0.0 copy-start.2
  0.7 0.0 copy-start.3
  0.7 0.7 %copy-done.1 = bf16[64,96]{1,0:T(8,128)(2,1)S(1)} copy-done((bf16[64,96]{1,0:T(8,128)(2,1)S(1)}, bf16[64,96]{1,0:T(8,128)(2,1)}, u32[]{:S(2)}) %copy-start.1) | copy-done | bytes 12312
  1.3 0.0 copy-done.2
  1.4 0.0 copy-done.3
  1.4 0.2 shard_map.76
  1.5 0.0 copy-start
  1.6 14.6 %all_to_all.15.mine_ref = bf16[8,64,128]{2,1,0:T(8,128)(2,1)S(1)} all-to-all(bf16[8,64,128]{2,1,0:T(8,128)(2,1)S(1)} %get-tuple-element.32.y_ref), channel_id=1, replica_groups=mesh['groups'=2,'row'=8,'col'=2] {'row'}, dimensions={0} | all-to-all | bytes 262144 | tf_op jit(solution)/shard_map/all_to_all | solution.py:472
  16.1 0.0 collective-permute-start
  16.1 0.0 copy-done
  16.1 0.7 %shard_map.77 = (bf16[128,1024]{1,0:T(8,128)(2,1)S(1)}, bf16[128,512]{1,0:T(8,128)(2,1)S(1)}, f32[1,1024]{1,0:T(1,128)S(1)}, f32[1,1024]{1,0:T(1,128)S(1)}, bf16[512,1024]{1,0:T(8,128)(2,1)S(1)}) custom-call(bf16[96,1024]{1,0:T(8,128)(2,1)S(1)} %bitcast.6, bf16[8,64,128]{2,1,0:T(8,128)(2,1)S(1)} %all_to_all.15.mine_ref), custom_call_target="tpu_custom_call" | custom-call | tf_op jit(solution)/shard_map/pallas_call | solution.py:430
  16.9 0.6 %collective-permute-done.other_ref = bf16[8,64,128]{2,1,0:T(8,128)(2,1)S(1)} collective-permute-done((bf16[8,64,128]{2,1,0:T(8,128)(2,1)S(1)}, bf16[8,64,128]{2,1,0:T(8,128)(2,1)S(1)}, u32[]{:S(2)}, u32[]{:S(2)}) %collective-permute-start) | collective-permute-done | bytes 131104 | tf_op jit(solution)/shard_map/ppermute | solution.py:446
  17.5 8.8 %shard_map.78 = (bf16[128,512]{1,0:T(8,128)(2,1)S(1)}, bf16[512,1024]{1,0:T(8,128)(2,1)S(1)}, bf16[512,1024]{1,0:T(8,128)(2,1)S(1)}, f32[1,1024]{1,0:T(1,128)S(1...) custom-call(bf16[128,1024]{1,0:T(8,128)(2,1)S(1)} %get-tuple-element.33.xa_ref, ...), custom_call_target="tpu_custom_call" | custom-call | tf_op jit(solution)/shard_map/pallas_call | solution.py:430
  26.2 9.5 %all_to_all.16.l_ref = f32[16,8,128]{2,1,0:T(8,128)S(1)} all-to-all(f32[16,8,128]{2,1,0:T(8,128)S(1)} %get-tuple-element.40), channel_id=1, replica_groups=mesh['groups'=2,'row'=8,'col'=2] {'row','col'}, dimensions={0} | all-to-all | bytes 131072 | tf_op jit(solution)/shard_map/all_to_all | solution.py:492
  35.7 1.2 %shard_map.79 = (f32[1,1024]{1,0:T(1,128)S(1)}, f32[1,1024]{1,0:T(1,128)S(1)}, f32[1,1024]{1,0:T(1,128)S(1)}, f32[8,128]{1,0:T(8,128)S(1)}, bf16[208,1024]{1,0:T...) custom-call(bf16[128,1024]{1,0:T(8,128)(2,1)S(1)} %get-tuple-element.33.xa_ref, ...), custom_call_target="tpu_custom_call" | custom-call | tf_op jit(solution)/shard_map/pallas_call | solution.py:430
  36.9 0.1 collective-permute-start.1
  37.0 0.5 %shard_map.80 = (f32[96,512]{1,0:T(8,128)S(1)}, f32[1,1024]{1,0:T(1,128)S(1)}, f32[1,1024]{1,0:T(1,128)S(1)}) custom-call(bf16[128,1024]{1,0:T(8,128)(2,1)S(1)} %get-tuple-element.33.xa_ref, bf16[208,1024]{1,0:T(8,128)(2,1)S(1)} %get-tuple-element.45.xs_ref, f32[1,1024]{1,0:T(1,128)S(1)} %get-tuple-element.46.v_ref, ...), custom_call_target="tpu_custom_call" | custom-call | tf_op jit(solution)/shard_map/pallas_call | solution.py:430
  37.5 0.8 %collective-permute-done.1.got_ref = bf16[112,512]{1,0:T(8,128)(2,1)S(1)} collective-permute-done((bf16[112,512]{1,0:T(8,128)(2,1)S(1)}, bf16[112,512]{1,0:T(8,128)(2,1)S(1)}, u32[]{:S(2)}, u32[]{:S(2)}) %collective-permute-start.1) | collective-permute-done | bytes 114720 | tf_op jit(solution)/shard_map/ppermute | solution.py:446
  38.3 0.1 shard_map.81
  38.4 10.0 %all_to_all.17.got_ref = bf16[8,64,128]{2,1,0:T(8,128)(2,1)S(1)} all-to-all(bf16[8,64,128]{2,1,0:T(8,128)(2,1)S(1)} %shard_map.81), channel_id=1, replica_groups=mesh['groups'=2,'row'=8,'col'=2] {'row'}, dimensions={0} | all-to-all | bytes 262144 | tf_op jit(solution)/shard_map/all_to_all | solution.py:509
  48.4 1.5 %shard_map.82 = (f32[1,1024]{1,0:T(1,128)}, f32[1,64]{1,0:T(1,128)}, f32[96,1024]{1,0:T(8,128)}, f32[64,96]{1,0:T(8,128)}) custom-call(bf16[128,1024]{1,0:T(8,128)(2,1)S(1)} %get-tuple-element.33.xa_ref, f32[1,1024]{1,0:T(1,128)S(1)} %get-tuple-element.34.la_ref, f32[1,1024]{1,0:T(1,128)S(1)} %get-tuple-element.48.norm_ref, ...), custom_call_target="tpu_custom_call" | custom-call | tf_op jit(solution)/shard_map/pallas_call | solution.py:430
  (1 shorter events, 0.0 us)
Async XLA Ops:
  0.6 0.7 %copy-start.1 = (bf16[64,96]{1,0:T(8,128)(2,1)S(1)}, bf16[64,96]{1,0:T(8,128)(2,1)}, u32[]{:S(2)}) copy-start(bf16[64,96]{1,0:T(8,128)(2,1)} %y_ref.1) | copy-start | bytes 36868
  0.7 0.7 %copy-start.2 = (bf16[1024]{0:T(1024)(128)(2,1)S(1)}, bf16[1024]{0:T(1024)(128)(2,1)}, u32[]{:S(2)}) copy-start(bf16[1024]{0:T(1024)(128)(2,1)} %param.6) | copy-start | bytes 6148
  0.7 0.7 %copy-start.3 = (bf16[64]{0:T(256)(128)(2,1)S(1)}, bf16[64]{0:T(256)(128)(2,1)}, u32[]{:S(2)}) copy-start(bf16[64]{0:T(256)(128)(2,1)} %param.7) | copy-start | bytes 388
  1.5 14.6 %copy-start = (bf16[1024,96]{0,1:T(8,128)(2,1)S(1)}, bf16[1024,96]{0,1:T(8,128)(2,1)}, u32[]{:S(2)}) copy-start(bf16[1024,96]{0,1:T(8,128)(2,1)} %param.4) | copy-start | bytes 589828
  16.1 1.3 %collective-permute-start = (bf16[8,64,128]{2,1,0:T(8,128)(2,1)S(1)}, bf16[8,64,128]{2,1,0:T(8,128)(2,1)S(1)}, u32[]{:S(2)}, u32[]{:S(2)}) collective-permute-start(bf16[8,64,128]{2,1,0:T(8,128)(2,1)S(1)} %all_to_all.15.mine_ref), channel_id=1, source_target_pairs={{0,1},{1,0},{2,3},{3,2},{4,5},{5,4},{6,7},{7,6},{8,9},{9,8},{10,11... | collective-permute-start | bytes 393224 | tf_op jit(solution)/shard_map/ppermute | solution.py:446
  36.9 1.4 %collective-permute-start.1 = (bf16[112,512]{1,0:T(8,128)(2,1)S(1)}, bf16[112,512]{1,0:T(8,128)(2,1)S(1)}, u32[]{:S(2)}, u32[]{:S(2)}) collective-permute-start(bf16[112,512]{1,0:T(8,128)(2,1)S(1)} %get-tuple-element.55), channel_id=1, source_target_pairs={{0,1},{1,0},{2,3},{3,2},{4,5},{5,4},{6,7},{7,6},{8,9},{9,8},{10,11... | collective-permute-start | bytes 344072 | tf_op jit(solution)/shard_map/ppermute | solution.py:446

commit v18 on v17

--- a/solution.py
+++ b/solution.py
@@ -328,15 +328,13 @@
         total = total * v_other[:, t]
         totals.append(total)
         part = yo_ref[:width, t].astype(F32) * total - moment * v_other[:, t]
-        send_ref[:width, t] = part.astype(BF16)
+        send_ref[:width, t] = part
     s_other = jnp.concatenate(totals, axis=1)
     ext = lax.dot_general(xs_ref[2 * width :, :], km_ref[...], ACROSS, preferred_element_type=F32)
     s_mine = sum_pieces(ext) * v_mine
     sum_ref[...] = jnp.concatenate([s_mine, s_other], axis=1)
-    high_m, high_o = s_mine.astype(BF16).astype(F32), s_other.astype(BF16).astype(F32)
-    index = lax.broadcasted_iota(jnp.int32, (PAD, half), 0)
-    ext = select(index, {0: high_m, 1: high_o, 2: s_mine - high_m, 3: s_other - high_o})
-    send_ref[width:, :] = ext.astype(BF16)
+    index = lax.broadcasted_iota(jnp.int32, (8, half), 0)
+    send_ref[width:, :] = select(index, {0: s_mine, 1: s_other})
 
 
 def keep_kernel(log_nx, xa_ref, xs_ref, v_ref, sum_ref, ym_ref, yo_ref, km_ref, keep_ref, norm_ref, q_ref):
@@ -357,10 +355,9 @@
     rows = out_ref.shape[0]
     yd = half // rows
     base = yd * width // LANES
-    ext = got_ref[width:, :].astype(F32)
-    other = jnp.concatenate([ext[1:2] + ext[3:4], ext[0:1] + ext[2:3]], axis=1)
+    other = jnp.concatenate([got_ref[width + 1 : width + 2, :], got_ref[width : width + 1, :]], axis=1)
     sums = sums_out(to_lanes(sum_ref[...] + other)).astype(BF16)
-    total = keep_ref[...] + got_ref[:width, :].astype(F32)
+    total = keep_ref[...] + got_ref[:width, :]
     for r in range(rows):
         out_ref[r, :base, :] = pack(total[:, r * yd : (r + 1) * yd]).astype(BF16)
         out_ref[r, base:, :] = sums
@@ -494,7 +491,7 @@
         run(second_kernel, log_ny),
         (
             shape((1, n)), shape((1, n)), shape((1, ny)), shape((count, LANES)),
-            shape((2 * width + PAD, n), BF16), shape((1, ny)), shape((width + PAD, half), BF16),
+            shape((2 * width + PAD, n), BF16), shape((1, ny)), shape((width + 8, half)),
         ),
         [], limit, xa, log_a, omega, mu, lse, yt_mine, yt_other, kept_mine, kept_other,
     )

time: 50.2 us -> 50.3 us (level)
  no operation moved by 1% of the time
where the time goes in v18:
time: 50.3 us; the launch traced here: 50 us
  blocking collectives  34 us (68%)
  Pallas kernels  13 us (26%)
  waiting for transfers between devices  1.54 us (3%)
  between operations  0.71 us (1%)
  local copies, waits for them, and re-layouts  0.69 us (1%)
    all_to_all x1, blocking collectives, on_device(): y_mine = lax.all_to_all(y_own, 'row', 0, 0, tiled=True)  14.6 us
    pallas_call x8, Pallas kernels, call(): pl.pallas_call(kernel, out_shape=outs, in_specs=[pl.BlockSpec(memory_spac...  13 us
    all_to_all x1, blocking collectives, on_device(): part = lax.all_to_all(part, 'row', 0, 0, tiled=True)  9.96 us
    all_to_all x1, blocking collectives, on_device(): lse = lax.all_to_all(lse, AXES, 0, 0, tiled=True)  9.48 us
    ppermute x2, waiting for transfers between devices, swap(): return lax.ppermute(value, 'col', [(0, 1), (1, 0)])  1.54 us
  transfers between devices with their start and end apart: 2, of which 2 were waited for; matrix products, arithmetic and copies ran while one was open for 0% of the time, Pallas kernels for 3%

profile of v18, /device:TPU:0, one launch (start us, length us, event | category | flops | bytes accessed | tf_op | source)
XLA Modules:
  0.0 50.0 jit_solution(17368655722137385828)
XLA Ops:
  0.6 0.0 copy-start.1
  0.7 0.0 copy-start.2
  0.7 0.0 copy-start.3
  0.7 0.7 %copy-done.1 = bf16[64,96]{1,0:T(8,128)(2,1)S(1)} copy-done((bf16[64,96]{1,0:T(8,128)(2,1)S(1)}, bf16[64,96]{1,0:T(8,128)(2,1)}, u32[]{:S(2)}) %copy-start.1) | copy-done | bytes 12312
  1.3 0.0 copy-done.2
  1.4 0.0 copy-done.3
  1.4 0.2 shard_map.76
  1.5 0.0 copy-start
  1.6 14.6 %all_to_all.15.mine_ref = bf16[8,64,128]{2,1,0:T(8,128)(2,1)S(1)} all-to-all(bf16[8,64,128]{2,1,0:T(8,128)(2,1)S(1)} %get-tuple-element.32.y_ref), channel_id=1, replica_groups=mesh['groups'=2,'row'=8,'col'=2] {'row'}, dimensions={0} | all-to-all | bytes 262144 | tf_op jit(solution)/shard_map/all_to_all | solution.py:469
  16.1 0.0 collective-permute-start
  16.1 0.0 copy-done
  16.1 0.7 %shard_map.77 = (bf16[128,1024]{1,0:T(8,128)(2,1)S(1)}, bf16[128,512]{1,0:T(8,128)(2,1)S(1)}, f32[1,1024]{1,0:T(1,128)S(1)}, f32[1,1024]{1,0:T(1,128)S(1)}, bf16[512,1024]{1,0:T(8,128)(2,1)S(1)}) custom-call(bf16[96,1024]{1,0:T(8,128)(2,1)S(1)} %bitcast.6, bf16[8,64,128]{2,1,0:T(8,128)(2,1)S(1)} %all_to_all.15.mine_ref), custom_call_target="tpu_custom_call" | custom-call | tf_op jit(solution)/shard_map/pallas_call | solution.py:427
  16.9 0.6 %collective-permute-done.other_ref = bf16[8,64,128]{2,1,0:T(8,128)(2,1)S(1)} collective-permute-done((bf16[8,64,128]{2,1,0:T(8,128)(2,1)S(1)}, bf16[8,64,128]{2,1,0:T(8,128)(2,1)S(1)}, u32[]{:S(2)}, u32[]{:S(2)}) %collective-permute-start) | collective-permute-done | bytes 131104 | tf_op jit(solution)/shard_map/ppermute | solution.py:443
  17.5 8.8 %shard_map.78 = (bf16[128,512]{1,0:T(8,128)(2,1)S(1)}, bf16[512,1024]{1,0:T(8,128)(2,1)S(1)}, bf16[512,1024]{1,0:T(8,128)(2,1)S(1)}, f32[1,1024]{1,0:T(1,128)S(1...) custom-call(bf16[128,1024]{1,0:T(8,128)(2,1)S(1)} %get-tuple-element.33.xa_ref, ...), custom_call_target="tpu_custom_call" | custom-call | tf_op jit(solution)/shard_map/pallas_call | solution.py:427
  26.2 9.5 %all_to_all.16.l_ref = f32[16,8,128]{2,1,0:T(8,128)S(1)} all-to-all(f32[16,8,128]{2,1,0:T(8,128)S(1)} %get-tuple-element.40), channel_id=1, replica_groups=mesh['groups'=2,'row'=8,'col'=2] {'row','col'}, dimensions={0} | all-to-all | bytes 131072 | tf_op jit(solution)/shard_map/all_to_all | solution.py:489
  35.7 1.2 %shard_map.79 = (f32[1,1024]{1,0:T(1,128)S(1)}, f32[1,1024]{1,0:T(1,128)S(1)}, f32[1,1024]{1,0:T(1,128)S(1)}, f32[8,128]{1,0:T(8,128)S(1)}, bf16[208,1024]{1,0:T...) custom-call(bf16[128,1024]{1,0:T(8,128)(2,1)S(1)} %get-tuple-element.33.xa_ref, ...), custom_call_target="tpu_custom_call" | custom-call | tf_op jit(solution)/shard_map/pallas_call | solution.py:427
  36.9 0.1 collective-permute-start.1
  37.0 0.5 %shard_map.80 = (f32[96,512]{1,0:T(8,128)S(1)}, f32[1,1024]{1,0:T(1,128)S(1)}, f32[1,1024]{1,0:T(1,128)S(1)}) custom-call(bf16[128,1024]{1,0:T(8,128)(2,1)S(1)} %get-tuple-element.33.xa_ref, bf16[208,1024]{1,0:T(8,128)(2,1)S(1)} %get-tuple-element.45.xs_ref, f32[1,1024]{1,0:T(1,128)S(1)} %get-tuple-element.46.v_ref, ...), custom_call_target="tpu_custom_call" | custom-call | tf_op jit(solution)/shard_map/pallas_call | solution.py:427
  37.5 0.9 %collective-permute-done.1.got_ref = f32[104,512]{1,0:T(8,128)S(1)} collective-permute-done((f32[104,512]{1,0:T(8,128)S(1)}, f32[104,512]{1,0:T(8,128)S(1)}, u32[]{:S(2)}, u32[]{:S(2)}) %collective-permute-start.1) | collective-permute-done | bytes 213024 | tf_op jit(solution)/shard_map/ppermute | solution.py:443
  38.4 0.1 shard_map.81
  38.5 10.0 %all_to_all.17.got_ref = bf16[8,64,128]{2,1,0:T(8,128)(2,1)S(1)} all-to-all(bf16[8,64,128]{2,1,0:T(8,128)(2,1)S(1)} %shard_map.81), channel_id=1, replica_groups=mesh['groups'=2,'row'=8,'col'=2] {'row'}, dimensions={0} | all-to-all | bytes 262144 | tf_op jit(solution)/shard_map/all_to_all | solution.py:506
  48.5 1.5 %shard_map.82 = (f32[1,1024]{1,0:T(1,128)}, f32[1,64]{1,0:T(1,128)}, f32[96,1024]{1,0:T(8,128)}, f32[64,96]{1,0:T(8,128)}) custom-call(bf16[128,1024]{1,0:T(8,128)(2,1)S(1)} %get-tuple-element.33.xa_ref, f32[1,1024]{1,0:T(1,128)S(1)} %get-tuple-element.34.la_ref, f32[1,1024]{1,0:T(1,128)S(1)} %get-tuple-element.48.norm_ref, ...), custom_call_target="tpu_custom_call" | custom-call | tf_op jit(solution)/shard_map/pallas_call | solution.py:427
  (1 shorter events, 0.0 us)
Async XLA Ops:
  0.6 0.7 %copy-start.1 = (bf16[64,96]{1,0:T(8,128)(2,1)S(1)}, bf16[64,96]{1,0:T(8,128)(2,1)}, u32[]{:S(2)}) copy-start(bf16[64,96]{1,0:T(8,128)(2,1)} %y_ref.1) | copy-start | bytes 36868
  0.7 0.7 %copy-start.2 = (bf16[1024]{0:T(1024)(128)(2,1)S(1)}, bf16[1024]{0:T(1024)(128)(2,1)}, u32[]{:S(2)}) copy-start(bf16[1024]{0:T(1024)(128)(2,1)} %param.6) | copy-start | bytes 6148
  0.7 0.7 %copy-start.3 = (bf16[64]{0:T(256)(128)(2,1)S(1)}, bf16[64]{0:T(256)(128)(2,1)}, u32[]{:S(2)}) copy-start(bf16[64]{0:T(256)(128)(2,1)} %param.7) | copy-start | bytes 388
  1.5 14.6 %copy-start = (bf16[1024,96]{0,1:T(8,128)(2,1)S(1)}, bf16[1024,96]{0,1:T(8,128)(2,1)}, u32[]{:S(2)}) copy-start(bf16[1024,96]{0,1:T(8,128)(2,1)} %param.4) | copy-start | bytes 589828
  16.1 1.3 %collective-permute-start = (bf16[8,64,128]{2,1,0:T(8,128)(2,1)S(1)}, bf16[8,64,128]{2,1,0:T(8,128)(2,1)S(1)}, u32[]{:S(2)}, u32[]{:S(2)}) collective-permute-start(bf16[8,64,128]{2,1,0:T(8,128)(2,1)S(1)} %all_to_all.15.mine_ref), channel_id=1, source_target_pairs={{0,1},{1,0},{2,3},{3,2},{4,5},{5,4},{6,7},{7,6},{8,9},{9,8},{10,11... | collective-permute-start | bytes 393224 | tf_op jit(solution)/shard_map/ppermute | solution.py:443
  36.9 1.5 %collective-permute-start.1 = (f32[104,512]{1,0:T(8,128)S(1)}, f32[104,512]{1,0:T(8,128)S(1)}, u32[]{:S(2)}, u32[]{:S(2)}) collective-permute-start(f32[104,512]{1,0:T(8,128)S(1)} %get-tuple-element.55), channel_id=1, source_target_pairs={{0,1},{1,0},{2,3},{3,2},{4,5},{5,4},{6,7},{7,6},{8,9},{9,8},{10,11... | collective-permute-start | bytes 638984 | tf_op jit(solution)/shard_map/ppermute | solution.py:443

commit v19 on v18

--- a/solution.py
+++ b/solution.py
@@ -379,6 +379,7 @@
 ):
     width, n = gx_ref.shape
     ny = q_ref.shape[1]
+    half = ny // 2
     yd = y_ref.shape[1]
     base = yd * width // LANES
     count = ny // LANES
@@ -390,28 +391,15 @@
         move.start()
         moves.append(move)
 
-    log_row = la_ref[...] - jnp.log(r_ref[...])
-    f_ref[...] = norm_ref[...] / width + EPSILON * (kappa * b_ref[...] - log_row)
-    leave(f_ref, f_hbm)
     total = got_ref[0].astype(F32)
     for k in range(1, got_ref.shape[0]):
         total = total + got_ref[k].astype(F32)
     sums = total[base : base + count] + total[base + count : base + 2 * count]
     sum_ref[...] = sums
-    colsum = own_part(sum_ref, yd)
-    c_term = own_part(c_ref, yd)
-    own = y_ref[0].astype(F32)
-    gy_ref[...] = unpack(total[:base], yd).T * (
-        jnp.exp(own[:, width + 6 : width + 7]) * to_column(1.0 / colsum)
-    )
-    leave(gy_ref, gy_hbm)
-    norm = to_row(jnp.sum(own[:, :width] * own[:, :width], axis=1, keepdims=True))
-    pot_ref[...] = norm / width - EPSILON * (jnp.log(colsum) - kappa * c_term)
-    leave(pot_ref, pot_hbm)
-    half = ny // 2
     yt = jnp.concatenate([ym_ref[:width, :], yo_ref[:width, :]], axis=1)
     stack(ys_ref, width, yt, q_ref[...] / from_lanes(sums))
-    for k in range(n // TILE):
+
+    def tile(k):
         t = slice(k * TILE, (k + 1) * TILE)
         product = jnp.dot(ys_ref[:, :half], km_ref[:, t], preferred_element_type=F32) + jnp.dot(
             ys_ref[:, half:], ko_ref[:, t], preferred_element_type=F32
@@ -419,6 +407,23 @@
         moved, weight = unstack(product, width)
         gx_ref[:, t] = (xa_ref[:width, t].astype(F32) * weight - moved) * (wr_ref[:, t] * (1.0 / ny))
         leave(gx_ref.at[:, t], gx_hbm.at[:, t])
+
+    tile(0)
+    log_row = la_ref[...] - jnp.log(r_ref[...])
+    f_ref[...] = norm_ref[...] / width + EPSILON * (kappa * b_ref[...] - log_row)
+    leave(f_ref, f_hbm)
+    colsum = own_part(sum_ref, yd)
+    c_term = own_part(c_ref, yd)
+    own = y_ref[0].astype(F32)
+    gy_ref[...] = unpack(total[:base], yd).T * (
+        jnp.exp(own[:, width + 6 : width + 7]) * to_column(1.0 / colsum)
+    )
+    leave(gy_ref, gy_hbm)
+    norm = to_row(jnp.sum(own[:, :width] * own[:, :width], axis=1, keepdims=True))
+    pot_ref[...] = norm / width - EPSILON * (jnp.log(colsum) - kappa * c_term)
+    leave(pot_ref, pot_hbm)
+    for k in range(1, n // TILE):
+        tile(k)
     for move in moves:
         move.wait()
 

time: 50.3 us -> 50.3 us (level)
  no operation moved by 1% of the time
where the time goes in v19:
time: 50.3 us; the launch traced here: 50 us
  blocking collectives  34 us (68%)
  Pallas kernels  13 us (26%)
  waiting for transfers between devices  1.54 us (3%)
  between operations  0.71 us (1%)
  local copies, waits for them, and re-layouts  0.69 us (1%)
    all_to_all x1, blocking collectives, on_device(): y_mine = lax.all_to_all(y_own, 'row', 0, 0, tiled=True)  14.6 us
    pallas_call x8, Pallas kernels, call(): pl.pallas_call(kernel, out_shape=outs, in_specs=[pl.BlockSpec(memory_spac...  13 us
    all_to_all x1, blocking collectives, on_device(): part = lax.all_to_all(part, 'row', 0, 0, tiled=True)  9.96 us
    all_to_all x1, blocking collectives, on_device(): lse = lax.all_to_all(lse, AXES, 0, 0, tiled=True)  9.48 us
    ppermute x2, waiting for transfers between devices, swap(): return lax.ppermute(value, 'col', [(0, 1), (1, 0)])  1.54 us
  transfers between devices with their start and end apart: 2, of which 2 were waited for; matrix products, arithmetic and copies ran while one was open for 0% of the time, Pallas kernels for 3%

profile of v19, /device:TPU:0, one launch (start us, length us, event | category | flops | bytes accessed | tf_op | source)
XLA Modules:
  0.0 50.0 jit_solution(12283763363553464836)
XLA Ops:
  0.6 0.0 copy-start.1
  0.7 0.0 copy-start.2
  0.7 0.0 copy-start.3
  0.7 0.7 %copy-done.1 = bf16[64,96]{1,0:T(8,128)(2,1)S(1)} copy-done((bf16[64,96]{1,0:T(8,128)(2,1)S(1)}, bf16[64,96]{1,0:T(8,128)(2,1)}, u32[]{:S(2)}) %copy-start.1) | copy-done | bytes 12312
  1.3 0.0 copy-done.2
  1.4 0.0 copy-done.3
  1.4 0.2 shard_map.76
  1.5 0.0 copy-start
  1.6 14.6 %all_to_all.15.mine_ref = bf16[8,64,128]{2,1,0:T(8,128)(2,1)S(1)} all-to-all(bf16[8,64,128]{2,1,0:T(8,128)(2,1)S(1)} %get-tuple-element.32.y_ref), channel_id=1, replica_groups=mesh['groups'=2,'row'=8,'col'=2] {'row'}, dimensions={0} | all-to-all | bytes 262144 | tf_op jit(solution)/shard_map/all_to_all | solution.py:474
  16.1 0.0 collective-permute-start
  16.1 0.0 copy-done
  16.1 0.7 %shard_map.77 = (bf16[128,1024]{1,0:T(8,128)(2,1)S(1)}, bf16[128,512]{1,0:T(8,128)(2,1)S(1)}, f32[1,1024]{1,0:T(1,128)S(1)}, f32[1,1024]{1,0:T(1,128)S(1)}, bf16[512,1024]{1,0:T(8,128)(2,1)S(1)}) custom-call(bf16[96,1024]{1,0:T(8,128)(2,1)S(1)} %bitcast.6, bf16[8,64,128]{2,1,0:T(8,128)(2,1)S(1)} %all_to_all.15.mine_ref), custom_call_target="tpu_custom_call" | custom-call | tf_op jit(solution)/shard_map/pallas_call | solution.py:432
  16.9 0.6 %collective-permute-done.other_ref = bf16[8,64,128]{2,1,0:T(8,128)(2,1)S(1)} collective-permute-done((bf16[8,64,128]{2,1,0:T(8,128)(2,1)S(1)}, bf16[8,64,128]{2,1,0:T(8,128)(2,1)S(1)}, u32[]{:S(2)}, u32[]{:S(2)}) %collective-permute-start) | collective-permute-done | bytes 131104 | tf_op jit(solution)/shard_map/ppermute | solution.py:448
  17.5 8.8 %shard_map.78 = (bf16[128,512]{1,0:T(8,128)(2,1)S(1)}, bf16[512,1024]{1,0:T(8,128)(2,1)S(1)}, bf16[512,1024]{1,0:T(8,128)(2,1)S(1)}, f32[1,1024]{1,0:T(1,128)S(1...) custom-call(bf16[128,1024]{1,0:T(8,128)(2,1)S(1)} %get-tuple-element.33.xa_ref, ...), custom_call_target="tpu_custom_call" | custom-call | tf_op jit(solution)/shard_map/pallas_call | solution.py:432
  26.2 9.5 %all_to_all.16.l_ref = f32[16,8,128]{2,1,0:T(8,128)S(1)} all-to-all(f32[16,8,128]{2,1,0:T(8,128)S(1)} %get-tuple-element.40), channel_id=1, replica_groups=mesh['groups'=2,'row'=8,'col'=2] {'row','col'}, dimensions={0} | all-to-all | bytes 131072 | tf_op jit(solution)/shard_map/all_to_all | solution.py:494
  35.7 1.2 %shard_map.79 = (f32[1,1024]{1,0:T(1,128)S(1)}, f32[1,1024]{1,0:T(1,128)S(1)}, f32[1,1024]{1,0:T(1,128)S(1)}, f32[8,128]{1,0:T(8,128)S(1)}, bf16[208,1024]{1,0:T...) custom-call(bf16[128,1024]{1,0:T(8,128)(2,1)S(1)} %get-tuple-element.33.xa_ref, ...), custom_call_target="tpu_custom_call" | custom-call | tf_op jit(solution)/shard_map/pallas_call | solution.py:432
  36.9 0.1 collective-permute-start.1
  37.0 0.5 %shard_map.80 = (f32[96,512]{1,0:T(8,128)S(1)}, f32[1,1024]{1,0:T(1,128)S(1)}, f32[1,1024]{1,0:T(1,128)S(1)}) custom-call(bf16[128,1024]{1,0:T(8,128)(2,1)S(1)} %get-tuple-element.33.xa_ref, bf16[208,1024]{1,0:T(8,128)(2,1)S(1)} %get-tuple-element.45.xs_ref, f32[1,1024]{1,0:T(1,128)S(1)} %get-tuple-element.46.v_ref, ...), custom_call_target="tpu_custom_call" | custom-call | tf_op jit(solution)/shard_map/pallas_call | solution.py:432
  37.5 0.9 %collective-permute-done.1.got_ref = f32[104,512]{1,0:T(8,128)S(1)} collective-permute-done((f32[104,512]{1,0:T(8,128)S(1)}, f32[104,512]{1,0:T(8,128)S(1)}, u32[]{:S(2)}, u32[]{:S(2)}) %collective-permute-start.1) | collective-permute-done | bytes 213024 | tf_op jit(solution)/shard_map/ppermute | solution.py:448
  38.4 0.1 shard_map.81
  38.5 10.0 %all_to_all.17.got_ref = bf16[8,64,128]{2,1,0:T(8,128)(2,1)S(1)} all-to-all(bf16[8,64,128]{2,1,0:T(8,128)(2,1)S(1)} %shard_map.81), channel_id=1, replica_groups=mesh['groups'=2,'row'=8,'col'=2] {'row'}, dimensions={0} | all-to-all | bytes 262144 | tf_op jit(solution)/shard_map/all_to_all | solution.py:511
  48.5 1.5 %shard_map.82 = (f32[1,1024]{1,0:T(1,128)}, f32[1,64]{1,0:T(1,128)}, f32[96,1024]{1,0:T(8,128)}, f32[64,96]{1,0:T(8,128)}) custom-call(bf16[128,1024]{1,0:T(8,128)(2,1)S(1)} %get-tuple-element.33.xa_ref, f32[1,1024]{1,0:T(1,128)S(1)} %get-tuple-element.34.la_ref, f32[1,1024]{1,0:T(1,128)S(1)} %get-tuple-element.48.norm_ref, ...), custom_call_target="tpu_custom_call" | custom-call | tf_op jit(solution)/shard_map/pallas_call | solution.py:432
  (1 shorter events, 0.0 us)
Async XLA Ops:
  0.6 0.7 %copy-start.1 = (bf16[64,96]{1,0:T(8,128)(2,1)S(1)}, bf16[64,96]{1,0:T(8,128)(2,1)}, u32[]{:S(2)}) copy-start(bf16[64,96]{1,0:T(8,128)(2,1)} %y_ref.1) | copy-start | bytes 36868
  0.7 0.7 %copy-start.2 = (bf16[1024]{0:T(1024)(128)(2,1)S(1)}, bf16[1024]{0:T(1024)(128)(2,1)}, u32[]{:S(2)}) copy-start(bf16[1024]{0:T(1024)(128)(2,1)} %param.6) | copy-start | bytes 6148
  0.7 0.7 %copy-start.3 = (bf16[64]{0:T(256)(128)(2,1)S(1)}, bf16[64]{0:T(256)(128)(2,1)}, u32[]{:S(2)}) copy-start(bf16[64]{0:T(256)(128)(2,1)} %param.7) | copy-start | bytes 388
  1.5 14.6 %copy-start = (bf16[1024,96]{0,1:T(8,128)(2,1)S(1)}, bf16[1024,96]{0,1:T(8,128)(2,1)}, u32[]{:S(2)}) copy-start(bf16[1024,96]{0,1:T(8,128)(2,1)} %param.4) | copy-start | bytes 589828
  16.1 1.3 %collective-permute-start = (bf16[8,64,128]{2,1,0:T(8,128)(2,1)S(1)}, bf16[8,64,128]{2,1,0:T(8,128)(2,1)S(1)}, u32[]{:S(2)}, u32[]{:S(2)}) collective-permute-start(bf16[8,64,128]{2,1,0:T(8,128)(2,1)S(1)} %all_to_all.15.mine_ref), channel_id=1, source_target_pairs={{0,1},{1,0},{2,3},{3,2},{4,5},{5,4},{6,7},{7,6},{8,9},{9,8},{10,11... | collective-permute-start | bytes 393224 | tf_op jit(solution)/shard_map/ppermute | solution.py:448
  36.9 1.5 %collective-permute-start.1 = (f32[104,512]{1,0:T(8,128)S(1)}, f32[104,512]{1,0:T(8,128)S(1)}, u32[]{:S(2)}, u32[]{:S(2)}) collective-permute-start(f32[104,512]{1,0:T(8,128)S(1)} %get-tuple-element.55), channel_id=1, source_target_pairs={{0,1},{1,0},{2,3},{3,2},{4,5},{5,4},{6,7},{7,6},{8,9},{9,8},{10,11... | collective-permute-start | bytes 638984 | tf_op jit(solution)/shard_map/ppermute | solution.py:448

commit v20 on v18

--- a/solution.py
+++ b/solution.py
@@ -91,7 +91,8 @@
 def exp_sum_down(z_ref, rows, scale, shift, keep=None):
     total = jnp.zeros((STEP, TILE), F32)
     for r in range(0, rows, STEP):
-        value = jnp.exp2((z_ref[r : r + STEP, :] - shift) * scale)
+        z = z_ref[r : r + STEP, :]
+        value = jnp.exp2((z if shift is None else z - shift) * scale)
         total = total + value
         if keep is not None:
             keep(r, value)
@@ -188,6 +189,7 @@
         total_ref[:, t] = exp_sum_down(z, half, scale, base, keep)
 
     for_tiles(n, product, z_ref, use)
+    xa_ref[width:, :] = extras_x(rows_index(n), -base_ref[...]).astype(BF16)
     yt_ref[...] = mine.T
 
 
@@ -211,7 +213,7 @@
         def keep(r, value):
             ko_ref[r : r + STEP, t] = value.astype(BF16)
 
-        sum_ref[:, t] = exp_sum_down(z, half, scale, base_ref[:, t], keep) + total_ref[:, t]
+        sum_ref[:, t] = exp_sum_down(z, half, scale, None, keep) + total_ref[:, t]
 
     for_tiles(n, product, z_ref, use)
     yt_ref[...] = other.T
@@ -256,7 +258,7 @@
                 value = jnp.exp2((scores(y_ref, xa_ref, t) - b_ref[...]) * scale)
                 sum_ref[...] = sum_ref[...] + jnp.sum(value, axis=0, keepdims=True)
 
-        b_ref[...] = (log_a - jnp.log(sum_ref[...])) * (LOG2E / scale) - b_ref[...]
+        b_ref[...] = (log_a - jnp.log(sum_ref[...])) * (LOG2E / scale) - b_ref[...] - base_ref[...]
         xb_ref[:width, :] = xa_ref[:width, :]
         xb_ref[width:, :] = extras_x(rows_index(n), b_ref[...]).astype(BF16)
         omega_ref[...] = jnp.ones((1, n), F32)

time: 50.3 us -> 50.3 us (level)
  no operation moved by 1% of the time
where the time goes in v20:
time: 50.3 us; the launch traced here: 49.9 us
  blocking collectives  34 us (68%)
  Pallas kernels  13 us (26%)
  waiting for transfers between devices  1.51 us (3%)
  between operations  0.72 us (1%)
  local copies, waits for them, and re-layouts  0.69 us (1%)
    all_to_all x1, blocking collectives, on_device(): y_mine = lax.all_to_all(y_own, 'row', 0, 0, tiled=True)  14.6 us
    pallas_call x8, Pallas kernels, call(): pl.pallas_call(kernel, out_shape=outs, in_specs=[pl.BlockSpec(memory_spac...  13 us
    all_to_all x1, blocking collectives, on_device(): part = lax.all_to_all(part, 'row', 0, 0, tiled=True)  9.96 us
    all_to_all x1, blocking collectives, on_device(): lse = lax.all_to_all(lse, AXES, 0, 0, tiled=True)  9.48 us
    ppermute x2, waiting for transfers between devices, swap(): return lax.ppermute(value, 'col', [(0, 1), (1, 0)])  1.51 us
  transfers between devices with their start and end apart: 2, of which 2 were waited for; matrix products, arithmetic and copies ran while one was open for 0% of the time, Pallas kernels for 3%

profile of v20, /device:TPU:0, one launch (start us, length us, event | category | flops | bytes accessed | tf_op | source)
XLA Modules:
  0.0 49.9 jit_solution(8457584917056243303)
XLA Ops:
  0.6 0.0 copy-start.1
  0.7 0.0 copy-start.2
  0.7 0.0 copy-start.3
  0.7 0.7 %copy-done.1 = bf16[64,96]{1,0:T(8,128)(2,1)S(1)} copy-done((bf16[64,96]{1,0:T(8,128)(2,1)S(1)}, bf16[64,96]{1,0:T(8,128)(2,1)}, u32[]{:S(2)}) %copy-start.1) | copy-done | bytes 12312
  1.3 0.0 copy-done.2
  1.4 0.0 copy-done.3
  1.4 0.2 shard_map.76
  1.5 0.0 copy-start
  1.6 14.6 %all_to_all.15.mine_ref = bf16[8,64,128]{2,1,0:T(8,128)(2,1)S(1)} all-to-all(bf16[8,64,128]{2,1,0:T(8,128)(2,1)S(1)} %get-tuple-element.32.y_ref), channel_id=1, replica_groups=mesh['groups'=2,'row'=8,'col'=2] {'row'}, dimensions={0} | all-to-all | bytes 262144 | tf_op jit(solution)/shard_map/all_to_all | solution.py:471
  16.1 0.0 collective-permute-start
  16.1 0.0 copy-done
  16.1 0.8 %shard_map.77 = (bf16[128,1024]{1,0:T(8,128)(2,1)S(1)}, bf16[128,512]{1,0:T(8,128)(2,1)S(1)}, f32[1,1024]{1,0:T(1,128)S(1)}, f32[1,1024]{1,0:T(1,128)S(1)}, bf16[512,1024]{1,0:T(8,128)(2,1)S(1)}) custom-call(bf16[96,1024]{1,0:T(8,128)(2,1)S(1)} %bitcast.6, bf16[8,64,128]{2,1,0:T(8,128)(2,1)S(1)} %all_to_all.15.mine_ref), custom_call_target="tpu_custom_call" | custom-call | tf_op jit(solution)/shard_map/pallas_call | solution.py:429
  16.9 0.6 %collective-permute-done.other_ref = bf16[8,64,128]{2,1,0:T(8,128)(2,1)S(1)} collective-permute-done((bf16[8,64,128]{2,1,0:T(8,128)(2,1)S(1)}, bf16[8,64,128]{2,1,0:T(8,128)(2,1)S(1)}, u32[]{:S(2)}, u32[]{:S(2)}) %collective-permute-start) | collective-permute-done | bytes 131104 | tf_op jit(solution)/shard_map/ppermute | solution.py:445
  17.5 8.7 %shard_map.78 = (bf16[128,512]{1,0:T(8,128)(2,1)S(1)}, bf16[512,1024]{1,0:T(8,128)(2,1)S(1)}, bf16[512,1024]{1,0:T(8,128)(2,1)S(1)}, f32[1,1024]{1,0:T(1,128)S(1...) custom-call(bf16[128,1024]{1,0:T(8,128)(2,1)S(1)} %get-tuple-element.33.xa_ref, ...), custom_call_target="tpu_custom_call" | custom-call | tf_op jit(solution)/shard_map/pallas_call | solution.py:429
  26.2 9.5 %all_to_all.16.l_ref = f32[16,8,128]{2,1,0:T(8,128)S(1)} all-to-all(f32[16,8,128]{2,1,0:T(8,128)S(1)} %get-tuple-element.40), channel_id=1, replica_groups=mesh['groups'=2,'row'=8,'col'=2] {'row','col'}, dimensions={0} | all-to-all | bytes 131072 | tf_op jit(solution)/shard_map/all_to_all | solution.py:491
  35.7 1.2 %shard_map.79 = (f32[1,1024]{1,0:T(1,128)S(1)}, f32[1,1024]{1,0:T(1,128)S(1)}, f32[1,1024]{1,0:T(1,128)S(1)}, f32[8,128]{1,0:T(8,128)S(1)}, bf16[208,1024]{1,0:T...) custom-call(bf16[128,1024]{1,0:T(8,128)(2,1)S(1)} %get-tuple-element.33.xa_ref, ...), custom_call_target="tpu_custom_call" | custom-call | tf_op jit(solution)/shard_map/pallas_call | solution.py:429
  36.9 0.1 collective-permute-start.1
  36.9 0.5 %shard_map.80 = (f32[96,512]{1,0:T(8,128)S(1)}, f32[1,1024]{1,0:T(1,128)S(1)}, f32[1,1024]{1,0:T(1,128)S(1)}) custom-call(bf16[128,1024]{1,0:T(8,128)(2,1)S(1)} %get-tuple-element.33.xa_ref, bf16[208,1024]{1,0:T(8,128)(2,1)S(1)} %get-tuple-element.45.xs_ref, f32[1,1024]{1,0:T(1,128)S(1)} %get-tuple-element.46.v_ref, ...), custom_call_target="tpu_custom_call" | custom-call | tf_op jit(solution)/shard_map/pallas_call | solution.py:429
  37.5 0.9 %collective-permute-done.1.got_ref = f32[104,512]{1,0:T(8,128)S(1)} collective-permute-done((f32[104,512]{1,0:T(8,128)S(1)}, f32[104,512]{1,0:T(8,128)S(1)}, u32[]{:S(2)}, u32[]{:S(2)}) %collective-permute-start.1) | collective-permute-done | bytes 213024 | tf_op jit(solution)/shard_map/ppermute | solution.py:445
  38.4 0.1 shard_map.81
  38.5 10.0 %all_to_all.17.got_ref = bf16[8,64,128]{2,1,0:T(8,128)(2,1)S(1)} all-to-all(bf16[8,64,128]{2,1,0:T(8,128)(2,1)S(1)} %shard_map.81), channel_id=1, replica_groups=mesh['groups'=2,'row'=8,'col'=2] {'row'}, dimensions={0} | all-to-all | bytes 262144 | tf_op jit(solution)/shard_map/all_to_all | solution.py:508
  48.5 1.5 %shard_map.82 = (f32[1,1024]{1,0:T(1,128)}, f32[1,64]{1,0:T(1,128)}, f32[96,1024]{1,0:T(8,128)}, f32[64,96]{1,0:T(8,128)}) custom-call(bf16[128,1024]{1,0:T(8,128)(2,1)S(1)} %get-tuple-element.33.xa_ref, f32[1,1024]{1,0:T(1,128)S(1)} %get-tuple-element.34.la_ref, f32[1,1024]{1,0:T(1,128)S(1)} %get-tuple-element.48.norm_ref, ...), custom_call_target="tpu_custom_call" | custom-call | tf_op jit(solution)/shard_map/pallas_call | solution.py:429
  (1 shorter events, 0.0 us)
Async XLA Ops:
  0.6 0.7 %copy-start.1 = (bf16[64,96]{1,0:T(8,128)(2,1)S(1)}, bf16[64,96]{1,0:T(8,128)(2,1)}, u32[]{:S(2)}) copy-start(bf16[64,96]{1,0:T(8,128)(2,1)} %y_ref.1) | copy-start | bytes 36868
  0.7 0.7 %copy-start.2 = (bf16[1024]{0:T(1024)(128)(2,1)S(1)}, bf16[1024]{0:T(1024)(128)(2,1)}, u32[]{:S(2)}) copy-start(bf16[1024]{0:T(1024)(128)(2,1)} %param.6) | copy-start | bytes 6148
  0.7 0.7 %copy-start.3 = (bf16[64]{0:T(256)(128)(2,1)S(1)}, bf16[64]{0:T(256)(128)(2,1)}, u32[]{:S(2)}) copy-start(bf16[64]{0:T(256)(128)(2,1)} %param.7) | copy-start | bytes 388
  1.5 14.6 %copy-start = (bf16[1024,96]{0,1:T(8,128)(2,1)S(1)}, bf16[1024,96]{0,1:T(8,128)(2,1)}, u32[]{:S(2)}) copy-start(bf16[1024,96]{0,1:T(8,128)(2,1)} %param.4) | copy-start | bytes 589828
  16.1 1.3 %collective-permute-start = (bf16[8,64,128]{2,1,0:T(8,128)(2,1)S(1)}, bf16[8,64,128]{2,1,0:T(8,128)(2,1)S(1)}, u32[]{:S(2)}, u32[]{:S(2)}) collective-permute-start(bf16[8,64,128]{2,1,0:T(8,128)(2,1)S(1)} %all_to_all.15.mine_ref), channel_id=1, source_target_pairs={{0,1},{1,0},{2,3},{3,2},{4,5},{5,4},{6,7},{7,6},{8,9},{9,8},{10,11... | collective-permute-start | bytes 393224 | tf_op jit(solution)/shard_map/ppermute | solution.py:445
  36.9 1.5 %collective-permute-start.1 = (f32[104,512]{1,0:T(8,128)S(1)}, f32[104,512]{1,0:T(8,128)S(1)}, u32[]{:S(2)}, u32[]{:S(2)}) collective-permute-start(f32[104,512]{1,0:T(8,128)S(1)} %get-tuple-element.55), channel_id=1, source_target_pairs={{0,1},{1,0},{2,3},{3,2},{4,5},{5,4},{6,7},{7,6},{8,9},{9,8},{10,11... | collective-permute-start | bytes 638984 | tf_op jit(solution)/shard_map/ppermute | solution.py:445

commit v21 on v20

--- a/solution.py
+++ b/solution.py
@@ -195,7 +195,7 @@
 
 def first_kernel(
     xa_ref, la_ref, mine_ref, other_ref, base_ref, total_ref, km0_ref,
-    yt_ref, km_ref, ko_ref, b_ref, omega_ref, mu_ref, l_ref, xb_ref, z_ref, sum_ref, lse_ref, sem,
+    yt_ref, km_ref, ko_ref, b_ref, omega_ref, mu_ref, l_ref, xb_ref, z_ref, sum_ref, lse_ref,
 ):
     rows, yd, depth = other_ref.shape
     n = xa_ref.shape[1]
@@ -203,8 +203,6 @@
     half = rows * yd
     scale = kappa_of(width) * LOG2E
     other = other_ref[...].reshape(half, depth)
-    move = pltpu.make_async_copy(km0_ref, km_ref, sem)
-    move.start()
 
     def product(t):
         return jnp.dot(other, xa_ref[:, t], preferred_element_type=F32)
@@ -223,11 +221,11 @@
     omega = jnp.exp(log_a) * (2.0**LIFT / total)
     omega_ref[...] = omega
     left = piece_rows(omega)
-    move.wait()
+    km_ref[...] = km0_ref[...]
     sums = jnp.concatenate(
         [
             sum_pieces(lax.dot_general(left, ref[...], ACROSS, preferred_element_type=F32))
-            for ref in (km_ref, ko_ref)
+            for ref in (km0_ref, ko_ref)
         ],
         axis=1,
     )
@@ -485,7 +483,7 @@
             shape((depth, half), BF16), shape((half, n), BF16), shape((half, n), BF16), shape((1, n)),
             shape((1, n)), shape((1, ny)), shape((2 * rows, count, LANES)),
         ),
-        [vmem((depth, n), BF16), vmem((slots, half, TILE), F32), vmem((1, n), F32), vmem((1, ny), F32), pltpu.SemaphoreType.DMA],
+        [vmem((depth, n), BF16), vmem((slots, half, TILE), F32), vmem((1, n), F32), vmem((1, ny), F32)],
         limit, xa, log_a, y_mine, y_other, base, total, kept_mine,
     )
     lse = lax.all_to_all(lse, AXES, 0, 0, tiled=True)

time: 50.3 us -> 50.1 us (level)
  no operation moved by 1% of the time
where the time goes in v21:
time: 50.1 us; the launch traced here: 49.8 us
  blocking collectives  34 us (68%)
  Pallas kernels  12.8 us (26%)
  waiting for transfers between devices  1.51 us (3%)
  between operations  0.72 us (1%)
  local copies, waits for them, and re-layouts  0.69 us (1%)
    all_to_all x1, blocking collectives, on_device(): y_mine = lax.all_to_all(y_own, 'row', 0, 0, tiled=True)  14.6 us
    pallas_call x8, Pallas kernels, call(): pl.pallas_call(kernel, out_shape=outs, in_specs=[pl.BlockSpec(memory_spac...  12.8 us
    all_to_all x1, blocking collectives, on_device(): part = lax.all_to_all(part, 'row', 0, 0, tiled=True)  9.96 us
    all_to_all x1, blocking collectives, on_device(): lse = lax.all_to_all(lse, AXES, 0, 0, tiled=True)  9.48 us
    ppermute x2, waiting for transfers between devices, swap(): return lax.ppermute(value, 'col', [(0, 1), (1, 0)])  1.51 us
  transfers between devices with their start and end apart: 2, of which 2 were waited for; matrix products, arithmetic and copies ran while one was open for 0% of the time, Pallas kernels for 3%

profile of v21, /device:TPU:0, one launch (start us, length us, event | category | flops | bytes accessed | tf_op | source)
XLA Modules:
  0.0 49.8 jit_solution(3130881572930144801)
XLA Ops:
  0.6 0.0 copy-start.1
  0.7 0.0 copy-start.2
  0.7 0.0 copy-start.3
  0.7 0.7 %copy-done.1 = bf16[64,96]{1,0:T(8,128)(2,1)S(1)} copy-done((bf16[64,96]{1,0:T(8,128)(2,1)S(1)}, bf16[64,96]{1,0:T(8,128)(2,1)}, u32[]{:S(2)}) %copy-start.1) | copy-done | bytes 12312
  1.3 0.0 copy-done.2
  1.4 0.0 copy-done.3
  1.4 0.2 shard_map.76
  1.5 0.0 copy-start
  1.6 14.6 %all_to_all.15.mine_ref = bf16[8,64,128]{2,1,0:T(8,128)(2,1)S(1)} all-to-all(bf16[8,64,128]{2,1,0:T(8,128)(2,1)S(1)} %get-tuple-element.32.y_ref), channel_id=1, replica_groups=mesh['groups'=2,'row'=8,'col'=2] {'row'}, dimensions={0} | all-to-all | bytes 262144 | tf_op jit(solution)/shard_map/all_to_all | solution.py:469
  16.1 0.0 collective-permute-start
  16.1 0.0 copy-done
  16.1 0.8 %shard_map.77 = (bf16[128,1024]{1,0:T(8,128)(2,1)S(1)}, bf16[128,512]{1,0:T(8,128)(2,1)S(1)}, f32[1,1024]{1,0:T(1,128)S(1)}, f32[1,1024]{1,0:T(1,128)S(1)}, bf16[512,1024]{1,0:T(8,128)(2,1)S(1)}) custom-call(bf16[96,1024]{1,0:T(8,128)(2,1)S(1)} %bitcast.6, bf16[8,64,128]{2,1,0:T(8,128)(2,1)S(1)} %all_to_all.15.mine_ref), custom_call_target="tpu_custom_call" | custom-call | tf_op jit(solution)/shard_map/pallas_call | solution.py:427
  16.9 0.6 %collective-permute-done.other_ref = bf16[8,64,128]{2,1,0:T(8,128)(2,1)S(1)} collective-permute-done((bf16[8,64,128]{2,1,0:T(8,128)(2,1)S(1)}, bf16[8,64,128]{2,1,0:T(8,128)(2,1)S(1)}, u32[]{:S(2)}, u32[]{:S(2)}) %collective-permute-start) | collective-permute-done | bytes 131104 | tf_op jit(solution)/shard_map/ppermute | solution.py:443
  17.5 8.6 %shard_map.78 = (bf16[128,512]{1,0:T(8,128)(2,1)S(1)}, bf16[512,1024]{1,0:T(8,128)(2,1)S(1)}, bf16[512,1024]{1,0:T(8,128)(2,1)S(1)}, f32[1,1024]{1,0:T(1,128)S(1...) custom-call(bf16[128,1024]{1,0:T(8,128)(2,1)S(1)} %get-tuple-element.33.xa_ref, ...), custom_call_target="tpu_custom_call" | custom-call | tf_op jit(solution)/shard_map/pallas_call | solution.py:427
  26.1 9.5 %all_to_all.16.l_ref = f32[16,8,128]{2,1,0:T(8,128)S(1)} all-to-all(f32[16,8,128]{2,1,0:T(8,128)S(1)} %get-tuple-element.40), channel_id=1, replica_groups=mesh['groups'=2,'row'=8,'col'=2] {'row','col'}, dimensions={0} | all-to-all | bytes 131072 | tf_op jit(solution)/shard_map/all_to_all | solution.py:489
  35.5 1.2 %shard_map.79 = (f32[1,1024]{1,0:T(1,128)S(1)}, f32[1,1024]{1,0:T(1,128)S(1)}, f32[1,1024]{1,0:T(1,128)S(1)}, f32[8,128]{1,0:T(8,128)S(1)}, bf16[208,1024]{1,0:T...) custom-call(bf16[128,1024]{1,0:T(8,128)(2,1)S(1)} %get-tuple-element.33.xa_ref, ...), custom_call_target="tpu_custom_call" | custom-call | tf_op jit(solution)/shard_map/pallas_call | solution.py:427
  36.7 0.1 collective-permute-start.1
  36.8 0.5 %shard_map.80 = (f32[96,512]{1,0:T(8,128)S(1)}, f32[1,1024]{1,0:T(1,128)S(1)}, f32[1,1024]{1,0:T(1,128)S(1)}) custom-call(bf16[128,1024]{1,0:T(8,128)(2,1)S(1)} %get-tuple-element.33.xa_ref, bf16[208,1024]{1,0:T(8,128)(2,1)S(1)} %get-tuple-element.45.xs_ref, f32[1,1024]{1,0:T(1,128)S(1)} %get-tuple-element.46.v_ref, ...), custom_call_target="tpu_custom_call" | custom-call | tf_op jit(solution)/shard_map/pallas_call | solution.py:427
  37.3 0.9 %collective-permute-done.1.got_ref = f32[104,512]{1,0:T(8,128)S(1)} collective-permute-done((f32[104,512]{1,0:T(8,128)S(1)}, f32[104,512]{1,0:T(8,128)S(1)}, u32[]{:S(2)}, u32[]{:S(2)}) %collective-permute-start.1) | collective-permute-done | bytes 213024 | tf_op jit(solution)/shard_map/ppermute | solution.py:443
  38.3 0.1 shard_map.81
  38.4 10.0 %all_to_all.17.got_ref = bf16[8,64,128]{2,1,0:T(8,128)(2,1)S(1)} all-to-all(bf16[8,64,128]{2,1,0:T(8,128)(2,1)S(1)} %shard_map.81), channel_id=1, replica_groups=mesh['groups'=2,'row'=8,'col'=2] {'row'}, dimensions={0} | all-to-all | bytes 262144 | tf_op jit(solution)/shard_map/all_to_all | solution.py:506
  48.3 1.5 %shard_map.82 = (f32[1,1024]{1,0:T(1,128)}, f32[1,64]{1,0:T(1,128)}, f32[96,1024]{1,0:T(8,128)}, f32[64,96]{1,0:T(8,128)}) custom-call(bf16[128,1024]{1,0:T(8,128)(2,1)S(1)} %get-tuple-element.33.xa_ref, f32[1,1024]{1,0:T(1,128)S(1)} %get-tuple-element.34.la_ref, f32[1,1024]{1,0:T(1,128)S(1)} %get-tuple-element.48.norm_ref, ...), custom_call_target="tpu_custom_call" | custom-call | tf_op jit(solution)/shard_map/pallas_call | solution.py:427
  (1 shorter events, 0.0 us)
Async XLA Ops:
  0.6 0.7 %copy-start.1 = (bf16[64,96]{1,0:T(8,128)(2,1)S(1)}, bf16[64,96]{1,0:T(8,128)(2,1)}, u32[]{:S(2)}) copy-start(bf16[64,96]{1,0:T(8,128)(2,1)} %y_ref.1) | copy-start | bytes 36868
  0.7 0.7 %copy-start.2 = (bf16[1024]{0:T(1024)(128)(2,1)S(1)}, bf16[1024]{0:T(1024)(128)(2,1)}, u32[]{:S(2)}) copy-start(bf16[1024]{0:T(1024)(128)(2,1)} %param.6) | copy-start | bytes 6148
  0.7 0.7 %copy-start.3 = (bf16[64]{0:T(256)(128)(2,1)S(1)}, bf16[64]{0:T(256)(128)(2,1)}, u32[]{:S(2)}) copy-start(bf16[64]{0:T(256)(128)(2,1)} %param.7) | copy-start | bytes 388
  1.5 14.6 %copy-start = (bf16[1024,96]{0,1:T(8,128)(2,1)S(1)}, bf16[1024,96]{0,1:T(8,128)(2,1)}, u32[]{:S(2)}) copy-start(bf16[1024,96]{0,1:T(8,128)(2,1)} %param.4) | copy-start | bytes 589828
  16.1 1.3 %collective-permute-start = (bf16[8,64,128]{2,1,0:T(8,128)(2,1)S(1)}, bf16[8,64,128]{2,1,0:T(8,128)(2,1)S(1)}, u32[]{:S(2)}, u32[]{:S(2)}) collective-permute-start(bf16[8,64,128]{2,1,0:T(8,128)(2,1)S(1)} %all_to_all.15.mine_ref), channel_id=1, source_target_pairs={{0,1},{1,0},{2,3},{3,2},{4,5},{5,4},{6,7},{7,6},{8,9},{9,8},{10,11... | collective-permute-start | bytes 393224 | tf_op jit(solution)/shard_map/ppermute | solution.py:443
  36.7 1.5 %collective-permute-start.1 = (f32[104,512]{1,0:T(8,128)S(1)}, f32[104,512]{1,0:T(8,128)S(1)}, u32[]{:S(2)}, u32[]{:S(2)}) collective-permute-start(f32[104,512]{1,0:T(8,128)S(1)} %get-tuple-element.55), channel_id=1, source_target_pairs={{0,1},{1,0},{2,3},{3,2},{4,5},{5,4},{6,7},{7,6},{8,9},{9,8},{10,11... | collective-permute-start | bytes 638984 | tf_op jit(solution)/shard_map/ppermute | solution.py:443
